TPU v7x, 32 devices: a whole 2x2x4 slice. The times are simulated.
32 devices in a mesh: seg: 8 (over y, x, core), bond: 4 (over z).
Axes of the slice: x: 2, y: 2, z: 4, core: 2. Of those that a mesh axis runs over, the one named last changes fastest.
Arguments:
- left_env: bfloat16 [8, 128, 128, 128], P('seg', None, 'bond'), may hold values from -1 to 1, as said below
- right_env: bfloat16 [8, 128, 128, 128], P('seg', None, 'bond'), may hold values from -1 to 1, as said below
- mpo_site: bfloat16 [8, 128, 32, 8, 8], P('seg', 'bond'), may hold values from -1 to 1, as said below
- start_state: bfloat16 [8, 128, 8, 128], P('seg'), may hold values from -6 to 6
Outputs:
- new_state: bfloat16 [8, 128, 8, 128], P('seg')
- new_left: bfloat16 [8, 128, 128, 128], P('seg', None, 'bond')
- energy: float32 [8], P('seg')
- second_image: float32 [8, 128, 8, 128], P('seg', 'bond')
Inputs may be any that keep to these rules, and one draw needn't show every extreme that they name: left_env[s, a, w, c] equals left_env[s, c, w, a]. right_env[s, b, w, c] equals right_env[s, c, w, b]. mpo_site[s, w, u, i, j] equals mpo_site[s, w, u, j, i].
All inputs are finite; a program needn't handle non-finite values.
Results may differ from a plain program's by a relative error of at most 0.01.
Values may be sent and summed in bfloat16 or wider, within the bound.
No kernel may reach another device: no remote copies, remote signals or barrier semaphores. Data moves between devices by JAX's collectives and lax.ppermute only.
A program may use at most 64 MiB of HBM per device.

v0:
```python
import jax
import jax.numpy as jnp
from jax import lax
from jax.sharding import PartitionSpec as P

epsilon = 1e-06


def shifted(value, axis, steps):
    count = lax.axis_size(axis)
    pairs = [(source, (source + steps) % count) for source in range(count)]
    return lax.ppermute(value, axis, pairs)


def first_section(left_block, vector):
    height, width_block = (left_block.shape[0], left_block.shape[1])
    return jnp.dot(
        left_block.reshape(height * width_block, height),
        vector.reshape(height, -1),
        preferred_element_type=jnp.float32,
    )


def couple_terms(mixed_terms, mpo_block, height, levels):
    width_block = mpo_block.shape[0]
    shaped = mixed_terms.astype(jnp.bfloat16).reshape(height, width_block, levels, height)
    return jnp.einsum(
        "vust,avtb->asub", mpo_block, shaped, preferred_element_type=jnp.float32
    ).astype(jnp.bfloat16)


def image_rows(coupled, right_block, row_count):
    height, levels, width_block, _ = coupled.shape
    flat_right = right_block.reshape(height, width_block * height)
    result = lax.dot_general(
        coupled.reshape(row_count * levels, width_block * height),
        flat_right,
        (((1,), (1,)), ((), ())),
        preferred_element_type=jnp.float32,
    )
    return result.reshape(row_count, levels, height)


def ritz_pair(rayleigh, curvature, residual_size):
    middle = 0.5 * (rayleigh + curvature)
    half_gap = 0.5 * (rayleigh - curvature)
    lowest = middle - jnp.sqrt(half_gap * half_gap + residual_size * residual_size)
    offset = lowest - rayleigh
    length_value = jnp.sqrt(residual_size * residual_size + offset * offset)
    return (lowest, residual_size / length_value, offset / length_value)


def grow_left(left_block, mpo_block, new_state):
    height, width_block, levels = (left_block.shape[0], left_block.shape[1], new_state.shape[1])
    coupled = couple_terms(first_section(left_block, new_state), mpo_block, height, levels)
    grown = lax.dot_general(
        new_state.reshape(height * levels, height),
        coupled.reshape(height * levels, width_block * height),
        (((0,), (0,)), ((), ())),
        preferred_element_type=jnp.float32,
    )
    return grown.astype(jnp.bfloat16).reshape(height, width_block, height)


def body(left_env, right_env, mpo_site, start_state):
    left_block = left_env[0]
    mpo_block = mpo_site[0]
    height, width_block, levels = (left_block.shape[0], left_block.shape[1], start_state.shape[2])
    entries = height * levels * height
    share_rows = height // lax.axis_size("bond")
    offset_rows = lax.axis_index("bond") * share_rows
    begin_vec = start_state[0].astype(jnp.float32)
    first_basis = begin_vec / jnp.sqrt(jnp.sum(begin_vec * begin_vec) / entries + epsilon)
    first_coupled = couple_terms(
        first_section(left_block, first_basis.astype(jnp.bfloat16)), mpo_block, height, levels
    )
    right_block = shifted(right_env, "seg", -1)[0]
    first_image = lax.psum(image_rows(first_coupled, right_block, height), "bond")
    rayleigh = jnp.sum(first_basis * first_image) / entries
    residual = first_image - rayleigh * first_basis
    residual_size = jnp.sqrt(jnp.sum(residual * residual) / entries + epsilon)
    second_basis = residual / residual_size
    second_coupled = couple_terms(
        first_section(left_block, second_basis.astype(jnp.bfloat16)), mpo_block, height, levels
    )
    second_image = lax.psum(image_rows(second_coupled, right_block, height), "bond")
    curvature = jnp.sum(second_basis * second_image) / entries
    lowest, first_weight, second_weight = ritz_pair(rayleigh, curvature, residual_size)
    new_state = (first_weight * first_basis + second_weight * second_basis).astype(jnp.bfloat16)
    image_share = lax.dynamic_slice_in_dim(second_image, offset_rows, share_rows, 0)
    new_left = grow_left(left_block, mpo_block, new_state)
    return (new_state[None], new_left[None], jnp.reshape(lowest, (1,)), image_share[None])


def solution(mesh):
    in_specs = (
        P("seg", None, "bond", None),
        P("seg", None, "bond", None),
        P("seg", "bond", None, None, None),
        P("seg", None, None, None),
    )
    out_specs = (
        P("seg", None, None, None),
        P("seg", None, "bond", None),
        P("seg"),
        P("seg", "bond", None, None),
    )
    return jax.shard_map(body, mesh=mesh, in_specs=in_specs, out_specs=out_specs, check_vma=False)
```

profile of v0, /device:TPU:0, one launch (start us, length us, event | category | flops | bytes accessed | tf_op | source)
XLA Modules:
  0.0 268.7 jit_solution(9610326620233881587)
XLA Ops:
  7.2 3.4 %collective-permute-start = (bf16[1,128,32,128]{3,2,1,0:T(8,128)(2,1)}, bf16[1,128,32,128]{3,2,1,0:T(8,128)(2,1)}, u32[]{:S(2)}, u32[]{:S(2)}) collective-permute-start(bf16[1,128,32,128]{3,2,1,0:T(8,128)(2,1)} %param.5), channel_id=1, source_target_pairs={{0,28},{4,0},{8,4},{12,8},{16,12},{20,16},{24,20},{28,24},{1,29},{... | collective-permute-start | bytes 3145736 | tf_op jit(solution)/shard_map/ppermute | solution.py:12
  10.6 1.7 fusion.12
  13.0 1.0 fusion.22
  14.2 5.6 %convert_bitcast_fusion.2 = bf16[4096,1024]{0,1:T(8,128)(2,1)} fusion(bf16[128,1024]{0,1:T(8,128)(2,1)S(1)} %bitcast.166, bf16[4096,128]{1,0:T(8,128)(2,1)S(1)} %bitcast.156), kind=kOutput, calls=%fused_computation.11 | convolution fusion | flops 1077936128 | bytes 9699328 | tf_op jit(solution)/shard_map/dot_general | solution.py:17
  19.8 12.0 %copy.20 = bf16[4096,1024]{1,0:T(8,128)(2,1)} copy(bf16[4096,1024]{0,1:T(8,128)(2,1)} %convert_bitcast_fusion.2) | data formatting | bytes 16777216 | tf_op jit(solution)/shard_map/convert_element_type | solution.py:26
  31.7 8.8 %copy.61 = bf16[512,8,8,128]{3,2,1,0:T(8,128)(2,1)} copy(bf16[512,8,8,128]{3,1,2,0:T(8,128)(2,1)} %bitcast.159) | data formatting | bytes 16777216
  40.5 9.0 %fusion.3 = bf16[128,8,32,128]{3,2,1,0:T(8,128)(2,1)} fusion(bf16[1,32,32,8,8]{2,4,3,1,0:T(8,128)(2,1)S(1)} %copy-done.2, bf16[128,32,8,128]{3,2,1,0:T(8,128)(2,1)} %bitcast.160), kind=kOutput, calls=%fused_computation.12 | convolution fusion | flops 2151677952 | bytes 16908288 | tf_op jit(solution)/shard_map/vust,avtb->asub/dot_general | solution.py:27
  49.6 13.3 %dot_general.33 = bf16[128,8,4096]{2,1,0:T(8,128)(2,1)} reshape(bf16[128,8,32,128]{3,2,1,0:T(8,128)(2,1)} %fusion.3) | data formatting | bytes 16777216 | tf_op jit(solution)/shard_map/dot_general | solution.py:35
  62.9 1.6 reshape.58
  64.5 5.7 %fusion.24 = f32[128,8,128]{2,1,0:T(8,128)S(1)} fusion(bf16[128,8,4096]{2,1,0:T(8,128)(2,1)} %dot_general.33, bf16[128,4096,1]{1,0,2:T(8,128)(2,1)S(1)} %reshape.58), kind=kOutput, calls=%fused_computation.39 | convolution fusion | flops 1073741824 | bytes 9961472 | tf_op jit(solution)/shard_map/dot_general | solution.py:35
  70.2 0.9 copy.40
  71.3 37.7 %all-reduce.3.cloned.1.call-done = f32[128,8,128]{2,0,1:T(8,128)} async-done(((f32[128,8,128]{2,0,1:T(8,128)}), f32[128,8,128]{2,0,1:T(8,128)}) %all-reduce.3.cloned.1.call-update) | async-done | bytes 524304 | tf_op jit(solution)/shard_map/psum | solution.py:78
  109.1 1.8 fusion.16
  111.5 1.8 multiply_reduce_fusion.1
  114.0 1.9 fusion.23
  115.9 1.8 copy.24
  117.6 6.5 %convert_bitcast_fusion.1 = bf16[4096,1024]{0,1:T(8,128)(2,1)} fusion(bf16[128,1024]{0,1:T(8,128)(2,1)} %bitcast.167, bf16[4096,128]{1,0:T(8,128)(2,1)S(1)} %bitcast.157), kind=kOutput, calls=%fused_computation.10 | convolution fusion | flops 1077936128 | bytes 9699328 | tf_op jit(solution)/shard_map/dot_general | solution.py:17
  124.2 12.0 %copy.25 = bf16[4096,1024]{1,0:T(8,128)(2,1)} copy(bf16[4096,1024]{0,1:T(8,128)(2,1)} %convert_bitcast_fusion.1) | data formatting | bytes 16777216 | tf_op jit(solution)/shard_map/convert_element_type | solution.py:26
  136.1 8.8 %copy.62 = bf16[512,8,8,128]{3,2,1,0:T(8,128)(2,1)} copy(bf16[512,8,8,128]{3,1,2,0:T(8,128)(2,1)} %bitcast.161) | data formatting | bytes 16777216
  144.9 9.0 %fusion.4 = bf16[128,8,32,128]{3,2,1,0:T(8,128)(2,1)} fusion(bf16[1,32,32,8,8]{2,4,3,1,0:T(8,128)(2,1)S(1)} %copy-done.2, bf16[128,32,8,128]{3,2,1,0:T(8,128)(2,1)} %bitcast.162), kind=kOutput, calls=%fused_computation.13 | convolution fusion | flops 2151677952 | bytes 16908288 | tf_op jit(solution)/shard_map/vust,avtb->asub/dot_general | solution.py:27
  153.9 13.3 %dot_general.37 = bf16[128,8,4096]{2,1,0:T(8,128)(2,1)} reshape(bf16[128,8,32,128]{3,2,1,0:T(8,128)(2,1)} %fusion.4) | data formatting | bytes 16777216 | tf_op jit(solution)/shard_map/dot_general | solution.py:35
  167.2 5.7 %fusion.25 = f32[128,8,128]{2,1,0:T(8,128)S(1)} fusion(bf16[128,8,4096]{2,1,0:T(8,128)(2,1)} %dot_general.37, bf16[128,4096,1]{1,0,2:T(8,128)(2,1)S(1)} %reshape.58), kind=kOutput, calls=%fused_computation.40 | convolution fusion | flops 1073741824 | bytes 9961472 | tf_op jit(solution)/shard_map/dot_general | solution.py:35
  172.9 0.9 copy.45
  173.8 38.4 %all-reduce.5.cloned.1.call-done = f32[128,8,128]{2,0,1:T(8,128)} async-done(((f32[128,8,128]{2,0,1:T(8,128)}), f32[128,8,128]{2,0,1:T(8,128)}) %all-reduce.5.cloned.1.call-update) | async-done | bytes 524304 | tf_op jit(solution)/shard_map/psum | solution.py:86
  212.3 1.8 multiply_reduce_fusion
  216.1 5.6 %convert_bitcast_fusion = bf16[4096,1024]{0,1:T(8,128)(2,1)} fusion(bf16[128,1024]{0,1:T(8,128)(2,1)S(1)} %bitcast.168, bf16[4096,128]{1,0:T(8,128)(2,1)S(1)} %bitcast.158), kind=kOutput, calls=%fused_computation.9 | convolution fusion | flops 1077936128 | bytes 9699328 | tf_op jit(solution)/shard_map/dot_general | solution.py:17
  221.6 12.0 %copy.31 = bf16[4096,1024]{1,0:T(8,128)(2,1)} copy(bf16[4096,1024]{0,1:T(8,128)(2,1)} %convert_bitcast_fusion) | data formatting | bytes 16777216 | tf_op jit(solution)/shard_map/convert_element_type | solution.py:26
  233.6 8.8 %copy.63 = bf16[512,8,8,128]{3,2,1,0:T(8,128)(2,1)} copy(bf16[512,8,8,128]{3,1,2,0:T(8,128)(2,1)} %bitcast.163) | data formatting | bytes 16777216
  242.4 9.0 %fusion.5 = bf16[128,8,32,128]{3,2,1,0:T(8,128)(2,1)} fusion(bf16[1,32,32,8,8]{2,4,3,1,0:T(8,128)(2,1)S(1)} %copy-done.2, bf16[128,32,8,128]{3,2,1,0:T(8,128)(2,1)} %bitcast.164), kind=kOutput, calls=%fused_computation.14 | convolution fusion | flops 2151677952 | bytes 16908288 | tf_op jit(solution)/shard_map/vust,avtb->asub/dot_general | solution.py:27
  251.4 6.5 %fusion.9 = bf16[16,8,32,128]{3,1,2,0:T(8,128)(2,1)S(1)} fusion(bf16[128,8,32,128]{3,2,1,0:T(8,128)(2,1)} %fusion.5, bf16[128,8,128]{2,0,1:T(8,128)(2,1)S(1)} %fusion.19), kind=kOutput, calls=%fused_computation.16 | convolution fusion | flops 1074266112 | bytes 9699328 | tf_op jit(solution)/shard_map/dot_general | solution.py:56
  257.9 1.2 copy.65
  259.1 0.9 constant_dynamic-slice_fusion
  (16 shorter events, 2.4 us)
Async XLA Ops:
  7.2 7.0 %copy-start = (bf16[1,128,32,128]{3,2,1,0:T(8,128)(2,1)S(1)}, bf16[1,128,32,128]{3,2,1,0:T(8,128)(2,1)}, u32[]{:S(2)}) copy-start(bf16[1,128,32,128]{3,2,1,0:T(8,128)(2,1)} %param.4) | copy-start | bytes 3145732
  7.2 101.9 %all-reduce.3.cloned.1.call-start = ((), (), s32[]{:S(2)}) async-start(), calls=%async_computation | async-start | bytes 1048576 | tf_op jit(solution)/shard_map/psum | solution.py:78
  7.2 55.7 %collective-permute-start = (bf16[1,128,32,128]{3,2,1,0:T(8,128)(2,1)}, bf16[1,128,32,128]{3,2,1,0:T(8,128)(2,1)}, u32[]{:S(2)}, u32[]{:S(2)}) collective-permute-start(bf16[1,128,32,128]{3,2,1,0:T(8,128)(2,1)} %param.5), channel_id=1, source_target_pairs={{0,28},{4,0},{8,4},{12,8},{16,12},{20,16},{24,20},{28,24},{1,29},{... | collective-permute-start | bytes 3145736 | tf_op jit(solution)/shard_map/ppermute | solution.py:12
  31.7 8.8 %copy-start.2 = (bf16[1,32,32,8,8]{2,4,3,1,0:T(8,128)(2,1)S(1)}, bf16[1,32,32,8,8]{2,4,3,1,0:T(8,128)(2,1)}, u32[]{:S(2)}) copy-start(bf16[1,32,32,8,8]{2,4,3,1,0:T(8,128)(2,1)} %param.6) | copy-start | bytes 393220
  62.9 46.2 %copy-start.1 = (bf16[1,128,8,128]{3,2,1,0:T(8,128)(2,1)S(1)}, bf16[1,128,8,128]{3,2,1,0:T(8,128)(2,1)}, u32[]{:S(2)}) copy-start(bf16[1,128,8,128]{3,2,1,0:T(8,128)(2,1)} %param.7) | copy-start | bytes 786436
  71.1 141.2 %all-reduce.5.cloned.1.call-start = ((), (), s32[]{:S(2)}) async-start(), calls=%async_computation.1 | async-start | bytes 1048576 | tf_op jit(solution)/shard_map/psum | solution.py:86
Sparse Core Ops, SparseCore 0:
  71.2 37.7 all-reduce.2
  174.0 38.2 all-reduce.4
where the time goes:
time: 271 us; the launch traced here: 269 us
  local copies, waits for them, and re-layouts  98 us (36%)
  waiting for transfers between devices  76.2 us (28%)
  matrix products  62.7 us (23%)
  between operations  18.1 us (7%)
  other arithmetic  10 us (4%)
  starting transfers between devices  3.65 us (1%)
    psum x1, waiting for transfers between devices, body(): lax.psum(image_rows(second_coupled, right_block, height), 'bond')  38.4 us
    psum x1, waiting for transfers between devices, body(): lax.psum(image_rows(first_coupled, right_block, height), 'bond')  37.7 us
    convert_element_type x3, local copies, waits for them, and re-layouts, couple_terms(): mixed_terms.astype(jnp.bfloat16)  35.9 us
    unnamed x11, local copies, waits for them, and re-layouts  28.4 us
    dot_general x4, local copies, waits for them, and re-layouts, image_rows(): lax.dot_general(coupled.reshape(row_count * levels, width_block * height)...  28.4 us
    dot_general x3, matrix products, couple_terms(): jnp.einsum('vust,avtb->asub', mpo_block, shaped, preferred_element_type=j...  27.1 us
    dot_general x3, matrix products, first_section(): jnp.dot(left_block.reshape(height * width_block, height), vector.reshape(...  17.6 us
    dot_general x2, matrix products, image_rows(): lax.dot_general(coupled.reshape(row_count * levels, width_block * height)...  11.4 us
  transfers between devices with their start and end apart: 3, of which 2 were waited for; matrix products, arithmetic and copies ran while one was open for 19% of the time, Pallas kernels for 0%

commit v1 on v0

v1 whole, which is shorter than its diff:
```python
import functools

import jax
import jax.numpy as jnp
from jax import lax
from jax.experimental import pallas as pl
from jax.experimental.pallas import tpu as pltpu
from jax.sharding import PartitionSpec as P

epsilon = 1e-06
bf16 = jnp.bfloat16
f32 = jnp.float32
VMEM_BLOCK = pl.BlockSpec(memory_space=pltpu.VMEM)
TAIL = 16


def params(megabytes):
    return pltpu.CompilerParams(vmem_limit_bytes=megabytes << 20)


def cost(flops, size):
    return pl.CostEstimate(flops=flops, bytes_accessed=size, transcendentals=0)


def by_level(rows_ref, height, levels):
    parts = [rows_ref[pl.ds(t, height, stride=levels), :] for t in range(levels)]
    return jnp.concatenate(parts, axis=1).astype(bf16)


def couple(left_ref, vector, mpo, coupled_ref, chunk):
    height, width, _ = left_ref.shape
    levels = vector.shape[1] // height
    right_width = mpo.shape[0] // levels

    def step(index, carry):
        first = index * chunk
        mixed = jnp.dot(
            left_ref[pl.ds(first, chunk)].reshape(chunk * width, height), vector, preferred_element_type=f32
        )
        for pair in range(0, chunk, 2):
            columns = []
            for row in (pair, pair + 1):
                pieces = [
                    mixed[row * width : (row + 1) * width, t * height : (t + 1) * height] for t in range(levels)
                ]
                columns.append(jnp.concatenate(pieces, axis=0))
            both = jnp.concatenate(columns, axis=1).astype(bf16)
            result = jnp.dot(mpo, both, preferred_element_type=f32)
            halves = [
                result[:, k * height : (k + 1) * height].reshape(right_width, levels, height) for k in (0, 1)
            ]
            place = pl.multiple_of((first + pair) * levels, 2 * levels)
            coupled_ref[:, pl.ds(place, 2 * levels), :] = jnp.concatenate(halves, axis=1).astype(bf16)
        return carry

    lax.fori_loop(0, height // chunk, step, 0)


def image(coupled_ref, right, image_ref, chunk):
    width, rows, _ = coupled_ref.shape

    def step(index, carry):
        place = pl.ds(pl.multiple_of(index * chunk, chunk), chunk)
        terms = jnp.concatenate([coupled_ref[u, place, :] for u in range(width)], axis=1)
        image_ref[place, :] = jnp.dot(terms, right[...], preferred_element_type=f32)
        return carry

    lax.fori_loop(0, rows // chunk, step, 0)


def first_kernel(start_ref, left_ref, mpo_ref, coupled_ref, basis_ref):
    height, levels, _ = start_ref.shape
    start = start_ref[...].astype(f32)
    scale = lax.rsqrt(jnp.sum(start * start) / (height * levels * height) + epsilon)
    basis_ref[...] = (start * scale).reshape(height * levels, height)
    couple(left_ref, by_level(basis_ref, height, levels), mpo_ref[...], coupled_ref, 32)


def first_image_kernel(coupled_ref, right_ref, image_ref, right_rows_ref, wide, total):
    height, width, _ = right_ref.shape
    wide[...] = right_ref[...].astype(f32).reshape(height * width, height)
    for u in range(width):
        right_rows_ref[u * height : (u + 1) * height, :] = wide[pl.ds(u, height, stride=width), :].astype(bf16)
    image(coupled_ref, right_rows_ref, total, 256)
    image_ref[...] = total[...].astype(bf16).reshape(image_ref.shape)


def second_kernel(
    image_ref, basis_ref, left_ref, mpo_ref, right_ref, coupled_ref, second_ref, send_ref, scalar_ref, total
):
    height, width, _ = left_ref.shape
    rows = basis_ref.shape[0]
    levels = rows // height
    entries = rows * height
    basis = basis_ref[...]
    first_image = image_ref[...].astype(f32)
    rayleigh = jnp.sum(basis * first_image) / entries
    residual = first_image - rayleigh * basis
    residual_size = jnp.sqrt(jnp.sum(residual * residual) / entries + epsilon)
    second_ref[...] = residual / residual_size
    couple(left_ref, by_level(second_ref, height, levels), mpo_ref[...], coupled_ref, 32)
    image(coupled_ref, right_ref, total, 256)
    value = jnp.sum(second_ref[...] * total[...]) / entries
    count, block, _ = send_ref.shape
    block -= TAIL
    send_ref[:, :block, :] = total[...].astype(bf16).reshape(count, block, height)
    high = value.astype(bf16).astype(f32)
    middle = (value - high).astype(bf16).astype(f32)
    low = value - high - middle
    lane = lax.broadcasted_iota(jnp.int32, (TAIL, height), 1)
    tail = jnp.where(lane == 0, high, jnp.where(lane == 1, middle, jnp.where(lane == 2, low, 0.0))).astype(bf16)
    for k in range(count):
        send_ref[k, block:, :] = tail
    scalar_ref[0] = rayleigh
    scalar_ref[1] = residual_size


def grow_kernel(basis_ref, second_ref, first_coupled_ref, second_coupled_ref, one_ref, cross_ref, two_ref, turned):
    width, _, height = first_coupled_ref.shape
    turned[:height, :] = basis_ref[...].T.astype(bf16)
    turned[height:, :] = second_ref[...].T.astype(bf16)
    for u in range(0, width, 2):
        both = jnp.concatenate([first_coupled_ref[u], first_coupled_ref[u + 1]], axis=1)
        from_first = jnp.dot(turned[...], both, preferred_element_type=f32)
        both = jnp.concatenate([second_coupled_ref[u], second_coupled_ref[u + 1]], axis=1)
        from_second = jnp.dot(turned[...], both, preferred_element_type=f32)
        for k in (0, 1):
            place = pl.ds(u + k, height, stride=width)
            lanes = slice(k * height, (k + 1) * height)
            one_ref[place, :] = from_first[:height, lanes]
            cross_ref[place, :] = from_first[height:, lanes] + from_second[:height, lanes]
            two_ref[place, :] = from_second[height:, lanes]


def last_kernel(parts_ref, scalar_ref, basis_ref, second_ref, one_ref, cross_ref, two_ref, state_ref, left_ref, energy_ref, share_ref):
    count, block, height = parts_ref.shape
    block -= TAIL
    tails = parts_ref[:, block:, :].astype(f32)
    lane = lax.broadcasted_iota(jnp.int32, tails.shape, 2)
    row = lax.broadcasted_iota(jnp.int32, tails.shape, 1)
    curvature = jnp.sum(jnp.where((lane < 3) & (row == 0), tails, 0.0))
    rayleigh, residual_size = scalar_ref[0], scalar_ref[1]
    middle = 0.5 * (rayleigh + curvature)
    half_gap = 0.5 * (rayleigh - curvature)
    lowest = middle - jnp.sqrt(half_gap * half_gap + residual_size * residual_size)
    offset = lowest - rayleigh
    length = jnp.sqrt(residual_size * residual_size + offset * offset)
    one, two = residual_size / length, offset / length
    energy_ref[...] = jnp.full(energy_ref.shape, lowest, f32)
    state_ref[...] = (one * basis_ref[...] + two * second_ref[...]).astype(bf16).reshape(state_ref.shape)
    grown = (one * one) * one_ref[...] + (one * two) * cross_ref[...] + (two * two) * two_ref[...]
    left_ref[...] = grown.astype(bf16).reshape(left_ref.shape)
    share = jnp.sum(parts_ref[:, :block, :].astype(f32), axis=0)
    share_ref[...] = share.reshape(share_ref.shape)


def on_chip(shape, dtype):
    return pltpu.VMEM(shape, dtype)


def scatter(blocks, axis):
    count = lax.axis_size(axis)
    me = lax.axis_index(axis)
    received = jnp.zeros_like(blocks)
    received = lax.dynamic_update_index_in_dim(received, lax.dynamic_index_in_dim(blocks, me, 0, False), me, 0)
    for step in order(count):
        pairs = [(source, (source + step) % count) for source in range(count)]
        there = lax.ppermute(lax.dynamic_index_in_dim(blocks, (me + step) % count, 0, False), axis, pairs)
        received = lax.dynamic_update_index_in_dim(received, there, (me - step) % count, 0)
    return received


def gather(block, axis):
    count = lax.axis_size(axis)
    me = lax.axis_index(axis)
    received = jnp.zeros((count,) + block.shape, block.dtype)
    received = lax.dynamic_update_index_in_dim(received, block, me, 0)
    for step in order(count):
        pairs = [(source, (source + step) % count) for source in range(count)]
        received = lax.dynamic_update_index_in_dim(received, lax.ppermute(block, axis, pairs), (me - step) % count, 0)
    return received


def order(count):
    return sorted(range(1, count), key=lambda step: -min(step, count - step))


def body(left_env, right_env, mpo_site, start_state):
    left, mpo, start = left_env[0], mpo_site[0], start_state[0]
    height, width, _ = left.shape
    levels = start.shape[1]
    rows = height * levels
    count = lax.axis_size("bond")
    block = rows // count
    segments = lax.axis_size("seg")
    pairs = [(source, (source - 1) % segments) for source in range(segments)]
    right = lax.ppermute(right_env, "seg", pairs)[0]
    mpo_rows = jnp.transpose(mpo, (1, 2, 3, 0)).reshape(width * levels, levels * width)
    apply_flops = 4 * rows * height * width * height

    coupled_shape = (width, rows, height)
    first_coupled, basis = pl.pallas_call(
        first_kernel,
        out_shape=(on_chip(coupled_shape, bf16), on_chip((rows, height), f32)),
        in_specs=[VMEM_BLOCK] * 3,
        out_specs=(VMEM_BLOCK,) * 2,
        compiler_params=params(24),
        cost_estimate=cost(2 * apply_flops, 8 << 20),
        name="first_coupled",
    )(start, left, mpo_rows)
    partial, right_rows = pl.pallas_call(
        first_image_kernel,
        out_shape=(on_chip((count, block, height), bf16), on_chip((width * height, height), bf16)),
        in_specs=[VMEM_BLOCK] * 2,
        out_specs=(VMEM_BLOCK,) * 2,
        scratch_shapes=[pltpu.VMEM((height * width, height), f32), pltpu.VMEM((rows, height), f32)],
        compiler_params=params(24),
        name="first_image",
    )(first_coupled, right)
    own = jnp.sum(scatter(partial, "bond").astype(f32), axis=0).astype(bf16)
    first_image = gather(own, "bond").reshape(rows, height)
    second_coupled, second, sends, scalars = pl.pallas_call(
        second_kernel,
        out_shape=(
            on_chip(coupled_shape, bf16),
            on_chip((rows, height), f32),
            on_chip((count, block + TAIL, height), bf16),
            jax.ShapeDtypeStruct((2,), f32),
        ),
        in_specs=[VMEM_BLOCK] * 5,
        out_specs=(VMEM_BLOCK,) * 3 + (pl.BlockSpec(memory_space=pltpu.SMEM),),
        scratch_shapes=[pltpu.VMEM((rows, height), f32)],
        compiler_params=params(24),
        name="second_image",
    )(first_image, basis, left, mpo_rows, right_rows)
    received = scatter(sends, "bond")
    grown_shape = (height * width, height)
    one, cross, two = pl.pallas_call(
        grow_kernel,
        out_shape=(on_chip(grown_shape, f32),) * 3,
        in_specs=[VMEM_BLOCK] * 4,
        out_specs=(VMEM_BLOCK,) * 3,
        scratch_shapes=[pltpu.VMEM((2 * height, rows), bf16)],
        compiler_params=params(24),
        cost_estimate=cost(2 * apply_flops, 16 << 20),
        name="grow_terms",
    )(basis, second, first_coupled, second_coupled)
    new_state, new_left, energy, share = pl.pallas_call(
        last_kernel,
        out_shape=(
            jax.ShapeDtypeStruct((height, levels, height), bf16),
            jax.ShapeDtypeStruct((height, width, height), bf16),
            jax.ShapeDtypeStruct((1, height), f32),
            jax.ShapeDtypeStruct((height // count, levels, height), f32),
        ),
        in_specs=[VMEM_BLOCK, pl.BlockSpec(memory_space=pltpu.SMEM)] + [VMEM_BLOCK] * 5,
        out_specs=(VMEM_BLOCK,) * 4,
        compiler_params=params(24),
        name="last",
    )(received, scalars, basis, second, one, cross, two)
    return (new_state[None], new_left[None], energy[0, :1], share[None])


def solution(mesh):
    in_specs = (
        P("seg", None, "bond", None),
        P("seg", None, "bond", None),
        P("seg", "bond", None, None, None),
        P("seg", None, None, None),
    )
    out_specs = (
        P("seg", None, None, None),
        P("seg", None, "bond", None),
        P("seg"),
        P("seg", "bond", None, None),
    )
    return jax.shard_map(body, mesh=mesh, in_specs=in_specs, out_specs=out_specs, check_vma=False)
```

time: 271 us -> 67.3 us (0.25)
  local copies, waits for them, and re-layouts: 98 us -> 8.36 us
  waiting for transfers between devices: 76.2 us -> 7.77 us
  matrix products: 62.7 us -> 0 us
  Pallas kernels: 0 us -> 30.1 us
  between operations: 18.1 us -> 0.83 us
  starting transfers between devices: 3.65 us -> 20 us
  other arithmetic: 10 us -> 0.04 us
    psum x2 -> x0, waiting for transfers between devices: 76.2 us -> none  [the longest x1 38.4 us: body(): lax.psum(image_rows(second_coupled, right_block, height), 'bond')]
    dot_general x9 -> x0, matrix products: 62.7 us -> none  [the longest x3 27.1 us: couple_terms(): jnp.einsum('vust,avtb->asub', mpo_block, shaped, preferred_element_type=j...]
    convert_element_type x6 -> x0, local copies, waits for them, and re-layouts: 38 us -> none  [the longest x3 35.9 us: couple_terms(): mixed_terms.astype(jnp.bfloat16)]
    pallas_call x0 -> x5, Pallas kernels: none -> 30.1 us  [the longest x1 9.19 us: body(): pl.pallas_call(second_kernel, out_shape=(on_chip(coupled_shape, bf16), on...]
    dot_general x4 -> x0, local copies, waits for them, and re-layouts: 28.4 us -> none  [image_rows(): lax.dot_general(coupled.reshape(row_count * levels, width_block * height)...]
    unnamed x11 -> x10, local copies, waits for them, and re-layouts: 28.4 us -> 5.56 us
    ppermute x1 -> x10, starting transfers between devices: 3.39 us -> 20 us  [the longest x6 11 us: scatter(): lax.ppermute(lax.dynamic_index_in_dim(blocks, (me + step) % count, 0, Fal...]
    ppermute x1 -> x10, waiting for transfers between devices: 0.01 us -> 7.77 us  [the longest x3 2.96 us: gather(): lax.ppermute(block, axis, pairs)]
  transfers between devices with their start and end apart: 3 -> 10, of which waited for: 2 -> 7; matrix products, arithmetic and copies ran while one was open for 19% -> 4% of each run, Pallas kernels for 0% -> 20%
where the time goes in v1:
time: 67.3 us; the launch traced here: 67 us
  Pallas kernels  30.1 us (45%)
  starting transfers between devices  20 us (30%)
  local copies, waits for them, and re-layouts  8.36 us (12%)
  waiting for transfers between devices  7.77 us (12%)
  between operations  0.83 us (1%)
    ppermute x6, starting transfers between devices, scatter(): lax.ppermute(lax.dynamic_index_in_dim(blocks, (me + step) % count, 0, Fal...  11 us
    pallas_call x1, Pallas kernels, body(): pl.pallas_call(second_kernel, out_shape=(on_chip(coupled_shape, bf16), on...  9.19 us
    pallas_call x1, Pallas kernels, body(): pl.pallas_call(grow_kernel, out_shape=(on_chip(grown_shape, f32),) * 3, i...  7.7 us
    pallas_call x1, Pallas kernels, body(): pl.pallas_call(first_kernel, out_shape=(on_chip(coupled_shape, bf16), on_...  5.83 us
    ppermute x3, starting transfers between devices, gather(): lax.ppermute(block, axis, pairs)  5.56 us
    unnamed x10, local copies, waits for them, and re-layouts  5.56 us
    pallas_call x1, Pallas kernels, body(): pl.pallas_call(first_image_kernel, out_shape=(on_chip((count, block, heig...  4.56 us
    ppermute x1, starting transfers between devices, body(): right = lax.ppermute(right_env, 'seg', pairs)[0]  3.39 us
  transfers between devices with their start and end apart: 10, of which 7 were waited for; matrix products, arithmetic and copies ran while one was open for 4% of the time, Pallas kernels for 20%

profile of v1, /device:TPU:0, one launch (start us, length us, event | category | flops | bytes accessed | tf_op | source)
XLA Modules:
  0.0 67.0 jit_solution(2583140859426263421)
XLA Ops:
  0.6 3.4 %collective-permute-start = (bf16[1,128,32,128]{3,2,1,0:T(8,128)(2,1)}, bf16[1,128,32,128]{3,2,1,0:T(8,128)(2,1)S(1)}, u32[]{:S(2)}, u32[]{:S(2)}) collective-permute-start(bf16[1,128,32,128]{3,2,1,0:T(8,128)(2,1)} %param.5), channel_id=1, source_target_pairs={{0,28},{4,0},{8,4},{12,8},{16,12},{20,16},{24,20},{28,24},{1,29},{... | collective-permute-start | bytes 3145736 | tf_op jit(solution)/shard_map/ppermute | solution.py:197
  4.0 2.1 %copy.8 = bf16[32,8,8,32]{3,2,1,0:T(8,128)(2,1)S(1)} copy(bf16[32,8,8,32]{0,2,1,3:T(8,128)(2,1)} %bitcast.51) | data formatting | bytes 262144 | tf_op jit(solution)/shard_map/transpose | solution.py:198
  6.1 0.4 reshape.14.mpo_ref
  6.5 0.0 copy-start.2
  6.5 1.2 %copy-done.2 = bf16[1,128,32,128]{3,2,1,0:T(8,128)(2,1)S(1)} copy-done((bf16[1,128,32,128]{3,2,1,0:T(8,128)(2,1)S(1)}, bf16[1,128,32,128]{3,2,1,0:T(8,128)(2,1)}, u32[]{:S(2)}) %copy-start.2) | copy-done | bytes 1048600
  7.7 0.9 %copy-done.4 = bf16[1,128,8,128]{3,2,1,0:T(8,128)(2,1)S(1)} copy-done((bf16[1,128,8,128]{3,2,1,0:T(8,128)(2,1)S(1)}, bf16[1,128,8,128]{3,2,1,0:T(8,128)(2,1)}, u32[]{:S(2)}) %copy-start.4) | copy-done | bytes 262168
  8.7 5.8 %first_coupled.1 = (bf16[32,1024,128]{2,1,0:T(8,128)(2,1)S(1)}, f32[1024,128]{1,0:T(8,128)S(1)}) custom-call(bf16[128,8,128]{2,1,0:T(8,128)(2,1)S(1)} %bitcast.50, bf16[128,32,128]{2,1,0:T(8,128)(2,1)S(1)} %bitcast.46, bf16[256,256]{1,0:T(8,128)(2,1)S(1)} %reshape.14.mpo_ref), custom_call_target="tpu_custom_call" | custom-call | flops 4294967296 | bytes 8388608 | tf_op jit(solution)/shard_map/first_coupled/pallas_call | solution.py:202
  14.5 2.1 %collective-permute-done = bf16[1,128,32,128]{3,2,1,0:T(8,128)(2,1)S(1)} collective-permute-done((bf16[1,128,32,128]{3,2,1,0:T(8,128)(2,1)}, bf16[1,128,32,128]{3,2,1,0:T(8,128)(2,1)S(1)}, u32[]{:S(2)}, u32[]{:S(2)}) %collective-permute-start) | collective-permute-done | bytes 1048608 | tf_op jit(solution)/shard_map/ppermute | solution.py:197
  16.7 4.6 %first_image.1 = (bf16[4,256,128]{2,1,0:T(8,128)(2,1)S(1)}, bf16[4096,128]{1,0:T(8,128)(2,1)S(1)}) custom-call(bf16[32,1024,128]{2,1,0:T(8,128)(2,1)S(1)} %get-tuple-element.19.coupled_ref.first_coupled_ref, bf16[128,32,128]{2,1,0:T(8,128)(2,1)S(1)} %bitcast.48), custom_call_target="tpu_custom_call" | custom-call | tf_op jit(solution)/shard_map/first_image/pallas_call | solution.py:211
  21.2 0.0 copy-start.3
  21.3 2.7 %collective-permute-start.1 = (bf16[256,128]{1,0:T(8,128)(2,1)S(1)}, bf16[256,128]{1,0:T(8,128)(2,1)S(1)}, u32[]{:S(2)}, u32[]{:S(2)}) collective-permute-start(bf16[256,128]{1,0:T(8,128)(2,1)S(1)} %get-tuple-element.40), channel_id=1, source_target_pairs={{0,2},{1,3},{2,0},{3,1},{4,6},{5,7},{6,4},{7,5},{8,10},{9,11},{10,... | collective-permute-start | bytes 196616 | tf_op jit(solution)/shard_map/ppermute | solution.py:168
  24.0 1.6 %collective-permute-start.2 = (bf16[256,128]{1,0:T(8,128)(2,1)S(1)}, bf16[256,128]{1,0:T(8,128)(2,1)S(1)}, u32[]{:S(2)}, u32[]{:S(2)}) collective-permute-start(bf16[256,128]{1,0:T(8,128)(2,1)S(1)} %get-tuple-element.39), channel_id=1, source_target_pairs={{0,1},{1,2},{2,3},{3,0},{4,5},{5,6},{6,7},{7,4},{8,9},{9,10},{10,1... | collective-permute-start | bytes 196616 | tf_op jit(solution)/shard_map/ppermute | solution.py:168
  25.6 2.3 %collective-permute-start.3 = (bf16[256,128]{1,0:T(8,128)(2,1)S(1)}, bf16[256,128]{1,0:T(8,128)(2,1)S(1)}, u32[]{:S(2)}, u32[]{:S(2)}) collective-permute-start(bf16[256,128]{1,0:T(8,128)(2,1)S(1)} %get-tuple-element.38), channel_id=1, source_target_pairs={{0,3},{1,0},{2,1},{3,2},{4,7},{5,4},{6,5},{7,6},{8,11},{9,8},{10,9... | collective-permute-start | bytes 196616 | tf_op jit(solution)/shard_map/ppermute | solution.py:168
  27.8 0.9 %collective-permute-done.1 = bf16[256,128]{1,0:T(8,128)(2,1)S(1)} collective-permute-done((bf16[256,128]{1,0:T(8,128)(2,1)S(1)}, bf16[256,128]{1,0:T(8,128)(2,1)S(1)}, u32[]{:S(2)}, u32[]{:S(2)}) %collective-permute-start.1) | collective-permute-done | bytes 65568 | tf_op jit(solution)/shard_map/ppermute | solution.py:168
  28.7 1.5 %collective-permute-done.2 = bf16[256,128]{1,0:T(8,128)(2,1)S(1)} collective-permute-done((bf16[256,128]{1,0:T(8,128)(2,1)S(1)}, bf16[256,128]{1,0:T(8,128)(2,1)S(1)}, u32[]{:S(2)}, u32[]{:S(2)}) %collective-permute-start.2) | collective-permute-done | bytes 65568 | tf_op jit(solution)/shard_map/ppermute | solution.py:168
  30.2 0.3 collective-permute-done.3
  30.6 1.7 %collective-permute-start.4 = (bf16[256,128]{1,0:T(8,128)(2,1)S(1)}, bf16[256,128]{1,0:T(8,128)(2,1)S(1)}, u32[]{:S(2)}, u32[]{:S(2)}) collective-permute-start(bf16[256,128]{1,0:T(8,128)(2,1)S(1)} %reduce_sum.12), channel_id=1, source_target_pairs={{0,2},{1,3},{2,0},{3,1},{4,6},{5,7},{6,4},{7,5},{8,10},{9,11},{10,... | collective-permute-start | bytes 196616 | tf_op jit(solution)/shard_map/ppermute | solution.py:180
  32.3 2.2 %collective-permute-start.5 = (bf16[256,128]{1,0:T(8,128)(2,1)S(1)}, bf16[256,128]{1,0:T(8,128)(2,1)S(1)}, u32[]{:S(2)}, u32[]{:S(2)}) collective-permute-start(bf16[256,128]{1,0:T(8,128)(2,1)S(1)} %reduce_sum.12), channel_id=1, source_target_pairs={{0,1},{1,2},{2,3},{3,0},{4,5},{5,6},{6,7},{7,4},{8,9},{9,10},{10,1... | collective-permute-start | bytes 196616 | tf_op jit(solution)/shard_map/ppermute | solution.py:180
  34.6 1.6 %collective-permute-start.6 = (bf16[256,128]{1,0:T(8,128)(2,1)S(1)}, bf16[256,128]{1,0:T(8,128)(2,1)S(1)}, u32[]{:S(2)}, u32[]{:S(2)}) collective-permute-start(bf16[256,128]{1,0:T(8,128)(2,1)S(1)} %reduce_sum.12), channel_id=1, source_target_pairs={{0,3},{1,0},{2,1},{3,2},{4,7},{5,4},{6,5},{7,6},{8,11},{9,8},{10,9... | collective-permute-start | bytes 196616 | tf_op jit(solution)/shard_map/ppermute | solution.py:180
  36.2 1.4 %collective-permute-done.4 = bf16[256,128]{1,0:T(8,128)(2,1)S(1)} collective-permute-done((bf16[256,128]{1,0:T(8,128)(2,1)S(1)}, bf16[256,128]{1,0:T(8,128)(2,1)S(1)}, u32[]{:S(2)}, u32[]{:S(2)}) %collective-permute-start.4) | collective-permute-done | bytes 65568 | tf_op jit(solution)/shard_map/ppermute | solution.py:180
  37.7 0.9 %collective-permute-done.5 = bf16[256,128]{1,0:T(8,128)(2,1)S(1)} collective-permute-done((bf16[256,128]{1,0:T(8,128)(2,1)S(1)}, bf16[256,128]{1,0:T(8,128)(2,1)S(1)}, u32[]{:S(2)}, u32[]{:S(2)}) %collective-permute-start.5) | collective-permute-done | bytes 65568 | tf_op jit(solution)/shard_map/ppermute | solution.py:180
  38.6 0.7 collective-permute-done.6
  39.2 9.2 %second_image.1 = (bf16[32,1024,128]{2,1,0:T(8,128)(2,1)S(1)}, f32[1024,128]{1,0:T(8,128)S(1)}, bf16[4,272,128]{2,1,0:T(8,128)(2,1)S(1)}, f32[2]{0:T(128)S(1)}) custom-call(bf16[1024,128]{1,0:T(8,128)(2,1)S(1)} %bitcast.49, f32[1024,128]{1,0:T(8,128)S(1)} %get-tuple-element.21.basis_ref, bf16[128,32,128]{2,1,0:T(8,128)(2,1)S(1)} %bitcast.47, ...), custom_call_target="tpu_custom_call" | custom-call | tf_op jit(solution)/shard_map/second_image/pallas_call | solution.py:222
  48.5 0.7 %collective-permute-start.7 = (bf16[272,128]{1,0:T(8,128)(2,1)S(1)}, bf16[272,128]{1,0:T(8,128)(2,1)S(1)}, u32[]{:S(2)}, u32[]{:S(2)}) collective-permute-start(bf16[272,128]{1,0:T(8,128)(2,1)S(1)} %get-tuple-element.36), channel_id=1, source_target_pairs={{0,2},{1,3},{2,0},{3,1},{4,6},{5,7},{6,4},{7,5},{8,10},{9,11},{10,... | collective-permute-start | bytes 208904 | tf_op jit(solution)/shard_map/ppermute | solution.py:168
  49.2 2.9 %collective-permute-start.8 = (bf16[272,128]{1,0:T(8,128)(2,1)S(1)}, bf16[272,128]{1,0:T(8,128)(2,1)S(1)}, u32[]{:S(2)}, u32[]{:S(2)}) collective-permute-start(bf16[272,128]{1,0:T(8,128)(2,1)S(1)} %get-tuple-element.35), channel_id=1, source_target_pairs={{0,1},{1,2},{2,3},{3,0},{4,5},{5,6},{6,7},{7,4},{8,9},{9,10},{10,1... | collective-permute-start | bytes 208904 | tf_op jit(solution)/shard_map/ppermute | solution.py:168
  52.2 0.9 %collective-permute-start.9 = (bf16[272,128]{1,0:T(8,128)(2,1)S(1)}, bf16[272,128]{1,0:T(8,128)(2,1)S(1)}, u32[]{:S(2)}, u32[]{:S(2)}) collective-permute-start(bf16[272,128]{1,0:T(8,128)(2,1)S(1)} %get-tuple-element.34), channel_id=1, source_target_pairs={{0,3},{1,0},{2,1},{3,2},{4,7},{5,4},{6,5},{7,6},{8,11},{9,8},{10,9... | collective-permute-start | bytes 208904 | tf_op jit(solution)/shard_map/ppermute | solution.py:168
  53.1 3.4 %copy-done.1 = bf16[32,1024,128]{2,1,0:T(8,128)(2,1)S(1)} copy-done((bf16[32,1024,128]{2,1,0:T(8,128)(2,1)S(1)}, bf16[32,1024,128]{2,1,0:T(8,128)(2,1)}, u32[]{:S(2)}) %copy-start.1) | copy-done | bytes 8388632
  56.4 7.7 %grow_terms.1 = (f32[4096,128]{1,0:T(8,128)S(1)}, f32[4096,128]{1,0:T(8,128)S(1)}, f32[4096,128]{1,0:T(8,128)S(1)}) custom-call(f32[1024,128]{1,0:T(8,128)S(1)} %get-tuple-element.21.basis_ref, f32[1024,128]{1,0:T(8,128)S(1)} %get-tuple-element.25.second_ref, bf16[32,1024,128]{2,1,0:T(8,128)(2,1)S(1)} %copy-done.1, ...), custom_call_target="tpu_custom_call" | custom-call | flops 4294967296 | bytes 16777216 | tf_op jit(solution)/shard_map/grow_terms/pallas_call | solution.py:238
  64.2 0.0 collective-permute-done.7
  64.2 0.0 collective-permute-done.8
  64.2 0.0 collective-permute-done.9
  64.3 2.8 %last.1 = (bf16[128,8,128]{2,1,0:T(8,128)(2,1)}, bf16[128,32,128]{2,1,0:T(8,128)(2,1)}, f32[1,128]{1,0:T(1,128)}, f32[32,8,128]{2,1,0:T(8,128)}) custom-call(bf16[4,272,128]{2,1,0:T(8,128)(2,1)S(1)} %bitcast_dynamic-update-slice_fusion.parts_ref, f32[2]{0:T(128)S(1)} %get-tuple-element.24.scalar_ref, f32[1024,128]{1,0:T(8,128)S(1)} %get-tuple-element.21.basis_ref, ...), custom_call_target="tpu_custom_call" | custom-call | tf_op jit(solution)/shard_map/last/pallas_call | solution.py:248
  (21 shorter events, 0.4 us)
Async XLA Ops:
  0.6 16.0 %collective-permute-start = (bf16[1,128,32,128]{3,2,1,0:T(8,128)(2,1)}, bf16[1,128,32,128]{3,2,1,0:T(8,128)(2,1)S(1)}, u32[]{:S(2)}, u32[]{:S(2)}) collective-permute-start(bf16[1,128,32,128]{3,2,1,0:T(8,128)(2,1)} %param.5), channel_id=1, source_target_pairs={{0,28},{4,0},{8,4},{12,8},{16,12},{20,16},{24,20},{28,24},{1,29},{... | collective-permute-start | bytes 3145736 | tf_op jit(solution)/shard_map/ppermute | solution.py:197
  6.5 1.2 %copy-start.2 = (bf16[1,128,32,128]{3,2,1,0:T(8,128)(2,1)S(1)}, bf16[1,128,32,128]{3,2,1,0:T(8,128)(2,1)}, u32[]{:S(2)}) copy-start(bf16[1,128,32,128]{3,2,1,0:T(8,128)(2,1)} %param.4) | copy-start | bytes 3145732
  7.7 0.9 %copy-start.4 = (bf16[1,128,8,128]{3,2,1,0:T(8,128)(2,1)S(1)}, bf16[1,128,8,128]{3,2,1,0:T(8,128)(2,1)}, u32[]{:S(2)}) copy-start(bf16[1,128,8,128]{3,2,1,0:T(8,128)(2,1)} %param.7) | copy-start | bytes 786436
  14.5 6.7 %copy-start = (bf16[32,1024,128]{2,1,0:T(8,128)(2,1)}, bf16[32,1024,128]{2,1,0:T(8,128)(2,1)S(1)}, u32[]{:S(2)}) copy-start(bf16[32,1024,128]{2,1,0:T(8,128)(2,1)S(1)} %get-tuple-element.19.coupled_ref.first_coupled_ref) | copy-start | bytes 25165828
  21.2 18.0 %copy-start.3 = (bf16[1,128,32,128]{3,2,1,0:T(8,128)(2,1)S(1)}, bf16[1,128,32,128]{3,2,1,0:T(8,128)(2,1)}, u32[]{:S(2)}) copy-start(bf16[1,128,32,128]{3,2,1,0:T(8,128)(2,1)} %param.4) | copy-start | bytes 3145732
  21.3 7.3 %collective-permute-start.1 = (bf16[256,128]{1,0:T(8,128)(2,1)S(1)}, bf16[256,128]{1,0:T(8,128)(2,1)S(1)}, u32[]{:S(2)}, u32[]{:S(2)}) collective-permute-start(bf16[256,128]{1,0:T(8,128)(2,1)S(1)} %get-tuple-element.40), channel_id=1, source_target_pairs={{0,2},{1,3},{2,0},{3,1},{4,6},{5,7},{6,4},{7,5},{8,10},{9,11},{10,... | collective-permute-start | bytes 196616 | tf_op jit(solution)/shard_map/ppermute | solution.py:168
  24.0 6.2 %collective-permute-start.2 = (bf16[256,128]{1,0:T(8,128)(2,1)S(1)}, bf16[256,128]{1,0:T(8,128)(2,1)S(1)}, u32[]{:S(2)}, u32[]{:S(2)}) collective-permute-start(bf16[256,128]{1,0:T(8,128)(2,1)S(1)} %get-tuple-element.39), channel_id=1, source_target_pairs={{0,1},{1,2},{2,3},{3,0},{4,5},{5,6},{6,7},{7,4},{8,9},{9,10},{10,1... | collective-permute-start | bytes 196616 | tf_op jit(solution)/shard_map/ppermute | solution.py:168
  25.6 5.0 %collective-permute-start.3 = (bf16[256,128]{1,0:T(8,128)(2,1)S(1)}, bf16[256,128]{1,0:T(8,128)(2,1)S(1)}, u32[]{:S(2)}, u32[]{:S(2)}) collective-permute-start(bf16[256,128]{1,0:T(8,128)(2,1)S(1)} %get-tuple-element.38), channel_id=1, source_target_pairs={{0,3},{1,0},{2,1},{3,2},{4,7},{5,4},{6,5},{7,6},{8,11},{9,8},{10,9... | collective-permute-start | bytes 196616 | tf_op jit(solution)/shard_map/ppermute | solution.py:168
  30.6 7.1 %collective-permute-start.4 = (bf16[256,128]{1,0:T(8,128)(2,1)S(1)}, bf16[256,128]{1,0:T(8,128)(2,1)S(1)}, u32[]{:S(2)}, u32[]{:S(2)}) collective-permute-start(bf16[256,128]{1,0:T(8,128)(2,1)S(1)} %reduce_sum.12), channel_id=1, source_target_pairs={{0,2},{1,3},{2,0},{3,1},{4,6},{5,7},{6,4},{7,5},{8,10},{9,11},{10,... | collective-permute-start | bytes 196616 | tf_op jit(solution)/shard_map/ppermute | solution.py:180
  32.3 6.2 %collective-permute-start.5 = (bf16[256,128]{1,0:T(8,128)(2,1)S(1)}, bf16[256,128]{1,0:T(8,128)(2,1)S(1)}, u32[]{:S(2)}, u32[]{:S(2)}) collective-permute-start(bf16[256,128]{1,0:T(8,128)(2,1)S(1)} %reduce_sum.12), channel_id=1, source_target_pairs={{0,1},{1,2},{2,3},{3,0},{4,5},{5,6},{6,7},{7,4},{8,9},{9,10},{10,1... | collective-permute-start | bytes 196616 | tf_op jit(solution)/shard_map/ppermute | solution.py:180
  34.6 4.6 %collective-permute-start.6 = (bf16[256,128]{1,0:T(8,128)(2,1)S(1)}, bf16[256,128]{1,0:T(8,128)(2,1)S(1)}, u32[]{:S(2)}, u32[]{:S(2)}) collective-permute-start(bf16[256,128]{1,0:T(8,128)(2,1)S(1)} %reduce_sum.12), channel_id=1, source_target_pairs={{0,3},{1,0},{2,1},{3,2},{4,7},{5,4},{6,5},{7,6},{8,11},{9,8},{10,9... | collective-permute-start | bytes 196616 | tf_op jit(solution)/shard_map/ppermute | solution.py:180
  48.5 15.6 %collective-permute-start.7 = (bf16[272,128]{1,0:T(8,128)(2,1)S(1)}, bf16[272,128]{1,0:T(8,128)(2,1)S(1)}, u32[]{:S(2)}, u32[]{:S(2)}) collective-permute-start(bf16[272,128]{1,0:T(8,128)(2,1)S(1)} %get-tuple-element.36), channel_id=1, source_target_pairs={{0,2},{1,3},{2,0},{3,1},{4,6},{5,7},{6,4},{7,5},{8,10},{9,11},{10,... | collective-permute-start | bytes 208904 | tf_op jit(solution)/shard_map/ppermute | solution.py:168
  49.2 15.0 %collective-permute-start.8 = (bf16[272,128]{1,0:T(8,128)(2,1)S(1)}, bf16[272,128]{1,0:T(8,128)(2,1)S(1)}, u32[]{:S(2)}, u32[]{:S(2)}) collective-permute-start(bf16[272,128]{1,0:T(8,128)(2,1)S(1)} %get-tuple-element.35), channel_id=1, source_target_pairs={{0,1},{1,2},{2,3},{3,0},{4,5},{5,6},{6,7},{7,4},{8,9},{9,10},{10,1... | collective-permute-start | bytes 208904 | tf_op jit(solution)/shard_map/ppermute | solution.py:168
  52.2 12.1 %collective-permute-start.9 = (bf16[272,128]{1,0:T(8,128)(2,1)S(1)}, bf16[272,128]{1,0:T(8,128)(2,1)S(1)}, u32[]{:S(2)}, u32[]{:S(2)}) collective-permute-start(bf16[272,128]{1,0:T(8,128)(2,1)S(1)} %get-tuple-element.34), channel_id=1, source_target_pairs={{0,3},{1,0},{2,1},{3,2},{4,7},{5,4},{6,5},{7,6},{8,11},{9,8},{10,9... | collective-permute-start | bytes 208904 | tf_op jit(solution)/shard_map/ppermute | solution.py:168
  53.1 3.4 %copy-start.1 = (bf16[32,1024,128]{2,1,0:T(8,128)(2,1)S(1)}, bf16[32,1024,128]{2,1,0:T(8,128)(2,1)}, u32[]{:S(2)}) copy-start(bf16[32,1024,128]{2,1,0:T(8,128)(2,1)} %copy-done) | copy-start | bytes 25165828

commit v2 on v1

--- a/solution.py
+++ b/solution.py
@@ -76,13 +76,19 @@
     couple(left_ref, by_level(basis_ref, height, levels), mpo_ref[...], coupled_ref, 32)
 
 
-def first_image_kernel(coupled_ref, right_ref, image_ref, right_rows_ref, wide, total):
+def rows_kernel(right_ref, right_rows_ref, wide):
     height, width, _ = right_ref.shape
     wide[...] = right_ref[...].astype(f32).reshape(height * width, height)
     for u in range(width):
         right_rows_ref[u * height : (u + 1) * height, :] = wide[pl.ds(u, height, stride=width), :].astype(bf16)
-    image(coupled_ref, right_rows_ref, total, 256)
-    image_ref[...] = total[...].astype(bf16).reshape(image_ref.shape)
+
+
+def block_image_kernel(where_ref, coupled_ref, right_ref, image_ref):
+    width, _, height = coupled_ref.shape
+    block = image_ref.shape[0]
+    place = pl.ds(pl.multiple_of(where_ref[0] * block, block), block)
+    terms = jnp.concatenate([coupled_ref[u, place, :] for u in range(width)], axis=1)
+    image_ref[...] = jnp.dot(terms, right_ref[...], preferred_element_type=f32).astype(image_ref.dtype)
 
 
 def second_kernel(
@@ -115,21 +121,31 @@
     scalar_ref[1] = residual_size
 
 
-def grow_kernel(basis_ref, second_ref, first_coupled_ref, second_coupled_ref, one_ref, cross_ref, two_ref, turned):
-    width, _, height = first_coupled_ref.shape
+def pair_of(coupled_ref, u):
+    return jnp.concatenate([coupled_ref[u], coupled_ref[u + 1]], axis=1)
+
+
+def grow_first_kernel(basis_ref, coupled_ref, one_ref, turned):
+    width, _, height = coupled_ref.shape
+    turned[...] = basis_ref[...].T.astype(bf16)
+    for u in range(0, width, 2):
+        grown = jnp.dot(turned[...], pair_of(coupled_ref, u), preferred_element_type=f32)
+        for k in (0, 1):
+            one_ref[pl.ds(u + k, height, stride=width), :] = grown[:, k * height : (k + 1) * height]
+
+
+def grow_second_kernel(basis_ref, second_ref, coupled_ref, cross_ref, two_ref, turned):
+    width, _, height = coupled_ref.shape
     turned[:height, :] = basis_ref[...].T.astype(bf16)
     turned[height:, :] = second_ref[...].T.astype(bf16)
     for u in range(0, width, 2):
-        both = jnp.concatenate([first_coupled_ref[u], first_coupled_ref[u + 1]], axis=1)
-        from_first = jnp.dot(turned[...], both, preferred_element_type=f32)
-        both = jnp.concatenate([second_coupled_ref[u], second_coupled_ref[u + 1]], axis=1)
-        from_second = jnp.dot(turned[...], both, preferred_element_type=f32)
+        grown = jnp.dot(turned[...], pair_of(coupled_ref, u), preferred_element_type=f32)
         for k in (0, 1):
             place = pl.ds(u + k, height, stride=width)
             lanes = slice(k * height, (k + 1) * height)
-            one_ref[place, :] = from_first[:height, lanes]
-            cross_ref[place, :] = from_first[height:, lanes] + from_second[:height, lanes]
-            two_ref[place, :] = from_second[height:, lanes]
+            mixed = grown[:height, lanes]
+            cross_ref[place, :] = mixed + mixed.T
+            two_ref[place, :] = grown[height:, lanes]
 
 
 def last_kernel(parts_ref, scalar_ref, basis_ref, second_ref, one_ref, cross_ref, two_ref, state_ref, left_ref, energy_ref, share_ref):
@@ -158,15 +174,18 @@
     return pltpu.VMEM(shape, dtype)
 
 
-def scatter(blocks, axis):
+def scatter(block_of, axis):
     count = lax.axis_size(axis)
     me = lax.axis_index(axis)
-    received = jnp.zeros_like(blocks)
-    received = lax.dynamic_update_index_in_dim(received, lax.dynamic_index_in_dim(blocks, me, 0, False), me, 0)
+    arrived = []
     for step in order(count):
         pairs = [(source, (source + step) % count) for source in range(count)]
-        there = lax.ppermute(lax.dynamic_index_in_dim(blocks, (me + step) % count, 0, False), axis, pairs)
-        received = lax.dynamic_update_index_in_dim(received, there, (me - step) % count, 0)
+        arrived.append(((me - step) % count, lax.ppermute(block_of((me + step) % count), axis, pairs)))
+    own = block_of(me)
+    received = jnp.zeros((count,) + own.shape, own.dtype)
+    received = lax.dynamic_update_index_in_dim(received, own, me, 0)
+    for source, there in arrived:
+        received = lax.dynamic_update_index_in_dim(received, there, source, 0)
     return received
 
 
@@ -204,20 +223,42 @@
         out_shape=(on_chip(coupled_shape, bf16), on_chip((rows, height), f32)),
         in_specs=[VMEM_BLOCK] * 3,
         out_specs=(VMEM_BLOCK,) * 2,
-        compiler_params=params(24),
+        compiler_params=params(16),
         cost_estimate=cost(2 * apply_flops, 8 << 20),
         name="first_coupled",
     )(start, left, mpo_rows)
-    partial, right_rows = pl.pallas_call(
-        first_image_kernel,
-        out_shape=(on_chip((count, block, height), bf16), on_chip((width * height, height), bf16)),
+    right_rows = pl.pallas_call(
+        rows_kernel,
+        out_shape=on_chip((width * height, height), bf16),
+        in_specs=[VMEM_BLOCK],
+        out_specs=VMEM_BLOCK,
+        scratch_shapes=[pltpu.VMEM((height * width, height), f32)],
+        compiler_params=params(8),
+        name="right_rows",
+    )(right)
+
+    def block_image(where):
+        return pl.pallas_call(
+            block_image_kernel,
+            out_shape=on_chip((block, height), bf16),
+            in_specs=[pl.BlockSpec(memory_space=pltpu.SMEM)] + [VMEM_BLOCK] * 2,
+            out_specs=VMEM_BLOCK,
+            compiler_params=params(8),
+            cost_estimate=cost(apply_flops // (2 * count), 8 << 20),
+            name="block_image",
+        )(where.reshape(1), first_coupled, right_rows)
+
+    one = pl.pallas_call(
+        grow_first_kernel,
+        out_shape=on_chip((height * width, height), f32),
         in_specs=[VMEM_BLOCK] * 2,
-        out_specs=(VMEM_BLOCK,) * 2,
-        scratch_shapes=[pltpu.VMEM((height * width, height), f32), pltpu.VMEM((rows, height), f32)],
-        compiler_params=params(24),
-        name="first_image",
-    )(first_coupled, right)
-    own = jnp.sum(scatter(partial, "bond").astype(f32), axis=0).astype(bf16)
+        out_specs=VMEM_BLOCK,
+        scratch_shapes=[pltpu.VMEM((height, rows), bf16)],
+        compiler_params=params(8),
+        cost_estimate=cost(apply_flops, 8 << 20),
+        name="grow_first",
+    )(basis, first_coupled)
+    own = jnp.sum(scatter(block_image, "bond").astype(f32), axis=0).astype(bf16)
     first_image = gather(own, "bond").reshape(rows, height)
     second_coupled, second, sends, scalars = pl.pallas_call(
         second_kernel,
@@ -230,21 +271,21 @@
         in_specs=[VMEM_BLOCK] * 5,
         out_specs=(VMEM_BLOCK,) * 3 + (pl.BlockSpec(memory_space=pltpu.SMEM),),
         scratch_shapes=[pltpu.VMEM((rows, height), f32)],
-        compiler_params=params(24),
+        compiler_params=params(16),
         name="second_image",
     )(first_image, basis, left, mpo_rows, right_rows)
-    received = scatter(sends, "bond")
+    received = scatter(lambda where: lax.dynamic_index_in_dim(sends, where, 0, False), "bond")
     grown_shape = (height * width, height)
-    one, cross, two = pl.pallas_call(
-        grow_kernel,
-        out_shape=(on_chip(grown_shape, f32),) * 3,
-        in_specs=[VMEM_BLOCK] * 4,
-        out_specs=(VMEM_BLOCK,) * 3,
+    cross, two = pl.pallas_call(
+        grow_second_kernel,
+        out_shape=(on_chip(grown_shape, f32),) * 2,
+        in_specs=[VMEM_BLOCK] * 3,
+        out_specs=(VMEM_BLOCK,) * 2,
         scratch_shapes=[pltpu.VMEM((2 * height, rows), bf16)],
-        compiler_params=params(24),
+        compiler_params=params(16),
         cost_estimate=cost(2 * apply_flops, 16 << 20),
-        name="grow_terms",
-    )(basis, second, first_coupled, second_coupled)
+        name="grow_second",
+    )(basis, second, second_coupled)
     new_state, new_left, energy, share = pl.pallas_call(
         last_kernel,
         out_shape=(
@@ -255,7 +296,7 @@
         ),
         in_specs=[VMEM_BLOCK, pl.BlockSpec(memory_space=pltpu.SMEM)] + [VMEM_BLOCK] * 5,
         out_specs=(VMEM_BLOCK,) * 4,
-        compiler_params=params(24),
+        compiler_params=params(16),
         name="last",
     )(received, scalars, basis, second, one, cross, two)
     return (new_state[None], new_left[None], energy[0, :1], share[None])

time: 67.3 us -> 67.1 us (level)
  starting transfers between devices: 20 us -> 17.4 us
  local copies, waits for them, and re-layouts: 8.36 us -> 10.3 us
  Pallas kernels: 30.1 us -> 29.3 us
    ppermute x1, waiting for transfers between devices: 2.11 us -> 0.01 us  [body(): right = lax.ppermute(right_env, 'seg', pairs)[0]]
    ppermute x3, waiting for transfers between devices: 2.96 us -> 4.73 us  [gather(): lax.ppermute(block, axis, pairs)]
    ppermute x3, starting transfers between devices: 5.56 us -> 3.92 us  [gather(): lax.ppermute(block, axis, pairs)]
    unnamed x10 -> x16, local copies, waits for them, and re-layouts: 5.56 us -> 6.63 us
    dynamic_update_slice x1, local copies, waits for them, and re-layouts: 0.02 us -> 0.91 us  [gather(): received = lax.dynamic_update_index_in_dim(received, block, me, 0)]
    ppermute x6, starting transfers between devices: 11 us -> 10.1 us  [scatter(): lax.ppermute(block_of((me + step) % count), axis, pairs)]
    pallas_call x2 -> x7, Pallas kernels: 12.3 us -> 11.5 us  [the longest x1 4.67 us: body(): pl.pallas_call(grow_second_kernel, out_shape=(on_chip(grown_shape, f32),)...]
    ppermute x6, waiting for transfers between devices: 2.69 us -> 3.38 us  [scatter(): lax.ppermute(block_of((me + step) % count), axis, pairs)]
  transfers between devices with their start and end apart: 10 -> 10, of which waited for: 7 -> 5; matrix products, arithmetic and copies ran while one was open for 4% -> 5% of each run, Pallas kernels for 20% -> 19%
where the time goes in v2:
time: 67.1 us; the launch traced here: 66.7 us
  Pallas kernels  29.3 us (44%)
  starting transfers between devices  17.4 us (26%)
  local copies, waits for them, and re-layouts  10.3 us (15%)
  waiting for transfers between devices  8.11 us (12%)
  between operations  0.88 us (1%)
    ppermute x6, starting transfers between devices, scatter(): lax.ppermute(block_of((me + step) % count), axis, pairs)  10.1 us
    pallas_call x1, Pallas kernels, body(): pl.pallas_call(second_kernel, out_shape=(on_chip(coupled_shape, bf16), on...  9.2 us
    unnamed x16, local copies, waits for them, and re-layouts  6.63 us
    pallas_call x1, Pallas kernels, body(): pl.pallas_call(first_kernel, out_shape=(on_chip(coupled_shape, bf16), on_...  5.83 us
    ppermute x3, waiting for transfers between devices, gather(): lax.ppermute(block, axis, pairs)  4.73 us
    pallas_call x1, Pallas kernels, body(): pl.pallas_call(grow_second_kernel, out_shape=(on_chip(grown_shape, f32),)...  4.67 us
    ppermute x3, starting transfers between devices, gather(): lax.ppermute(block, axis, pairs)  3.92 us
    ppermute x1, starting transfers between devices, body(): right = lax.ppermute(right_env, 'seg', pairs)[0]  3.39 us
  transfers between devices with their start and end apart: 10, of which 5 were waited for; matrix products, arithmetic and copies ran while one was open for 5% of the time, Pallas kernels for 19%

profile of v2, /device:TPU:0, one launch (start us, length us, event | category | flops | bytes accessed | tf_op | source)
XLA Modules:
  0.0 66.7 jit_solution(16909083826921663370)
XLA Ops:
  0.6 3.4 %collective-permute-start = (bf16[1,128,32,128]{3,2,1,0:T(8,128)(2,1)}, bf16[1,128,32,128]{3,2,1,0:T(8,128)(2,1)S(1)}, u32[]{:S(2)}, u32[]{:S(2)}) collective-permute-start(bf16[1,128,32,128]{3,2,1,0:T(8,128)(2,1)} %param.5), channel_id=1, source_target_pairs={{0,28},{4,0},{8,4},{12,8},{16,12},{20,16},{24,20},{28,24},{1,29},{... | collective-permute-start | bytes 3145736 | tf_op jit(solution)/shard_map/ppermute | solution.py:216
  4.0 2.1 %copy.8 = bf16[32,8,8,32]{3,2,1,0:T(8,128)(2,1)S(1)} copy(bf16[32,8,8,32]{0,2,1,3:T(8,128)(2,1)} %bitcast.51) | data formatting | bytes 262144 | tf_op jit(solution)/shard_map/transpose | solution.py:217
  6.1 0.4 reshape.27.mpo_ref
  6.5 1.2 %copy-done.3 = bf16[1,128,32,128]{3,2,1,0:T(8,128)(2,1)S(1)} copy-done((bf16[1,128,32,128]{3,2,1,0:T(8,128)(2,1)S(1)}, bf16[1,128,32,128]{3,2,1,0:T(8,128)(2,1)}, u32[]{:S(2)}) %copy-start.3) | copy-done | bytes 1048600
  7.8 0.9 %copy-done.7 = bf16[1,128,8,128]{3,2,1,0:T(8,128)(2,1)S(1)} copy-done((bf16[1,128,8,128]{3,2,1,0:T(8,128)(2,1)S(1)}, bf16[1,128,8,128]{3,2,1,0:T(8,128)(2,1)}, u32[]{:S(2)}) %copy-start.7) | copy-done | bytes 262168
  8.7 5.8 %first_coupled.1 = (bf16[32,1024,128]{2,1,0:T(8,128)(2,1)S(1)}, f32[1024,128]{1,0:T(8,128)S(1)}) custom-call(bf16[128,8,128]{2,1,0:T(8,128)(2,1)S(1)} %bitcast.50, bf16[128,32,128]{2,1,0:T(8,128)(2,1)S(1)} %bitcast.46, bf16[256,256]{1,0:T(8,128)(2,1)S(1)} %reshape.27.mpo_ref), custom_call_target="tpu_custom_call" | custom-call | flops 4294967296 | bytes 8388608 | tf_op jit(solution)/shard_map/first_coupled/pallas_call | solution.py:221
  14.6 2.3 %grow_first.1.one_ref = f32[4096,128]{1,0:T(8,128)S(1)} custom-call(f32[1024,128]{1,0:T(8,128)S(1)} %get-tuple-element.17.basis_ref, bf16[32,1024,128]{2,1,0:T(8,128)(2,1)S(1)} %get-tuple-element.16.coupled_ref), custom_call_target="tpu_custom_call" | custom-call | flops 2147483648 | bytes 8388608 | tf_op jit(solution)/shard_map/grow_first/pallas_call | solution.py:251
  16.9 1.0 %copy-done.5 = bf16[1,128,32,128]{3,2,1,0:T(8,128)(2,1)} copy-done((bf16[1,128,32,128]{3,2,1,0:T(8,128)(2,1)}, bf16[1,128,32,128]{3,2,1,0:T(8,128)(2,1)S(1)}, u32[]{:S(2)}) %copy-start.5) | copy-done | bytes 1048600
  17.9 1.2 %copy-done.6 = bf16[1,128,32,128]{3,2,1,0:T(8,128)(2,1)S(1)} copy-done((bf16[1,128,32,128]{3,2,1,0:T(8,128)(2,1)S(1)}, bf16[1,128,32,128]{3,2,1,0:T(8,128)(2,1)}, u32[]{:S(2)}) %copy-start.6) | copy-done | bytes 1048600
  19.1 1.7 %right_rows.1.right_ref = bf16[4096,128]{1,0:T(8,128)(2,1)S(1)} custom-call(bf16[128,32,128]{2,1,0:T(8,128)(2,1)S(1)} %bitcast.49), custom_call_target="tpu_custom_call" | custom-call | tf_op jit(solution)/shard_map/right_rows/pallas_call | solution.py:230
  20.9 0.7 %block_image.7 = bf16[256,128]{1,0:T(8,128)(2,1)S(1)} custom-call(s32[1]{0:T(128)} %bitcast.11.where_ref, bf16[32,1024,128]{2,1,0:T(8,128)(2,1)S(1)} %get-tuple-element.16.coupled_ref, bf16[4096,128]{1,0:T(8,128)(2,1)S(1)} %right_rows.1.right_ref), custom_call_target="tpu_custom_call" | custom-call | flops 268435456 | bytes 8388608 | tf_op jit(solution)/shard_map/block_image/pallas_call | solution.py:241
  21.6 0.7 %block_image.6 = bf16[256,128]{1,0:T(8,128)(2,1)S(1)} custom-call(s32[1]{0:T(128)} %bitcast.9.where_ref, bf16[32,1024,128]{2,1,0:T(8,128)(2,1)S(1)} %get-tuple-element.16.coupled_ref, bf16[4096,128]{1,0:T(8,128)(2,1)S(1)} %right_rows.1.right_ref), custom_call_target="tpu_custom_call" | custom-call | flops 268435456 | bytes 8388608 | tf_op jit(solution)/shard_map/block_image/pallas_call | solution.py:241
  22.3 0.7 %block_image.5 = bf16[256,128]{1,0:T(8,128)(2,1)S(1)} custom-call(s32[1]{0:T(128)} %bitcast.7.where_ref, bf16[32,1024,128]{2,1,0:T(8,128)(2,1)S(1)} %get-tuple-element.16.coupled_ref, bf16[4096,128]{1,0:T(8,128)(2,1)S(1)} %right_rows.1.right_ref), custom_call_target="tpu_custom_call" | custom-call | flops 268435456 | bytes 8388608 | tf_op jit(solution)/shard_map/block_image/pallas_call | solution.py:241
  23.0 0.7 %block_image.4 = bf16[256,128]{1,0:T(8,128)(2,1)S(1)} custom-call(s32[1]{0:T(128)} %bitcast.where_ref, bf16[32,1024,128]{2,1,0:T(8,128)(2,1)S(1)} %get-tuple-element.16.coupled_ref, bf16[4096,128]{1,0:T(8,128)(2,1)S(1)} %right_rows.1.right_ref), custom_call_target="tpu_custom_call" | custom-call | flops 268435456 | bytes 8388608 | tf_op jit(solution)/shard_map/block_image/pallas_call | solution.py:241
  23.7 2.7 %collective-permute-start.1 = (bf16[256,128]{1,0:T(8,128)(2,1)S(1)}, bf16[256,128]{1,0:T(8,128)(2,1)S(1)}, u32[]{:S(2)}, u32[]{:S(2)}) collective-permute-start(bf16[256,128]{1,0:T(8,128)(2,1)S(1)} %block_image.5), channel_id=1, source_target_pairs={{0,2},{1,3},{2,0},{3,1},{4,6},{5,7},{6,4},{7,5},{8,10},{9,11},{10,... | collective-permute-start | bytes 196616 | tf_op jit(solution)/shard_map/ppermute | solution.py:183
  26.3 1.6 %collective-permute-start.2 = (bf16[256,128]{1,0:T(8,128)(2,1)S(1)}, bf16[256,128]{1,0:T(8,128)(2,1)S(1)}, u32[]{:S(2)}, u32[]{:S(2)}) collective-permute-start(bf16[256,128]{1,0:T(8,128)(2,1)S(1)} %block_image.6), channel_id=1, source_target_pairs={{0,1},{1,2},{2,3},{3,0},{4,5},{5,6},{6,7},{7,4},{8,9},{9,10},{10,1... | collective-permute-start | bytes 196616 | tf_op jit(solution)/shard_map/ppermute | solution.py:183
  27.9 2.3 %collective-permute-start.3 = (bf16[256,128]{1,0:T(8,128)(2,1)S(1)}, bf16[256,128]{1,0:T(8,128)(2,1)S(1)}, u32[]{:S(2)}, u32[]{:S(2)}) collective-permute-start(bf16[256,128]{1,0:T(8,128)(2,1)S(1)} %block_image.7), channel_id=1, source_target_pairs={{0,3},{1,0},{2,1},{3,2},{4,7},{5,4},{6,5},{7,6},{8,11},{9,8},{10,9... | collective-permute-start | bytes 196616 | tf_op jit(solution)/shard_map/ppermute | solution.py:183
  30.2 2.3 %collective-permute-done.2 = bf16[256,128]{1,0:T(8,128)(2,1)S(1)} collective-permute-done((bf16[256,128]{1,0:T(8,128)(2,1)S(1)}, bf16[256,128]{1,0:T(8,128)(2,1)S(1)}, u32[]{:S(2)}, u32[]{:S(2)}) %collective-permute-start.2) | collective-permute-done | bytes 65568 | tf_op jit(solution)/shard_map/ppermute | solution.py:183
  32.9 0.7 %reduce_sum.12 = bf16[256,128]{1,0:T(8,128)(2,1)} reduce(bf16[4,256,128]{2,1,0:T(8,128)(2,1)S(1)} %bitcast_dynamic-update-slice_fusion.7, bf16[]{:T(256)} %constant.101.clone.1), dimensions={0}, to_apply=%region_0.1 | reduce | flops 98304 | bytes 327682 | tf_op jit(solution)/shard_map/reduce_sum | solution.py:261
  33.5 3.4 %collective-permute-start.6 = (bf16[256,128]{1,0:T(8,128)(2,1)}, bf16[256,128]{1,0:T(8,128)(2,1)S(1)}, u32[]{:S(2)}, u32[]{:S(2)}) collective-permute-start(bf16[256,128]{1,0:T(8,128)(2,1)} %reduce_sum.12), channel_id=1, source_target_pairs={{0,3},{1,0},{2,1},{3,2},{4,7},{5,4},{6,5},{7,6},{8,11},{9,8},{10,9... | collective-permute-start | bytes 196616 | tf_op jit(solution)/shard_map/ppermute | solution.py:199
  36.9 0.6 collective-permute-start.4
  37.5 0.9 %bitcast_dynamic-update-slice_fusion.6 = bf16[4,256,128]{2,1,0:T(8,128)(2,1)S(1)} fusion(bf16[4,256,128]{2,1,0:T(8,128)(2,1)S(1)} %broadcast.9, s32[]{:T(128)S(6)} %select_n.79, bf16[256,128]{1,0:T(8,128)(2,1)} %reduce_sum.12), kind=kLoop, calls=%fused_computation.10 | loop fusion | bytes 131076 | tf_op jit(solution)/shard_map/jit(dynamic_update_index_in_dim)/dynamic_update_slice | solution.py:196
  38.4 3.8 %collective-permute-done.4 = bf16[256,128]{1,0:T(8,128)(2,1)S(1)} collective-permute-done((bf16[256,128]{1,0:T(8,128)(2,1)}, bf16[256,128]{1,0:T(8,128)(2,1)S(1)}, u32[]{:S(2)}, u32[]{:S(2)}) %collective-permute-start.4) | collective-permute-done | bytes 65568 | tf_op jit(solution)/shard_map/ppermute | solution.py:199
  42.3 0.9 %collective-permute-done.5 = bf16[256,128]{1,0:T(8,128)(2,1)S(1)} collective-permute-done((bf16[256,128]{1,0:T(8,128)(2,1)}, bf16[256,128]{1,0:T(8,128)(2,1)S(1)}, u32[]{:S(2)}, u32[]{:S(2)}) %collective-permute-start.5) | collective-permute-done | bytes 65568 | tf_op jit(solution)/shard_map/ppermute | solution.py:199
  43.2 1.0 %copy-done.1 = f32[1024,128]{1,0:T(8,128)S(1)} copy-done((f32[1024,128]{1,0:T(8,128)S(1)}, f32[1024,128]{1,0:T(8,128)}, u32[]{:S(2)}) %copy-start.1) | copy-done | bytes 524312
  44.3 1.2 %copy-done.4 = bf16[1,128,32,128]{3,2,1,0:T(8,128)(2,1)S(1)} copy-done((bf16[1,128,32,128]{3,2,1,0:T(8,128)(2,1)S(1)}, bf16[1,128,32,128]{3,2,1,0:T(8,128)(2,1)}, u32[]{:S(2)}) %copy-start.4) | copy-done | bytes 1048600
  45.5 9.2 %second_image.1 = (bf16[32,1024,128]{2,1,0:T(8,128)(2,1)S(1)}, f32[1024,128]{1,0:T(8,128)S(1)}, bf16[4,272,128]{2,1,0:T(8,128)(2,1)S(1)}, f32[2]{0:T(128)S(1)}) custom-call(bf16[1024,128]{1,0:T(8,128)(2,1)S(1)} %bitcast.48, f32[1024,128]{1,0:T(8,128)S(1)} %copy-done.1, bf16[128,32,128]{2,1,0:T(8,128)(2,1)S(1)} %bitcast.47, ...), custom_call_target="tpu_custom_call" | custom-call | tf_op jit(solution)/shard_map/second_image/pallas_call | solution.py:263
  54.8 3.0 %collective-permute-start.9 = (bf16[272,128]{1,0:T(8,128)(2,1)S(1)}, bf16[272,128]{1,0:T(8,128)(2,1)S(1)}, u32[]{:S(2)}, u32[]{:S(2)}) collective-permute-start(bf16[272,128]{1,0:T(8,128)(2,1)S(1)} %get-tuple-element.28), channel_id=1, source_target_pairs={{0,3},{1,0},{2,1},{3,2},{4,7},{5,4},{6,5},{7,6},{8,11},{9,8},{10,9... | collective-permute-start | bytes 208904 | tf_op jit(solution)/shard_map/ppermute | solution.py:183
  57.8 0.6 collective-permute-start.7
  58.4 4.7 %grow_second.1 = (f32[4096,128]{1,0:T(8,128)S(1)}, f32[4096,128]{1,0:T(8,128)S(1)}) custom-call(f32[1024,128]{1,0:T(8,128)S(1)} %copy-done.2, f32[1024,128]{1,0:T(8,128)S(1)} %get-tuple-element.20.second_ref, bf16[32,1024,128]{2,1,0:T(8,128)(2,1)S(1)} %get-tuple-element.21.coupled_ref), custom_call_target="tpu_custom_call" | custom-call | flops 4294967296 | bytes 16777216 | tf_op jit(solution)/shard_map/grow_second/pallas_call | solution.py:279
  63.1 0.8 %collective-permute-done.8 = bf16[272,128]{1,0:T(8,128)(2,1)S(1)} collective-permute-done((bf16[272,128]{1,0:T(8,128)(2,1)S(1)}, bf16[272,128]{1,0:T(8,128)(2,1)S(1)}, u32[]{:S(2)}, u32[]{:S(2)}) %collective-permute-start.8) | collective-permute-done | bytes 69664 | tf_op jit(solution)/shard_map/ppermute | solution.py:183
  64.0 2.8 %last.1 = (bf16[128,8,128]{2,1,0:T(8,128)(2,1)}, bf16[128,32,128]{2,1,0:T(8,128)(2,1)}, f32[1,128]{1,0:T(1,128)}, f32[32,8,128]{2,1,0:T(8,128)}) custom-call(bf16[4,272,128]{2,1,0:T(8,128)(2,1)S(1)} %bitcast_dynamic-update-slice_fusion.parts_ref, f32[2]{0:T(128)S(1)} %get-tuple-element.19.scalar_ref, f32[1024,128]{1,0:T(8,128)S(1)} %copy-done.2, ...), custom_call_target="tpu_custom_call" | custom-call | tf_op jit(solution)/shard_map/last/pallas_call | solution.py:289
  (32 shorter events, 0.6 us)
Async XLA Ops:
  0.6 16.3 %collective-permute-start = (bf16[1,128,32,128]{3,2,1,0:T(8,128)(2,1)}, bf16[1,128,32,128]{3,2,1,0:T(8,128)(2,1)S(1)}, u32[]{:S(2)}, u32[]{:S(2)}) collective-permute-start(bf16[1,128,32,128]{3,2,1,0:T(8,128)(2,1)} %param.5), channel_id=1, source_target_pairs={{0,28},{4,0},{8,4},{12,8},{16,12},{20,16},{24,20},{28,24},{1,29},{... | collective-permute-start | bytes 3145736 | tf_op jit(solution)/shard_map/ppermute | solution.py:216
  6.5 1.2 %copy-start.3 = (bf16[1,128,32,128]{3,2,1,0:T(8,128)(2,1)S(1)}, bf16[1,128,32,128]{3,2,1,0:T(8,128)(2,1)}, u32[]{:S(2)}) copy-start(bf16[1,128,32,128]{3,2,1,0:T(8,128)(2,1)} %param.4) | copy-start | bytes 3145732
  7.8 0.9 %copy-start.7 = (bf16[1,128,8,128]{3,2,1,0:T(8,128)(2,1)S(1)}, bf16[1,128,8,128]{3,2,1,0:T(8,128)(2,1)}, u32[]{:S(2)}) copy-start(bf16[1,128,8,128]{3,2,1,0:T(8,128)(2,1)} %param.7) | copy-start | bytes 786436
  14.5 2.3 %copy-start = (f32[1024,128]{1,0:T(8,128)}, f32[1024,128]{1,0:T(8,128)S(1)}, u32[]{:S(2)}) copy-start(f32[1024,128]{1,0:T(8,128)S(1)} %get-tuple-element.17.basis_ref) | copy-start | bytes 1572868
  16.9 1.0 %copy-start.5 = (bf16[1,128,32,128]{3,2,1,0:T(8,128)(2,1)}, bf16[1,128,32,128]{3,2,1,0:T(8,128)(2,1)S(1)}, u32[]{:S(2)}) copy-start(bf16[1,128,32,128]{3,2,1,0:T(8,128)(2,1)S(1)} %collective-permute-done) | copy-start | bytes 3145732
  17.9 1.2 %copy-start.6 = (bf16[1,128,32,128]{3,2,1,0:T(8,128)(2,1)S(1)}, bf16[1,128,32,128]{3,2,1,0:T(8,128)(2,1)}, u32[]{:S(2)}) copy-start(bf16[1,128,32,128]{3,2,1,0:T(8,128)(2,1)} %copy-done.5) | copy-start | bytes 3145732
  23.7 6.5 %collective-permute-start.1 = (bf16[256,128]{1,0:T(8,128)(2,1)S(1)}, bf16[256,128]{1,0:T(8,128)(2,1)S(1)}, u32[]{:S(2)}, u32[]{:S(2)}) collective-permute-start(bf16[256,128]{1,0:T(8,128)(2,1)S(1)} %block_image.5), channel_id=1, source_target_pairs={{0,2},{1,3},{2,0},{3,1},{4,6},{5,7},{6,4},{7,5},{8,10},{9,11},{10,... | collective-permute-start | bytes 196616 | tf_op jit(solution)/shard_map/ppermute | solution.py:183
  26.3 6.2 %collective-permute-start.2 = (bf16[256,128]{1,0:T(8,128)(2,1)S(1)}, bf16[256,128]{1,0:T(8,128)(2,1)S(1)}, u32[]{:S(2)}, u32[]{:S(2)}) collective-permute-start(bf16[256,128]{1,0:T(8,128)(2,1)S(1)} %block_image.6), channel_id=1, source_target_pairs={{0,1},{1,2},{2,3},{3,0},{4,5},{5,6},{6,7},{7,4},{8,9},{9,10},{10,1... | collective-permute-start | bytes 196616 | tf_op jit(solution)/shard_map/ppermute | solution.py:183
  27.9 5.0 %collective-permute-start.3 = (bf16[256,128]{1,0:T(8,128)(2,1)S(1)}, bf16[256,128]{1,0:T(8,128)(2,1)S(1)}, u32[]{:S(2)}, u32[]{:S(2)}) collective-permute-start(bf16[256,128]{1,0:T(8,128)(2,1)S(1)} %block_image.7), channel_id=1, source_target_pairs={{0,3},{1,0},{2,1},{3,2},{4,7},{5,4},{6,5},{7,6},{8,11},{9,8},{10,9... | collective-permute-start | bytes 196616 | tf_op jit(solution)/shard_map/ppermute | solution.py:183
  33.5 9.6 %collective-permute-start.6 = (bf16[256,128]{1,0:T(8,128)(2,1)}, bf16[256,128]{1,0:T(8,128)(2,1)S(1)}, u32[]{:S(2)}, u32[]{:S(2)}) collective-permute-start(bf16[256,128]{1,0:T(8,128)(2,1)} %reduce_sum.12), channel_id=1, source_target_pairs={{0,3},{1,0},{2,1},{3,2},{4,7},{5,4},{6,5},{7,6},{8,11},{9,8},{10,9... | collective-permute-start | bytes 196616 | tf_op jit(solution)/shard_map/ppermute | solution.py:199
  36.9 6.3 %collective-permute-start.5 = (bf16[256,128]{1,0:T(8,128)(2,1)}, bf16[256,128]{1,0:T(8,128)(2,1)S(1)}, u32[]{:S(2)}, u32[]{:S(2)}) collective-permute-start(bf16[256,128]{1,0:T(8,128)(2,1)} %reduce_sum.12), channel_id=1, source_target_pairs={{0,1},{1,2},{2,3},{3,0},{4,5},{5,6},{6,7},{7,4},{8,9},{9,10},{10,1... | collective-permute-start | bytes 196616 | tf_op jit(solution)/shard_map/ppermute | solution.py:199
  36.9 5.4 %collective-permute-start.4 = (bf16[256,128]{1,0:T(8,128)(2,1)}, bf16[256,128]{1,0:T(8,128)(2,1)S(1)}, u32[]{:S(2)}, u32[]{:S(2)}) collective-permute-start(bf16[256,128]{1,0:T(8,128)(2,1)} %reduce_sum.12), channel_id=1, source_target_pairs={{0,2},{1,3},{2,0},{3,1},{4,6},{5,7},{6,4},{7,5},{8,10},{9,11},{10,... | collective-permute-start | bytes 196616 | tf_op jit(solution)/shard_map/ppermute | solution.py:199
  37.5 20.9 %copy-start.2 = (f32[1024,128]{1,0:T(8,128)S(1)}, f32[1024,128]{1,0:T(8,128)}, u32[]{:S(2)}) copy-start(f32[1024,128]{1,0:T(8,128)} %copy-done) | copy-start | bytes 1572868
  43.2 1.0 %copy-start.1 = (f32[1024,128]{1,0:T(8,128)S(1)}, f32[1024,128]{1,0:T(8,128)}, u32[]{:S(2)}) copy-start(f32[1024,128]{1,0:T(8,128)} %copy-done) | copy-start | bytes 1572868
  44.3 1.2 %copy-start.4 = (bf16[1,128,32,128]{3,2,1,0:T(8,128)(2,1)S(1)}, bf16[1,128,32,128]{3,2,1,0:T(8,128)(2,1)}, u32[]{:S(2)}) copy-start(bf16[1,128,32,128]{3,2,1,0:T(8,128)(2,1)} %param.4) | copy-start | bytes 3145732
  54.8 9.1 %collective-permute-start.9 = (bf16[272,128]{1,0:T(8,128)(2,1)S(1)}, bf16[272,128]{1,0:T(8,128)(2,1)S(1)}, u32[]{:S(2)}, u32[]{:S(2)}) collective-permute-start(bf16[272,128]{1,0:T(8,128)(2,1)S(1)} %get-tuple-element.28), channel_id=1, source_target_pairs={{0,3},{1,0},{2,1},{3,2},{4,7},{5,4},{6,5},{7,6},{8,11},{9,8},{10,9... | collective-permute-start | bytes 208904 | tf_op jit(solution)/shard_map/ppermute | solution.py:183
  57.8 6.1 %collective-permute-start.8 = (bf16[272,128]{1,0:T(8,128)(2,1)S(1)}, bf16[272,128]{1,0:T(8,128)(2,1)S(1)}, u32[]{:S(2)}, u32[]{:S(2)}) collective-permute-start(bf16[272,128]{1,0:T(8,128)(2,1)S(1)} %get-tuple-element.29), channel_id=1, source_target_pairs={{0,1},{1,2},{2,3},{3,0},{4,5},{5,6},{6,7},{7,4},{8,9},{9,10},{10,1... | collective-permute-start | bytes 208904 | tf_op jit(solution)/shard_map/ppermute | solution.py:183
  57.8 5.3 %collective-permute-start.7 = (bf16[272,128]{1,0:T(8,128)(2,1)S(1)}, bf16[272,128]{1,0:T(8,128)(2,1)S(1)}, u32[]{:S(2)}, u32[]{:S(2)}) collective-permute-start(bf16[272,128]{1,0:T(8,128)(2,1)S(1)} %get-tuple-element.30), channel_id=1, source_target_pairs={{0,2},{1,3},{2,0},{3,1},{4,6},{5,7},{6,4},{7,5},{8,10},{9,11},{10,... | collective-permute-start | bytes 208904 | tf_op jit(solution)/shard_map/ppermute | solution.py:183

commit v3 on v2

v3 whole, which is shorter than its diff:
```python
import functools

import jax
import jax.numpy as jnp
from jax import lax
from jax.experimental import pallas as pl
from jax.experimental.pallas import tpu as pltpu
from jax.sharding import PartitionSpec as P

epsilon = 1e-06
bf16 = jnp.bfloat16
f32 = jnp.float32
VMEM_BLOCK = pl.BlockSpec(memory_space=pltpu.VMEM)
SMEM_BLOCK = pl.BlockSpec(memory_space=pltpu.SMEM)
HBM_BLOCK = pl.BlockSpec(memory_space=pltpu.HBM)
DMA = pltpu.SemaphoreType.DMA
TAIL = 16


def params(megabytes):
    return pltpu.CompilerParams(vmem_limit_bytes=megabytes << 20)


def cost(flops, size):
    return pl.CostEstimate(flops=flops, bytes_accessed=size, transcendentals=0)


def on_chip(shape, dtype):
    return pltpu.VMEM(shape, dtype)


def normalised(start):
    height, levels, _ = start.shape
    start = start.astype(f32)
    scale = lax.rsqrt(jnp.sum(start * start) / (height * levels * height) + epsilon)
    return (start * scale).reshape(height * levels, height)


def by_level(rows_ref, height, levels):
    parts = [rows_ref[pl.ds(t, height, stride=levels), :] for t in range(levels)]
    return jnp.concatenate(parts, axis=1).astype(bf16)


def couple(left_ref, vector, mpo, coupled_ref, chunk):
    height, width, _ = left_ref.shape
    levels = vector.shape[1] // height
    right_width = mpo.shape[0] // levels

    def step(index, carry):
        first = index * chunk
        mixed = jnp.dot(
            left_ref[pl.ds(first, chunk)].reshape(chunk * width, height), vector, preferred_element_type=f32
        )
        for pair in range(0, chunk, 2):
            columns = []
            for row in (pair, pair + 1):
                pieces = [
                    mixed[row * width : (row + 1) * width, t * height : (t + 1) * height] for t in range(levels)
                ]
                columns.append(jnp.concatenate(pieces, axis=0))
            both = jnp.concatenate(columns, axis=1).astype(bf16)
            result = jnp.dot(mpo, both, preferred_element_type=f32)
            halves = [
                result[:, k * height : (k + 1) * height].reshape(right_width, levels, height) for k in (0, 1)
            ]
            place = pl.multiple_of((first + pair) * levels, 2 * levels)
            coupled_ref[:, pl.ds(place, 2 * levels), :] = jnp.concatenate(halves, axis=1).astype(bf16)
        return carry

    lax.fori_loop(0, height // chunk, step, 0)


def image(coupled_ref, right, image_ref, chunk):
    width, rows, _ = coupled_ref.shape

    def step(index, carry):
        place = pl.ds(pl.multiple_of(index * chunk, chunk), chunk)
        terms = jnp.concatenate([coupled_ref[u, place, :] for u in range(width)], axis=1)
        image_ref[place, :] = jnp.dot(terms, right[...], preferred_element_type=f32)
        return carry

    lax.fori_loop(0, rows // chunk, step, 0)


def begin_kernel(right_hbm, left_hbm, start_hbm, folded_ref, left_ref, vector_ref, basis_ref, right, start, rows, sems):
    height, width, _ = right.shape
    levels = start.shape[1]
    half = height // 2
    copies = [
        pltpu.make_async_copy(right_hbm, right, sems.at[0]),
        pltpu.make_async_copy(start_hbm, start, sems.at[1]),
        pltpu.make_async_copy(left_hbm, left_ref, sems.at[2]),
    ]
    for copy in copies:
        copy.start()
    copies[0].wait()
    lower = right[half:].astype(f32)
    row = lax.broadcasted_iota(jnp.int32, lower.shape, 0)
    lane = lax.broadcasted_iota(jnp.int32, lower.shape, 2)
    turned = pltpu.roll(lower, half, 2)
    folded_ref[:half] = jnp.where(lane >= row, right[:half].astype(f32), turned).astype(bf16)
    folded_ref[half] = jnp.sum(jnp.where(lane == row + half, lower, 0.0), axis=0).astype(bf16)
    copies[1].wait()
    rows[...] = normalised(start[...])
    basis_ref[...] = rows[...].astype(bf16)
    vector_ref[...] = by_level(rows, height, levels)
    copies[2].wait()


def first_kernel(vector_ref, left_ref, mpo_ref, coupled_ref):
    couple(left_ref, vector_ref[...], mpo_ref[...], coupled_ref, 32)


def unfold_kernel(folded_ref, right_ref, wide):
    half, width, height = folded_ref.shape
    half -= 1
    wide[...] = folded_ref[:half].astype(f32).reshape(half * width, height)
    diagonal = folded_ref[half].astype(f32)
    row = lax.broadcasted_iota(jnp.int32, (half, height), 0)
    lane = lax.broadcasted_iota(jnp.int32, (half, height), 1)
    for u in range(width):
        one = wide[pl.ds(u, half, stride=width), :]
        turned = jnp.concatenate([one, one], axis=0).T
        upper = jnp.where((lane < half) & (lane < row), turned[:half], one)
        corner = jnp.where(lane == row + half, diagonal[u : u + 1, :], turned[:half])
        corner = jnp.where(lane < row + half, pltpu.roll(one, half, 1), corner)
        lower = jnp.where(lane < half, turned[half:], corner)
        right_ref[u * height : u * height + half, :] = upper.astype(bf16)
        right_ref[u * height + half : (u + 1) * height, :] = lower.astype(bf16)


def block_image(where, coupled_ref, right_ref, block):
    width = coupled_ref.shape[0]
    place = pl.ds(pl.multiple_of(where * block, block), block)
    terms = jnp.concatenate([coupled_ref[u, place, :] for u in range(width)], axis=1)
    return jnp.dot(terms, right_ref[...], preferred_element_type=f32)


def block_images_kernel(where_ref, coupled_ref, right_ref, *image_refs):
    for k, image_ref in enumerate(image_refs):
        image_ref[...] = block_image(where_ref[k], coupled_ref, right_ref, image_ref.shape[0]).astype(bf16)


def own_image_kernel(where_ref, coupled_ref, right_ref, arrived_ref, image_ref):
    own = block_image(where_ref[0], coupled_ref, right_ref, image_ref.shape[0])
    image_ref[...] = own + arrived_ref[...].astype(f32)


def sum_kernel(own_ref, *refs):
    total = own_ref[...]
    for ref in refs[:-1]:
        total = total + ref[...].astype(f32)
    refs[-1][...] = total.astype(bf16)


def second_kernel(count, where_ref, *refs):
    blocks, refs = refs[:count], refs[count:]
    start_hbm, left_hbm, mpo_ref, right_ref, coupled_ref, basis_ref, second_ref, scalar_ref = refs[:8]
    sends, (start, left, total, sems) = refs[8 : 8 + count], refs[8 + count :]
    start_copy = pltpu.make_async_copy(start_hbm, start, sems.at[0])
    left_copy = pltpu.make_async_copy(left_hbm, left, sems.at[1])
    start_copy.start()
    left_copy.start()
    height, width, _ = left.shape
    rows = basis_ref.shape[0]
    levels = rows // height
    entries = rows * height
    block = blocks[0].shape[0]
    for k in range(count):
        place = pl.ds(pl.multiple_of(where_ref[k] * block, block), block)
        total[place, :] = blocks[k][...].astype(f32)
    start_copy.wait()
    basis_ref[...] = normalised(start[...])
    basis = basis_ref[...]
    first_image = total[...]
    rayleigh = jnp.sum(basis * first_image) / entries
    residual = first_image - rayleigh * basis
    residual_size = jnp.sqrt(jnp.sum(residual * residual) / entries + epsilon)
    second_ref[...] = residual / residual_size
    vector = by_level(second_ref, height, levels)
    left_copy.wait()
    couple(left, vector, mpo_ref[...], coupled_ref, 32)
    image(coupled_ref, right_ref, total, 256)
    value = jnp.sum(second_ref[...] * total[...]) / entries
    high = value.astype(bf16).astype(f32)
    middle = (value - high).astype(bf16).astype(f32)
    low = value - high - middle
    lane = lax.broadcasted_iota(jnp.int32, (TAIL, height), 1)
    tail = jnp.where(lane == 0, high, jnp.where(lane == 1, middle, jnp.where(lane == 2, low, 0.0))).astype(bf16)
    for k in range(count):
        place = pl.ds(pl.multiple_of(where_ref[count + k] * block, block), block)
        sends[k][:block, :] = total[place, :].astype(bf16)
        sends[k][block:, :] = tail
    scalar_ref[0] = rayleigh
    scalar_ref[1] = residual_size


def pair_of(coupled_ref, u):
    return jnp.concatenate([coupled_ref[u], coupled_ref[u + 1]], axis=1)


def grow_first_kernel(after_ref, basis_ref, coupled_ref, one_ref, turned):
    del after_ref
    width, _, height = coupled_ref.shape
    turned[...] = basis_ref[...].astype(f32).T.astype(bf16)
    for u in range(0, width, 2):
        grown = jnp.dot(turned[...], pair_of(coupled_ref, u), preferred_element_type=f32)
        for k in (0, 1):
            one_ref[pl.ds(u + k, height, stride=width), :] = grown[:, k * height : (k + 1) * height]


def grow_second_kernel(basis_ref, second_ref, coupled_ref, cross_ref, two_ref, turned):
    width, _, height = coupled_ref.shape
    turned[:height, :] = basis_ref[...].T.astype(bf16)
    turned[height:, :] = second_ref[...].T.astype(bf16)
    for u in range(0, width, 2):
        grown = jnp.dot(turned[...], pair_of(coupled_ref, u), preferred_element_type=f32)
        for k in (0, 1):
            place = pl.ds(u + k, height, stride=width)
            lanes = slice(k * height, (k + 1) * height)
            mixed = grown[:height, lanes]
            cross_ref[place, :] = mixed + mixed.T
            two_ref[place, :] = grown[height:, lanes]


def last_kernel(count, where_ref, *refs):
    parts, refs = refs[:count], refs[count:]
    scalar_ref, basis_ref, second_ref, one_ref, cross_ref, two_ref = refs[:6]
    state_ref, left_ref, energy_ref, share_ref = refs[6:]
    block, height = parts[0].shape
    block -= TAIL
    lane = lax.broadcasted_iota(jnp.int32, (TAIL, height), 1)
    row = lax.broadcasted_iota(jnp.int32, (TAIL, height), 0)
    values = [jnp.sum(jnp.where((lane < 3) & (row == 0), part[block:, :].astype(f32), 0.0)) for part in parts]
    curvature = jnp.float32(0.0)
    for device in range(count):
        for k in range(count):
            curvature = curvature + jnp.where(where_ref[k] == device, values[k], 0.0)
    rayleigh, residual_size = scalar_ref[0], scalar_ref[1]
    middle = 0.5 * (rayleigh + curvature)
    half_gap = 0.5 * (rayleigh - curvature)
    lowest = middle - jnp.sqrt(half_gap * half_gap + residual_size * residual_size)
    offset = lowest - rayleigh
    length = jnp.sqrt(residual_size * residual_size + offset * offset)
    one, two = residual_size / length, offset / length
    energy_ref[...] = jnp.full(energy_ref.shape, lowest, f32)
    state_ref[...] = (one * basis_ref[...] + two * second_ref[...]).astype(bf16).reshape(state_ref.shape)
    grown = (one * one) * one_ref[...] + (one * two) * cross_ref[...] + (two * two) * two_ref[...]
    left_ref[...] = grown.astype(bf16).reshape(left_ref.shape)
    share = parts[0][:block, :].astype(f32)
    for part in parts[1:]:
        share = share + part[:block, :].astype(f32)
    share_ref[...] = share.reshape(share_ref.shape)


def order(count):
    return sorted(range(1, count), key=lambda step: -min(step, count - step))


def sent(value, axis, step):
    count = lax.axis_size(axis)
    return lax.ppermute(value, axis, [(source, (source + step) % count) for source in range(count)])


def body(left_env, right_env, mpo_site, start_state):
    left, right, mpo, start = left_env[0], right_env[0], mpo_site[0], start_state[0]
    height, width, _ = left.shape
    levels = start.shape[1]
    rows = height * levels
    count = lax.axis_size("bond")
    me = lax.axis_index("bond")
    block = rows // count
    steps = order(count)
    targets = jnp.stack([(me + step) % count for step in steps] + [me]).astype(jnp.int32)
    sources = jnp.stack([(me - step) % count for step in steps] + [me]).astype(jnp.int32)
    apply_flops = 4 * rows * height * width * height

    mpo_rows = jnp.transpose(mpo, (1, 2, 3, 0)).reshape(width * levels, levels * width)
    folded, left_near, vector, basis = pl.pallas_call(
        begin_kernel,
        out_shape=(
            on_chip((height // 2 + 1, width, height), bf16),
            on_chip(left.shape, bf16),
            on_chip((height, rows), bf16),
            on_chip((rows, height), bf16),
        ),
        in_specs=[HBM_BLOCK] * 3,
        out_specs=(VMEM_BLOCK,) * 4,
        scratch_shapes=[
            pltpu.VMEM(right.shape, bf16),
            pltpu.VMEM(start.shape, bf16),
            pltpu.VMEM((rows, height), f32),
            DMA((3,)),
        ],
        compiler_params=params(8),
        name="begin",
    )(right, left, start)
    folded = sent(folded, "seg", -1)
    first_coupled = pl.pallas_call(
        first_kernel,
        out_shape=on_chip((width, rows, height), bf16),
        in_specs=[VMEM_BLOCK] * 3,
        out_specs=VMEM_BLOCK,
        compiler_params=params(8),
        cost_estimate=cost(2 * apply_flops, 8 << 20),
        name="first_coupled",
    )(vector, left_near, mpo_rows)
    right_rows = pl.pallas_call(
        unfold_kernel,
        out_shape=on_chip((width * height, height), bf16),
        in_specs=[VMEM_BLOCK],
        out_specs=VMEM_BLOCK,
        scratch_shapes=[pltpu.VMEM((height // 2 * width, height), f32)],
        compiler_params=params(8),
        name="unfold",
    )(folded)

    def block_images(targets, name):
        return pl.pallas_call(
            block_images_kernel,
            out_shape=(on_chip((block, height), bf16),) * targets.shape[0],
            in_specs=[SMEM_BLOCK] + [VMEM_BLOCK] * 2,
            out_specs=(VMEM_BLOCK,) * targets.shape[0],
            compiler_params=params(8),
            cost_estimate=cost(apply_flops * targets.shape[0] // (2 * count), 8 << 20),
            name=name,
        )(targets, first_coupled, right_rows)

    sends = block_images(targets[:1], "image_first") + block_images(targets[1:-1], "image_rest")
    arrived = [sent(value, "bond", step) for value, step in zip(sends, steps)]
    own = pl.pallas_call(
        own_image_kernel,
        out_shape=on_chip((block, height), f32),
        in_specs=[SMEM_BLOCK] + [VMEM_BLOCK] * 3,
        out_specs=VMEM_BLOCK,
        compiler_params=params(8),
        cost_estimate=cost(apply_flops // (2 * count), 8 << 20),
        name="image_own",
    )(targets[-1:], first_coupled, right_rows, arrived[0])
    own = pl.pallas_call(
        sum_kernel,
        out_shape=on_chip((block, height), bf16),
        in_specs=[VMEM_BLOCK] * (count - 1),
        out_specs=VMEM_BLOCK,
        compiler_params=params(4),
        name="sum",
    )(own, *arrived[1:])
    grown_shape = (height * width, height)
    one = pl.pallas_call(
        grow_first_kernel,
        out_shape=on_chip(grown_shape, f32),
        in_specs=[VMEM_BLOCK] * 3,
        out_specs=VMEM_BLOCK,
        scratch_shapes=[pltpu.VMEM((height, rows), bf16)],
        compiler_params=params(8),
        cost_estimate=cost(apply_flops, 8 << 20),
        name="grow_first",
    )(own, basis, first_coupled)
    blocks = [sent(own, "bond", step) for step in steps] + [own]
    outcome = pl.pallas_call(
        functools.partial(second_kernel, count),
        out_shape=(
            on_chip((width, rows, height), bf16),
            on_chip((rows, height), f32),
            on_chip((rows, height), f32),
            jax.ShapeDtypeStruct((2,), f32),
        )
        + (on_chip((block + TAIL, height), bf16),) * count,
        in_specs=[SMEM_BLOCK] + [VMEM_BLOCK] * count + [HBM_BLOCK] * 2 + [VMEM_BLOCK] * 2,
        out_specs=(VMEM_BLOCK,) * 3 + (SMEM_BLOCK,) + (VMEM_BLOCK,) * count,
        scratch_shapes=[
            pltpu.VMEM(start.shape, bf16),
            pltpu.VMEM(left.shape, bf16),
            pltpu.VMEM((rows, height), f32),
            DMA((2,)),
        ],
        compiler_params=params(12),
        name="second_image",
    )(jnp.concatenate([sources, targets]), *blocks, start, left, mpo_rows, right_rows)
    second_coupled, basis, second, scalars = outcome[:4]
    sends = outcome[4:]
    parts = [sent(value, "bond", step) for value, step in zip(sends, steps)] + [sends[-1]]
    cross, two = pl.pallas_call(
        grow_second_kernel,
        out_shape=(on_chip(grown_shape, f32),) * 2,
        in_specs=[VMEM_BLOCK] * 3,
        out_specs=(VMEM_BLOCK,) * 2,
        scratch_shapes=[pltpu.VMEM((2 * height, rows), bf16)],
        compiler_params=params(8),
        cost_estimate=cost(2 * apply_flops, 16 << 20),
        name="grow_second",
    )(basis, second, second_coupled)
    new_state, new_left, energy, share = pl.pallas_call(
        functools.partial(last_kernel, count),
        out_shape=(
            jax.ShapeDtypeStruct((height, levels, height), bf16),
            jax.ShapeDtypeStruct((height, width, height), bf16),
            jax.ShapeDtypeStruct((1, height), f32),
            jax.ShapeDtypeStruct((height // count, levels, height), f32),
        ),
        in_specs=[SMEM_BLOCK] + [VMEM_BLOCK] * count + [SMEM_BLOCK] + [VMEM_BLOCK] * 5,
        out_specs=(VMEM_BLOCK,) * 4,
        compiler_params=params(12),
        name="last",
    )(sources, *parts, scalars, basis, second, one, cross, two)
    return (new_state[None], new_left[None], energy[0, :1], share[None])


def solution(mesh):
    in_specs = (
        P("seg", None, "bond", None),
        P("seg", None, "bond", None),
        P("seg", "bond", None, None, None),
        P("seg", None, None, None),
    )
    out_specs = (
        P("seg", None, None, None),
        P("seg", None, "bond", None),
        P("seg"),
        P("seg", "bond", None, None),
    )
    return jax.shard_map(body, mesh=mesh, in_specs=in_specs, out_specs=out_specs, check_vma=False)
```

time: 67.1 us -> 61.1 us (0.911)
  waiting for transfers between devices: 8.11 us -> 2.94 us
  Pallas kernels: 29.3 us -> 30.6 us
  local copies, waits for them, and re-layouts: 10.3 us -> 9.33 us
    ppermute x10, waiting for transfers between devices: 8.11 us -> 2.94 us  [sent(): lax.ppermute(value, axis, [(source, (source + step) % count) for source i...]
    pallas_call x9 -> x10, Pallas kernels: 24.7 us -> 25.9 us  [the longest x1 10.2 us: body(): pl.pallas_call(functools.partial(second_kernel, count), out_shape=(on_chi...]
    dynamic_update_slice x11 -> x0, local copies, waits for them, and re-layouts: 1.07 us -> none  [the longest x1 0.91 us: gather(): received = lax.dynamic_update_index_in_dim(received, block, me, 0)]
    reduce_sum x1 -> x0, other arithmetic: 0.67 us -> none  [body(): own = jnp.sum(scatter(block_image, 'bond').astype(f32), axis=0).astype(bf16)]
  transfers between devices with their start and end apart: 10 -> 10, of which waited for: 5 -> 1; matrix products, arithmetic and copies ran while one was open for 5% -> 4% of each run, Pallas kernels for 19% -> 25%
where the time goes in v3:
time: 61.1 us; the launch traced here: 60.7 us
  Pallas kernels  30.6 us (50%)
  starting transfers between devices  16.9 us (28%)
  local copies, waits for them, and re-layouts  9.33 us (15%)
  waiting for transfers between devices  2.94 us (5%)
  between operations  0.87 us (1%)
    ppermute x10, starting transfers between devices, sent(): lax.ppermute(value, axis, [(source, (source + step) % count) for source i...  16.9 us
    pallas_call x1, Pallas kernels, body(): pl.pallas_call(functools.partial(second_kernel, count), out_shape=(on_chi...  10.2 us
    unnamed x16, local copies, waits for them, and re-layouts  6.79 us
    pallas_call x1, Pallas kernels, body(): pl.pallas_call(first_kernel, out_shape=on_chip((width, rows, height), bf1...  5.43 us
    pallas_call x1, Pallas kernels, body(): pl.pallas_call(grow_second_kernel, out_shape=(on_chip(grown_shape, f32),)...  4.66 us
    ppermute x10, waiting for transfers between devices, sent(): lax.ppermute(value, axis, [(source, (source + step) % count) for source i...  2.94 us
    pallas_call x1, Pallas kernels, body(): pl.pallas_call(functools.partial(last_kernel, count), out_shape=(jax.Shap...  2.8 us
    pallas_call x2, Pallas kernels, block_images(): pl.pallas_call(block_images_kernel, out_shape=(on_chip((block, height), b...  2.5 us
  transfers between devices with their start and end apart: 10, of which 1 were waited for; matrix products, arithmetic and copies ran while one was open for 4% of the time, Pallas kernels for 25%

profile of v3, /device:TPU:0, one launch (start us, length us, event | category | flops | bytes accessed | tf_op | source)
XLA Modules:
  0.0 60.7 jit_solution(3764023362039389575)
XLA Ops:
  0.6 0.0 copy-start.3
  0.6 1.2 %copy-done.3 = bf16[1,128,32,128]{3,2,1,0:T(8,128)(2,1)S(1)} copy-done((bf16[1,128,32,128]{3,2,1,0:T(8,128)(2,1)S(1)}, bf16[1,128,32,128]{3,2,1,0:T(8,128)(2,1)}, u32[]{:S(2)}) %copy-start.3) | copy-done | bytes 1048600
  1.9 0.9 %copy-done.5 = bf16[1,128,8,128]{3,2,1,0:T(8,128)(2,1)S(1)} copy-done((bf16[1,128,8,128]{3,2,1,0:T(8,128)(2,1)S(1)}, bf16[1,128,8,128]{3,2,1,0:T(8,128)(2,1)}, u32[]{:S(2)}) %copy-start.5) | copy-done | bytes 262168
  2.8 1.2 %copy-done.7 = bf16[1,128,32,128]{3,2,1,0:T(8,128)(2,1)S(1)} copy-done((bf16[1,128,32,128]{3,2,1,0:T(8,128)(2,1)S(1)}, bf16[1,128,32,128]{3,2,1,0:T(8,128)(2,1)}, u32[]{:S(2)}) %copy-start.7) | copy-done | bytes 1048600
  4.0 0.9 %begin.1 = (bf16[65,32,128]{2,1,0:T(8,128)(2,1)S(1)}, bf16[128,32,128]{2,1,0:T(8,128)(2,1)S(1)}, bf16[128,1024]{1,0:T(8,128)(2,1)S(1)}, bf16[1024,128]{1,0:T(8,128)(2,1)S(1)}) custom-call(bf16[128,32,128]{2,1,0:T(8,128)(2,1)S(1)} %bitcast.24, bf16[128,32,128]{2,1,0:T(8,128)(2,1)S(1)} %bitcast.20, bf16[128,8,128]{2,1,0:T(8,128)(2,1)S(1)} %bitcast.22), custom_call_target="tpu_custom_call" | custom-call | tf_op jit(solution)/shard_map/begin/pallas_call | solution.py:279
  4.9 3.4 %collective-permute-start = (bf16[65,32,128]{2,1,0:T(8,128)(2,1)S(1)}, bf16[65,32,128]{2,1,0:T(8,128)(2,1)S(1)}, u32[]{:S(2)}, u32[]{:S(2)}) collective-permute-start(bf16[65,32,128]{2,1,0:T(8,128)(2,1)S(1)} %get-tuple-element.26), channel_id=1, source_target_pairs={{0,28},{4,0},{8,4},{12,8},{16,12},{20,16},{24,20},{28,24},{1,29},{... | collective-permute-start | bytes 1597448 | tf_op jit(solution)/shard_map/ppermute | solution.py:262
  8.3 2.1 %copy.8 = bf16[32,8,8,32]{3,2,1,0:T(8,128)(2,1)S(1)} copy(bf16[32,8,8,32]{0,2,1,3:T(8,128)(2,1)} %bitcast.25) | data formatting | bytes 262144 | tf_op jit(solution)/shard_map/transpose | solution.py:278
  10.4 0.4 reshape.11.mpo_ref.refs_6_
  10.9 0.1 pad_add_fusion.1.where_ref
  10.9 5.4 %first_coupled.1.coupled_ref = bf16[32,1024,128]{2,1,0:T(8,128)(2,1)S(1)} custom-call(bf16[128,1024]{1,0:T(8,128)(2,1)S(1)} %get-tuple-element.24.vector_ref, bf16[128,32,128]{2,1,0:T(8,128)(2,1)S(1)} %get-tuple-element.25.left_ref, bf16[256,256]{1,0:T(8,128)(2,1)S(1)} %reshape.11.mpo_ref.refs_6_), custom_call_target="tpu_custom_call" | custom-call | flops 4294967296 | bytes 8388608 | tf_op jit(solution)/shard_map/first_coupled/pallas_call | solution.py:299
  16.4 0.0 collective-permute-done.folded_ref
  16.4 1.0 %unfold.1.right_ref.refs_7_ = bf16[4096,128]{1,0:T(8,128)(2,1)S(1)} custom-call(bf16[65,32,128]{2,1,0:T(8,128)(2,1)S(1)} %collective-permute-done.folded_ref), custom_call_target="tpu_custom_call" | custom-call | tf_op jit(solution)/shard_map/unfold/pallas_call | solution.py:308
  17.4 0.7 %image_first.1 = bf16[256,128]{1,0:T(8,128)(2,1)S(1)} custom-call(s32[1]{0:T(128)} %bitcast.4.where_ref, bf16[32,1024,128]{2,1,0:T(8,128)(2,1)S(1)} %first_coupled.1.coupled_ref, bf16[4096,128]{1,0:T(8,128)(2,1)S(1)} %unfold.1.right_ref.refs_7_), custom_call_target="tpu_custom_call" | custom-call | flops 268435456 | bytes 8388608 | tf_op jit(solution)/shard_map/image_first/pallas_call | solution.py:319
  18.1 2.7 %collective-permute-start.1 = (bf16[256,128]{1,0:T(8,128)(2,1)S(1)}, bf16[256,128]{1,0:T(8,128)(2,1)S(1)}, u32[]{:S(2)}, u32[]{:S(2)}) collective-permute-start(bf16[256,128]{1,0:T(8,128)(2,1)S(1)} %image_first.1), channel_id=1, source_target_pairs={{0,2},{1,3},{2,0},{3,1},{4,6},{5,7},{6,4},{7,5},{8,10},{9,11},{10,... | collective-permute-start | bytes 196616 | tf_op jit(solution)/shard_map/ppermute | solution.py:262
  20.8 1.8 %image_rest.1 = (bf16[256,128]{1,0:T(8,128)(2,1)S(1)}, bf16[256,128]{1,0:T(8,128)(2,1)S(1)}) custom-call(s32[2]{0:T(128)S(1)} %pad_add_fusion.1.where_ref, bf16[32,1024,128]{2,1,0:T(8,128)(2,1)S(1)} %first_coupled.1.coupled_ref, bf16[4096,128]{1,0:T(8,128)(2,1)S(1)} %unfold.1.right_ref.refs_7_), custom_call_target="tpu_custom_call" | custom-call | flops 536870912 | bytes 8388608 | tf_op jit(solution)/shard_map/image_rest/pallas_call | solution.py:319
  22.6 1.6 %collective-permute-start.2 = (bf16[256,128]{1,0:T(8,128)(2,1)S(1)}, bf16[256,128]{1,0:T(8,128)(2,1)S(1)}, u32[]{:S(2)}, u32[]{:S(2)}) collective-permute-start(bf16[256,128]{1,0:T(8,128)(2,1)S(1)} %get-tuple-element.27), channel_id=1, source_target_pairs={{0,1},{1,2},{2,3},{3,0},{4,5},{5,6},{6,7},{7,4},{8,9},{9,10},{10,1... | collective-permute-start | bytes 196616 | tf_op jit(solution)/shard_map/ppermute | solution.py:262
  24.2 2.2 %collective-permute-start.3 = (bf16[256,128]{1,0:T(8,128)(2,1)S(1)}, bf16[256,128]{1,0:T(8,128)(2,1)S(1)}, u32[]{:S(2)}, u32[]{:S(2)}) collective-permute-start(bf16[256,128]{1,0:T(8,128)(2,1)S(1)} %get-tuple-element.28), channel_id=1, source_target_pairs={{0,3},{1,0},{2,1},{3,2},{4,7},{5,4},{6,5},{7,6},{8,11},{9,8},{10,9... | collective-permute-start | bytes 196616 | tf_op jit(solution)/shard_map/ppermute | solution.py:262
  26.5 0.1 pad_add_fusion.where_ref
  26.6 0.1 concatenate.5.where_ref
  26.7 3.4 %copy-done.1 = bf16[32,1024,128]{2,1,0:T(8,128)(2,1)S(1)} copy-done((bf16[32,1024,128]{2,1,0:T(8,128)(2,1)S(1)}, bf16[32,1024,128]{2,1,0:T(8,128)(2,1)}, u32[]{:S(2)}) %copy-start.1) | copy-done | bytes 8388632
  30.0 0.7 %image_own.1.own_ref = f32[256,128]{1,0:T(8,128)S(1)} custom-call(s32[1]{0:T(128)} %bitcast.3.where_ref, bf16[32,1024,128]{2,1,0:T(8,128)(2,1)S(1)} %copy-done.1, bf16[4096,128]{1,0:T(8,128)(2,1)S(1)} %unfold.1.right_ref.refs_7_, bf16[256,128]{1,0:T(8,128)(2,1)S(1)} %collective-permute-done.1.arrived_ref), custom_call_target="tpu_custom_call" | custom-call | flops 268435456 | bytes 8388608 | tf_op jit(solution)/shard_map/image_own/pallas_call | solution.py:331
  30.8 1.8 %collective-permute-start.6 = (bf16[256,128]{1,0:T(8,128)(2,1)S(1)}, bf16[256,128]{1,0:T(8,128)(2,1)S(1)}, u32[]{:S(2)}, u32[]{:S(2)}) collective-permute-start(bf16[256,128]{1,0:T(8,128)(2,1)S(1)} %sum.1.refs_3_.after_ref), channel_id=1, source_target_pairs={{0,3},{1,0},{2,1},{3,2},{4,7},{5,4},{6,5},{7,6},{8,11},{9,8},{10,9... | collective-permute-start | bytes 196616 | tf_op jit(solution)/shard_map/ppermute | solution.py:262
  32.6 0.2 collective-permute-start.5
  32.9 0.6 collective-permute-start.4
  33.4 2.4 %grow_first.1.refs_7_ = f32[4096,128]{1,0:T(8,128)S(1)} custom-call(bf16[256,128]{1,0:T(8,128)(2,1)S(1)} %sum.1.refs_3_.after_ref, bf16[1024,128]{1,0:T(8,128)(2,1)S(1)} %get-tuple-element.36.basis_ref, bf16[32,1024,128]{2,1,0:T(8,128)(2,1)S(1)} %copy-done.2), custom_call_target="tpu_custom_call" | custom-call | flops 2147483648 | bytes 8388608 | tf_op jit(solution)/shard_map/grow_first/pallas_call | solution.py:349
  35.8 2.9 %collective-permute-done.5.refs_1_ = bf16[256,128]{1,0:T(8,128)(2,1)S(1)} collective-permute-done((bf16[256,128]{1,0:T(8,128)(2,1)S(1)}, bf16[256,128]{1,0:T(8,128)(2,1)S(1)}, u32[]{:S(2)}, u32[]{:S(2)}) %collective-permute-start.5) | collective-permute-done | bytes 65568 | tf_op jit(solution)/shard_map/ppermute | solution.py:262
  38.8 10.2 %second_image.1 = (bf16[32,1024,128]{2,1,0:T(8,128)(2,1)S(1)}, f32[1024,128]{1,0:T(8,128)S(1)}, f32[1024,128]{1,0:T(8,128)S(1)}, f32[2]{0:T(128)S(1)}, bf16[272,...) custom-call(s32[8]{0:T(128)S(1)} %concatenate.5.where_ref, ...), custom_call_target="tpu_custom_call" | custom-call | tf_op jit(solution)/shard_map/second_image/pallas_call | solution.py:360
  48.9 0.5 collective-permute-start.7
  49.4 3.0 %collective-permute-start.8 = (bf16[272,128]{1,0:T(8,128)(2,1)S(1)}, bf16[272,128]{1,0:T(8,128)(2,1)S(1)}, u32[]{:S(2)}, u32[]{:S(2)}) collective-permute-start(bf16[272,128]{1,0:T(8,128)(2,1)S(1)} %get-tuple-element.30), channel_id=1, source_target_pairs={{0,1},{1,2},{2,3},{3,0},{4,5},{5,6},{6,7},{7,4},{8,9},{9,10},{10,1... | collective-permute-start | bytes 208904 | tf_op jit(solution)/shard_map/ppermute | solution.py:262
  52.4 0.8 %collective-permute-start.9 = (bf16[272,128]{1,0:T(8,128)(2,1)S(1)}, bf16[272,128]{1,0:T(8,128)(2,1)S(1)}, u32[]{:S(2)}, u32[]{:S(2)}) collective-permute-start(bf16[272,128]{1,0:T(8,128)(2,1)S(1)} %get-tuple-element.31), channel_id=1, source_target_pairs={{0,3},{1,0},{2,1},{3,2},{4,7},{5,4},{6,5},{7,6},{8,11},{9,8},{10,9... | collective-permute-start | bytes 208904 | tf_op jit(solution)/shard_map/ppermute | solution.py:262
  53.3 4.7 %grow_second.1 = (f32[4096,128]{1,0:T(8,128)S(1)}, f32[4096,128]{1,0:T(8,128)S(1)}) custom-call(f32[1024,128]{1,0:T(8,128)S(1)} %get-tuple-element.34.basis_ref.refs_5_, f32[1024,128]{1,0:T(8,128)S(1)} %get-tuple-element.35.second_ref.refs_6_, bf16[32,1024,128]{2,1,0:T(8,128)(2,1)S(1)} %get-tuple-element.37.coupled_ref), custom_call_target="tpu_custom_call" | custom-call | flops 4294967296 | bytes 16777216 | tf_op jit(solution)/shard_map/grow_second/pallas_call | solution.py:383
  57.9 2.8 %last.1 = (bf16[128,8,128]{2,1,0:T(8,128)(2,1)}, bf16[128,32,128]{2,1,0:T(8,128)(2,1)}, f32[1,128]{1,0:T(1,128)}, f32[32,8,128]{2,1,0:T(8,128)}) custom-call(s32[4]{0:T(128)S(1)} %pad_add_fusion.where_ref, bf16[272,128]{1,0:T(8,128)(2,1)S(1)} %collective-permute-done.7.refs_0_, bf16[272,128]{1,0:T(8,128)(2,1)S(1)} %collective-permute-done.8.refs_1_, ...), custom_call_target="tpu_custom_call" | custom-call | tf_op jit(solution)/shard_map/last/pallas_call | solution.py:393
  (20 shorter events, 0.1 us)
Async XLA Ops:
  0.6 1.2 %copy-start.3 = (bf16[1,128,32,128]{3,2,1,0:T(8,128)(2,1)S(1)}, bf16[1,128,32,128]{3,2,1,0:T(8,128)(2,1)}, u32[]{:S(2)}) copy-start(bf16[1,128,32,128]{3,2,1,0:T(8,128)(2,1)} %param.4) | copy-start | bytes 3145732
  1.9 0.9 %copy-start.5 = (bf16[1,128,8,128]{3,2,1,0:T(8,128)(2,1)S(1)}, bf16[1,128,8,128]{3,2,1,0:T(8,128)(2,1)}, u32[]{:S(2)}) copy-start(bf16[1,128,8,128]{3,2,1,0:T(8,128)(2,1)} %param.7) | copy-start | bytes 786436
  2.8 1.2 %copy-start.7 = (bf16[1,128,32,128]{3,2,1,0:T(8,128)(2,1)S(1)}, bf16[1,128,32,128]{3,2,1,0:T(8,128)(2,1)}, u32[]{:S(2)}) copy-start(bf16[1,128,32,128]{3,2,1,0:T(8,128)(2,1)} %param.5) | copy-start | bytes 3145732
  4.9 11.4 %collective-permute-start = (bf16[65,32,128]{2,1,0:T(8,128)(2,1)S(1)}, bf16[65,32,128]{2,1,0:T(8,128)(2,1)S(1)}, u32[]{:S(2)}, u32[]{:S(2)}) collective-permute-start(bf16[65,32,128]{2,1,0:T(8,128)(2,1)S(1)} %get-tuple-element.26), channel_id=1, source_target_pairs={{0,28},{4,0},{8,4},{12,8},{16,12},{20,16},{24,20},{28,24},{1,29},{... | collective-permute-start | bytes 1597448 | tf_op jit(solution)/shard_map/ppermute | solution.py:262
  16.4 4.4 %copy-start = (bf16[32,1024,128]{2,1,0:T(8,128)(2,1)}, bf16[32,1024,128]{2,1,0:T(8,128)(2,1)S(1)}, u32[]{:S(2)}) copy-start(bf16[32,1024,128]{2,1,0:T(8,128)(2,1)S(1)} %first_coupled.1.coupled_ref) | copy-start | bytes 25165828
  18.1 8.5 %collective-permute-start.1 = (bf16[256,128]{1,0:T(8,128)(2,1)S(1)}, bf16[256,128]{1,0:T(8,128)(2,1)S(1)}, u32[]{:S(2)}, u32[]{:S(2)}) collective-permute-start(bf16[256,128]{1,0:T(8,128)(2,1)S(1)} %image_first.1), channel_id=1, source_target_pairs={{0,2},{1,3},{2,0},{3,1},{4,6},{5,7},{6,4},{7,5},{8,10},{9,11},{10,... | collective-permute-start | bytes 196616 | tf_op jit(solution)/shard_map/ppermute | solution.py:262
  22.6 8.1 %collective-permute-start.2 = (bf16[256,128]{1,0:T(8,128)(2,1)S(1)}, bf16[256,128]{1,0:T(8,128)(2,1)S(1)}, u32[]{:S(2)}, u32[]{:S(2)}) collective-permute-start(bf16[256,128]{1,0:T(8,128)(2,1)S(1)} %get-tuple-element.27), channel_id=1, source_target_pairs={{0,1},{1,2},{2,3},{3,0},{4,5},{5,6},{6,7},{7,4},{8,9},{9,10},{10,1... | collective-permute-start | bytes 196616 | tf_op jit(solution)/shard_map/ppermute | solution.py:262
  24.2 6.5 %collective-permute-start.3 = (bf16[256,128]{1,0:T(8,128)(2,1)S(1)}, bf16[256,128]{1,0:T(8,128)(2,1)S(1)}, u32[]{:S(2)}, u32[]{:S(2)}) collective-permute-start(bf16[256,128]{1,0:T(8,128)(2,1)S(1)} %get-tuple-element.28), channel_id=1, source_target_pairs={{0,3},{1,0},{2,1},{3,2},{4,7},{5,4},{6,5},{7,6},{8,11},{9,8},{10,9... | collective-permute-start | bytes 196616 | tf_op jit(solution)/shard_map/ppermute | solution.py:262
  26.6 3.4 %copy-start.1 = (bf16[32,1024,128]{2,1,0:T(8,128)(2,1)S(1)}, bf16[32,1024,128]{2,1,0:T(8,128)(2,1)}, u32[]{:S(2)}) copy-start(bf16[32,1024,128]{2,1,0:T(8,128)(2,1)} %copy-done) | copy-start | bytes 25165828
  30.0 3.4 %copy-start.2 = (bf16[32,1024,128]{2,1,0:T(8,128)(2,1)S(1)}, bf16[32,1024,128]{2,1,0:T(8,128)(2,1)}, u32[]{:S(2)}) copy-start(bf16[32,1024,128]{2,1,0:T(8,128)(2,1)} %copy-done) | copy-start | bytes 25165828
  30.8 5.0 %collective-permute-start.6 = (bf16[256,128]{1,0:T(8,128)(2,1)S(1)}, bf16[256,128]{1,0:T(8,128)(2,1)S(1)}, u32[]{:S(2)}, u32[]{:S(2)}) collective-permute-start(bf16[256,128]{1,0:T(8,128)(2,1)S(1)} %sum.1.refs_3_.after_ref), channel_id=1, source_target_pairs={{0,3},{1,0},{2,1},{3,2},{4,7},{5,4},{6,5},{7,6},{8,11},{9,8},{10,9... | collective-permute-start | bytes 196616 | tf_op jit(solution)/shard_map/ppermute | solution.py:262
  32.6 6.1 %collective-permute-start.5 = (bf16[256,128]{1,0:T(8,128)(2,1)S(1)}, bf16[256,128]{1,0:T(8,128)(2,1)S(1)}, u32[]{:S(2)}, u32[]{:S(2)}) collective-permute-start(bf16[256,128]{1,0:T(8,128)(2,1)S(1)} %sum.1.refs_3_.after_ref), channel_id=1, source_target_pairs={{0,1},{1,2},{2,3},{3,0},{4,5},{5,6},{6,7},{7,4},{8,9},{9,10},{10,1... | collective-permute-start | bytes 196616 | tf_op jit(solution)/shard_map/ppermute | solution.py:262
  32.9 5.9 %collective-permute-start.4 = (bf16[256,128]{1,0:T(8,128)(2,1)S(1)}, bf16[256,128]{1,0:T(8,128)(2,1)S(1)}, u32[]{:S(2)}, u32[]{:S(2)}) collective-permute-start(bf16[256,128]{1,0:T(8,128)(2,1)S(1)} %sum.1.refs_3_.after_ref), channel_id=1, source_target_pairs={{0,2},{1,3},{2,0},{3,1},{4,6},{5,7},{6,4},{7,5},{8,10},{9,11},{10,... | collective-permute-start | bytes 196616 | tf_op jit(solution)/shard_map/ppermute | solution.py:262
  33.4 5.3 %copy-start.4 = (bf16[1,128,32,128]{3,2,1,0:T(8,128)(2,1)S(1)}, bf16[1,128,32,128]{3,2,1,0:T(8,128)(2,1)}, u32[]{:S(2)}) copy-start(bf16[1,128,32,128]{3,2,1,0:T(8,128)(2,1)} %param.4) | copy-start | bytes 3145732
  33.4 5.3 %copy-start.6 = (bf16[1,128,8,128]{3,2,1,0:T(8,128)(2,1)S(1)}, bf16[1,128,8,128]{3,2,1,0:T(8,128)(2,1)}, u32[]{:S(2)}) copy-start(bf16[1,128,8,128]{3,2,1,0:T(8,128)(2,1)} %param.7) | copy-start | bytes 786436
  48.9 9.0 %collective-permute-start.7 = (bf16[272,128]{1,0:T(8,128)(2,1)S(1)}, bf16[272,128]{1,0:T(8,128)(2,1)S(1)}, u32[]{:S(2)}, u32[]{:S(2)}) collective-permute-start(bf16[272,128]{1,0:T(8,128)(2,1)S(1)} %get-tuple-element.29), channel_id=1, source_target_pairs={{0,2},{1,3},{2,0},{3,1},{4,6},{5,7},{6,4},{7,5},{8,10},{9,11},{10,... | collective-permute-start | bytes 208904 | tf_op jit(solution)/shard_map/ppermute | solution.py:262
  49.4 8.5 %collective-permute-start.8 = (bf16[272,128]{1,0:T(8,128)(2,1)S(1)}, bf16[272,128]{1,0:T(8,128)(2,1)S(1)}, u32[]{:S(2)}, u32[]{:S(2)}) collective-permute-start(bf16[272,128]{1,0:T(8,128)(2,1)S(1)} %get-tuple-element.30), channel_id=1, source_target_pairs={{0,1},{1,2},{2,3},{3,0},{4,5},{5,6},{6,7},{7,4},{8,9},{9,10},{10,1... | collective-permute-start | bytes 208904 | tf_op jit(solution)/shard_map/ppermute | solution.py:262
  52.4 5.5 %collective-permute-start.9 = (bf16[272,128]{1,0:T(8,128)(2,1)S(1)}, bf16[272,128]{1,0:T(8,128)(2,1)S(1)}, u32[]{:S(2)}, u32[]{:S(2)}) collective-permute-start(bf16[272,128]{1,0:T(8,128)(2,1)S(1)} %get-tuple-element.31), channel_id=1, source_target_pairs={{0,3},{1,0},{2,1},{3,2},{4,7},{5,4},{6,5},{7,6},{8,11},{9,8},{10,9... | collective-permute-start | bytes 208904 | tf_op jit(solution)/shard_map/ppermute | solution.py:262

commit v4 on v3

--- a/solution.py
+++ b/solution.py
@@ -82,7 +82,7 @@
     lax.fori_loop(0, rows // chunk, step, 0)
 
 
-def begin_kernel(right_hbm, left_hbm, start_hbm, folded_ref, left_ref, vector_ref, basis_ref, right, start, rows, sems):
+def begin_kernel(right_hbm, left_hbm, start_hbm, folded_ref, left_ref, vector_ref, basis_ref, right, start, sems):
     height, width, _ = right.shape
     levels = start.shape[1]
     half = height // 2
@@ -101,14 +101,25 @@
     folded_ref[:half] = jnp.where(lane >= row, right[:half].astype(f32), turned).astype(bf16)
     folded_ref[half] = jnp.sum(jnp.where(lane == row + half, lower, 0.0), axis=0).astype(bf16)
     copies[1].wait()
-    rows[...] = normalised(start[...])
-    basis_ref[...] = rows[...].astype(bf16)
-    vector_ref[...] = by_level(rows, height, levels)
+    basis_ref[...] = normalised(start[...])
+    vector_ref[...] = by_level(basis_ref, height, levels)
     copies[2].wait()
 
 
-def first_kernel(vector_ref, left_ref, mpo_ref, coupled_ref):
-    couple(left_ref, vector_ref[...], mpo_ref[...], coupled_ref, 32)
+def reorder(size, first, second):
+    row = lax.broadcasted_iota(jnp.int32, (size, size), 0)
+    lane = lax.broadcasted_iota(jnp.int32, (size, size), 1)
+    return jnp.where((row // second == lane % first) & (row % second == lane // first), 1.0, 0.0).astype(bf16)
+
+
+def first_kernel(vector_ref, left_ref, mpo_ref, coupled_ref, mpo_rows_ref):
+    width, levels, _, right_width = mpo_ref.shape
+    terms = [mpo_ref[:, s].astype(f32).reshape(width * levels, right_width).T for s in range(levels)]
+    terms = jnp.concatenate(terms, axis=0).astype(bf16)
+    terms = jnp.dot(reorder(right_width * levels, right_width, levels), terms, preferred_element_type=f32)
+    terms = jnp.dot(terms.astype(bf16), reorder(width * levels, width, levels), preferred_element_type=f32)
+    mpo_rows_ref[...] = terms.astype(bf16)
+    couple(left_ref, vector_ref[...], mpo_rows_ref[...], coupled_ref, 32)
 
 
 def unfold_kernel(folded_ref, right_ref, wide):
@@ -136,13 +147,18 @@
     return jnp.dot(terms, right_ref[...], preferred_element_type=f32)
 
 
-def block_images_kernel(where_ref, coupled_ref, right_ref, *image_refs):
-    for k, image_ref in enumerate(image_refs):
-        image_ref[...] = block_image(where_ref[k], coupled_ref, right_ref, image_ref.shape[0]).astype(bf16)
-
-
-def own_image_kernel(where_ref, coupled_ref, right_ref, arrived_ref, image_ref):
-    own = block_image(where_ref[0], coupled_ref, right_ref, image_ref.shape[0])
+def other(step):
+    count = lax.axis_size("bond")
+    return lax.rem(lax.axis_index("bond") + (step + count), count)
+
+
+def block_images_kernel(steps, coupled_ref, right_ref, *image_refs):
+    for step, image_ref in zip(steps, image_refs):
+        image_ref[...] = block_image(other(step), coupled_ref, right_ref, image_ref.shape[0]).astype(bf16)
+
+
+def own_image_kernel(coupled_ref, right_ref, arrived_ref, image_ref):
+    own = block_image(other(0), coupled_ref, right_ref, image_ref.shape[0])
     image_ref[...] = own + arrived_ref[...].astype(f32)
 
 
@@ -153,33 +169,26 @@
     refs[-1][...] = total.astype(bf16)
 
 
-def second_kernel(count, where_ref, *refs):
+def second_kernel(steps, *refs):
+    count = len(steps)
     blocks, refs = refs[:count], refs[count:]
-    start_hbm, left_hbm, mpo_ref, right_ref, coupled_ref, basis_ref, second_ref, scalar_ref = refs[:8]
-    sends, (start, left, total, sems) = refs[8 : 8 + count], refs[8 + count :]
-    start_copy = pltpu.make_async_copy(start_hbm, start, sems.at[0])
-    left_copy = pltpu.make_async_copy(left_hbm, left, sems.at[1])
-    start_copy.start()
-    left_copy.start()
-    height, width, _ = left.shape
+    basis_ref, left_ref, mpo_ref, right_ref, coupled_ref, second_ref, scalar_ref = refs[:7]
+    sends, total = refs[7 : 7 + count], refs[7 + count]
+    height, width, _ = left_ref.shape
     rows = basis_ref.shape[0]
     levels = rows // height
     entries = rows * height
     block = blocks[0].shape[0]
-    for k in range(count):
-        place = pl.ds(pl.multiple_of(where_ref[k] * block, block), block)
+    for k, step in enumerate(steps):
+        place = pl.ds(pl.multiple_of(other(-step) * block, block), block)
         total[place, :] = blocks[k][...].astype(f32)
-    start_copy.wait()
-    basis_ref[...] = normalised(start[...])
     basis = basis_ref[...]
     first_image = total[...]
     rayleigh = jnp.sum(basis * first_image) / entries
     residual = first_image - rayleigh * basis
     residual_size = jnp.sqrt(jnp.sum(residual * residual) / entries + epsilon)
     second_ref[...] = residual / residual_size
-    vector = by_level(second_ref, height, levels)
-    left_copy.wait()
-    couple(left, vector, mpo_ref[...], coupled_ref, 32)
+    couple(left_ref, by_level(second_ref, height, levels), mpo_ref[...], coupled_ref, 32)
     image(coupled_ref, right_ref, total, 256)
     value = jnp.sum(second_ref[...] * total[...]) / entries
     high = value.astype(bf16).astype(f32)
@@ -187,8 +196,8 @@
     low = value - high - middle
     lane = lax.broadcasted_iota(jnp.int32, (TAIL, height), 1)
     tail = jnp.where(lane == 0, high, jnp.where(lane == 1, middle, jnp.where(lane == 2, low, 0.0))).astype(bf16)
-    for k in range(count):
-        place = pl.ds(pl.multiple_of(where_ref[count + k] * block, block), block)
+    for k, step in enumerate(steps):
+        place = pl.ds(pl.multiple_of(other(step) * block, block), block)
         sends[k][:block, :] = total[place, :].astype(bf16)
         sends[k][block:, :] = tail
     scalar_ref[0] = rayleigh
@@ -202,7 +211,7 @@
 def grow_first_kernel(after_ref, basis_ref, coupled_ref, one_ref, turned):
     del after_ref
     width, _, height = coupled_ref.shape
-    turned[...] = basis_ref[...].astype(f32).T.astype(bf16)
+    turned[...] = basis_ref[...].T.astype(bf16)
     for u in range(0, width, 2):
         grown = jnp.dot(turned[...], pair_of(coupled_ref, u), preferred_element_type=f32)
         for k in (0, 1):
@@ -223,19 +232,21 @@
             two_ref[place, :] = grown[height:, lanes]
 
 
-def last_kernel(count, where_ref, *refs):
+def last_kernel(steps, *refs):
+    count = len(steps)
     parts, refs = refs[:count], refs[count:]
     scalar_ref, basis_ref, second_ref, one_ref, cross_ref, two_ref = refs[:6]
-    state_ref, left_ref, energy_ref, share_ref = refs[6:]
+    state_hbm, left_hbm, energy_ref, share_hbm, state, left, share, sems = refs[6:]
     block, height = parts[0].shape
     block -= TAIL
     lane = lax.broadcasted_iota(jnp.int32, (TAIL, height), 1)
     row = lax.broadcasted_iota(jnp.int32, (TAIL, height), 0)
     values = [jnp.sum(jnp.where((lane < 3) & (row == 0), part[block:, :].astype(f32), 0.0)) for part in parts]
+    sources = [other(-step) for step in steps]
     curvature = jnp.float32(0.0)
     for device in range(count):
-        for k in range(count):
-            curvature = curvature + jnp.where(where_ref[k] == device, values[k], 0.0)
+        for source, value in zip(sources, values):
+            curvature = curvature + jnp.where(source == device, value, 0.0)
     rayleigh, residual_size = scalar_ref[0], scalar_ref[1]
     middle = 0.5 * (rayleigh + curvature)
     half_gap = 0.5 * (rayleigh - curvature)
@@ -243,14 +254,31 @@
     offset = lowest - rayleigh
     length = jnp.sqrt(residual_size * residual_size + offset * offset)
     one, two = residual_size / length, offset / length
+    weights = (one * one, one * two, two * two)
+    copies = []
+
+    def send(source, target):
+        copies.append(pltpu.make_async_copy(source, target, sems.at[len(copies)]))
+        copies[-1].start()
+
+    pieces = sems.shape[0] - 2
+    size = left.shape[0] // pieces
+    width = left.shape[1]
+    for k in range(pieces):
+        place = slice(k * size * width, (k + 1) * size * width)
+        grown = weights[0] * one_ref[place, :] + weights[1] * cross_ref[place, :] + weights[2] * two_ref[place, :]
+        left[k * size : (k + 1) * size] = grown.astype(bf16).reshape(size, width, height)
+        send(left.at[pl.ds(k * size, size)], left_hbm.at[pl.ds(k * size, size)])
+    state[...] = (one * basis_ref[...] + two * second_ref[...]).astype(bf16).reshape(state.shape)
+    send(state, state_hbm)
+    total = parts[0][:block, :].astype(f32)
+    for part in parts[1:]:
+        total = total + part[:block, :].astype(f32)
+    share[...] = total.reshape(share.shape)
+    send(share, share_hbm)
     energy_ref[...] = jnp.full(energy_ref.shape, lowest, f32)
-    state_ref[...] = (one * basis_ref[...] + two * second_ref[...]).astype(bf16).reshape(state_ref.shape)
-    grown = (one * one) * one_ref[...] + (one * two) * cross_ref[...] + (two * two) * two_ref[...]
-    left_ref[...] = grown.astype(bf16).reshape(left_ref.shape)
-    share = parts[0][:block, :].astype(f32)
-    for part in parts[1:]:
-        share = share + part[:block, :].astype(f32)
-    share_ref[...] = share.reshape(share_ref.shape)
+    for copy in copies:
+        copy.wait()
 
 
 def order(count):
@@ -268,43 +296,38 @@
     levels = start.shape[1]
     rows = height * levels
     count = lax.axis_size("bond")
-    me = lax.axis_index("bond")
     block = rows // count
     steps = order(count)
-    targets = jnp.stack([(me + step) % count for step in steps] + [me]).astype(jnp.int32)
-    sources = jnp.stack([(me - step) % count for step in steps] + [me]).astype(jnp.int32)
+    with_own = tuple(steps) + (0,)
     apply_flops = 4 * rows * height * width * height
 
-    mpo_rows = jnp.transpose(mpo, (1, 2, 3, 0)).reshape(width * levels, levels * width)
     folded, left_near, vector, basis = pl.pallas_call(
         begin_kernel,
         out_shape=(
             on_chip((height // 2 + 1, width, height), bf16),
             on_chip(left.shape, bf16),
             on_chip((height, rows), bf16),
-            on_chip((rows, height), bf16),
+            on_chip((rows, height), f32),
         ),
         in_specs=[HBM_BLOCK] * 3,
         out_specs=(VMEM_BLOCK,) * 4,
-        scratch_shapes=[
-            pltpu.VMEM(right.shape, bf16),
-            pltpu.VMEM(start.shape, bf16),
-            pltpu.VMEM((rows, height), f32),
-            DMA((3,)),
-        ],
-        compiler_params=params(8),
+        scratch_shapes=[pltpu.VMEM(right.shape, bf16), pltpu.VMEM(start.shape, bf16), DMA((3,))],
+        compiler_params=params(61),
         name="begin",
     )(right, left, start)
     folded = sent(folded, "seg", -1)
-    first_coupled = pl.pallas_call(
+    first_coupled, mpo_rows = pl.pallas_call(
         first_kernel,
-        out_shape=on_chip((width, rows, height), bf16),
+        out_shape=(
+            on_chip((width, rows, height), bf16),
+            on_chip((width * levels, levels * width), bf16),
+        ),
         in_specs=[VMEM_BLOCK] * 3,
-        out_specs=VMEM_BLOCK,
+        out_specs=(VMEM_BLOCK,) * 2,
         compiler_params=params(8),
         cost_estimate=cost(2 * apply_flops, 8 << 20),
         name="first_coupled",
-    )(vector, left_near, mpo_rows)
+    )(vector, left_near, jnp.transpose(mpo, (0, 2, 3, 1)))
     right_rows = pl.pallas_call(
         unfold_kernel,
         out_shape=on_chip((width * height, height), bf16),
@@ -315,28 +338,28 @@
         name="unfold",
     )(folded)
 
-    def block_images(targets, name):
+    def block_images(steps, name):
         return pl.pallas_call(
-            block_images_kernel,
-            out_shape=(on_chip((block, height), bf16),) * targets.shape[0],
-            in_specs=[SMEM_BLOCK] + [VMEM_BLOCK] * 2,
-            out_specs=(VMEM_BLOCK,) * targets.shape[0],
+            functools.partial(block_images_kernel, steps),
+            out_shape=(on_chip((block, height), bf16),) * len(steps),
+            in_specs=[VMEM_BLOCK] * 2,
+            out_specs=(VMEM_BLOCK,) * len(steps),
             compiler_params=params(8),
-            cost_estimate=cost(apply_flops * targets.shape[0] // (2 * count), 8 << 20),
+            cost_estimate=cost(apply_flops * len(steps) // (2 * count), 8 << 20),
             name=name,
-        )(targets, first_coupled, right_rows)
-
-    sends = block_images(targets[:1], "image_first") + block_images(targets[1:-1], "image_rest")
+        )(first_coupled, right_rows)
+
+    sends = tuple(block_images(steps[:1], "image_first")) + tuple(block_images(steps[1:], "image_rest"))
     arrived = [sent(value, "bond", step) for value, step in zip(sends, steps)]
     own = pl.pallas_call(
         own_image_kernel,
         out_shape=on_chip((block, height), f32),
-        in_specs=[SMEM_BLOCK] + [VMEM_BLOCK] * 3,
+        in_specs=[VMEM_BLOCK] * 3,
         out_specs=VMEM_BLOCK,
         compiler_params=params(8),
         cost_estimate=cost(apply_flops // (2 * count), 8 << 20),
         name="image_own",
-    )(targets[-1:], first_coupled, right_rows, arrived[0])
+    )(first_coupled, right_rows, arrived[0])
     own = pl.pallas_call(
         sum_kernel,
         out_shape=on_chip((block, height), bf16),
@@ -358,27 +381,21 @@
     )(own, basis, first_coupled)
     blocks = [sent(own, "bond", step) for step in steps] + [own]
     outcome = pl.pallas_call(
-        functools.partial(second_kernel, count),
+        functools.partial(second_kernel, with_own),
         out_shape=(
             on_chip((width, rows, height), bf16),
-            on_chip((rows, height), f32),
             on_chip((rows, height), f32),
             jax.ShapeDtypeStruct((2,), f32),
         )
         + (on_chip((block + TAIL, height), bf16),) * count,
-        in_specs=[SMEM_BLOCK] + [VMEM_BLOCK] * count + [HBM_BLOCK] * 2 + [VMEM_BLOCK] * 2,
-        out_specs=(VMEM_BLOCK,) * 3 + (SMEM_BLOCK,) + (VMEM_BLOCK,) * count,
-        scratch_shapes=[
-            pltpu.VMEM(start.shape, bf16),
-            pltpu.VMEM(left.shape, bf16),
-            pltpu.VMEM((rows, height), f32),
-            DMA((2,)),
-        ],
+        in_specs=[VMEM_BLOCK] * (count + 4),
+        out_specs=(VMEM_BLOCK,) * 2 + (SMEM_BLOCK,) + (VMEM_BLOCK,) * count,
+        scratch_shapes=[pltpu.VMEM((rows, height), f32)],
         compiler_params=params(12),
         name="second_image",
-    )(jnp.concatenate([sources, targets]), *blocks, start, left, mpo_rows, right_rows)
-    second_coupled, basis, second, scalars = outcome[:4]
-    sends = outcome[4:]
+    )(*blocks, basis, left_near, mpo_rows, right_rows)
+    second_coupled, second, scalars = outcome[:3]
+    sends = outcome[3:]
     parts = [sent(value, "bond", step) for value, step in zip(sends, steps)] + [sends[-1]]
     cross, two = pl.pallas_call(
         grow_second_kernel,
@@ -390,19 +407,21 @@
         cost_estimate=cost(2 * apply_flops, 16 << 20),
         name="grow_second",
     )(basis, second, second_coupled)
+    outputs = (
+        jax.ShapeDtypeStruct((height, levels, height), bf16),
+        jax.ShapeDtypeStruct((height, width, height), bf16),
+        jax.ShapeDtypeStruct((1, height), f32),
+        jax.ShapeDtypeStruct((height // count, levels, height), f32),
+    )
     new_state, new_left, energy, share = pl.pallas_call(
-        functools.partial(last_kernel, count),
-        out_shape=(
-            jax.ShapeDtypeStruct((height, levels, height), bf16),
-            jax.ShapeDtypeStruct((height, width, height), bf16),
-            jax.ShapeDtypeStruct((1, height), f32),
-            jax.ShapeDtypeStruct((height // count, levels, height), f32),
-        ),
-        in_specs=[SMEM_BLOCK] + [VMEM_BLOCK] * count + [SMEM_BLOCK] + [VMEM_BLOCK] * 5,
-        out_specs=(VMEM_BLOCK,) * 4,
+        functools.partial(last_kernel, with_own),
+        out_shape=outputs,
+        in_specs=[VMEM_BLOCK] * count + [SMEM_BLOCK] + [VMEM_BLOCK] * 5,
+        out_specs=(HBM_BLOCK, HBM_BLOCK, VMEM_BLOCK, HBM_BLOCK),
+        scratch_shapes=[pltpu.VMEM(outputs[k].shape, outputs[k].dtype) for k in (0, 1, 3)] + [DMA((6,))],
         compiler_params=params(12),
         name="last",
-    )(sources, *parts, scalars, basis, second, one, cross, two)
+    )(*parts, scalars, basis, second, one, cross, two)
     return (new_state[None], new_left[None], energy[0, :1], share[None])
 
 

time: 61.1 us -> 56.2 us (0.920)
  local copies, waits for them, and re-layouts: 9.33 us -> 0.01 us
  waiting for transfers between devices: 2.94 us -> 5.95 us
  starting transfers between devices: 16.9 us -> 18.3 us
    unnamed x16 -> x2, local copies, waits for them, and re-layouts: 6.79 us -> 0.01 us
    ppermute x10, waiting for transfers between devices: 2.94 us -> 5.95 us  [sent(): lax.ppermute(value, axis, [(source, (source + step) % count) for source i...]
    transpose x1 -> x0, local copies, waits for them, and re-layouts: 2.11 us -> none  [body(): jnp.transpose(mpo, (1, 2, 3, 0)).reshape(width * levels, levels * width)]
    ppermute x10, starting transfers between devices: 16.9 us -> 18.3 us  [sent(): lax.ppermute(value, axis, [(source, (source + step) % count) for source i...]
    pallas_call x1, Pallas kernels: 0.9 us -> 1.98 us  [body(): pl.pallas_call(begin_kernel, out_shape=(on_chip((height // 2 + 1, width,...]
    pallas_call x5, Pallas kernels: 20.9 us -> 20.1 us  [the longest x1 9.23 us: body(): pl.pallas_call(functools.partial(second_kernel, with_own), out_shape=(on_...]
  transfers between devices with their start and end apart: 10 -> 10, of which waited for: 1 -> 4; matrix products, arithmetic and copies ran while one was open for 4% -> 0% of each run, Pallas kernels for 25% -> 27%
where the time goes in v4:
time: 56.2 us; the launch traced here: 56 us
  Pallas kernels  30.8 us (55%)
  starting transfers between devices  18.3 us (33%)
  waiting for transfers between devices  5.95 us (11%)
  between operations  0.91 us (2%)
    ppermute x10, starting transfers between devices, sent(): lax.ppermute(value, axis, [(source, (source + step) % count) for source i...  18.3 us
    pallas_call x1, Pallas kernels, body(): pl.pallas_call(functools.partial(second_kernel, with_own), out_shape=(on_...  9.23 us
    ppermute x10, waiting for transfers between devices, sent(): lax.ppermute(value, axis, [(source, (source + step) % count) for source i...  5.95 us
    pallas_call x1, Pallas kernels, body(): pl.pallas_call(first_kernel, out_shape=(on_chip((width, rows, height), bf...  5.93 us
    pallas_call x1, Pallas kernels, body(): pl.pallas_call(grow_second_kernel, out_shape=(on_chip(grown_shape, f32),)...  4.67 us
    pallas_call x1, Pallas kernels, body(): pl.pallas_call(functools.partial(last_kernel, with_own), out_shape=output...  3.02 us
    pallas_call x1, Pallas kernels, body(): pl.pallas_call(grow_first_kernel, out_shape=on_chip(grown_shape, f32), in...  2.35 us
    pallas_call x1, Pallas kernels, body(): pl.pallas_call(begin_kernel, out_shape=(on_chip((height // 2 + 1, width,...  1.98 us
  transfers between devices with their start and end apart: 10, of which 4 were waited for; matrix products, arithmetic and copies ran while one was open for 0% of the time, Pallas kernels for 27%

profile of v4, /device:TPU:0, one launch (start us, length us, event | category | flops | bytes accessed | tf_op | source)
XLA Modules:
  0.0 56.0 jit_solution(9298124946602202143)
XLA Ops:
  0.6 0.0 copy-start
  0.6 2.0 %begin.1 = (bf16[65,32,128]{2,1,0:T(8,128)(2,1)S(1)}, bf16[128,32,128]{2,1,0:T(8,128)(2,1)S(1)}, bf16[128,1024]{1,0:T(8,128)(2,1)S(1)}, f32[1024,128]{1,0:T(8,128)S(1)}) custom-call(bf16[128,32,128]{2,1,0:T(8,128)(2,1)} %bitcast.12, bf16[128,32,128]{2,1,0:T(8,128)(2,1)} %bitcast.13, bf16[128,8,128]{2,1,0:T(8,128)(2,1)} %bitcast.14), custom_call_target="tpu_custom_call" | custom-call | tf_op jit(solution)/shard_map/begin/pallas_call | solution.py:304
  2.6 3.4 %collective-permute-start = (bf16[65,32,128]{2,1,0:T(8,128)(2,1)S(1)}, bf16[65,32,128]{2,1,0:T(8,128)(2,1)S(1)}, u32[]{:S(2)}, u32[]{:S(2)}) collective-permute-start(bf16[65,32,128]{2,1,0:T(8,128)(2,1)S(1)} %get-tuple-element.28), channel_id=1, source_target_pairs={{0,28},{4,0},{8,4},{12,8},{16,12},{20,16},{24,20},{28,24},{1,29},{... | collective-permute-start | bytes 1597448 | tf_op jit(solution)/shard_map/ppermute | solution.py:290
  6.0 0.0 copy-done
  6.0 5.9 %first_coupled.1 = (bf16[32,1024,128]{2,1,0:T(8,128)(2,1)S(1)}, bf16[256,256]{1,0:T(8,128)(2,1)S(1)}) custom-call(bf16[128,1024]{1,0:T(8,128)(2,1)S(1)} %get-tuple-element.25.vector_ref, bf16[128,32,128]{2,1,0:T(8,128)(2,1)S(1)} %get-tuple-element.26.left_ref.refs_5_, bf16[32,8,8,32]{3,2,1,0:T(8,128)(2,1)S(1)} %bitcast.11), custom_call_target="tpu_custom_call" | custom-call | flops 4294967296 | bytes 8388608 | tf_op jit(solution)/shard_map/first_coupled/pallas_call | solution.py:319
  11.9 0.9 %collective-permute-done.folded_ref = bf16[65,32,128]{2,1,0:T(8,128)(2,1)S(1)} collective-permute-done((bf16[65,32,128]{2,1,0:T(8,128)(2,1)S(1)}, bf16[65,32,128]{2,1,0:T(8,128)(2,1)S(1)}, u32[]{:S(2)}, u32[]{:S(2)}) %collective-permute-start) | collective-permute-done | bytes 532512 | tf_op jit(solution)/shard_map/ppermute | solution.py:290
  12.8 1.0 %unfold.1.right_ref.refs_7_ = bf16[4096,128]{1,0:T(8,128)(2,1)S(1)} custom-call(bf16[65,32,128]{2,1,0:T(8,128)(2,1)S(1)} %collective-permute-done.folded_ref), custom_call_target="tpu_custom_call" | custom-call | tf_op jit(solution)/shard_map/unfold/pallas_call | solution.py:331
  13.8 0.7 %image_first.1 = bf16[256,128]{1,0:T(8,128)(2,1)S(1)} custom-call(bf16[32,1024,128]{2,1,0:T(8,128)(2,1)S(1)} %get-tuple-element.27.coupled_ref, bf16[4096,128]{1,0:T(8,128)(2,1)S(1)} %unfold.1.right_ref.refs_7_), custom_call_target="tpu_custom_call" | custom-call | flops 268435456 | bytes 8388608 | tf_op jit(solution)/shard_map/image_first/pallas_call | solution.py:342
  14.5 2.7 %collective-permute-start.1 = (bf16[256,128]{1,0:T(8,128)(2,1)S(1)}, bf16[256,128]{1,0:T(8,128)(2,1)S(1)}, u32[]{:S(2)}, u32[]{:S(2)}) collective-permute-start(bf16[256,128]{1,0:T(8,128)(2,1)S(1)} %image_first.1), channel_id=1, source_target_pairs={{0,2},{1,3},{2,0},{3,1},{4,6},{5,7},{6,4},{7,5},{8,10},{9,11},{10,... | collective-permute-start | bytes 196616 | tf_op jit(solution)/shard_map/ppermute | solution.py:290
  17.2 1.2 %image_rest.1 = (bf16[256,128]{1,0:T(8,128)(2,1)S(1)}, bf16[256,128]{1,0:T(8,128)(2,1)S(1)}) custom-call(bf16[32,1024,128]{2,1,0:T(8,128)(2,1)S(1)} %get-tuple-element.27.coupled_ref, bf16[4096,128]{1,0:T(8,128)(2,1)S(1)} %unfold.1.right_ref.refs_7_), custom_call_target="tpu_custom_call" | custom-call | flops 536870912 | bytes 8388608 | tf_op jit(solution)/shard_map/image_rest/pallas_call | solution.py:342
  18.4 1.6 %collective-permute-start.2 = (bf16[256,128]{1,0:T(8,128)(2,1)S(1)}, bf16[256,128]{1,0:T(8,128)(2,1)S(1)}, u32[]{:S(2)}, u32[]{:S(2)}) collective-permute-start(bf16[256,128]{1,0:T(8,128)(2,1)S(1)} %get-tuple-element.29), channel_id=1, source_target_pairs={{0,1},{1,2},{2,3},{3,0},{4,5},{5,6},{6,7},{7,4},{8,9},{9,10},{10,1... | collective-permute-start | bytes 196616 | tf_op jit(solution)/shard_map/ppermute | solution.py:290
  20.0 2.2 %collective-permute-start.3 = (bf16[256,128]{1,0:T(8,128)(2,1)S(1)}, bf16[256,128]{1,0:T(8,128)(2,1)S(1)}, u32[]{:S(2)}, u32[]{:S(2)}) collective-permute-start(bf16[256,128]{1,0:T(8,128)(2,1)S(1)} %get-tuple-element.30), channel_id=1, source_target_pairs={{0,3},{1,0},{2,1},{3,2},{4,7},{5,4},{6,5},{7,6},{8,11},{9,8},{10,9... | collective-permute-start | bytes 196616 | tf_op jit(solution)/shard_map/ppermute | solution.py:290
  22.3 0.0 collective-permute-done.1.arrived_ref
  22.3 0.7 %image_own.1.own_ref = f32[256,128]{1,0:T(8,128)S(1)} custom-call(bf16[32,1024,128]{2,1,0:T(8,128)(2,1)S(1)} %get-tuple-element.27.coupled_ref, bf16[4096,128]{1,0:T(8,128)(2,1)S(1)} %unfold.1.right_ref.refs_7_, bf16[256,128]{1,0:T(8,128)(2,1)S(1)} %collective-permute-done.1.arrived_ref), custom_call_target="tpu_custom_call" | custom-call | flops 268435456 | bytes 8388608 | tf_op jit(solution)/shard_map/image_own/pallas_call | solution.py:354
  23.0 1.7 %collective-permute-done.2.refs_0_ = bf16[256,128]{1,0:T(8,128)(2,1)S(1)} collective-permute-done((bf16[256,128]{1,0:T(8,128)(2,1)S(1)}, bf16[256,128]{1,0:T(8,128)(2,1)S(1)}, u32[]{:S(2)}, u32[]{:S(2)}) %collective-permute-start.2) | collective-permute-done | bytes 65568 | tf_op jit(solution)/shard_map/ppermute | solution.py:290
  24.7 0.3 collective-permute-done.3.refs_1_
  25.0 3.4 %collective-permute-start.6 = (bf16[256,128]{1,0:T(8,128)(2,1)S(1)}, bf16[256,128]{1,0:T(8,128)(2,1)S(1)}, u32[]{:S(2)}, u32[]{:S(2)}) collective-permute-start(bf16[256,128]{1,0:T(8,128)(2,1)S(1)} %sum.1.refs_3_.after_ref), channel_id=1, source_target_pairs={{0,3},{1,0},{2,1},{3,2},{4,7},{5,4},{6,5},{7,6},{8,11},{9,8},{10,9... | collective-permute-start | bytes 196616 | tf_op jit(solution)/shard_map/ppermute | solution.py:290
  28.5 0.0 collective-permute-start.5
  28.5 0.6 %collective-permute-start.4 = (bf16[256,128]{1,0:T(8,128)(2,1)S(1)}, bf16[256,128]{1,0:T(8,128)(2,1)S(1)}, u32[]{:S(2)}, u32[]{:S(2)}) collective-permute-start(bf16[256,128]{1,0:T(8,128)(2,1)S(1)} %sum.1.refs_3_.after_ref), channel_id=1, source_target_pairs={{0,2},{1,3},{2,0},{3,1},{4,6},{5,7},{6,4},{7,5},{8,10},{9,11},{10,... | collective-permute-start | bytes 196616 | tf_op jit(solution)/shard_map/ppermute | solution.py:290
  29.1 2.3 %grow_first.1.refs_7_ = f32[4096,128]{1,0:T(8,128)S(1)} custom-call(bf16[256,128]{1,0:T(8,128)(2,1)S(1)} %sum.1.refs_3_.after_ref, f32[1024,128]{1,0:T(8,128)S(1)} %get-tuple-element.31.refs_4_.basis_ref.refs_5_, bf16[32,1024,128]{2,1,0:T(8,128)(2,1)S(1)} %get-tuple-element.27.coupled_ref), custom_call_target="tpu_custom_call" | custom-call | flops 2147483648 | bytes 8388608 | tf_op jit(solution)/shard_map/grow_first/pallas_call | solution.py:372
  31.4 0.0 collective-permute-done.6.refs_2_
  31.5 3.1 %collective-permute-done.5.refs_1_ = bf16[256,128]{1,0:T(8,128)(2,1)S(1)} collective-permute-done((bf16[256,128]{1,0:T(8,128)(2,1)S(1)}, bf16[256,128]{1,0:T(8,128)(2,1)S(1)}, u32[]{:S(2)}, u32[]{:S(2)}) %collective-permute-start.5) | collective-permute-done | bytes 65568 | tf_op jit(solution)/shard_map/ppermute | solution.py:290
  34.5 0.0 collective-permute-done.4.refs_0_
  34.5 9.2 %second_image.1 = (bf16[32,1024,128]{2,1,0:T(8,128)(2,1)S(1)}, f32[1024,128]{1,0:T(8,128)S(1)}, f32[2]{0:T(128)S(1)}, bf16[272,128]{1,0:T(8,128)(2,1)S(1)}, bf16...) custom-call(bf16[256,128]{1,0:T(8,128)(2,1)S(1)} %collective-permute-done.4.refs_0_, ...), custom_call_target="tpu_custom_call" | custom-call | tf_op jit(solution)/shard_map/second_image/pallas_call | solution.py:383
  43.8 0.6 %collective-permute-start.7 = (bf16[272,128]{1,0:T(8,128)(2,1)S(1)}, bf16[272,128]{1,0:T(8,128)(2,1)S(1)}, u32[]{:S(2)}, u32[]{:S(2)}) collective-permute-start(bf16[272,128]{1,0:T(8,128)(2,1)S(1)} %get-tuple-element.33), channel_id=1, source_target_pairs={{0,2},{1,3},{2,0},{3,1},{4,6},{5,7},{6,4},{7,5},{8,10},{9,11},{10,... | collective-permute-start | bytes 208904 | tf_op jit(solution)/shard_map/ppermute | solution.py:290
  44.3 3.0 %collective-permute-start.8 = (bf16[272,128]{1,0:T(8,128)(2,1)S(1)}, bf16[272,128]{1,0:T(8,128)(2,1)S(1)}, u32[]{:S(2)}, u32[]{:S(2)}) collective-permute-start(bf16[272,128]{1,0:T(8,128)(2,1)S(1)} %get-tuple-element.34), channel_id=1, source_target_pairs={{0,1},{1,2},{2,3},{3,0},{4,5},{5,6},{6,7},{7,4},{8,9},{9,10},{10,1... | collective-permute-start | bytes 208904 | tf_op jit(solution)/shard_map/ppermute | solution.py:290
  47.3 0.8 %collective-permute-start.9 = (bf16[272,128]{1,0:T(8,128)(2,1)S(1)}, bf16[272,128]{1,0:T(8,128)(2,1)S(1)}, u32[]{:S(2)}, u32[]{:S(2)}) collective-permute-start(bf16[272,128]{1,0:T(8,128)(2,1)S(1)} %get-tuple-element.35), channel_id=1, source_target_pairs={{0,3},{1,0},{2,1},{3,2},{4,7},{5,4},{6,5},{7,6},{8,11},{9,8},{10,9... | collective-permute-start | bytes 208904 | tf_op jit(solution)/shard_map/ppermute | solution.py:290
  48.2 4.7 %grow_second.1 = (f32[4096,128]{1,0:T(8,128)S(1)}, f32[4096,128]{1,0:T(8,128)S(1)}) custom-call(f32[1024,128]{1,0:T(8,128)S(1)} %get-tuple-element.31.refs_4_.basis_ref.refs_5_, f32[1024,128]{1,0:T(8,128)S(1)} %get-tuple-element.38.second_ref.refs_6_, bf16[32,1024,128]{2,1,0:T(8,128)(2,1)S(1)} %get-tuple-element.39.coupled_ref), custom_call_target="tpu_custom_call" | custom-call | flops 4294967296 | bytes 16777216 | tf_op jit(solution)/shard_map/grow_second/pallas_call | solution.py:400
  52.8 0.0 collective-permute-done.7.refs_0_
  52.8 0.0 collective-permute-done.8.refs_1_
  52.9 0.0 collective-permute-done.9.refs_2_
  52.9 3.0 %last.1 = (bf16[128,8,128]{2,1,0:T(8,128)(2,1)}, bf16[128,32,128]{2,1,0:T(8,128)(2,1)}, f32[1,128]{1,0:T(1,128)}, f32[32,8,128]{2,1,0:T(8,128)}) custom-call(bf16[272,128]{1,0:T(8,128)(2,1)S(1)} %collective-permute-done.7.refs_0_, bf16[272,128]{1,0:T(8,128)(2,1)S(1)} %collective-permute-done.8.refs_1_, bf16[272,128]{1,0:T(8,128)(2,1)S(1)} %collective-permute-done.9.refs_2_, ...), custom_call_target="tpu_custom_call" | custom-call | tf_op jit(solution)/shard_map/last/pallas_call | solution.py:416
  (1 shorter events, 0.0 us)
Async XLA Ops:
  0.6 5.4 %copy-start = (bf16[1,32,32,8,8]{2,4,3,1,0:T(8,128)(2,1)S(1)}, bf16[1,32,32,8,8]{2,4,3,1,0:T(8,128)(2,1)}, u32[]{:S(2)}) copy-start(bf16[1,32,32,8,8]{2,4,3,1,0:T(8,128)(2,1)} %param.6) | copy-start | bytes 393220
  2.6 10.2 %collective-permute-start = (bf16[65,32,128]{2,1,0:T(8,128)(2,1)S(1)}, bf16[65,32,128]{2,1,0:T(8,128)(2,1)S(1)}, u32[]{:S(2)}, u32[]{:S(2)}) collective-permute-start(bf16[65,32,128]{2,1,0:T(8,128)(2,1)S(1)} %get-tuple-element.28), channel_id=1, source_target_pairs={{0,28},{4,0},{8,4},{12,8},{16,12},{20,16},{24,20},{28,24},{1,29},{... | collective-permute-start | bytes 1597448 | tf_op jit(solution)/shard_map/ppermute | solution.py:290
  14.5 7.8 %collective-permute-start.1 = (bf16[256,128]{1,0:T(8,128)(2,1)S(1)}, bf16[256,128]{1,0:T(8,128)(2,1)S(1)}, u32[]{:S(2)}, u32[]{:S(2)}) collective-permute-start(bf16[256,128]{1,0:T(8,128)(2,1)S(1)} %image_first.1), channel_id=1, source_target_pairs={{0,2},{1,3},{2,0},{3,1},{4,6},{5,7},{6,4},{7,5},{8,10},{9,11},{10,... | collective-permute-start | bytes 196616 | tf_op jit(solution)/shard_map/ppermute | solution.py:290
  18.4 6.3 %collective-permute-start.2 = (bf16[256,128]{1,0:T(8,128)(2,1)S(1)}, bf16[256,128]{1,0:T(8,128)(2,1)S(1)}, u32[]{:S(2)}, u32[]{:S(2)}) collective-permute-start(bf16[256,128]{1,0:T(8,128)(2,1)S(1)} %get-tuple-element.29), channel_id=1, source_target_pairs={{0,1},{1,2},{2,3},{3,0},{4,5},{5,6},{6,7},{7,4},{8,9},{9,10},{10,1... | collective-permute-start | bytes 196616 | tf_op jit(solution)/shard_map/ppermute | solution.py:290
  20.0 5.0 %collective-permute-start.3 = (bf16[256,128]{1,0:T(8,128)(2,1)S(1)}, bf16[256,128]{1,0:T(8,128)(2,1)S(1)}, u32[]{:S(2)}, u32[]{:S(2)}) collective-permute-start(bf16[256,128]{1,0:T(8,128)(2,1)S(1)} %get-tuple-element.30), channel_id=1, source_target_pairs={{0,3},{1,0},{2,1},{3,2},{4,7},{5,4},{6,5},{7,6},{8,11},{9,8},{10,9... | collective-permute-start | bytes 196616 | tf_op jit(solution)/shard_map/ppermute | solution.py:290
  25.0 6.4 %collective-permute-start.6 = (bf16[256,128]{1,0:T(8,128)(2,1)S(1)}, bf16[256,128]{1,0:T(8,128)(2,1)S(1)}, u32[]{:S(2)}, u32[]{:S(2)}) collective-permute-start(bf16[256,128]{1,0:T(8,128)(2,1)S(1)} %sum.1.refs_3_.after_ref), channel_id=1, source_target_pairs={{0,3},{1,0},{2,1},{3,2},{4,7},{5,4},{6,5},{7,6},{8,11},{9,8},{10,9... | collective-permute-start | bytes 196616 | tf_op jit(solution)/shard_map/ppermute | solution.py:290
  28.5 6.1 %collective-permute-start.5 = (bf16[256,128]{1,0:T(8,128)(2,1)S(1)}, bf16[256,128]{1,0:T(8,128)(2,1)S(1)}, u32[]{:S(2)}, u32[]{:S(2)}) collective-permute-start(bf16[256,128]{1,0:T(8,128)(2,1)S(1)} %sum.1.refs_3_.after_ref), channel_id=1, source_target_pairs={{0,1},{1,2},{2,3},{3,0},{4,5},{5,6},{6,7},{7,4},{8,9},{9,10},{10,1... | collective-permute-start | bytes 196616 | tf_op jit(solution)/shard_map/ppermute | solution.py:290
  28.5 6.1 %collective-permute-start.4 = (bf16[256,128]{1,0:T(8,128)(2,1)S(1)}, bf16[256,128]{1,0:T(8,128)(2,1)S(1)}, u32[]{:S(2)}, u32[]{:S(2)}) collective-permute-start(bf16[256,128]{1,0:T(8,128)(2,1)S(1)} %sum.1.refs_3_.after_ref), channel_id=1, source_target_pairs={{0,2},{1,3},{2,0},{3,1},{4,6},{5,7},{6,4},{7,5},{8,10},{9,11},{10,... | collective-permute-start | bytes 196616 | tf_op jit(solution)/shard_map/ppermute | solution.py:290
  43.8 9.1 %collective-permute-start.7 = (bf16[272,128]{1,0:T(8,128)(2,1)S(1)}, bf16[272,128]{1,0:T(8,128)(2,1)S(1)}, u32[]{:S(2)}, u32[]{:S(2)}) collective-permute-start(bf16[272,128]{1,0:T(8,128)(2,1)S(1)} %get-tuple-element.33), channel_id=1, source_target_pairs={{0,2},{1,3},{2,0},{3,1},{4,6},{5,7},{6,4},{7,5},{8,10},{9,11},{10,... | collective-permute-start | bytes 208904 | tf_op jit(solution)/shard_map/ppermute | solution.py:290
  44.3 8.5 %collective-permute-start.8 = (bf16[272,128]{1,0:T(8,128)(2,1)S(1)}, bf16[272,128]{1,0:T(8,128)(2,1)S(1)}, u32[]{:S(2)}, u32[]{:S(2)}) collective-permute-start(bf16[272,128]{1,0:T(8,128)(2,1)S(1)} %get-tuple-element.34), channel_id=1, source_target_pairs={{0,1},{1,2},{2,3},{3,0},{4,5},{5,6},{6,7},{7,4},{8,9},{9,10},{10,1... | collective-permute-start | bytes 208904 | tf_op jit(solution)/shard_map/ppermute | solution.py:290
  47.3 5.5 %collective-permute-start.9 = (bf16[272,128]{1,0:T(8,128)(2,1)S(1)}, bf16[272,128]{1,0:T(8,128)(2,1)S(1)}, u32[]{:S(2)}, u32[]{:S(2)}) collective-permute-start(bf16[272,128]{1,0:T(8,128)(2,1)S(1)} %get-tuple-element.35), channel_id=1, source_target_pairs={{0,3},{1,0},{2,1},{3,2},{4,7},{5,4},{6,5},{7,6},{8,11},{9,8},{10,9... | collective-permute-start | bytes 208904 | tf_op jit(solution)/shard_map/ppermute | solution.py:290

commit v5 on v4

--- a/solution.py
+++ b/solution.py
@@ -11,7 +11,6 @@
 bf16 = jnp.bfloat16
 f32 = jnp.float32
 VMEM_BLOCK = pl.BlockSpec(memory_space=pltpu.VMEM)
-SMEM_BLOCK = pl.BlockSpec(memory_space=pltpu.SMEM)
 HBM_BLOCK = pl.BlockSpec(memory_space=pltpu.HBM)
 DMA = pltpu.SemaphoreType.DMA
 TAIL = 16
@@ -41,12 +40,14 @@
     return jnp.concatenate(parts, axis=1).astype(bf16)
 
 
-def couple(left_ref, vector, mpo, coupled_ref, chunk):
+def couple(left_ref, vector, mpo, coupled_ref, chunk, await_left=None):
     height, width, _ = left_ref.shape
     levels = vector.shape[1] // height
     right_width = mpo.shape[0] // levels
 
     def step(index, carry):
+        if await_left is not None:
+            await_left(index)
         first = index * chunk
         mixed = jnp.dot(
             left_ref[pl.ds(first, chunk)].reshape(chunk * width, height), vector, preferred_element_type=f32
@@ -70,40 +71,29 @@
     lax.fori_loop(0, height // chunk, step, 0)
 
 
-def image(coupled_ref, right, image_ref, chunk):
-    width, rows, _ = coupled_ref.shape
-
-    def step(index, carry):
-        place = pl.ds(pl.multiple_of(index * chunk, chunk), chunk)
-        terms = jnp.concatenate([coupled_ref[u, place, :] for u in range(width)], axis=1)
-        image_ref[place, :] = jnp.dot(terms, right[...], preferred_element_type=f32)
-        return carry
-
-    lax.fori_loop(0, rows // chunk, step, 0)
-
-
-def begin_kernel(right_hbm, left_hbm, start_hbm, folded_ref, left_ref, vector_ref, basis_ref, right, start, sems):
+def fold_kernel(right_hbm, folded_ref, right, sems):
     height, width, _ = right.shape
-    levels = start.shape[1]
     half = height // 2
-    copies = [
-        pltpu.make_async_copy(right_hbm, right, sems.at[0]),
-        pltpu.make_async_copy(start_hbm, start, sems.at[1]),
-        pltpu.make_async_copy(left_hbm, left_ref, sems.at[2]),
-    ]
-    for copy in copies:
-        copy.start()
-    copies[0].wait()
-    lower = right[half:].astype(f32)
-    row = lax.broadcasted_iota(jnp.int32, lower.shape, 0)
-    lane = lax.broadcasted_iota(jnp.int32, lower.shape, 2)
-    turned = pltpu.roll(lower, half, 2)
-    folded_ref[:half] = jnp.where(lane >= row, right[:half].astype(f32), turned).astype(bf16)
-    folded_ref[half] = jnp.sum(jnp.where(lane == row + half, lower, 0.0), axis=0).astype(bf16)
-    copies[1].wait()
-    basis_ref[...] = normalised(start[...])
-    vector_ref[...] = by_level(basis_ref, height, levels)
-    copies[2].wait()
+    pieces = sems.shape[0] // 2
+    size = half // pieces
+    copies = []
+    for k in range(pieces):
+        for first in (k * size, half + k * size):
+            rows = pl.ds(first, size)
+            copies.append(pltpu.make_async_copy(right_hbm.at[rows], right.at[rows], sems.at[len(copies)]))
+            copies[-1].start()
+    diagonal = jnp.zeros((width, height), f32)
+    for k in range(pieces):
+        copies[2 * k].wait()
+        copies[2 * k + 1].wait()
+        lower = right[half + k * size : half + (k + 1) * size].astype(f32)
+        row = lax.broadcasted_iota(jnp.int32, lower.shape, 0) + k * size
+        lane = lax.broadcasted_iota(jnp.int32, lower.shape, 2)
+        turned = pltpu.roll(lower, half, 2)
+        upper = right[k * size : (k + 1) * size].astype(f32)
+        folded_ref[k * size : (k + 1) * size] = jnp.where(lane >= row, upper, turned).astype(bf16)
+        diagonal = diagonal + jnp.sum(jnp.where(lane == row + half, lower, 0.0), axis=0)
+    folded_ref[half] = diagonal.astype(bf16)
 
 
 def reorder(size, first, second):
@@ -112,14 +102,30 @@
     return jnp.where((row // second == lane % first) & (row % second == lane // first), 1.0, 0.0).astype(bf16)
 
 
-def first_kernel(vector_ref, left_ref, mpo_ref, coupled_ref, mpo_rows_ref):
+def first_kernel(start_hbm, left_hbm, mpo_hbm, coupled_ref, mpo_rows_ref, basis_ref, start, left, mpo_ref, sems):
+    chunk = left.shape[0] // (sems.shape[0] - 2)
+
+    def left_copy(index):
+        place = pl.ds(index * chunk, chunk)
+        return pltpu.make_async_copy(left_hbm.at[place], left.at[place], sems.at[index])
+
+    mpo_copy = pltpu.make_async_copy(mpo_hbm, mpo_ref, sems.at[sems.shape[0] - 1])
+    start_copy = pltpu.make_async_copy(start_hbm, start, sems.at[sems.shape[0] - 2])
+    mpo_copy.start()
+    start_copy.start()
+    for index in range(sems.shape[0] - 2):
+        left_copy(index).start()
+    mpo_copy.wait()
     width, levels, _, right_width = mpo_ref.shape
     terms = [mpo_ref[:, s].astype(f32).reshape(width * levels, right_width).T for s in range(levels)]
     terms = jnp.concatenate(terms, axis=0).astype(bf16)
     terms = jnp.dot(reorder(right_width * levels, right_width, levels), terms, preferred_element_type=f32)
     terms = jnp.dot(terms.astype(bf16), reorder(width * levels, width, levels), preferred_element_type=f32)
     mpo_rows_ref[...] = terms.astype(bf16)
-    couple(left_ref, vector_ref[...], mpo_rows_ref[...], coupled_ref, 32)
+    start_copy.wait()
+    basis_ref[...] = normalised(start[...])
+    vector = by_level(basis_ref, left.shape[0], levels)
+    couple(left, vector, mpo_rows_ref[...], coupled_ref, chunk, lambda index: left_copy(index).wait())
 
 
 def unfold_kernel(folded_ref, right_ref, wide):
@@ -147,9 +153,12 @@
     return jnp.dot(terms, right_ref[...], preferred_element_type=f32)
 
 
+def partner(me, step, count):
+    return me ^ step if count & (count - 1) == 0 else lax.rem(count - me + step, count)
+
+
 def other(step):
-    count = lax.axis_size("bond")
-    return lax.rem(lax.axis_index("bond") + (step + count), count)
+    return partner(lax.axis_index("bond"), step, lax.axis_size("bond"))
 
 
 def block_images_kernel(steps, coupled_ref, right_ref, *image_refs):
@@ -173,35 +182,40 @@
     count = len(steps)
     blocks, refs = refs[:count], refs[count:]
     basis_ref, left_ref, mpo_ref, right_ref, coupled_ref, second_ref, scalar_ref = refs[:7]
-    sends, total = refs[7 : 7 + count], refs[7 + count]
-    height, width, _ = left_ref.shape
+    sends = refs[7:]
+    height = left_ref.shape[0]
     rows = basis_ref.shape[0]
     levels = rows // height
     entries = rows * height
     block = blocks[0].shape[0]
-    for k, step in enumerate(steps):
-        place = pl.ds(pl.multiple_of(other(-step) * block, block), block)
-        total[place, :] = blocks[k][...].astype(f32)
-    basis = basis_ref[...]
-    first_image = total[...]
-    rayleigh = jnp.sum(basis * first_image) / entries
-    residual = first_image - rayleigh * basis
-    residual_size = jnp.sqrt(jnp.sum(residual * residual) / entries + epsilon)
-    second_ref[...] = residual / residual_size
+    places = [pl.ds(pl.multiple_of(other(step) * block, block), block) for step in steps]
+    product = jnp.zeros((1, height), f32)
+    for image_ref, place in zip(blocks, places):
+        product += jnp.sum(basis_ref[place, :] * image_ref[...].astype(f32), axis=0, keepdims=True)
+    rayleigh = jnp.sum(product, axis=1, keepdims=True) / entries
+    square = jnp.zeros((1, height), f32)
+    for image_ref, place in zip(blocks, places):
+        residual = image_ref[...].astype(f32) - rayleigh * basis_ref[place, :]
+        second_ref[place, :] = residual
+        square += jnp.sum(residual * residual, axis=0, keepdims=True)
+    residual_size = jnp.sqrt(jnp.sum(square, axis=1, keepdims=True) / entries + epsilon)
+    second_ref[...] = second_ref[...] * (1.0 / residual_size)
+    scalar_ref[0:1, :] = jnp.broadcast_to(rayleigh, (1, height))
+    scalar_ref[1:2, :] = jnp.broadcast_to(residual_size, (1, height))
     couple(left_ref, by_level(second_ref, height, levels), mpo_ref[...], coupled_ref, 32)
-    image(coupled_ref, right_ref, total, 256)
-    value = jnp.sum(second_ref[...] * total[...]) / entries
+    product = jnp.zeros((1, height), f32)
+    for step, place, send_ref in zip(steps, places, sends):
+        terms = block_image(other(step), coupled_ref, right_ref, block)
+        product += jnp.sum(second_ref[place, :] * terms, axis=0, keepdims=True)
+        send_ref[:block, :] = terms.astype(bf16)
+    value = jnp.sum(product, axis=1, keepdims=True) / entries
     high = value.astype(bf16).astype(f32)
     middle = (value - high).astype(bf16).astype(f32)
     low = value - high - middle
     lane = lax.broadcasted_iota(jnp.int32, (TAIL, height), 1)
     tail = jnp.where(lane == 0, high, jnp.where(lane == 1, middle, jnp.where(lane == 2, low, 0.0))).astype(bf16)
-    for k, step in enumerate(steps):
-        place = pl.ds(pl.multiple_of(other(step) * block, block), block)
-        sends[k][:block, :] = total[place, :].astype(bf16)
-        sends[k][block:, :] = tail
-    scalar_ref[0] = rayleigh
-    scalar_ref[1] = residual_size
+    for send_ref in sends:
+        send_ref[block:, :] = tail
 
 
 def pair_of(coupled_ref, u):
@@ -236,18 +250,20 @@
     count = len(steps)
     parts, refs = refs[:count], refs[count:]
     scalar_ref, basis_ref, second_ref, one_ref, cross_ref, two_ref = refs[:6]
-    state_hbm, left_hbm, energy_ref, share_hbm, state, left, share, sems = refs[6:]
+    state_hbm, left_hbm, energy_hbm, share_hbm, state, left, energy, share, sems = refs[6:]
     block, height = parts[0].shape
     block -= TAIL
+    width = left.shape[1]
     lane = lax.broadcasted_iota(jnp.int32, (TAIL, height), 1)
     row = lax.broadcasted_iota(jnp.int32, (TAIL, height), 0)
-    values = [jnp.sum(jnp.where((lane < 3) & (row == 0), part[block:, :].astype(f32), 0.0)) for part in parts]
-    sources = [other(-step) for step in steps]
-    curvature = jnp.float32(0.0)
+    carried = (lane < 3) & (row == 0)
+    values = [jnp.sum(jnp.where(carried, part[block:, :].astype(f32), 0.0), keepdims=True) for part in parts]
+    sources = [other(step) for step in steps]
+    curvature = jnp.zeros((1, 1), f32)
     for device in range(count):
         for source, value in zip(sources, values):
             curvature = curvature + jnp.where(source == device, value, 0.0)
-    rayleigh, residual_size = scalar_ref[0], scalar_ref[1]
+    rayleigh, residual_size = scalar_ref[0:1, :], scalar_ref[1:2, :]
     middle = 0.5 * (rayleigh + curvature)
     half_gap = 0.5 * (rayleigh - curvature)
     lowest = middle - jnp.sqrt(half_gap * half_gap + residual_size * residual_size)
@@ -255,39 +271,53 @@
     length = jnp.sqrt(residual_size * residual_size + offset * offset)
     one, two = residual_size / length, offset / length
     weights = (one * one, one * two, two * two)
-    copies = []
-
-    def send(source, target):
-        copies.append(pltpu.make_async_copy(source, target, sems.at[len(copies)]))
-        copies[-1].start()
-
-    pieces = sems.shape[0] - 2
+    pieces = sems.shape[0] - 3
     size = left.shape[0] // pieces
-    width = left.shape[1]
-    for k in range(pieces):
-        place = slice(k * size * width, (k + 1) * size * width)
+
+    def copy(source, target, k):
+        return pltpu.make_async_copy(source, target, sems.at[pieces + k])
+
+    def piece_copy(k):
+        place = pl.ds(k * size, size)
+        return pltpu.make_async_copy(left.at[place], left_hbm.at[place], sems.at[k])
+
+    def grow(k, carry):
+        place = pl.ds(pl.multiple_of(k * size * width, size * width), size * width)
         grown = weights[0] * one_ref[place, :] + weights[1] * cross_ref[place, :] + weights[2] * two_ref[place, :]
-        left[k * size : (k + 1) * size] = grown.astype(bf16).reshape(size, width, height)
-        send(left.at[pl.ds(k * size, size)], left_hbm.at[pl.ds(k * size, size)])
-    state[...] = (one * basis_ref[...] + two * second_ref[...]).astype(bf16).reshape(state.shape)
-    send(state, state_hbm)
+        left[pl.ds(k * size, size)] = grown.astype(bf16).reshape(size, width, height)
+        piece_copy(k).start()
+        return carry
+
+    def combine(k, carry):
+        place = pl.ds(pl.multiple_of(k * height, height), height)
+        mixed = one * basis_ref[place, :] + two * second_ref[place, :]
+        share_of = height // state.shape[1]
+        state[pl.ds(k * share_of, share_of)] = mixed.astype(bf16).reshape(share_of, state.shape[1], height)
+        return carry
+
+    def finish(k, carry):
+        piece_copy(k).wait()
+        return carry
+
+    energy[...] = lowest
+    copy(energy, energy_hbm, 0).start()
+    lax.fori_loop(0, pieces, grow, 0)
+    lax.fori_loop(0, state.shape[1], combine, 0)
+    copy(state, state_hbm, 1).start()
     total = parts[0][:block, :].astype(f32)
     for part in parts[1:]:
         total = total + part[:block, :].astype(f32)
     share[...] = total.reshape(share.shape)
-    send(share, share_hbm)
-    energy_ref[...] = jnp.full(energy_ref.shape, lowest, f32)
-    for copy in copies:
-        copy.wait()
-
-
-def order(count):
-    return sorted(range(1, count), key=lambda step: -min(step, count - step))
-
-
-def sent(value, axis, step):
-    count = lax.axis_size(axis)
-    return lax.ppermute(value, axis, [(source, (source + step) % count) for source in range(count)])
+    copy(share, share_hbm, 2).start()
+    lax.fori_loop(0, pieces, finish, 0)
+    copy(energy, energy_hbm, 0).wait()
+    copy(state, state_hbm, 1).wait()
+    copy(share, share_hbm, 2).wait()
+
+
+def exchanged(value, step):
+    count = lax.axis_size("bond")
+    return lax.ppermute(value, "bond", [(source, int(partner(source, step, count))) for source in range(count)])
 
 
 def body(left_env, right_env, mpo_site, start_state):
@@ -297,37 +327,41 @@
     rows = height * levels
     count = lax.axis_size("bond")
     block = rows // count
-    steps = order(count)
-    with_own = tuple(steps) + (0,)
+    steps = tuple(range(count - 1, 0, -1)) if count & (count - 1) == 0 else tuple(range(count))
+    with_own = steps + (0,)
     apply_flops = 4 * rows * height * width * height
 
-    folded, left_near, vector, basis = pl.pallas_call(
-        begin_kernel,
-        out_shape=(
-            on_chip((height // 2 + 1, width, height), bf16),
-            on_chip(left.shape, bf16),
-            on_chip((height, rows), bf16),
-            on_chip((rows, height), f32),
-        ),
-        in_specs=[HBM_BLOCK] * 3,
-        out_specs=(VMEM_BLOCK,) * 4,
-        scratch_shapes=[pltpu.VMEM(right.shape, bf16), pltpu.VMEM(start.shape, bf16), DMA((3,))],
-        compiler_params=params(61),
-        name="begin",
-    )(right, left, start)
-    folded = sent(folded, "seg", -1)
-    first_coupled, mpo_rows = pl.pallas_call(
+    folded = pl.pallas_call(
+        fold_kernel,
+        out_shape=on_chip((height // 2 + 1, width, height), bf16),
+        in_specs=[HBM_BLOCK],
+        out_specs=VMEM_BLOCK,
+        scratch_shapes=[pltpu.VMEM(right.shape, bf16), DMA((8,))],
+        compiler_params=params(58),
+        name="fold",
+    )(right)
+    pairs = [(source, (source - 1) % lax.axis_size("seg")) for source in range(lax.axis_size("seg"))]
+    folded = lax.ppermute(folded, "seg", pairs)
+    mpo_sorted = jnp.transpose(mpo, (0, 2, 3, 1))
+    first_coupled, mpo_rows, basis = pl.pallas_call(
         first_kernel,
         out_shape=(
             on_chip((width, rows, height), bf16),
             on_chip((width * levels, levels * width), bf16),
+            on_chip((rows, height), f32),
         ),
-        in_specs=[VMEM_BLOCK] * 3,
-        out_specs=(VMEM_BLOCK,) * 2,
-        compiler_params=params(8),
+        in_specs=[HBM_BLOCK] * 3,
+        out_specs=(VMEM_BLOCK,) * 3,
+        scratch_shapes=[
+            pltpu.VMEM(start.shape, bf16),
+            pltpu.VMEM(left.shape, bf16),
+            pltpu.VMEM(mpo_sorted.shape, bf16),
+            DMA((6,)),
+        ],
+        compiler_params=params(53),
         cost_estimate=cost(2 * apply_flops, 8 << 20),
         name="first_coupled",
-    )(vector, left_near, jnp.transpose(mpo, (0, 2, 3, 1)))
+    )(start, left, mpo_sorted)
     right_rows = pl.pallas_call(
         unfold_kernel,
         out_shape=on_chip((width * height, height), bf16),
@@ -350,7 +384,7 @@
         )(first_coupled, right_rows)
 
     sends = tuple(block_images(steps[:1], "image_first")) + tuple(block_images(steps[1:], "image_rest"))
-    arrived = [sent(value, "bond", step) for value, step in zip(sends, steps)]
+    arrived = [exchanged(value, step) for value, step in zip(sends, steps)]
     own = pl.pallas_call(
         own_image_kernel,
         out_shape=on_chip((block, height), f32),
@@ -379,24 +413,23 @@
         cost_estimate=cost(apply_flops, 8 << 20),
         name="grow_first",
     )(own, basis, first_coupled)
-    blocks = [sent(own, "bond", step) for step in steps] + [own]
+    blocks = [exchanged(own, step) for step in steps] + [own]
     outcome = pl.pallas_call(
         functools.partial(second_kernel, with_own),
         out_shape=(
             on_chip((width, rows, height), bf16),
             on_chip((rows, height), f32),
-            jax.ShapeDtypeStruct((2,), f32),
+            on_chip((8, height), f32),
         )
         + (on_chip((block + TAIL, height), bf16),) * count,
         in_specs=[VMEM_BLOCK] * (count + 4),
-        out_specs=(VMEM_BLOCK,) * 2 + (SMEM_BLOCK,) + (VMEM_BLOCK,) * count,
-        scratch_shapes=[pltpu.VMEM((rows, height), f32)],
+        out_specs=(VMEM_BLOCK,) * (count + 3),
         compiler_params=params(12),
         name="second_image",
-    )(*blocks, basis, left_near, mpo_rows, right_rows)
+    )(*blocks, basis, left, mpo_rows, right_rows)
     second_coupled, second, scalars = outcome[:3]
     sends = outcome[3:]
-    parts = [sent(value, "bond", step) for value, step in zip(sends, steps)] + [sends[-1]]
+    parts = [exchanged(value, step) for value, step in zip(sends, steps)] + [sends[-1]]
     cross, two = pl.pallas_call(
         grow_second_kernel,
         out_shape=(on_chip(grown_shape, f32),) * 2,
@@ -416,9 +449,9 @@
     new_state, new_left, energy, share = pl.pallas_call(
         functools.partial(last_kernel, with_own),
         out_shape=outputs,
-        in_specs=[VMEM_BLOCK] * count + [SMEM_BLOCK] + [VMEM_BLOCK] * 5,
-        out_specs=(HBM_BLOCK, HBM_BLOCK, VMEM_BLOCK, HBM_BLOCK),
-        scratch_shapes=[pltpu.VMEM(outputs[k].shape, outputs[k].dtype) for k in (0, 1, 3)] + [DMA((6,))],
+        in_specs=[VMEM_BLOCK] * (count + 6),
+        out_specs=(HBM_BLOCK,) * 4,
+        scratch_shapes=[pltpu.VMEM(output.shape, output.dtype) for output in outputs] + [DMA((7,))],
         compiler_params=params(12),
         name="last",
     )(*parts, scalars, basis, second, one, cross, two)

time: 56.2 us -> 53.1 us (0.945)
  starting transfers between devices: 18.3 us -> 16.7 us
  Pallas kernels: 30.8 us -> 29.5 us
    ppermute x10, starting transfers between devices: 18.3 us -> 16.7 us  [the longest x9 13.4 us: exchanged(): lax.ppermute(value, 'bond', [(source, int(partner(source, step, count)))...]
    pallas_call x1, Pallas kernels: 3.02 us -> 1.5 us  [body(): pl.pallas_call(functools.partial(last_kernel, with_own), out_shape=output...]
    pallas_call x1, Pallas kernels: 5.93 us -> 7.43 us  [body(): pl.pallas_call(first_kernel, out_shape=(on_chip((width, rows, height), bf...]
    pallas_call x1, Pallas kernels: 9.23 us -> 8.47 us  [body(): pl.pallas_call(functools.partial(second_kernel, with_own), out_shape=(on_...]
  transfers between devices with their start and end apart: 10 -> 10, of which waited for: 4 -> 3; matrix products, arithmetic and copies ran while one was open for 0% -> 0% of each run, Pallas kernels for 27% -> 31%
where the time goes in v5:
time: 53.1 us; the launch traced here: 52.9 us
  Pallas kernels  29.5 us (56%)
  starting transfers between devices  16.7 us (31%)
  waiting for transfers between devices  5.73 us (11%)
  between operations  0.91 us (2%)
    ppermute x9, starting transfers between devices, exchanged(): lax.ppermute(value, 'bond', [(source, int(partner(source, step, count)))...  13.4 us
    pallas_call x1, Pallas kernels, body(): pl.pallas_call(functools.partial(second_kernel, with_own), out_shape=(on_...  8.47 us
    pallas_call x1, Pallas kernels, body(): pl.pallas_call(first_kernel, out_shape=(on_chip((width, rows, height), bf...  7.43 us
    ppermute x9, waiting for transfers between devices, exchanged(): lax.ppermute(value, 'bond', [(source, int(partner(source, step, count)))...  5.73 us
    pallas_call x1, Pallas kernels, body(): pl.pallas_call(grow_second_kernel, out_shape=(on_chip(grown_shape, f32),)...  4.67 us
    ppermute x1, starting transfers between devices, body(): folded = lax.ppermute(folded, 'seg', pairs)  3.39 us
    pallas_call x1, Pallas kernels, body(): pl.pallas_call(grow_first_kernel, out_shape=on_chip(grown_shape, f32), in...  2.32 us
    pallas_call x2, Pallas kernels, block_images(): pl.pallas_call(functools.partial(block_images_kernel, steps), out_shape=(...  1.94 us
  transfers between devices with their start and end apart: 10, of which 3 were waited for; matrix products, arithmetic and copies ran while one was open for 0% of the time, Pallas kernels for 31%

profile of v5, /device:TPU:0, one launch (start us, length us, event | category | flops | bytes accessed | tf_op | source)
XLA Modules:
  0.0 52.9 jit_solution(9906909405559040188)
XLA Ops:
  0.6 1.5 %fold.1 = bf16[65,32,128]{2,1,0:T(8,128)(2,1)S(1)} custom-call(bf16[128,32,128]{2,1,0:T(8,128)(2,1)} %bitcast.13), custom_call_target="tpu_custom_call" | custom-call | tf_op jit(solution)/shard_map/fold/pallas_call | solution.py:334
  2.1 3.4 %collective-permute-start = (bf16[65,32,128]{2,1,0:T(8,128)(2,1)S(1)}, bf16[65,32,128]{2,1,0:T(8,128)(2,1)S(1)}, u32[]{:S(2)}, u32[]{:S(2)}) collective-permute-start(bf16[65,32,128]{2,1,0:T(8,128)(2,1)S(1)} %fold.1), channel_id=1, source_target_pairs={{0,28},{4,0},{8,4},{12,8},{16,12},{20,16},{24,20},{28,24},{1,29},{... | collective-permute-start | bytes 1597448 | tf_op jit(solution)/shard_map/ppermute | solution.py:344
  5.5 7.4 %first_coupled.1 = (bf16[32,1024,128]{2,1,0:T(8,128)(2,1)S(1)}, bf16[256,256]{1,0:T(8,128)(2,1)S(1)}, f32[1024,128]{1,0:T(8,128)S(1)}) custom-call(bf16[128,8,128]{2,1,0:T(8,128)(2,1)} %bitcast.16, bf16[128,32,128]{2,1,0:T(8,128)(2,1)} %bitcast.11, bf16[32,8,8,32]{3,2,1,0:T(8,128)(2,1)} %bitcast.15), custom_call_target="tpu_custom_call" | custom-call | flops 4294967296 | bytes 8388608 | tf_op jit(solution)/shard_map/first_coupled/pallas_call | solution.py:346
  12.9 0.0 collective-permute-done.folded_ref
  13.0 1.0 %unfold.1.right_ref.refs_7_ = bf16[4096,128]{1,0:T(8,128)(2,1)S(1)} custom-call(bf16[65,32,128]{2,1,0:T(8,128)(2,1)S(1)} %collective-permute-done.folded_ref), custom_call_target="tpu_custom_call" | custom-call | tf_op jit(solution)/shard_map/unfold/pallas_call | solution.py:365
  14.0 0.7 %image_first.1 = bf16[256,128]{1,0:T(8,128)(2,1)S(1)} custom-call(bf16[32,1024,128]{2,1,0:T(8,128)(2,1)S(1)} %get-tuple-element.22.coupled_ref, bf16[4096,128]{1,0:T(8,128)(2,1)S(1)} %unfold.1.right_ref.refs_7_), custom_call_target="tpu_custom_call" | custom-call | flops 268435456 | bytes 8388608 | tf_op jit(solution)/shard_map/image_first/pallas_call | solution.py:376
  14.7 3.7 %collective-permute-start.1 = (bf16[256,128]{1,0:T(8,128)(2,1)S(1)}, bf16[256,128]{1,0:T(8,128)(2,1)S(1)}, u32[]{:S(2)}, u32[]{:S(2)}) collective-permute-start(bf16[256,128]{1,0:T(8,128)(2,1)S(1)} %image_first.1), channel_id=1, source_target_pairs={{0,3},{1,2},{2,1},{3,0},{4,7},{5,6},{6,5},{7,4},{8,11},{9,10},{10,... | collective-permute-start | bytes 196616 | tf_op jit(solution)/shard_map/ppermute | solution.py:320
  18.3 1.2 %image_rest.1 = (bf16[256,128]{1,0:T(8,128)(2,1)S(1)}, bf16[256,128]{1,0:T(8,128)(2,1)S(1)}) custom-call(bf16[32,1024,128]{2,1,0:T(8,128)(2,1)S(1)} %get-tuple-element.22.coupled_ref, bf16[4096,128]{1,0:T(8,128)(2,1)S(1)} %unfold.1.right_ref.refs_7_), custom_call_target="tpu_custom_call" | custom-call | flops 536870912 | bytes 8388608 | tf_op jit(solution)/shard_map/image_rest/pallas_call | solution.py:376
  19.6 0.1 collective-permute-start.2
  19.7 0.8 %collective-permute-start.3 = (bf16[256,128]{1,0:T(8,128)(2,1)S(1)}, bf16[256,128]{1,0:T(8,128)(2,1)S(1)}, u32[]{:S(2)}, u32[]{:S(2)}) collective-permute-start(bf16[256,128]{1,0:T(8,128)(2,1)S(1)} %get-tuple-element.24), channel_id=1, source_target_pairs={{0,1},{1,0},{2,3},{3,2},{4,5},{5,4},{6,7},{7,6},{8,9},{9,8},{10,11... | collective-permute-start | bytes 196616 | tf_op jit(solution)/shard_map/ppermute | solution.py:320
  20.4 0.4 collective-permute-done.1.arrived_ref
  20.8 0.7 %image_own.1.own_ref = f32[256,128]{1,0:T(8,128)S(1)} custom-call(bf16[32,1024,128]{2,1,0:T(8,128)(2,1)S(1)} %get-tuple-element.22.coupled_ref, bf16[4096,128]{1,0:T(8,128)(2,1)S(1)} %unfold.1.right_ref.refs_7_, bf16[256,128]{1,0:T(8,128)(2,1)S(1)} %collective-permute-done.1.arrived_ref), custom_call_target="tpu_custom_call" | custom-call | flops 268435456 | bytes 8388608 | tf_op jit(solution)/shard_map/image_own/pallas_call | solution.py:388
  21.5 3.4 %collective-permute-done.2.refs_0_ = bf16[256,128]{1,0:T(8,128)(2,1)S(1)} collective-permute-done((bf16[256,128]{1,0:T(8,128)(2,1)S(1)}, bf16[256,128]{1,0:T(8,128)(2,1)S(1)}, u32[]{:S(2)}, u32[]{:S(2)}) %collective-permute-start.2) | collective-permute-done | bytes 65568 | tf_op jit(solution)/shard_map/ppermute | solution.py:320
  24.9 0.0 collective-permute-done.3.refs_1_
  25.0 0.2 collective-permute-start.6
  25.1 2.5 %collective-permute-start.5 = (bf16[256,128]{1,0:T(8,128)(2,1)S(1)}, bf16[256,128]{1,0:T(8,128)(2,1)S(1)}, u32[]{:S(2)}, u32[]{:S(2)}) collective-permute-start(bf16[256,128]{1,0:T(8,128)(2,1)S(1)} %sum.1.refs_3_.after_ref), channel_id=1, source_target_pairs={{0,2},{1,3},{2,0},{3,1},{4,6},{5,7},{6,4},{7,5},{8,10},{9,11},{10,... | collective-permute-start | bytes 196616 | tf_op jit(solution)/shard_map/ppermute | solution.py:320
  27.6 1.8 %collective-permute-start.4 = (bf16[256,128]{1,0:T(8,128)(2,1)S(1)}, bf16[256,128]{1,0:T(8,128)(2,1)S(1)}, u32[]{:S(2)}, u32[]{:S(2)}) collective-permute-start(bf16[256,128]{1,0:T(8,128)(2,1)S(1)} %sum.1.refs_3_.after_ref), channel_id=1, source_target_pairs={{0,3},{1,2},{2,1},{3,0},{4,7},{5,6},{6,5},{7,4},{8,11},{9,10},{10,... | collective-permute-start | bytes 196616 | tf_op jit(solution)/shard_map/ppermute | solution.py:320
  29.4 0.0 copy-start
  29.4 2.3 %grow_first.1.refs_7_ = f32[4096,128]{1,0:T(8,128)S(1)} custom-call(bf16[256,128]{1,0:T(8,128)(2,1)S(1)} %sum.1.refs_3_.after_ref, f32[1024,128]{1,0:T(8,128)S(1)} %get-tuple-element.25.refs_4_.basis_ref.refs_5_, bf16[32,1024,128]{2,1,0:T(8,128)(2,1)S(1)} %get-tuple-element.22.coupled_ref), custom_call_target="tpu_custom_call" | custom-call | flops 2147483648 | bytes 8388608 | tf_op jit(solution)/shard_map/grow_first/pallas_call | solution.py:406
  31.7 0.0 collective-permute-done.6.refs_2_
  31.8 0.0 collective-permute-done.5.refs_1_
  31.8 1.9 %collective-permute-done.4.refs_0_ = bf16[256,128]{1,0:T(8,128)(2,1)S(1)} collective-permute-done((bf16[256,128]{1,0:T(8,128)(2,1)S(1)}, bf16[256,128]{1,0:T(8,128)(2,1)S(1)}, u32[]{:S(2)}, u32[]{:S(2)}) %collective-permute-start.4) | collective-permute-done | bytes 65568 | tf_op jit(solution)/shard_map/ppermute | solution.py:320
  33.7 0.0 copy-done
  33.7 8.5 %second_image.1 = (bf16[32,1024,128]{2,1,0:T(8,128)(2,1)S(1)}, f32[1024,128]{1,0:T(8,128)S(1)}, f32[8,128]{1,0:T(8,128)S(1)}, bf16[272,128]{1,0:T(8,128)(2,1)S(1...) custom-call(bf16[256,128]{1,0:T(8,128)(2,1)S(1)} %collective-permute-done.4.refs_0_, ...), custom_call_target="tpu_custom_call" | custom-call | tf_op jit(solution)/shard_map/second_image/pallas_call | solution.py:417
  42.2 1.9 %collective-permute-start.7 = (bf16[272,128]{1,0:T(8,128)(2,1)S(1)}, bf16[272,128]{1,0:T(8,128)(2,1)S(1)}, u32[]{:S(2)}, u32[]{:S(2)}) collective-permute-start(bf16[272,128]{1,0:T(8,128)(2,1)S(1)} %get-tuple-element.27), channel_id=1, source_target_pairs={{0,3},{1,2},{2,1},{3,0},{4,7},{5,6},{6,5},{7,4},{8,11},{9,10},{10,... | collective-permute-start | bytes 208904 | tf_op jit(solution)/shard_map/ppermute | solution.py:320
  44.1 0.0 collective-permute-start.8
  44.1 2.5 %collective-permute-start.9 = (bf16[272,128]{1,0:T(8,128)(2,1)S(1)}, bf16[272,128]{1,0:T(8,128)(2,1)S(1)}, u32[]{:S(2)}, u32[]{:S(2)}) collective-permute-start(bf16[272,128]{1,0:T(8,128)(2,1)S(1)} %get-tuple-element.29), channel_id=1, source_target_pairs={{0,1},{1,0},{2,3},{3,2},{4,5},{5,4},{6,7},{7,6},{8,9},{9,8},{10,11... | collective-permute-start | bytes 208904 | tf_op jit(solution)/shard_map/ppermute | solution.py:320
  46.6 4.7 %grow_second.1 = (f32[4096,128]{1,0:T(8,128)S(1)}, f32[4096,128]{1,0:T(8,128)S(1)}) custom-call(f32[1024,128]{1,0:T(8,128)S(1)} %get-tuple-element.25.refs_4_.basis_ref.refs_5_, f32[1024,128]{1,0:T(8,128)S(1)} %get-tuple-element.32.second_ref.refs_6_, bf16[32,1024,128]{2,1,0:T(8,128)(2,1)S(1)} %get-tuple-element.33.coupled_ref), custom_call_target="tpu_custom_call" | custom-call | flops 4294967296 | bytes 16777216 | tf_op jit(solution)/shard_map/grow_second/pallas_call | solution.py:433
  51.2 0.0 collective-permute-done.7.refs_0_
  51.2 0.0 collective-permute-done.8.refs_1_
  51.3 0.0 collective-permute-done.9.refs_2_
  51.3 1.5 %last.1 = (bf16[128,8,128]{2,1,0:T(8,128)(2,1)}, bf16[128,32,128]{2,1,0:T(8,128)(2,1)}, f32[1,128]{1,0:T(1,128)}, f32[32,8,128]{2,1,0:T(8,128)}) custom-call(bf16[272,128]{1,0:T(8,128)(2,1)S(1)} %collective-permute-done.7.refs_0_, bf16[272,128]{1,0:T(8,128)(2,1)S(1)} %collective-permute-done.8.refs_1_, bf16[272,128]{1,0:T(8,128)(2,1)S(1)} %collective-permute-done.9.refs_2_, ...), custom_call_target="tpu_custom_call" | custom-call | tf_op jit(solution)/shard_map/last/pallas_call | solution.py:449
  (1 shorter events, 0.0 us)
Async XLA Ops:
  2.1 10.8 %collective-permute-start = (bf16[65,32,128]{2,1,0:T(8,128)(2,1)S(1)}, bf16[65,32,128]{2,1,0:T(8,128)(2,1)S(1)}, u32[]{:S(2)}, u32[]{:S(2)}) collective-permute-start(bf16[65,32,128]{2,1,0:T(8,128)(2,1)S(1)} %fold.1), channel_id=1, source_target_pairs={{0,28},{4,0},{8,4},{12,8},{16,12},{20,16},{24,20},{28,24},{1,29},{... | collective-permute-start | bytes 1597448 | tf_op jit(solution)/shard_map/ppermute | solution.py:344
  14.7 6.1 %collective-permute-start.1 = (bf16[256,128]{1,0:T(8,128)(2,1)S(1)}, bf16[256,128]{1,0:T(8,128)(2,1)S(1)}, u32[]{:S(2)}, u32[]{:S(2)}) collective-permute-start(bf16[256,128]{1,0:T(8,128)(2,1)S(1)} %image_first.1), channel_id=1, source_target_pairs={{0,3},{1,2},{2,1},{3,0},{4,7},{5,6},{6,5},{7,4},{8,11},{9,10},{10,... | collective-permute-start | bytes 196616 | tf_op jit(solution)/shard_map/ppermute | solution.py:320
  19.6 5.3 %collective-permute-start.2 = (bf16[256,128]{1,0:T(8,128)(2,1)S(1)}, bf16[256,128]{1,0:T(8,128)(2,1)S(1)}, u32[]{:S(2)}, u32[]{:S(2)}) collective-permute-start(bf16[256,128]{1,0:T(8,128)(2,1)S(1)} %get-tuple-element.23), channel_id=1, source_target_pairs={{0,2},{1,3},{2,0},{3,1},{4,6},{5,7},{6,4},{7,5},{8,10},{9,11},{10,... | collective-permute-start | bytes 196616 | tf_op jit(solution)/shard_map/ppermute | solution.py:320
  19.7 5.3 %collective-permute-start.3 = (bf16[256,128]{1,0:T(8,128)(2,1)S(1)}, bf16[256,128]{1,0:T(8,128)(2,1)S(1)}, u32[]{:S(2)}, u32[]{:S(2)}) collective-permute-start(bf16[256,128]{1,0:T(8,128)(2,1)S(1)} %get-tuple-element.24), channel_id=1, source_target_pairs={{0,1},{1,0},{2,3},{3,2},{4,5},{5,4},{6,7},{7,6},{8,9},{9,8},{10,11... | collective-permute-start | bytes 196616 | tf_op jit(solution)/shard_map/ppermute | solution.py:320
  25.0 6.8 %collective-permute-start.6 = (bf16[256,128]{1,0:T(8,128)(2,1)S(1)}, bf16[256,128]{1,0:T(8,128)(2,1)S(1)}, u32[]{:S(2)}, u32[]{:S(2)}) collective-permute-start(bf16[256,128]{1,0:T(8,128)(2,1)S(1)} %sum.1.refs_3_.after_ref), channel_id=1, source_target_pairs={{0,1},{1,0},{2,3},{3,2},{4,5},{5,4},{6,7},{7,6},{8,9},{9,8},{10,11... | collective-permute-start | bytes 196616 | tf_op jit(solution)/shard_map/ppermute | solution.py:320
  25.1 6.6 %collective-permute-start.5 = (bf16[256,128]{1,0:T(8,128)(2,1)S(1)}, bf16[256,128]{1,0:T(8,128)(2,1)S(1)}, u32[]{:S(2)}, u32[]{:S(2)}) collective-permute-start(bf16[256,128]{1,0:T(8,128)(2,1)S(1)} %sum.1.refs_3_.after_ref), channel_id=1, source_target_pairs={{0,2},{1,3},{2,0},{3,1},{4,6},{5,7},{6,4},{7,5},{8,10},{9,11},{10,... | collective-permute-start | bytes 196616 | tf_op jit(solution)/shard_map/ppermute | solution.py:320
  27.6 6.1 %collective-permute-start.4 = (bf16[256,128]{1,0:T(8,128)(2,1)S(1)}, bf16[256,128]{1,0:T(8,128)(2,1)S(1)}, u32[]{:S(2)}, u32[]{:S(2)}) collective-permute-start(bf16[256,128]{1,0:T(8,128)(2,1)S(1)} %sum.1.refs_3_.after_ref), channel_id=1, source_target_pairs={{0,3},{1,2},{2,1},{3,0},{4,7},{5,6},{6,5},{7,4},{8,11},{9,10},{10,... | collective-permute-start | bytes 196616 | tf_op jit(solution)/shard_map/ppermute | solution.py:320
  29.4 4.3 %copy-start = (bf16[1,128,32,128]{3,2,1,0:T(8,128)(2,1)S(1)}, bf16[1,128,32,128]{3,2,1,0:T(8,128)(2,1)}, u32[]{:S(2)}) copy-start(bf16[1,128,32,128]{3,2,1,0:T(8,128)(2,1)} %param.4) | copy-start | bytes 3145732
  42.2 9.1 %collective-permute-start.7 = (bf16[272,128]{1,0:T(8,128)(2,1)S(1)}, bf16[272,128]{1,0:T(8,128)(2,1)S(1)}, u32[]{:S(2)}, u32[]{:S(2)}) collective-permute-start(bf16[272,128]{1,0:T(8,128)(2,1)S(1)} %get-tuple-element.27), channel_id=1, source_target_pairs={{0,3},{1,2},{2,1},{3,0},{4,7},{5,6},{6,5},{7,4},{8,11},{9,10},{10,... | collective-permute-start | bytes 208904 | tf_op jit(solution)/shard_map/ppermute | solution.py:320
  44.1 7.2 %collective-permute-start.8 = (bf16[272,128]{1,0:T(8,128)(2,1)S(1)}, bf16[272,128]{1,0:T(8,128)(2,1)S(1)}, u32[]{:S(2)}, u32[]{:S(2)}) collective-permute-start(bf16[272,128]{1,0:T(8,128)(2,1)S(1)} %get-tuple-element.28), channel_id=1, source_target_pairs={{0,2},{1,3},{2,0},{3,1},{4,6},{5,7},{6,4},{7,5},{8,10},{9,11},{10,... | collective-permute-start | bytes 208904 | tf_op jit(solution)/shard_map/ppermute | solution.py:320
  44.1 7.2 %collective-permute-start.9 = (bf16[272,128]{1,0:T(8,128)(2,1)S(1)}, bf16[272,128]{1,0:T(8,128)(2,1)S(1)}, u32[]{:S(2)}, u32[]{:S(2)}) collective-permute-start(bf16[272,128]{1,0:T(8,128)(2,1)S(1)} %get-tuple-element.29), channel_id=1, source_target_pairs={{0,1},{1,0},{2,3},{3,2},{4,5},{5,4},{6,7},{7,6},{8,9},{9,8},{10,11... | collective-permute-start | bytes 208904 | tf_op jit(solution)/shard_map/ppermute | solution.py:320

commit v6 on v5

--- a/solution.py
+++ b/solution.py
@@ -35,19 +35,17 @@
     return (start * scale).reshape(height * levels, height)
 
 
-def by_level(rows_ref, height, levels):
-    parts = [rows_ref[pl.ds(t, height, stride=levels), :] for t in range(levels)]
-    return jnp.concatenate(parts, axis=1).astype(bf16)
-
-
-def couple(left_ref, vector, mpo, coupled_ref, chunk, await_left=None):
+def by_level(rows, height, levels):
+    parts = jnp.swapaxes(rows.reshape(height, levels, height), 0, 1)
+    return jnp.concatenate([parts[t] for t in range(levels)], axis=1).astype(bf16)
+
+
+def couple(left_ref, vector, mpo, coupled_ref, chunk):
     height, width, _ = left_ref.shape
     levels = vector.shape[1] // height
     right_width = mpo.shape[0] // levels
 
     def step(index, carry):
-        if await_left is not None:
-            await_left(index)
         first = index * chunk
         mixed = jnp.dot(
             left_ref[pl.ds(first, chunk)].reshape(chunk * width, height), vector, preferred_element_type=f32
@@ -71,7 +69,7 @@
     lax.fori_loop(0, height // chunk, step, 0)
 
 
-def fold_kernel(right_hbm, folded_ref, right, sems):
+def fold_kernel(right_hbm, start_hbm, left_hbm, mpo_hbm, folded_ref, start_ref, left_ref, mpo_ref, right, sems, more_sems):
     height, width, _ = right.shape
     half = height // 2
     pieces = sems.shape[0] // 2
@@ -82,6 +80,9 @@
             rows = pl.ds(first, size)
             copies.append(pltpu.make_async_copy(right_hbm.at[rows], right.at[rows], sems.at[len(copies)]))
             copies[-1].start()
+    others = ((start_hbm, start_ref), (mpo_hbm, mpo_ref), (left_hbm, left_ref))
+    for k, (source, target) in enumerate(others):
+        pltpu.make_async_copy(source, target, more_sems.at[k]).start()
     diagonal = jnp.zeros((width, height), f32)
     for k in range(pieces):
         copies[2 * k].wait()
@@ -94,6 +95,8 @@
         folded_ref[k * size : (k + 1) * size] = jnp.where(lane >= row, upper, turned).astype(bf16)
         diagonal = diagonal + jnp.sum(jnp.where(lane == row + half, lower, 0.0), axis=0)
     folded_ref[half] = diagonal.astype(bf16)
+    for k, (source, target) in enumerate(others):
+        pltpu.make_async_copy(source, target, more_sems.at[k]).wait()
 
 
 def reorder(size, first, second):
@@ -102,48 +105,36 @@
     return jnp.where((row // second == lane % first) & (row % second == lane // first), 1.0, 0.0).astype(bf16)
 
 
-def first_kernel(start_hbm, left_hbm, mpo_hbm, coupled_ref, mpo_rows_ref, basis_ref, start, left, mpo_ref, sems):
-    chunk = left.shape[0] // (sems.shape[0] - 2)
-
-    def left_copy(index):
-        place = pl.ds(index * chunk, chunk)
-        return pltpu.make_async_copy(left_hbm.at[place], left.at[place], sems.at[index])
-
-    mpo_copy = pltpu.make_async_copy(mpo_hbm, mpo_ref, sems.at[sems.shape[0] - 1])
-    start_copy = pltpu.make_async_copy(start_hbm, start, sems.at[sems.shape[0] - 2])
-    mpo_copy.start()
-    start_copy.start()
-    for index in range(sems.shape[0] - 2):
-        left_copy(index).start()
-    mpo_copy.wait()
+def first_kernel(start_ref, left_ref, mpo_ref, coupled_ref, mpo_rows_ref, basis_ref):
     width, levels, _, right_width = mpo_ref.shape
     terms = [mpo_ref[:, s].astype(f32).reshape(width * levels, right_width).T for s in range(levels)]
     terms = jnp.concatenate(terms, axis=0).astype(bf16)
     terms = jnp.dot(reorder(right_width * levels, right_width, levels), terms, preferred_element_type=f32)
     terms = jnp.dot(terms.astype(bf16), reorder(width * levels, width, levels), preferred_element_type=f32)
     mpo_rows_ref[...] = terms.astype(bf16)
-    start_copy.wait()
-    basis_ref[...] = normalised(start[...])
-    vector = by_level(basis_ref, left.shape[0], levels)
-    couple(left, vector, mpo_rows_ref[...], coupled_ref, chunk, lambda index: left_copy(index).wait())
-
-
-def unfold_kernel(folded_ref, right_ref, wide):
+    basis_ref[...] = normalised(start_ref[...])
+    vector = by_level(basis_ref[...], left_ref.shape[0], levels)
+    couple(left_ref, vector, mpo_rows_ref[...], coupled_ref, 32)
+
+
+def unfold_kernel(folded_ref, right_ref):
     half, width, height = folded_ref.shape
     half -= 1
-    wide[...] = folded_ref[:half].astype(f32).reshape(half * width, height)
-    diagonal = folded_ref[half].astype(f32)
+    wide = folded_ref[...].astype(f32)
     row = lax.broadcasted_iota(jnp.int32, (half, height), 0)
     lane = lax.broadcasted_iota(jnp.int32, (half, height), 1)
-    for u in range(width):
-        one = wide[pl.ds(u, half, stride=width), :]
-        turned = jnp.concatenate([one, one], axis=0).T
-        upper = jnp.where((lane < half) & (lane < row), turned[:half], one)
-        corner = jnp.where(lane == row + half, diagonal[u : u + 1, :], turned[:half])
-        corner = jnp.where(lane < row + half, pltpu.roll(one, half, 1), corner)
-        lower = jnp.where(lane < half, turned[half:], corner)
-        right_ref[u * height : u * height + half, :] = upper.astype(bf16)
-        right_ref[u * height + half : (u + 1) * height, :] = lower.astype(bf16)
+    for first in range(0, width, 8):
+        group = jnp.swapaxes(wide[:half, first : first + 8], 0, 1)
+        for k in range(8):
+            u = first + k
+            one = group[k]
+            turned = jnp.concatenate([one, one], axis=0).T
+            upper = jnp.where((lane < half) & (lane < row), turned[:half], one)
+            corner = jnp.where(lane == row + half, wide[half, u : u + 1, :], turned[:half])
+            corner = jnp.where(lane < row + half, pltpu.roll(one, half, 1), corner)
+            lower = jnp.where(lane < half, turned[half:], corner)
+            right_ref[u * height : u * height + half, :] = upper.astype(bf16)
+            right_ref[u * height + half : (u + 1) * height, :] = lower.astype(bf16)
 
 
 def block_image(where, coupled_ref, right_ref, block):
@@ -161,14 +152,10 @@
     return partner(lax.axis_index("bond"), step, lax.axis_size("bond"))
 
 
-def block_images_kernel(steps, coupled_ref, right_ref, *image_refs):
+def images_kernel(steps, coupled_ref, right_ref, *image_refs):
     for step, image_ref in zip(steps, image_refs):
-        image_ref[...] = block_image(other(step), coupled_ref, right_ref, image_ref.shape[0]).astype(bf16)
-
-
-def own_image_kernel(coupled_ref, right_ref, arrived_ref, image_ref):
-    own = block_image(other(0), coupled_ref, right_ref, image_ref.shape[0])
-    image_ref[...] = own + arrived_ref[...].astype(f32)
+        terms = block_image(other(step), coupled_ref, right_ref, image_ref.shape[0])
+        image_ref[...] = terms.astype(image_ref.dtype)
 
 
 def sum_kernel(own_ref, *refs):
@@ -202,7 +189,7 @@
     second_ref[...] = second_ref[...] * (1.0 / residual_size)
     scalar_ref[0:1, :] = jnp.broadcast_to(rayleigh, (1, height))
     scalar_ref[1:2, :] = jnp.broadcast_to(residual_size, (1, height))
-    couple(left_ref, by_level(second_ref, height, levels), mpo_ref[...], coupled_ref, 32)
+    couple(left_ref, by_level(second_ref[...], height, levels), mpo_ref[...], coupled_ref, 32)
     product = jnp.zeros((1, height), f32)
     for step, place, send_ref in zip(steps, places, sends):
         terms = block_image(other(step), coupled_ref, right_ref, block)
@@ -222,28 +209,36 @@
     return jnp.concatenate([coupled_ref[u], coupled_ref[u + 1]], axis=1)
 
 
-def grow_first_kernel(after_ref, basis_ref, coupled_ref, one_ref, turned):
-    del after_ref
+def store_group(target_ref, first, group):
+    target_ref[:, first : first + len(group), :] = jnp.swapaxes(jnp.stack(group), 0, 1)
+
+
+def grow_first_kernel(basis_ref, coupled_ref, one_ref, turned):
     width, _, height = coupled_ref.shape
     turned[...] = basis_ref[...].T.astype(bf16)
-    for u in range(0, width, 2):
-        grown = jnp.dot(turned[...], pair_of(coupled_ref, u), preferred_element_type=f32)
-        for k in (0, 1):
-            one_ref[pl.ds(u + k, height, stride=width), :] = grown[:, k * height : (k + 1) * height]
+    for first in range(0, width, 8):
+        ones = []
+        for u in range(first, first + 8, 2):
+            grown = jnp.dot(turned[...], pair_of(coupled_ref, u), preferred_element_type=f32)
+            ones += [grown[:, k * height : (k + 1) * height] for k in (0, 1)]
+        store_group(one_ref, first, ones)
 
 
 def grow_second_kernel(basis_ref, second_ref, coupled_ref, cross_ref, two_ref, turned):
     width, _, height = coupled_ref.shape
     turned[:height, :] = basis_ref[...].T.astype(bf16)
     turned[height:, :] = second_ref[...].T.astype(bf16)
-    for u in range(0, width, 2):
-        grown = jnp.dot(turned[...], pair_of(coupled_ref, u), preferred_element_type=f32)
-        for k in (0, 1):
-            place = pl.ds(u + k, height, stride=width)
-            lanes = slice(k * height, (k + 1) * height)
-            mixed = grown[:height, lanes]
-            cross_ref[place, :] = mixed + mixed.T
-            two_ref[place, :] = grown[height:, lanes]
+    for first in range(0, width, 8):
+        crosses, twos = [], []
+        for u in range(first, first + 8, 2):
+            grown = jnp.dot(turned[...], pair_of(coupled_ref, u), preferred_element_type=f32)
+            for k in (0, 1):
+                lanes = slice(k * height, (k + 1) * height)
+                mixed = grown[:height, lanes]
+                crosses.append(mixed + mixed.T)
+                twos.append(grown[height:, lanes])
+        store_group(cross_ref, first, crosses)
+        store_group(two_ref, first, twos)
 
 
 def last_kernel(steps, *refs):
@@ -253,7 +248,6 @@
     state_hbm, left_hbm, energy_hbm, share_hbm, state, left, energy, share, sems = refs[6:]
     block, height = parts[0].shape
     block -= TAIL
-    width = left.shape[1]
     lane = lax.broadcasted_iota(jnp.int32, (TAIL, height), 1)
     row = lax.broadcasted_iota(jnp.int32, (TAIL, height), 0)
     carried = (lane < 3) & (row == 0)
@@ -270,7 +264,7 @@
     offset = lowest - rayleigh
     length = jnp.sqrt(residual_size * residual_size + offset * offset)
     one, two = residual_size / length, offset / length
-    weights = (one * one, one * two, two * two)
+    weights = [weight.reshape(1, 1, height) for weight in (one * one, one * two, two * two)]
     pieces = sems.shape[0] - 3
     size = left.shape[0] // pieces
 
@@ -282,9 +276,9 @@
         return pltpu.make_async_copy(left.at[place], left_hbm.at[place], sems.at[k])
 
     def grow(k, carry):
-        place = pl.ds(pl.multiple_of(k * size * width, size * width), size * width)
-        grown = weights[0] * one_ref[place, :] + weights[1] * cross_ref[place, :] + weights[2] * two_ref[place, :]
-        left[pl.ds(k * size, size)] = grown.astype(bf16).reshape(size, width, height)
+        place = pl.ds(k * size, size)
+        grown = weights[0] * one_ref[place] + weights[1] * cross_ref[place] + weights[2] * two_ref[place]
+        left[place] = grown.astype(bf16)
         piece_copy(k).start()
         return carry
 
@@ -331,18 +325,23 @@
     with_own = steps + (0,)
     apply_flops = 4 * rows * height * width * height
 
-    folded = pl.pallas_call(
+    mpo = jnp.transpose(mpo, (0, 2, 3, 1))
+    folded, start_near, left_near, mpo_near = pl.pallas_call(
         fold_kernel,
-        out_shape=on_chip((height // 2 + 1, width, height), bf16),
-        in_specs=[HBM_BLOCK],
-        out_specs=VMEM_BLOCK,
-        scratch_shapes=[pltpu.VMEM(right.shape, bf16), DMA((8,))],
-        compiler_params=params(58),
+        out_shape=(
+            on_chip((height // 2 + 1, width, height), bf16),
+            on_chip(start.shape, bf16),
+            on_chip(left.shape, bf16),
+            on_chip(mpo.shape, bf16),
+        ),
+        in_specs=[HBM_BLOCK] * 4,
+        out_specs=(VMEM_BLOCK,) * 4,
+        scratch_shapes=[pltpu.VMEM(right.shape, bf16), DMA((8,)), DMA((3,))],
+        compiler_params=params(61),
         name="fold",
-    )(right)
+    )(right, start, left, mpo)
     pairs = [(source, (source - 1) % lax.axis_size("seg")) for source in range(lax.axis_size("seg"))]
     folded = lax.ppermute(folded, "seg", pairs)
-    mpo_sorted = jnp.transpose(mpo, (0, 2, 3, 1))
     first_coupled, mpo_rows, basis = pl.pallas_call(
         first_kernel,
         out_shape=(
@@ -350,69 +349,50 @@
             on_chip((width * levels, levels * width), bf16),
             on_chip((rows, height), f32),
         ),
-        in_specs=[HBM_BLOCK] * 3,
+        in_specs=[VMEM_BLOCK] * 3,
         out_specs=(VMEM_BLOCK,) * 3,
-        scratch_shapes=[
-            pltpu.VMEM(start.shape, bf16),
-            pltpu.VMEM(left.shape, bf16),
-            pltpu.VMEM(mpo_sorted.shape, bf16),
-            DMA((6,)),
-        ],
-        compiler_params=params(53),
+        compiler_params=params(8),
         cost_estimate=cost(2 * apply_flops, 8 << 20),
         name="first_coupled",
-    )(start, left, mpo_sorted)
+    )(start_near, left_near, mpo_near)
     right_rows = pl.pallas_call(
         unfold_kernel,
         out_shape=on_chip((width * height, height), bf16),
         in_specs=[VMEM_BLOCK],
         out_specs=VMEM_BLOCK,
-        scratch_shapes=[pltpu.VMEM((height // 2 * width, height), f32)],
         compiler_params=params(8),
         name="unfold",
     )(folded)
 
-    def block_images(steps, name):
-        return pl.pallas_call(
-            functools.partial(block_images_kernel, steps),
-            out_shape=(on_chip((block, height), bf16),) * len(steps),
-            in_specs=[VMEM_BLOCK] * 2,
-            out_specs=(VMEM_BLOCK,) * len(steps),
-            compiler_params=params(8),
-            cost_estimate=cost(apply_flops * len(steps) // (2 * count), 8 << 20),
-            name=name,
-        )(first_coupled, right_rows)
-
-    sends = tuple(block_images(steps[:1], "image_first")) + tuple(block_images(steps[1:], "image_rest"))
+    *sends, own = pl.pallas_call(
+        functools.partial(images_kernel, with_own),
+        out_shape=(on_chip((block, height), bf16),) * len(steps) + (on_chip((block, height), f32),),
+        in_specs=[VMEM_BLOCK] * 2,
+        out_specs=(VMEM_BLOCK,) * count,
+        compiler_params=params(8),
+        cost_estimate=cost(apply_flops // 2, 8 << 20),
+        name="first_image",
+    )(first_coupled, right_rows)
     arrived = [exchanged(value, step) for value, step in zip(sends, steps)]
-    own = pl.pallas_call(
-        own_image_kernel,
-        out_shape=on_chip((block, height), f32),
-        in_specs=[VMEM_BLOCK] * 3,
-        out_specs=VMEM_BLOCK,
-        compiler_params=params(8),
-        cost_estimate=cost(apply_flops // (2 * count), 8 << 20),
-        name="image_own",
-    )(first_coupled, right_rows, arrived[0])
-    own = pl.pallas_call(
-        sum_kernel,
-        out_shape=on_chip((block, height), bf16),
-        in_specs=[VMEM_BLOCK] * (count - 1),
-        out_specs=VMEM_BLOCK,
-        compiler_params=params(4),
-        name="sum",
-    )(own, *arrived[1:])
-    grown_shape = (height * width, height)
+    grown_shape = (height, width, height)
     one = pl.pallas_call(
         grow_first_kernel,
         out_shape=on_chip(grown_shape, f32),
-        in_specs=[VMEM_BLOCK] * 3,
+        in_specs=[VMEM_BLOCK] * 2,
         out_specs=VMEM_BLOCK,
         scratch_shapes=[pltpu.VMEM((height, rows), bf16)],
         compiler_params=params(8),
         cost_estimate=cost(apply_flops, 8 << 20),
         name="grow_first",
-    )(own, basis, first_coupled)
+    )(basis, first_coupled)
+    own = pl.pallas_call(
+        sum_kernel,
+        out_shape=on_chip((block, height), bf16),
+        in_specs=[VMEM_BLOCK] * count,
+        out_specs=VMEM_BLOCK,
+        compiler_params=params(4),
+        name="sum",
+    )(own, *arrived)
     blocks = [exchanged(own, step) for step in steps] + [own]
     outcome = pl.pallas_call(
         functools.partial(second_kernel, with_own),
@@ -426,7 +406,7 @@
         out_specs=(VMEM_BLOCK,) * (count + 3),
         compiler_params=params(12),
         name="second_image",
-    )(*blocks, basis, left, mpo_rows, right_rows)
+    )(*blocks, basis, left_near, mpo_rows, right_rows)
     second_coupled, second, scalars = outcome[:3]
     sends = outcome[3:]
     parts = [exchanged(value, step) for value, step in zip(sends, steps)] + [sends[-1]]

time: 53.1 us -> 52.5 us (0.989)
  Pallas kernels: 29.5 us -> 25.5 us
  waiting for transfers between devices: 5.73 us -> 9.29 us
    ppermute x9, waiting for transfers between devices: 5.73 us -> 8.48 us  [exchanged(): lax.ppermute(value, 'bond', [(source, int(partner(source, step, count)))...]
    pallas_call x1, Pallas kernels: 4.67 us -> 2.96 us  [body(): pl.pallas_call(grow_second_kernel, out_shape=(on_chip(grown_shape, f32),)...]
    pallas_call x1, Pallas kernels: 7.43 us -> 5.98 us  [body(): pl.pallas_call(first_kernel, out_shape=(on_chip((width, rows, height), bf...]
    ppermute x1, waiting for transfers between devices: 0.01 us -> 0.8 us  [body(): folded = lax.ppermute(folded, 'seg', pairs)]
    pallas_call x1, Pallas kernels: 2.32 us -> 1.56 us  [body(): pl.pallas_call(grow_first_kernel, out_shape=on_chip(grown_shape, f32), in...]
    pallas_call x4 -> x2, Pallas kernels: 4.12 us -> 4.32 us  [the longest x1 2.33 us: body(): pl.pallas_call(functools.partial(images_kernel, with_own), out_shape=(on_...]
  transfers between devices with their start and end apart: 10 -> 10, of which waited for: 3 -> 6; matrix products, arithmetic and copies ran while one was open for 0% -> 0% of each run, Pallas kernels for 31% -> 20%
where the time goes in v6:
time: 52.5 us; the launch traced here: 52.3 us
  Pallas kernels  25.5 us (49%)
  starting transfers between devices  16.7 us (32%)
  waiting for transfers between devices  9.29 us (18%)
  between operations  0.86 us (2%)
    ppermute x9, starting transfers between devices, exchanged(): lax.ppermute(value, 'bond', [(source, int(partner(source, step, count)))...  13.3 us
    ppermute x9, waiting for transfers between devices, exchanged(): lax.ppermute(value, 'bond', [(source, int(partner(source, step, count)))...  8.48 us
    pallas_call x1, Pallas kernels, body(): pl.pallas_call(functools.partial(second_kernel, with_own), out_shape=(on_...  8.47 us
    pallas_call x1, Pallas kernels, body(): pl.pallas_call(first_kernel, out_shape=(on_chip((width, rows, height), bf...  5.98 us
    ppermute x1, starting transfers between devices, body(): folded = lax.ppermute(folded, 'seg', pairs)  3.39 us
    pallas_call x1, Pallas kernels, body(): pl.pallas_call(grow_second_kernel, out_shape=(on_chip(grown_shape, f32),)...  2.96 us
    pallas_call x1, Pallas kernels, body(): pl.pallas_call(functools.partial(images_kernel, with_own), out_shape=(on_...  2.33 us
    pallas_call x1, Pallas kernels, body(): pl.pallas_call(fold_kernel, out_shape=(on_chip((height // 2 + 1, width, h...  1.99 us
  transfers between devices with their start and end apart: 10, of which 6 were waited for; matrix products, arithmetic and copies ran while one was open for 0% of the time, Pallas kernels for 20%

profile of v6, /device:TPU:0, one launch (start us, length us, event | category | flops | bytes accessed | tf_op | source)
XLA Modules:
  0.0 52.3 jit_solution(3438518330349370534)
XLA Ops:
  0.6 2.0 %fold.1 = (bf16[65,32,128]{2,1,0:T(8,128)(2,1)S(1)}, bf16[128,8,128]{2,1,0:T(8,128)(2,1)S(1)}, bf16[128,32,128]{2,1,0:T(8,128)(2,1)S(1)}, bf16[32,8,8,32]{3,2,1,0:T(8,128)(2,1)S(1)}) custom-call(bf16[128,32,128]{2,1,0:T(8,128)(2,1)} %bitcast.11, bf16[128,8,128]{2,1,0:T(8,128)(2,1)} %bitcast.14, bf16[128,32,128]{2,1,0:T(8,128)(2,1)} %bitcast.12, ...), custom_call_target="tpu_custom_call" | custom-call | tf_op jit(solution)/shard_map/fold/pallas_call | solution.py:329
  2.6 3.4 %collective-permute-start = (bf16[65,32,128]{2,1,0:T(8,128)(2,1)S(1)}, bf16[65,32,128]{2,1,0:T(8,128)(2,1)S(1)}, u32[]{:S(2)}, u32[]{:S(2)}) collective-permute-start(bf16[65,32,128]{2,1,0:T(8,128)(2,1)S(1)} %get-tuple-element.32), channel_id=1, source_target_pairs={{0,28},{4,0},{8,4},{12,8},{16,12},{20,16},{24,20},{28,24},{1,29},{... | collective-permute-start | bytes 1597448 | tf_op jit(solution)/shard_map/ppermute | solution.py:344
  6.0 6.0 %first_coupled.1 = (bf16[32,1024,128]{2,1,0:T(8,128)(2,1)S(1)}, bf16[256,256]{1,0:T(8,128)(2,1)S(1)}, f32[1024,128]{1,0:T(8,128)S(1)}) custom-call(bf16[128,8,128]{2,1,0:T(8,128)(2,1)S(1)} %get-tuple-element.28.start_ref, bf16[128,32,128]{2,1,0:T(8,128)(2,1)S(1)} %get-tuple-element.29.left_ref.refs_5_, bf16[32,8,8,32]{3,2,1,0:T(8,128)(2,1)S(1)} %get-tuple-element.30.mpo_ref), custom_call_target="tpu_custom_call" | custom-call | flops 4294967296 | bytes 8388608 | tf_op jit(solution)/shard_map/first_coupled/pallas_call | solution.py:345
  12.0 0.8 %collective-permute-done.folded_ref = bf16[65,32,128]{2,1,0:T(8,128)(2,1)S(1)} collective-permute-done((bf16[65,32,128]{2,1,0:T(8,128)(2,1)S(1)}, bf16[65,32,128]{2,1,0:T(8,128)(2,1)S(1)}, u32[]{:S(2)}, u32[]{:S(2)}) %collective-permute-start) | collective-permute-done | bytes 532512 | tf_op jit(solution)/shard_map/ppermute | solution.py:344
  12.8 0.7 %unfold.1.right_ref.refs_7_ = bf16[4096,128]{1,0:T(8,128)(2,1)S(1)} custom-call(bf16[65,32,128]{2,1,0:T(8,128)(2,1)S(1)} %collective-permute-done.folded_ref), custom_call_target="tpu_custom_call" | custom-call | tf_op jit(solution)/shard_map/unfold/pallas_call | solution.py:358
  13.5 2.3 %first_image.1 = (bf16[256,128]{1,0:T(8,128)(2,1)S(1)}, bf16[256,128]{1,0:T(8,128)(2,1)S(1)}, bf16[256,128]{1,0:T(8,128)(2,1)S(1)}, f32[256,128]{1,0:T(8,128)S(1)}) custom-call(bf16[32,1024,128]{2,1,0:T(8,128)(2,1)S(1)} %get-tuple-element.31.coupled_ref, bf16[4096,128]{1,0:T(8,128)(2,1)S(1)} %unfold.1.right_ref.refs_7_), custom_call_target="tpu_custom_call" | custom-call | flops 1073741824 | bytes 8388608 | tf_op jit(solution)/shard_map/first_image/pallas_call | solution.py:367
  15.8 3.7 %collective-permute-start.1 = (bf16[256,128]{1,0:T(8,128)(2,1)S(1)}, bf16[256,128]{1,0:T(8,128)(2,1)S(1)}, u32[]{:S(2)}, u32[]{:S(2)}) collective-permute-start(bf16[256,128]{1,0:T(8,128)(2,1)S(1)} %get-tuple-element.34), channel_id=1, source_target_pairs={{0,3},{1,2},{2,1},{3,0},{4,7},{5,6},{6,5},{7,4},{8,11},{9,10},{10,... | collective-permute-start | bytes 196616 | tf_op jit(solution)/shard_map/ppermute | solution.py:314
  19.5 0.0 collective-permute-start.2
  19.5 0.8 %collective-permute-start.3 = (bf16[256,128]{1,0:T(8,128)(2,1)S(1)}, bf16[256,128]{1,0:T(8,128)(2,1)S(1)}, u32[]{:S(2)}, u32[]{:S(2)}) collective-permute-start(bf16[256,128]{1,0:T(8,128)(2,1)S(1)} %get-tuple-element.36), channel_id=1, source_target_pairs={{0,1},{1,0},{2,3},{3,2},{4,5},{5,4},{6,7},{7,6},{8,9},{9,8},{10,11... | collective-permute-start | bytes 196616 | tf_op jit(solution)/shard_map/ppermute | solution.py:314
  20.3 2.1 %collective-permute-done.1.refs_0_ = bf16[256,128]{1,0:T(8,128)(2,1)S(1)} collective-permute-done((bf16[256,128]{1,0:T(8,128)(2,1)S(1)}, bf16[256,128]{1,0:T(8,128)(2,1)S(1)}, u32[]{:S(2)}, u32[]{:S(2)}) %collective-permute-start.1) | collective-permute-done | bytes 65568 | tf_op jit(solution)/shard_map/ppermute | solution.py:314
  22.4 2.8 %collective-permute-done.2.refs_1_ = bf16[256,128]{1,0:T(8,128)(2,1)S(1)} collective-permute-done((bf16[256,128]{1,0:T(8,128)(2,1)S(1)}, bf16[256,128]{1,0:T(8,128)(2,1)S(1)}, u32[]{:S(2)}, u32[]{:S(2)}) %collective-permute-start.2) | collective-permute-done | bytes 65568 | tf_op jit(solution)/shard_map/ppermute | solution.py:314
  25.2 0.0 collective-permute-done.3.refs_2_
  25.2 1.1 %collective-permute-start.6 = (bf16[256,128]{1,0:T(8,128)(2,1)S(1)}, bf16[256,128]{1,0:T(8,128)(2,1)S(1)}, u32[]{:S(2)}, u32[]{:S(2)}) collective-permute-start(bf16[256,128]{1,0:T(8,128)(2,1)S(1)} %sum.1.refs_3_), channel_id=1, source_target_pairs={{0,1},{1,0},{2,3},{3,2},{4,5},{5,4},{6,7},{7,6},{8,9},{9,8},{10,11... | collective-permute-start | bytes 196616 | tf_op jit(solution)/shard_map/ppermute | solution.py:314
  26.3 2.2 %collective-permute-start.5 = (bf16[256,128]{1,0:T(8,128)(2,1)S(1)}, bf16[256,128]{1,0:T(8,128)(2,1)S(1)}, u32[]{:S(2)}, u32[]{:S(2)}) collective-permute-start(bf16[256,128]{1,0:T(8,128)(2,1)S(1)} %sum.1.refs_3_), channel_id=1, source_target_pairs={{0,2},{1,3},{2,0},{3,1},{4,6},{5,7},{6,4},{7,5},{8,10},{9,11},{10,... | collective-permute-start | bytes 196616 | tf_op jit(solution)/shard_map/ppermute | solution.py:314
  28.5 1.1 %collective-permute-start.4 = (bf16[256,128]{1,0:T(8,128)(2,1)S(1)}, bf16[256,128]{1,0:T(8,128)(2,1)S(1)}, u32[]{:S(2)}, u32[]{:S(2)}) collective-permute-start(bf16[256,128]{1,0:T(8,128)(2,1)S(1)} %sum.1.refs_3_), channel_id=1, source_target_pairs={{0,3},{1,2},{2,1},{3,0},{4,7},{5,6},{6,5},{7,4},{8,11},{9,10},{10,... | collective-permute-start | bytes 196616 | tf_op jit(solution)/shard_map/ppermute | solution.py:314
  29.6 1.6 %grow_first.1.refs_7_ = f32[128,32,128]{2,1,0:T(8,128)S(1)} custom-call(f32[1024,128]{1,0:T(8,128)S(1)} %get-tuple-element.37.refs_4_.basis_ref.refs_5_, bf16[32,1024,128]{2,1,0:T(8,128)(2,1)S(1)} %get-tuple-element.31.coupled_ref), custom_call_target="tpu_custom_call" | custom-call | flops 2147483648 | bytes 8388608 | tf_op jit(solution)/shard_map/grow_first/pallas_call | solution.py:378
  31.2 0.0 collective-permute-done.6.refs_2_
  31.2 1.9 %collective-permute-done.5.refs_1_ = bf16[256,128]{1,0:T(8,128)(2,1)S(1)} collective-permute-done((bf16[256,128]{1,0:T(8,128)(2,1)S(1)}, bf16[256,128]{1,0:T(8,128)(2,1)S(1)}, u32[]{:S(2)}, u32[]{:S(2)}) %collective-permute-start.5) | collective-permute-done | bytes 65568 | tf_op jit(solution)/shard_map/ppermute | solution.py:314
  33.1 1.5 %collective-permute-done.4.refs_0_ = bf16[256,128]{1,0:T(8,128)(2,1)S(1)} collective-permute-done((bf16[256,128]{1,0:T(8,128)(2,1)S(1)}, bf16[256,128]{1,0:T(8,128)(2,1)S(1)}, u32[]{:S(2)}, u32[]{:S(2)}) %collective-permute-start.4) | collective-permute-done | bytes 65568 | tf_op jit(solution)/shard_map/ppermute | solution.py:314
  34.6 8.5 %second_image.1 = (bf16[32,1024,128]{2,1,0:T(8,128)(2,1)S(1)}, f32[1024,128]{1,0:T(8,128)S(1)}, f32[8,128]{1,0:T(8,128)S(1)}, bf16[272,128]{1,0:T(8,128)(2,1)S(1...) custom-call(bf16[256,128]{1,0:T(8,128)(2,1)S(1)} %collective-permute-done.4.refs_0_, ...), custom_call_target="tpu_custom_call" | custom-call | tf_op jit(solution)/shard_map/second_image/pallas_call | solution.py:397
  43.1 1.2 %collective-permute-start.7 = (bf16[272,128]{1,0:T(8,128)(2,1)S(1)}, bf16[272,128]{1,0:T(8,128)(2,1)S(1)}, u32[]{:S(2)}, u32[]{:S(2)}) collective-permute-start(bf16[272,128]{1,0:T(8,128)(2,1)S(1)} %get-tuple-element.39), channel_id=1, source_target_pairs={{0,3},{1,2},{2,1},{3,0},{4,7},{5,6},{6,5},{7,4},{8,11},{9,10},{10,... | collective-permute-start | bytes 208904 | tf_op jit(solution)/shard_map/ppermute | solution.py:314
  44.2 0.1 collective-permute-start.8
  44.3 3.2 %collective-permute-start.9 = (bf16[272,128]{1,0:T(8,128)(2,1)S(1)}, bf16[272,128]{1,0:T(8,128)(2,1)S(1)}, u32[]{:S(2)}, u32[]{:S(2)}) collective-permute-start(bf16[272,128]{1,0:T(8,128)(2,1)S(1)} %get-tuple-element.41), channel_id=1, source_target_pairs={{0,1},{1,0},{2,3},{3,2},{4,5},{5,4},{6,7},{7,6},{8,9},{9,8},{10,11... | collective-permute-start | bytes 208904 | tf_op jit(solution)/shard_map/ppermute | solution.py:314
  47.5 3.0 %grow_second.1 = (f32[128,32,128]{2,1,0:T(8,128)S(1)}, f32[128,32,128]{2,1,0:T(8,128)S(1)}) custom-call(f32[1024,128]{1,0:T(8,128)S(1)} %get-tuple-element.37.refs_4_.basis_ref.refs_5_, f32[1024,128]{1,0:T(8,128)S(1)} %get-tuple-element.44.second_ref.refs_6_, bf16[32,1024,128]{2,1,0:T(8,128)(2,1)S(1)} %get-tuple-element.45.coupled_ref), custom_call_target="tpu_custom_call" | custom-call | flops 4294967296 | bytes 16777216 | tf_op jit(solution)/shard_map/grow_second/pallas_call | solution.py:413
  50.4 0.0 collective-permute-done.7.refs_0_
  50.4 0.2 collective-permute-done.8.refs_1_
  50.7 0.0 collective-permute-done.9.refs_2_
  50.7 1.5 %last.1 = (bf16[128,8,128]{2,1,0:T(8,128)(2,1)}, bf16[128,32,128]{2,1,0:T(8,128)(2,1)}, f32[1,128]{1,0:T(1,128)}, f32[32,8,128]{2,1,0:T(8,128)}) custom-call(bf16[272,128]{1,0:T(8,128)(2,1)S(1)} %collective-permute-done.7.refs_0_, bf16[272,128]{1,0:T(8,128)(2,1)S(1)} %collective-permute-done.8.refs_1_, bf16[272,128]{1,0:T(8,128)(2,1)S(1)} %collective-permute-done.9.refs_2_, ...), custom_call_target="tpu_custom_call" | custom-call | tf_op jit(solution)/shard_map/last/pallas_call | solution.py:429
  (1 shorter events, 0.0 us)
Async XLA Ops:
  2.6 10.2 %collective-permute-start = (bf16[65,32,128]{2,1,0:T(8,128)(2,1)S(1)}, bf16[65,32,128]{2,1,0:T(8,128)(2,1)S(1)}, u32[]{:S(2)}, u32[]{:S(2)}) collective-permute-start(bf16[65,32,128]{2,1,0:T(8,128)(2,1)S(1)} %get-tuple-element.32), channel_id=1, source_target_pairs={{0,28},{4,0},{8,4},{12,8},{16,12},{20,16},{24,20},{28,24},{1,29},{... | collective-permute-start | bytes 1597448 | tf_op jit(solution)/shard_map/ppermute | solution.py:344
  15.8 6.6 %collective-permute-start.1 = (bf16[256,128]{1,0:T(8,128)(2,1)S(1)}, bf16[256,128]{1,0:T(8,128)(2,1)S(1)}, u32[]{:S(2)}, u32[]{:S(2)}) collective-permute-start(bf16[256,128]{1,0:T(8,128)(2,1)S(1)} %get-tuple-element.34), channel_id=1, source_target_pairs={{0,3},{1,2},{2,1},{3,0},{4,7},{5,6},{6,5},{7,4},{8,11},{9,10},{10,... | collective-permute-start | bytes 196616 | tf_op jit(solution)/shard_map/ppermute | solution.py:314
  19.5 5.7 %collective-permute-start.2 = (bf16[256,128]{1,0:T(8,128)(2,1)S(1)}, bf16[256,128]{1,0:T(8,128)(2,1)S(1)}, u32[]{:S(2)}, u32[]{:S(2)}) collective-permute-start(bf16[256,128]{1,0:T(8,128)(2,1)S(1)} %get-tuple-element.35), channel_id=1, source_target_pairs={{0,2},{1,3},{2,0},{3,1},{4,6},{5,7},{6,4},{7,5},{8,10},{9,11},{10,... | collective-permute-start | bytes 196616 | tf_op jit(solution)/shard_map/ppermute | solution.py:314
  19.5 5.7 %collective-permute-start.3 = (bf16[256,128]{1,0:T(8,128)(2,1)S(1)}, bf16[256,128]{1,0:T(8,128)(2,1)S(1)}, u32[]{:S(2)}, u32[]{:S(2)}) collective-permute-start(bf16[256,128]{1,0:T(8,128)(2,1)S(1)} %get-tuple-element.36), channel_id=1, source_target_pairs={{0,1},{1,0},{2,3},{3,2},{4,5},{5,4},{6,7},{7,6},{8,9},{9,8},{10,11... | collective-permute-start | bytes 196616 | tf_op jit(solution)/shard_map/ppermute | solution.py:314
  25.2 6.0 %collective-permute-start.6 = (bf16[256,128]{1,0:T(8,128)(2,1)S(1)}, bf16[256,128]{1,0:T(8,128)(2,1)S(1)}, u32[]{:S(2)}, u32[]{:S(2)}) collective-permute-start(bf16[256,128]{1,0:T(8,128)(2,1)S(1)} %sum.1.refs_3_), channel_id=1, source_target_pairs={{0,1},{1,0},{2,3},{3,2},{4,5},{5,4},{6,7},{7,6},{8,9},{9,8},{10,11... | collective-permute-start | bytes 196616 | tf_op jit(solution)/shard_map/ppermute | solution.py:314
  26.3 6.8 %collective-permute-start.5 = (bf16[256,128]{1,0:T(8,128)(2,1)S(1)}, bf16[256,128]{1,0:T(8,128)(2,1)S(1)}, u32[]{:S(2)}, u32[]{:S(2)}) collective-permute-start(bf16[256,128]{1,0:T(8,128)(2,1)S(1)} %sum.1.refs_3_), channel_id=1, source_target_pairs={{0,2},{1,3},{2,0},{3,1},{4,6},{5,7},{6,4},{7,5},{8,10},{9,11},{10,... | collective-permute-start | bytes 196616 | tf_op jit(solution)/shard_map/ppermute | solution.py:314
  28.5 6.1 %collective-permute-start.4 = (bf16[256,128]{1,0:T(8,128)(2,1)S(1)}, bf16[256,128]{1,0:T(8,128)(2,1)S(1)}, u32[]{:S(2)}, u32[]{:S(2)}) collective-permute-start(bf16[256,128]{1,0:T(8,128)(2,1)S(1)} %sum.1.refs_3_), channel_id=1, source_target_pairs={{0,3},{1,2},{2,1},{3,0},{4,7},{5,6},{6,5},{7,4},{8,11},{9,10},{10,... | collective-permute-start | bytes 196616 | tf_op jit(solution)/shard_map/ppermute | solution.py:314
  43.1 7.4 %collective-permute-start.7 = (bf16[272,128]{1,0:T(8,128)(2,1)S(1)}, bf16[272,128]{1,0:T(8,128)(2,1)S(1)}, u32[]{:S(2)}, u32[]{:S(2)}) collective-permute-start(bf16[272,128]{1,0:T(8,128)(2,1)S(1)} %get-tuple-element.39), channel_id=1, source_target_pairs={{0,3},{1,2},{2,1},{3,0},{4,7},{5,6},{6,5},{7,4},{8,11},{9,10},{10,... | collective-permute-start | bytes 208904 | tf_op jit(solution)/shard_map/ppermute | solution.py:314
  44.2 6.4 %collective-permute-start.8 = (bf16[272,128]{1,0:T(8,128)(2,1)S(1)}, bf16[272,128]{1,0:T(8,128)(2,1)S(1)}, u32[]{:S(2)}, u32[]{:S(2)}) collective-permute-start(bf16[272,128]{1,0:T(8,128)(2,1)S(1)} %get-tuple-element.40), channel_id=1, source_target_pairs={{0,2},{1,3},{2,0},{3,1},{4,6},{5,7},{6,4},{7,5},{8,10},{9,11},{10,... | collective-permute-start | bytes 208904 | tf_op jit(solution)/shard_map/ppermute | solution.py:314
  44.3 6.4 %collective-permute-start.9 = (bf16[272,128]{1,0:T(8,128)(2,1)S(1)}, bf16[272,128]{1,0:T(8,128)(2,1)S(1)}, u32[]{:S(2)}, u32[]{:S(2)}) collective-permute-start(bf16[272,128]{1,0:T(8,128)(2,1)S(1)} %get-tuple-element.41), channel_id=1, source_target_pairs={{0,1},{1,0},{2,3},{3,2},{4,5},{5,4},{6,7},{7,6},{8,9},{9,8},{10,11... | collective-permute-start | bytes 208904 | tf_op jit(solution)/shard_map/ppermute | solution.py:314

commit v7 on v6

--- a/solution.py
+++ b/solution.py
@@ -44,11 +44,9 @@
     height, width, _ = left_ref.shape
     levels = vector.shape[1] // height
     right_width = mpo.shape[0] // levels
-
-    def step(index, carry):
-        first = index * chunk
+    for first in range(0, height, chunk):
         mixed = jnp.dot(
-            left_ref[pl.ds(first, chunk)].reshape(chunk * width, height), vector, preferred_element_type=f32
+            left_ref[first : first + chunk].reshape(chunk * width, height), vector, preferred_element_type=f32
         )
         for pair in range(0, chunk, 2):
             columns = []
@@ -62,27 +60,27 @@
             halves = [
                 result[:, k * height : (k + 1) * height].reshape(right_width, levels, height) for k in (0, 1)
             ]
-            place = pl.multiple_of((first + pair) * levels, 2 * levels)
-            coupled_ref[:, pl.ds(place, 2 * levels), :] = jnp.concatenate(halves, axis=1).astype(bf16)
-        return carry
-
-    lax.fori_loop(0, height // chunk, step, 0)
-
-
-def fold_kernel(right_hbm, start_hbm, left_hbm, mpo_hbm, folded_ref, start_ref, left_ref, mpo_ref, right, sems, more_sems):
+            place = (first + pair) * levels
+            coupled_ref[:, place : place + 2 * levels, :] = jnp.concatenate(halves, axis=1).astype(bf16)
+
+
+def fold_kernel(offset, more, right_hbm, *refs):
+    sources, folded_ref, targets = refs[:more], refs[more], refs[more + 1 : 2 * more + 1]
+    right, sems, more_sems = refs[2 * more + 1 :]
     height, width, _ = right.shape
     half = height // 2
     pieces = sems.shape[0] // 2
     size = half // pieces
+    columns = pl.ds(offset, width)
     copies = []
     for k in range(pieces):
         for first in (k * size, half + k * size):
             rows = pl.ds(first, size)
-            copies.append(pltpu.make_async_copy(right_hbm.at[rows], right.at[rows], sems.at[len(copies)]))
+            copies.append(pltpu.make_async_copy(right_hbm.at[rows, columns], right.at[rows], sems.at[len(copies)]))
             copies[-1].start()
-    others = ((start_hbm, start_ref), (mpo_hbm, mpo_ref), (left_hbm, left_ref))
-    for k, (source, target) in enumerate(others):
-        pltpu.make_async_copy(source, target, more_sems.at[k]).start()
+    others = [pltpu.make_async_copy(*pair, more_sems.at[k]) for k, pair in enumerate(zip(sources, targets))]
+    for copy in others:
+        copy.start()
     diagonal = jnp.zeros((width, height), f32)
     for k in range(pieces):
         copies[2 * k].wait()
@@ -95,8 +93,8 @@
         folded_ref[k * size : (k + 1) * size] = jnp.where(lane >= row, upper, turned).astype(bf16)
         diagonal = diagonal + jnp.sum(jnp.where(lane == row + half, lower, 0.0), axis=0)
     folded_ref[half] = diagonal.astype(bf16)
-    for k, (source, target) in enumerate(others):
-        pltpu.make_async_copy(source, target, more_sems.at[k]).wait()
+    for copy in others:
+        copy.wait()
 
 
 def reorder(size, first, second):
@@ -105,7 +103,7 @@
     return jnp.where((row // second == lane % first) & (row % second == lane // first), 1.0, 0.0).astype(bf16)
 
 
-def first_kernel(start_ref, left_ref, mpo_ref, coupled_ref, mpo_rows_ref, basis_ref):
+def first_kernel(start_ref, mpo_ref, left_ref, coupled_ref, mpo_rows_ref, basis_ref):
     width, levels, _, right_width = mpo_ref.shape
     terms = [mpo_ref[:, s].astype(f32).reshape(width * levels, right_width).T for s in range(levels)]
     terms = jnp.concatenate(terms, axis=0).astype(bf16)
@@ -137,11 +135,16 @@
             right_ref[u * height + half : (u + 1) * height, :] = lower.astype(bf16)
 
 
-def block_image(where, coupled_ref, right_ref, block):
-    width = coupled_ref.shape[0]
+def block_image(where, coupled_ref, right_refs, block):
+    height = coupled_ref.shape[2]
     place = pl.ds(pl.multiple_of(where * block, block), block)
-    terms = jnp.concatenate([coupled_ref[u, place, :] for u in range(width)], axis=1)
-    return jnp.dot(terms, right_ref[...], preferred_element_type=f32)
+    total, first = 0.0, 0
+    for right_ref in right_refs:
+        last = first + right_ref.shape[0] // height
+        terms = jnp.concatenate([coupled_ref[u, place, :] for u in range(first, last)], axis=1)
+        total = total + jnp.dot(terms, right_ref[...], preferred_element_type=f32)
+        first = last
+    return total
 
 
 def partner(me, step, count):
@@ -152,10 +155,15 @@
     return partner(lax.axis_index("bond"), step, lax.axis_size("bond"))
 
 
-def images_kernel(steps, coupled_ref, right_ref, *image_refs):
-    for step, image_ref in zip(steps, image_refs):
-        terms = block_image(other(step), coupled_ref, right_ref, image_ref.shape[0])
-        image_ref[...] = terms.astype(image_ref.dtype)
+def images_kernel(steps, groups, coupled_ref, *refs):
+    for step, image_ref in zip(steps, refs[groups:]):
+        image_ref[...] = block_image(other(step), coupled_ref, refs[:groups], image_ref.shape[0]).astype(bf16)
+
+
+def own_image_kernel(groups, arrived_ref, coupled_ref, *refs):
+    image_ref = refs[groups]
+    own = block_image(other(0), coupled_ref, refs[:groups], image_ref.shape[0])
+    image_ref[...] = own + arrived_ref[...].astype(f32)
 
 
 def sum_kernel(own_ref, *refs):
@@ -165,11 +173,12 @@
     refs[-1][...] = total.astype(bf16)
 
 
-def second_kernel(steps, *refs):
+def second_kernel(steps, groups, *refs):
     count = len(steps)
     blocks, refs = refs[:count], refs[count:]
-    basis_ref, left_ref, mpo_ref, right_ref, coupled_ref, second_ref, scalar_ref = refs[:7]
-    sends = refs[7:]
+    right_refs, refs = refs[:groups], refs[groups:]
+    basis_ref, left_ref, mpo_ref, coupled_ref, second_ref, scalar_ref = refs[:6]
+    sends = refs[6:]
     height = left_ref.shape[0]
     rows = basis_ref.shape[0]
     levels = rows // height
@@ -192,7 +201,7 @@
     couple(left_ref, by_level(second_ref[...], height, levels), mpo_ref[...], coupled_ref, 32)
     product = jnp.zeros((1, height), f32)
     for step, place, send_ref in zip(steps, places, sends):
-        terms = block_image(other(step), coupled_ref, right_ref, block)
+        terms = block_image(other(step), coupled_ref, right_refs, block)
         product += jnp.sum(second_ref[place, :] * terms, axis=0, keepdims=True)
         send_ref[:block, :] = terms.astype(bf16)
     value = jnp.sum(product, axis=1, keepdims=True) / entries
@@ -326,22 +335,27 @@
     apply_flops = 4 * rows * height * width * height
 
     mpo = jnp.transpose(mpo, (0, 2, 3, 1))
-    folded, start_near, left_near, mpo_near = pl.pallas_call(
-        fold_kernel,
-        out_shape=(
-            on_chip((height // 2 + 1, width, height), bf16),
-            on_chip(start.shape, bf16),
-            on_chip(left.shape, bf16),
-            on_chip(mpo.shape, bf16),
-        ),
-        in_specs=[HBM_BLOCK] * 4,
-        out_specs=(VMEM_BLOCK,) * 4,
-        scratch_shapes=[pltpu.VMEM(right.shape, bf16), DMA((8,)), DMA((3,))],
-        compiler_params=params(61),
-        name="fold",
-    )(right, start, left, mpo)
-    pairs = [(source, (source - 1) % lax.axis_size("seg")) for source in range(lax.axis_size("seg"))]
-    folded = lax.ppermute(folded, "seg", pairs)
+    groups = max(1, width // 16)
+    part = width // groups
+    folded_shape = (height // 2 + 1, part, height)
+    segments = lax.axis_size("seg")
+    pairs = [(source, (source - 1) % segments) for source in range(segments)]
+
+    def folded_part(k, more, grant):
+        folded, *brought = pl.pallas_call(
+            functools.partial(fold_kernel, k * part, len(more)),
+            out_shape=(on_chip(folded_shape, bf16),) + tuple(on_chip(x.shape, bf16) for x in more),
+            in_specs=[HBM_BLOCK] * (1 + len(more)),
+            out_specs=(VMEM_BLOCK,) * (1 + len(more)),
+            scratch_shapes=[pltpu.VMEM((height, part, height), bf16), DMA((4,)), DMA((max(1, len(more)),))],
+            compiler_params=params(grant),
+            name="fold",
+        )(right, *more)
+        return lax.ppermute(folded, "seg", pairs), brought
+
+    arriving = [folded_part(k, (), 62)[0] for k in range(groups - 1)]
+    folded, (start_near, mpo_near, left_near) = folded_part(groups - 1, (start, mpo, left), 60)
+    arriving.append(folded)
     first_coupled, mpo_rows, basis = pl.pallas_call(
         first_kernel,
         out_shape=(
@@ -351,28 +365,35 @@
         ),
         in_specs=[VMEM_BLOCK] * 3,
         out_specs=(VMEM_BLOCK,) * 3,
-        compiler_params=params(8),
+        compiler_params=params(12),
         cost_estimate=cost(2 * apply_flops, 8 << 20),
         name="first_coupled",
-    )(start_near, left_near, mpo_near)
-    right_rows = pl.pallas_call(
-        unfold_kernel,
-        out_shape=on_chip((width * height, height), bf16),
-        in_specs=[VMEM_BLOCK],
-        out_specs=VMEM_BLOCK,
-        compiler_params=params(8),
-        name="unfold",
-    )(folded)
-
-    *sends, own = pl.pallas_call(
-        functools.partial(images_kernel, with_own),
-        out_shape=(on_chip((block, height), bf16),) * len(steps) + (on_chip((block, height), f32),),
-        in_specs=[VMEM_BLOCK] * 2,
-        out_specs=(VMEM_BLOCK,) * count,
-        compiler_params=params(8),
-        cost_estimate=cost(apply_flops // 2, 8 << 20),
-        name="first_image",
-    )(first_coupled, right_rows)
+    )(start_near, mpo_near, left_near)
+    rights = [
+        pl.pallas_call(
+            unfold_kernel,
+            out_shape=on_chip((part * height, height), bf16),
+            in_specs=[VMEM_BLOCK],
+            out_specs=VMEM_BLOCK,
+            compiler_params=params(8),
+            cost_estimate=cost(1 << 20, 1 << 20),
+            name="unfold",
+        )(folded)
+        for folded in arriving
+    ]
+
+    def images(steps, name):
+        return pl.pallas_call(
+            functools.partial(images_kernel, steps, groups),
+            out_shape=(on_chip((block, height), bf16),) * len(steps),
+            in_specs=[VMEM_BLOCK] * (1 + groups),
+            out_specs=(VMEM_BLOCK,) * len(steps),
+            compiler_params=params(8),
+            cost_estimate=cost(apply_flops * len(steps) // (2 * count), 8 << 20),
+            name=name,
+        )(first_coupled, *rights)
+
+    sends = tuple(images(steps[:1], "image_first")) + tuple(images(steps[1:], "image_rest"))
     arrived = [exchanged(value, step) for value, step in zip(sends, steps)]
     grown_shape = (height, width, height)
     one = pl.pallas_call(
@@ -386,27 +407,36 @@
         name="grow_first",
     )(basis, first_coupled)
     own = pl.pallas_call(
+        functools.partial(own_image_kernel, groups),
+        out_shape=on_chip((block, height), f32),
+        in_specs=[VMEM_BLOCK] * (2 + groups),
+        out_specs=VMEM_BLOCK,
+        compiler_params=params(8),
+        cost_estimate=cost(apply_flops // (2 * count), 8 << 20),
+        name="image_own",
+    )(arrived[0], first_coupled, *rights)
+    own = pl.pallas_call(
         sum_kernel,
         out_shape=on_chip((block, height), bf16),
-        in_specs=[VMEM_BLOCK] * count,
+        in_specs=[VMEM_BLOCK] * (count - 1),
         out_specs=VMEM_BLOCK,
         compiler_params=params(4),
         name="sum",
-    )(own, *arrived)
+    )(own, *arrived[1:])
     blocks = [exchanged(own, step) for step in steps] + [own]
     outcome = pl.pallas_call(
-        functools.partial(second_kernel, with_own),
+        functools.partial(second_kernel, with_own, groups),
         out_shape=(
             on_chip((width, rows, height), bf16),
             on_chip((rows, height), f32),
             on_chip((8, height), f32),
         )
         + (on_chip((block + TAIL, height), bf16),) * count,
-        in_specs=[VMEM_BLOCK] * (count + 4),
+        in_specs=[VMEM_BLOCK] * (count + groups + 3),
         out_specs=(VMEM_BLOCK,) * (count + 3),
         compiler_params=params(12),
         name="second_image",
-    )(*blocks, basis, left_near, mpo_rows, right_rows)
+    )(*blocks, *rights, basis, left_near, mpo_rows)
     second_coupled, second, scalars = outcome[:3]
     sends = outcome[3:]
     parts = [exchanged(value, step) for value, step in zip(sends, steps)] + [sends[-1]]

time: 52.5 us -> 50.4 us (0.960)
  waiting for transfers between devices: 9.29 us -> 6.86 us
  starting transfers between devices: 16.7 us -> 17.5 us
    ppermute x9, waiting for transfers between devices: 8.48 us -> 6.86 us  [exchanged(): lax.ppermute(value, 'bond', [(source, int(partner(source, step, count)))...]
    pallas_call x1, Pallas kernels: 5.98 us -> 5.01 us  [body(): pl.pallas_call(first_kernel, out_shape=(on_chip((width, rows, height), bf...]
    ppermute x1 -> x2, waiting for transfers between devices: 0.8 us -> 0.01 us  [folded_part(): return (lax.ppermute(folded, 'seg', pairs), brought)]
    ppermute x1 -> x2, starting transfers between devices: 3.39 us -> 4.11 us  [folded_part(): return (lax.ppermute(folded, 'seg', pairs), brought)]
    pallas_call x4 -> x8, Pallas kernels: 13.5 us -> 13.9 us  [the longest x1 7.59 us: body(): pl.pallas_call(functools.partial(second_kernel, with_own, groups), out_sh...]
  transfers between devices with their start and end apart: 10 -> 11, of which waited for: 6 -> 5; matrix products, arithmetic and copies ran while one was open for 0% -> 0% of each run, Pallas kernels for 20% -> 27%
where the time goes in v7:
time: 50.4 us; the launch traced here: 50.2 us
  Pallas kernels  25 us (50%)
  starting transfers between devices  17.5 us (35%)
  waiting for transfers between devices  6.86 us (14%)
  between operations  0.91 us (2%)
    ppermute x9, starting transfers between devices, exchanged(): lax.ppermute(value, 'bond', [(source, int(partner(source, step, count)))...  13.4 us
    pallas_call x1, Pallas kernels, body(): pl.pallas_call(functools.partial(second_kernel, with_own, groups), out_sh...  7.59 us
    ppermute x9, waiting for transfers between devices, exchanged(): lax.ppermute(value, 'bond', [(source, int(partner(source, step, count)))...  6.86 us
    pallas_call x1, Pallas kernels, body(): pl.pallas_call(first_kernel, out_shape=(on_chip((width, rows, height), bf...  5.01 us
    ppermute x2, starting transfers between devices, folded_part(): return (lax.ppermute(folded, 'seg', pairs), brought)  4.11 us
    pallas_call x2, Pallas kernels, folded_part(): pl.pallas_call(functools.partial(fold_kernel, k * part, len(more)), out_s...  2.99 us
    pallas_call x1, Pallas kernels, body(): pl.pallas_call(grow_second_kernel, out_shape=(on_chip(grown_shape, f32),)...  2.96 us
    pallas_call x2, Pallas kernels, images(): pl.pallas_call(functools.partial(images_kernel, steps, groups), out_shape...  1.94 us
  transfers between devices with their start and end apart: 11, of which 5 were waited for; matrix products, arithmetic and copies ran while one was open for 0% of the time, Pallas kernels for 27%

profile of v7, /device:TPU:0, one launch (start us, length us, event | category | flops | bytes accessed | tf_op | source)
XLA Modules:
  0.0 50.2 jit_solution(101572604090590003)
XLA Ops:
  0.6 1.2 %fold.3 = bf16[65,16,128]{2,1,0:T(8,128)(2,1)S(1)} custom-call(bf16[128,32,128]{2,1,0:T(8,128)(2,1)} %bitcast.11), custom_call_target="tpu_custom_call" | custom-call | tf_op jit(solution)/shard_map/fold/pallas_call | solution.py:345
  1.9 3.4 %collective-permute-start = (bf16[65,16,128]{2,1,0:T(8,128)(2,1)S(1)}, bf16[65,16,128]{2,1,0:T(8,128)(2,1)S(1)}, u32[]{:S(2)}, u32[]{:S(2)}) collective-permute-start(bf16[65,16,128]{2,1,0:T(8,128)(2,1)S(1)} %fold.3), channel_id=1, source_target_pairs={{0,28},{4,0},{8,4},{12,8},{16,12},{20,16},{24,20},{28,24},{1,29},{... | collective-permute-start | bytes 798728 | tf_op jit(solution)/shard_map/ppermute | solution.py:354
  5.3 1.7 %fold.2 = (bf16[65,16,128]{2,1,0:T(8,128)(2,1)S(1)}, bf16[128,8,128]{2,1,0:T(8,128)(2,1)S(1)}, bf16[32,8,8,32]{3,2,1,0:T(8,128)(2,1)S(1)}, bf16[128,32,128]{2,1,0:T(8,128)(2,1)S(1)}) custom-call(bf16[128,32,128]{2,1,0:T(8,128)(2,1)} %bitcast.12, bf16[128,8,128]{2,1,0:T(8,128)(2,1)} %bitcast.15, bf16[32,8,8,32]{3,2,1,0:T(8,128)(2,1)} %bitcast.14, ...), custom_call_target="tpu_custom_call" | custom-call | tf_op jit(solution)/shard_map/fold/pallas_call | solution.py:345
  7.0 0.7 %collective-permute-start.1 = (bf16[65,16,128]{2,1,0:T(8,128)(2,1)S(1)}, bf16[65,16,128]{2,1,0:T(8,128)(2,1)S(1)}, u32[]{:S(2)}, u32[]{:S(2)}) collective-permute-start(bf16[65,16,128]{2,1,0:T(8,128)(2,1)S(1)} %get-tuple-element.30), channel_id=1, source_target_pairs={{0,28},{4,0},{8,4},{12,8},{16,12},{20,16},{24,20},{28,24},{1,29},{... | collective-permute-start | bytes 798728 | tf_op jit(solution)/shard_map/ppermute | solution.py:354
  7.7 5.0 %first_coupled.1 = (bf16[32,1024,128]{2,1,0:T(8,128)(2,1)S(1)}, bf16[256,256]{1,0:T(8,128)(2,1)S(1)}, f32[1024,128]{1,0:T(8,128)S(1)}) custom-call(bf16[128,8,128]{2,1,0:T(8,128)(2,1)S(1)} %get-tuple-element.26.start_ref, bf16[32,8,8,32]{3,2,1,0:T(8,128)(2,1)S(1)} %get-tuple-element.27.mpo_ref, bf16[128,32,128]{2,1,0:T(8,128)(2,1)S(1)} %get-tuple-element.28.left_ref.refs_7_), custom_call_target="tpu_custom_call" | custom-call | flops 4294967296 | bytes 8388608 | tf_op jit(solution)/shard_map/first_coupled/pallas_call | solution.py:359
  12.8 0.4 unfold.2.refs_0_.refs_4_
  13.1 0.0 collective-permute-done.1.folded_ref
  13.1 0.4 unfold.3.refs_1_.refs_5_
  13.5 0.7 %image_first.1 = bf16[256,128]{1,0:T(8,128)(2,1)S(1)} custom-call(bf16[32,1024,128]{2,1,0:T(8,128)(2,1)S(1)} %get-tuple-element.29.coupled_ref, bf16[2048,128]{1,0:T(8,128)(2,1)S(1)} %unfold.2.refs_0_.refs_4_, bf16[2048,128]{1,0:T(8,128)(2,1)S(1)} %unfold.3.refs_1_.refs_5_), custom_call_target="tpu_custom_call" | custom-call | flops 268435456 | bytes 8388608 | tf_op jit(solution)/shard_map/image_first/pallas_call | solution.py:386
  14.2 3.7 %collective-permute-start.2 = (bf16[256,128]{1,0:T(8,128)(2,1)S(1)}, bf16[256,128]{1,0:T(8,128)(2,1)S(1)}, u32[]{:S(2)}, u32[]{:S(2)}) collective-permute-start(bf16[256,128]{1,0:T(8,128)(2,1)S(1)} %image_first.1), channel_id=1, source_target_pairs={{0,3},{1,2},{2,1},{3,0},{4,7},{5,6},{6,5},{7,4},{8,11},{9,10},{10,... | collective-permute-start | bytes 196616 | tf_op jit(solution)/shard_map/ppermute | solution.py:323
  17.9 1.2 %image_rest.1 = (bf16[256,128]{1,0:T(8,128)(2,1)S(1)}, bf16[256,128]{1,0:T(8,128)(2,1)S(1)}) custom-call(bf16[32,1024,128]{2,1,0:T(8,128)(2,1)S(1)} %get-tuple-element.29.coupled_ref, bf16[2048,128]{1,0:T(8,128)(2,1)S(1)} %unfold.2.refs_0_.refs_4_, bf16[2048,128]{1,0:T(8,128)(2,1)S(1)} %unfold.3.refs_1_.refs_5_), custom_call_target="tpu_custom_call" | custom-call | flops 536870912 | bytes 8388608 | tf_op jit(solution)/shard_map/image_rest/pallas_call | solution.py:386
  19.1 0.1 collective-permute-start.3
  19.2 0.8 %collective-permute-start.4 = (bf16[256,128]{1,0:T(8,128)(2,1)S(1)}, bf16[256,128]{1,0:T(8,128)(2,1)S(1)}, u32[]{:S(2)}, u32[]{:S(2)}) collective-permute-start(bf16[256,128]{1,0:T(8,128)(2,1)S(1)} %get-tuple-element.32), channel_id=1, source_target_pairs={{0,1},{1,0},{2,3},{3,2},{4,5},{5,4},{6,7},{7,6},{8,9},{9,8},{10,11... | collective-permute-start | bytes 196616 | tf_op jit(solution)/shard_map/ppermute | solution.py:323
  20.0 0.4 collective-permute-done.2.arrived_ref
  20.4 0.7 %image_own.1.own_ref = f32[256,128]{1,0:T(8,128)S(1)} custom-call(bf16[256,128]{1,0:T(8,128)(2,1)S(1)} %collective-permute-done.2.arrived_ref, bf16[32,1024,128]{2,1,0:T(8,128)(2,1)S(1)} %get-tuple-element.29.coupled_ref, bf16[2048,128]{1,0:T(8,128)(2,1)S(1)} %unfold.2.refs_0_.refs_4_, bf16[2048,128]{1,0:T(8,128)(2,1)S(1)} %unfold.3.refs_1_.refs_5_), custom_call_target="tpu_custom_call" | custom-call | flops 268435456 | bytes 8388608 | tf_op jit(solution)/shard_map/image_own/pallas_call | solution.py:409
  21.1 3.3 %collective-permute-done.3.refs_0_ = bf16[256,128]{1,0:T(8,128)(2,1)S(1)} collective-permute-done((bf16[256,128]{1,0:T(8,128)(2,1)S(1)}, bf16[256,128]{1,0:T(8,128)(2,1)S(1)}, u32[]{:S(2)}, u32[]{:S(2)}) %collective-permute-start.3) | collective-permute-done | bytes 65568 | tf_op jit(solution)/shard_map/ppermute | solution.py:323
  24.4 0.0 collective-permute-done.4.refs_1_
  24.5 0.6 %collective-permute-start.7 = (bf16[256,128]{1,0:T(8,128)(2,1)S(1)}, bf16[256,128]{1,0:T(8,128)(2,1)S(1)}, u32[]{:S(2)}, u32[]{:S(2)}) collective-permute-start(bf16[256,128]{1,0:T(8,128)(2,1)S(1)} %sum.1.refs_3_), channel_id=1, source_target_pairs={{0,1},{1,0},{2,3},{3,2},{4,5},{5,4},{6,7},{7,6},{8,9},{9,8},{10,11... | collective-permute-start | bytes 196616 | tf_op jit(solution)/shard_map/ppermute | solution.py:323
  25.0 2.2 %collective-permute-start.6 = (bf16[256,128]{1,0:T(8,128)(2,1)S(1)}, bf16[256,128]{1,0:T(8,128)(2,1)S(1)}, u32[]{:S(2)}, u32[]{:S(2)}) collective-permute-start(bf16[256,128]{1,0:T(8,128)(2,1)S(1)} %sum.1.refs_3_), channel_id=1, source_target_pairs={{0,2},{1,3},{2,0},{3,1},{4,6},{5,7},{6,4},{7,5},{8,10},{9,11},{10,... | collective-permute-start | bytes 196616 | tf_op jit(solution)/shard_map/ppermute | solution.py:323
  27.2 1.7 %collective-permute-start.5 = (bf16[256,128]{1,0:T(8,128)(2,1)S(1)}, bf16[256,128]{1,0:T(8,128)(2,1)S(1)}, u32[]{:S(2)}, u32[]{:S(2)}) collective-permute-start(bf16[256,128]{1,0:T(8,128)(2,1)S(1)} %sum.1.refs_3_), channel_id=1, source_target_pairs={{0,3},{1,2},{2,1},{3,0},{4,7},{5,6},{6,5},{7,4},{8,11},{9,10},{10,... | collective-permute-start | bytes 196616 | tf_op jit(solution)/shard_map/ppermute | solution.py:323
  28.9 1.6 %grow_first.1.refs_7_ = f32[128,32,128]{2,1,0:T(8,128)S(1)} custom-call(f32[1024,128]{1,0:T(8,128)S(1)} %get-tuple-element.33.refs_6_.basis_ref.refs_5_, bf16[32,1024,128]{2,1,0:T(8,128)(2,1)S(1)} %get-tuple-element.29.coupled_ref), custom_call_target="tpu_custom_call" | custom-call | flops 2147483648 | bytes 8388608 | tf_op jit(solution)/shard_map/grow_first/pallas_call | solution.py:399
  30.5 1.5 %collective-permute-done.6.refs_1_ = bf16[256,128]{1,0:T(8,128)(2,1)S(1)} collective-permute-done((bf16[256,128]{1,0:T(8,128)(2,1)S(1)}, bf16[256,128]{1,0:T(8,128)(2,1)S(1)}, u32[]{:S(2)}, u32[]{:S(2)}) %collective-permute-start.6) | collective-permute-done | bytes 65568 | tf_op jit(solution)/shard_map/ppermute | solution.py:323
  31.9 1.4 %collective-permute-done.5.refs_0_ = bf16[256,128]{1,0:T(8,128)(2,1)S(1)} collective-permute-done((bf16[256,128]{1,0:T(8,128)(2,1)S(1)}, bf16[256,128]{1,0:T(8,128)(2,1)S(1)}, u32[]{:S(2)}, u32[]{:S(2)}) %collective-permute-start.5) | collective-permute-done | bytes 65568 | tf_op jit(solution)/shard_map/ppermute | solution.py:323
  33.3 7.6 %second_image.1 = (bf16[32,1024,128]{2,1,0:T(8,128)(2,1)S(1)}, f32[1024,128]{1,0:T(8,128)S(1)}, f32[8,128]{1,0:T(8,128)S(1)}, bf16[272,128]{1,0:T(8,128)(2,1)S(1...) custom-call(bf16[256,128]{1,0:T(8,128)(2,1)S(1)} %collective-permute-done.5.refs_0_, ...), custom_call_target="tpu_custom_call" | custom-call | tf_op jit(solution)/shard_map/second_image/pallas_call | solution.py:427
  40.9 1.7 %collective-permute-start.8 = (bf16[272,128]{1,0:T(8,128)(2,1)S(1)}, bf16[272,128]{1,0:T(8,128)(2,1)S(1)}, u32[]{:S(2)}, u32[]{:S(2)}) collective-permute-start(bf16[272,128]{1,0:T(8,128)(2,1)S(1)} %get-tuple-element.35), channel_id=1, source_target_pairs={{0,3},{1,2},{2,1},{3,0},{4,7},{5,6},{6,5},{7,4},{8,11},{9,10},{10,... | collective-permute-start | bytes 208904 | tf_op jit(solution)/shard_map/ppermute | solution.py:323
  42.7 0.0 collective-permute-start.9
  42.7 2.7 %collective-permute-start.10 = (bf16[272,128]{1,0:T(8,128)(2,1)S(1)}, bf16[272,128]{1,0:T(8,128)(2,1)S(1)}, u32[]{:S(2)}, u32[]{:S(2)}) collective-permute-start(bf16[272,128]{1,0:T(8,128)(2,1)S(1)} %get-tuple-element.37), channel_id=1, source_target_pairs={{0,1},{1,0},{2,3},{3,2},{4,5},{5,4},{6,7},{7,6},{8,9},{9,8},{10,11... | collective-permute-start | bytes 208904 | tf_op jit(solution)/shard_map/ppermute | solution.py:323
  45.3 3.0 %grow_second.1 = (f32[128,32,128]{2,1,0:T(8,128)S(1)}, f32[128,32,128]{2,1,0:T(8,128)S(1)}) custom-call(f32[1024,128]{1,0:T(8,128)S(1)} %get-tuple-element.33.refs_6_.basis_ref.refs_5_, f32[1024,128]{1,0:T(8,128)S(1)} %get-tuple-element.40.second_ref.refs_6_, bf16[32,1024,128]{2,1,0:T(8,128)(2,1)S(1)} %get-tuple-element.41.coupled_ref), custom_call_target="tpu_custom_call" | custom-call | flops 4294967296 | bytes 16777216 | tf_op jit(solution)/shard_map/grow_second/pallas_call | solution.py:443
  48.3 0.0 collective-permute-done.8.refs_0_
  48.3 0.2 collective-permute-done.9.refs_1_
  48.5 0.0 collective-permute-done.10.refs_2_
  48.5 1.5 %last.1 = (bf16[128,8,128]{2,1,0:T(8,128)(2,1)}, bf16[128,32,128]{2,1,0:T(8,128)(2,1)}, f32[1,128]{1,0:T(1,128)}, f32[32,8,128]{2,1,0:T(8,128)}) custom-call(bf16[272,128]{1,0:T(8,128)(2,1)S(1)} %collective-permute-done.8.refs_0_, bf16[272,128]{1,0:T(8,128)(2,1)S(1)} %collective-permute-done.9.refs_1_, bf16[272,128]{1,0:T(8,128)(2,1)S(1)} %collective-permute-done.10.refs_2_, ...), custom_call_target="tpu_custom_call" | custom-call | tf_op jit(solution)/shard_map/last/pallas_call | solution.py:459
  (3 shorter events, 0.0 us)
Async XLA Ops:
  1.9 10.9 %collective-permute-start = (bf16[65,16,128]{2,1,0:T(8,128)(2,1)S(1)}, bf16[65,16,128]{2,1,0:T(8,128)(2,1)S(1)}, u32[]{:S(2)}, u32[]{:S(2)}) collective-permute-start(bf16[65,16,128]{2,1,0:T(8,128)(2,1)S(1)} %fold.3), channel_id=1, source_target_pairs={{0,28},{4,0},{8,4},{12,8},{16,12},{20,16},{24,20},{28,24},{1,29},{... | collective-permute-start | bytes 798728 | tf_op jit(solution)/shard_map/ppermute | solution.py:354
  7.0 6.1 %collective-permute-start.1 = (bf16[65,16,128]{2,1,0:T(8,128)(2,1)S(1)}, bf16[65,16,128]{2,1,0:T(8,128)(2,1)S(1)}, u32[]{:S(2)}, u32[]{:S(2)}) collective-permute-start(bf16[65,16,128]{2,1,0:T(8,128)(2,1)S(1)} %get-tuple-element.30), channel_id=1, source_target_pairs={{0,28},{4,0},{8,4},{12,8},{16,12},{20,16},{24,20},{28,24},{1,29},{... | collective-permute-start | bytes 798728 | tf_op jit(solution)/shard_map/ppermute | solution.py:354
  14.2 6.2 %collective-permute-start.2 = (bf16[256,128]{1,0:T(8,128)(2,1)S(1)}, bf16[256,128]{1,0:T(8,128)(2,1)S(1)}, u32[]{:S(2)}, u32[]{:S(2)}) collective-permute-start(bf16[256,128]{1,0:T(8,128)(2,1)S(1)} %image_first.1), channel_id=1, source_target_pairs={{0,3},{1,2},{2,1},{3,0},{4,7},{5,6},{6,5},{7,4},{8,11},{9,10},{10,... | collective-permute-start | bytes 196616 | tf_op jit(solution)/shard_map/ppermute | solution.py:323
  19.1 5.3 %collective-permute-start.3 = (bf16[256,128]{1,0:T(8,128)(2,1)S(1)}, bf16[256,128]{1,0:T(8,128)(2,1)S(1)}, u32[]{:S(2)}, u32[]{:S(2)}) collective-permute-start(bf16[256,128]{1,0:T(8,128)(2,1)S(1)} %get-tuple-element.31), channel_id=1, source_target_pairs={{0,2},{1,3},{2,0},{3,1},{4,6},{5,7},{6,4},{7,5},{8,10},{9,11},{10,... | collective-permute-start | bytes 196616 | tf_op jit(solution)/shard_map/ppermute | solution.py:323
  19.2 5.2 %collective-permute-start.4 = (bf16[256,128]{1,0:T(8,128)(2,1)S(1)}, bf16[256,128]{1,0:T(8,128)(2,1)S(1)}, u32[]{:S(2)}, u32[]{:S(2)}) collective-permute-start(bf16[256,128]{1,0:T(8,128)(2,1)S(1)} %get-tuple-element.32), channel_id=1, source_target_pairs={{0,1},{1,0},{2,3},{3,2},{4,5},{5,4},{6,7},{7,6},{8,9},{9,8},{10,11... | collective-permute-start | bytes 196616 | tf_op jit(solution)/shard_map/ppermute | solution.py:323
  24.5 6.0 %collective-permute-start.7 = (bf16[256,128]{1,0:T(8,128)(2,1)S(1)}, bf16[256,128]{1,0:T(8,128)(2,1)S(1)}, u32[]{:S(2)}, u32[]{:S(2)}) collective-permute-start(bf16[256,128]{1,0:T(8,128)(2,1)S(1)} %sum.1.refs_3_), channel_id=1, source_target_pairs={{0,1},{1,0},{2,3},{3,2},{4,5},{5,4},{6,7},{7,6},{8,9},{9,8},{10,11... | collective-permute-start | bytes 196616 | tf_op jit(solution)/shard_map/ppermute | solution.py:323
  25.0 6.9 %collective-permute-start.6 = (bf16[256,128]{1,0:T(8,128)(2,1)S(1)}, bf16[256,128]{1,0:T(8,128)(2,1)S(1)}, u32[]{:S(2)}, u32[]{:S(2)}) collective-permute-start(bf16[256,128]{1,0:T(8,128)(2,1)S(1)} %sum.1.refs_3_), channel_id=1, source_target_pairs={{0,2},{1,3},{2,0},{3,1},{4,6},{5,7},{6,4},{7,5},{8,10},{9,11},{10,... | collective-permute-start | bytes 196616 | tf_op jit(solution)/shard_map/ppermute | solution.py:323
  27.2 6.1 %collective-permute-start.5 = (bf16[256,128]{1,0:T(8,128)(2,1)S(1)}, bf16[256,128]{1,0:T(8,128)(2,1)S(1)}, u32[]{:S(2)}, u32[]{:S(2)}) collective-permute-start(bf16[256,128]{1,0:T(8,128)(2,1)S(1)} %sum.1.refs_3_), channel_id=1, source_target_pairs={{0,3},{1,2},{2,1},{3,0},{4,7},{5,6},{6,5},{7,4},{8,11},{9,10},{10,... | collective-permute-start | bytes 196616 | tf_op jit(solution)/shard_map/ppermute | solution.py:323
  40.9 7.4 %collective-permute-start.8 = (bf16[272,128]{1,0:T(8,128)(2,1)S(1)}, bf16[272,128]{1,0:T(8,128)(2,1)S(1)}, u32[]{:S(2)}, u32[]{:S(2)}) collective-permute-start(bf16[272,128]{1,0:T(8,128)(2,1)S(1)} %get-tuple-element.35), channel_id=1, source_target_pairs={{0,3},{1,2},{2,1},{3,0},{4,7},{5,6},{6,5},{7,4},{8,11},{9,10},{10,... | collective-permute-start | bytes 208904 | tf_op jit(solution)/shard_map/ppermute | solution.py:323
  42.7 5.9 %collective-permute-start.9 = (bf16[272,128]{1,0:T(8,128)(2,1)S(1)}, bf16[272,128]{1,0:T(8,128)(2,1)S(1)}, u32[]{:S(2)}, u32[]{:S(2)}) collective-permute-start(bf16[272,128]{1,0:T(8,128)(2,1)S(1)} %get-tuple-element.36), channel_id=1, source_target_pairs={{0,2},{1,3},{2,0},{3,1},{4,6},{5,7},{6,4},{7,5},{8,10},{9,11},{10,... | collective-permute-start | bytes 208904 | tf_op jit(solution)/shard_map/ppermute | solution.py:323
  42.7 5.9 %collective-permute-start.10 = (bf16[272,128]{1,0:T(8,128)(2,1)S(1)}, bf16[272,128]{1,0:T(8,128)(2,1)S(1)}, u32[]{:S(2)}, u32[]{:S(2)}) collective-permute-start(bf16[272,128]{1,0:T(8,128)(2,1)S(1)} %get-tuple-element.37), channel_id=1, source_target_pairs={{0,1},{1,0},{2,3},{3,2},{4,5},{5,4},{6,7},{7,6},{8,9},{9,8},{10,11... | collective-permute-start | bytes 208904 | tf_op jit(solution)/shard_map/ppermute | solution.py:323

commit v8 on v7

--- a/solution.py
+++ b/solution.py
@@ -64,37 +64,40 @@
             coupled_ref[:, place : place + 2 * levels, :] = jnp.concatenate(halves, axis=1).astype(bf16)
 
 
-def fold_kernel(offset, more, right_hbm, *refs):
-    sources, folded_ref, targets = refs[:more], refs[more], refs[more + 1 : 2 * more + 1]
-    right, sems, more_sems = refs[2 * more + 1 :]
-    height, width, _ = right.shape
-    half = height // 2
-    pieces = sems.shape[0] // 2
-    size = half // pieces
-    columns = pl.ds(offset, width)
-    copies = []
-    for k in range(pieces):
-        for first in (k * size, half + k * size):
-            rows = pl.ds(first, size)
-            copies.append(pltpu.make_async_copy(right_hbm.at[rows, columns], right.at[rows], sems.at[len(copies)]))
-            copies[-1].start()
-    others = [pltpu.make_async_copy(*pair, more_sems.at[k]) for k, pair in enumerate(zip(sources, targets))]
-    for copy in others:
-        copy.start()
-    diagonal = jnp.zeros((width, height), f32)
-    for k in range(pieces):
-        copies[2 * k].wait()
-        copies[2 * k + 1].wait()
-        lower = right[half + k * size : half + (k + 1) * size].astype(f32)
-        row = lax.broadcasted_iota(jnp.int32, lower.shape, 0) + k * size
-        lane = lax.broadcasted_iota(jnp.int32, lower.shape, 2)
-        turned = pltpu.roll(lower, half, 2)
-        upper = right[k * size : (k + 1) * size].astype(f32)
-        folded_ref[k * size : (k + 1) * size] = jnp.where(lane >= row, upper, turned).astype(bf16)
-        diagonal = diagonal + jnp.sum(jnp.where(lane == row + half, lower, 0.0), axis=0)
-    folded_ref[half] = diagonal.astype(bf16)
-    for copy in others:
-        copy.wait()
+class Fold:
+    def __init__(self, right_hbm, offset, right, sems):
+        self.right = right
+        self.pieces = sems.shape[0] // 2
+        self.half = right.shape[0] // 2
+        self.size = self.half // self.pieces
+        columns = pl.ds(offset, right.shape[1])
+        self.copies = []
+        for k in range(self.pieces):
+            for first in (k * self.size, self.half + k * self.size):
+                rows = pl.ds(first, self.size)
+                source = right_hbm.at[rows, columns]
+                self.copies.append(pltpu.make_async_copy(source, right.at[rows], sems.at[len(self.copies)]))
+        for copy in self.copies:
+            copy.start()
+
+    def finish(self, folded_ref):
+        right, half, size = self.right, self.half, self.size
+        diagonal = jnp.zeros(right.shape[1:], f32)
+        for k in range(self.pieces):
+            self.copies[2 * k].wait()
+            self.copies[2 * k + 1].wait()
+            lower = right[half + k * size : half + (k + 1) * size].astype(f32)
+            row = lax.broadcasted_iota(jnp.int32, lower.shape, 0) + k * size
+            lane = lax.broadcasted_iota(jnp.int32, lower.shape, 2)
+            turned = pltpu.roll(lower, half, 2)
+            upper = right[k * size : (k + 1) * size].astype(f32)
+            folded_ref[k * size : (k + 1) * size] = jnp.where(lane >= row, upper, turned).astype(bf16)
+            diagonal = diagonal + jnp.sum(jnp.where(lane == row + half, lower, 0.0), axis=0)
+        folded_ref[half] = diagonal.astype(bf16)
+
+
+def fold_kernel(offset, right_hbm, folded_ref, right, sems):
+    Fold(right_hbm, offset, right, sems).finish(folded_ref)
 
 
 def reorder(size, first, second):
@@ -103,16 +106,33 @@
     return jnp.where((row // second == lane % first) & (row % second == lane // first), 1.0, 0.0).astype(bf16)
 
 
-def first_kernel(start_ref, mpo_ref, left_ref, coupled_ref, mpo_rows_ref, basis_ref):
-    width, levels, _, right_width = mpo_ref.shape
-    terms = [mpo_ref[:, s].astype(f32).reshape(width * levels, right_width).T for s in range(levels)]
+def prepare_kernel(offset, right_hbm, start_hbm, mpo_hbm, left_hbm, *refs):
+    folded_ref, basis_ref, vector_ref, mpo_rows_ref, left_ref, right, sems, start, mpo, more_sems = refs
+    start_copy = pltpu.make_async_copy(start_hbm, start, more_sems.at[0])
+    mpo_copy = pltpu.make_async_copy(mpo_hbm, mpo, more_sems.at[1])
+    left_copy = pltpu.make_async_copy(left_hbm, left_ref, more_sems.at[2])
+    start_copy.start()
+    mpo_copy.start()
+    fold = Fold(right_hbm, offset, right, sems)
+    left_copy.start()
+    height, levels, _ = start.shape
+    start_copy.wait()
+    basis = normalised(start[...])
+    basis_ref[...] = basis
+    vector_ref[...] = by_level(basis, height, levels)
+    width, _, _, right_width = mpo.shape
+    mpo_copy.wait()
+    terms = [mpo[:, s].astype(f32).reshape(width * levels, right_width).T for s in range(levels)]
     terms = jnp.concatenate(terms, axis=0).astype(bf16)
     terms = jnp.dot(reorder(right_width * levels, right_width, levels), terms, preferred_element_type=f32)
     terms = jnp.dot(terms.astype(bf16), reorder(width * levels, width, levels), preferred_element_type=f32)
     mpo_rows_ref[...] = terms.astype(bf16)
-    basis_ref[...] = normalised(start_ref[...])
-    vector = by_level(basis_ref[...], left_ref.shape[0], levels)
-    couple(left_ref, vector, mpo_rows_ref[...], coupled_ref, 32)
+    fold.finish(folded_ref)
+    left_copy.wait()
+
+
+def first_kernel(vector_ref, mpo_ref, left_ref, coupled_ref):
+    couple(left_ref, vector_ref[...], mpo_ref[...], coupled_ref, 32)
 
 
 def unfold_kernel(folded_ref, right_ref):
@@ -153,6 +173,12 @@
 
 def other(step):
     return partner(lax.axis_index("bond"), step, lax.axis_size("bond"))
+
+
+def first_image_kernel(step, groups, coupled_ref, folded_ref, *refs):
+    right_refs, image_ref = refs[:groups], refs[groups]
+    unfold_kernel(folded_ref, right_refs[-1])
+    image_ref[...] = block_image(other(step), coupled_ref, right_refs, image_ref.shape[0]).astype(bf16)
 
 
 def images_kernel(steps, groups, coupled_ref, *refs):
@@ -341,59 +367,78 @@
     segments = lax.axis_size("seg")
     pairs = [(source, (source - 1) % segments) for source in range(segments)]
 
-    def folded_part(k, more, grant):
-        folded, *brought = pl.pallas_call(
-            functools.partial(fold_kernel, k * part, len(more)),
-            out_shape=(on_chip(folded_shape, bf16),) + tuple(on_chip(x.shape, bf16) for x in more),
-            in_specs=[HBM_BLOCK] * (1 + len(more)),
-            out_specs=(VMEM_BLOCK,) * (1 + len(more)),
-            scratch_shapes=[pltpu.VMEM((height, part, height), bf16), DMA((4,)), DMA((max(1, len(more)),))],
-            compiler_params=params(grant),
+    right_scratch = [pltpu.VMEM((height, part, height), bf16), DMA((4,))]
+
+    def folded_part(k):
+        return pl.pallas_call(
+            functools.partial(fold_kernel, k * part),
+            out_shape=on_chip(folded_shape, bf16),
+            in_specs=[HBM_BLOCK],
+            out_specs=VMEM_BLOCK,
+            scratch_shapes=right_scratch,
+            compiler_params=params(62),
             name="fold",
-        )(right, *more)
-        return lax.ppermute(folded, "seg", pairs), brought
-
-    arriving = [folded_part(k, (), 62)[0] for k in range(groups - 1)]
-    folded, (start_near, mpo_near, left_near) = folded_part(groups - 1, (start, mpo, left), 60)
-    arriving.append(folded)
-    first_coupled, mpo_rows, basis = pl.pallas_call(
+        )(right)
+
+    arriving = [lax.ppermute(folded_part(k), "seg", pairs) for k in range(groups - 1)]
+    folded, basis, vector, mpo_rows, left_near = pl.pallas_call(
+        functools.partial(prepare_kernel, (groups - 1) * part),
+        out_shape=(
+            on_chip(folded_shape, bf16),
+            on_chip((rows, height), f32),
+            on_chip((height, rows), bf16),
+            on_chip((width * levels, levels * width), bf16),
+            on_chip(left.shape, bf16),
+        ),
+        in_specs=[HBM_BLOCK] * 4,
+        out_specs=(VMEM_BLOCK,) * 5,
+        scratch_shapes=right_scratch + [pltpu.VMEM(start.shape, bf16), pltpu.VMEM(mpo.shape, bf16), DMA((3,))],
+        compiler_params=params(60),
+        name="prepare",
+    )(right, start, mpo, left)
+    arriving.append(lax.ppermute(folded, "seg", pairs))
+    first_coupled = pl.pallas_call(
         first_kernel,
-        out_shape=(
-            on_chip((width, rows, height), bf16),
-            on_chip((width * levels, levels * width), bf16),
-            on_chip((rows, height), f32),
-        ),
+        out_shape=on_chip((width, rows, height), bf16),
         in_specs=[VMEM_BLOCK] * 3,
-        out_specs=(VMEM_BLOCK,) * 3,
+        out_specs=VMEM_BLOCK,
         compiler_params=params(12),
         cost_estimate=cost(2 * apply_flops, 8 << 20),
         name="first_coupled",
-    )(start_near, mpo_near, left_near)
+    )(vector, mpo_rows, left_near)
+    right_shape = on_chip((part * height, height), bf16)
     rights = [
         pl.pallas_call(
             unfold_kernel,
-            out_shape=on_chip((part * height, height), bf16),
+            out_shape=right_shape,
             in_specs=[VMEM_BLOCK],
             out_specs=VMEM_BLOCK,
             compiler_params=params(8),
             cost_estimate=cost(1 << 20, 1 << 20),
             name="unfold",
         )(folded)
-        for folded in arriving
+        for folded in arriving[:-1]
     ]
-
-    def images(steps, name):
-        return pl.pallas_call(
-            functools.partial(images_kernel, steps, groups),
-            out_shape=(on_chip((block, height), bf16),) * len(steps),
-            in_specs=[VMEM_BLOCK] * (1 + groups),
-            out_specs=(VMEM_BLOCK,) * len(steps),
-            compiler_params=params(8),
-            cost_estimate=cost(apply_flops * len(steps) // (2 * count), 8 << 20),
-            name=name,
-        )(first_coupled, *rights)
-
-    sends = tuple(images(steps[:1], "image_first")) + tuple(images(steps[1:], "image_rest"))
+    last_right, sending = pl.pallas_call(
+        functools.partial(first_image_kernel, steps[0], groups),
+        out_shape=(right_shape, on_chip((block, height), bf16)),
+        in_specs=[VMEM_BLOCK] * (1 + groups),
+        out_specs=(VMEM_BLOCK,) * 2,
+        compiler_params=params(8),
+        cost_estimate=cost(apply_flops // (2 * count), 8 << 20),
+        name="image_first",
+    )(first_coupled, arriving[-1], *rights)
+    rights.append(last_right)
+    others = pl.pallas_call(
+        functools.partial(images_kernel, steps[1:], groups),
+        out_shape=[on_chip((block, height), bf16)] * (count - 2),
+        in_specs=[VMEM_BLOCK] * (1 + groups),
+        out_specs=[VMEM_BLOCK] * (count - 2),
+        compiler_params=params(8),
+        cost_estimate=cost(apply_flops * (count - 2) // (2 * count), 8 << 20),
+        name="image_rest",
+    )(first_coupled, *rights)
+    sends = [sending, *others]
     arrived = [exchanged(value, step) for value, step in zip(sends, steps)]
     grown_shape = (height, width, height)
     one = pl.pallas_call(

time: 50.4 us -> 50.4 us (level)
    pallas_call x7 -> x6, Pallas kernels: 10.6 us -> 10.6 us  [the longest x1 4.58 us: body(): pl.pallas_call(first_kernel, out_shape=on_chip((width, rows, height), bf1...]
where the time goes in v8:
time: 50.4 us; the launch traced here: 50.2 us
  Pallas kernels  25 us (50%)
  starting transfers between devices  17.5 us (35%)
  waiting for transfers between devices  6.86 us (14%)
  between operations  0.9 us (2%)
    ppermute x9, starting transfers between devices, exchanged(): lax.ppermute(value, 'bond', [(source, int(partner(source, step, count)))...  13.4 us
    pallas_call x1, Pallas kernels, body(): pl.pallas_call(functools.partial(second_kernel, with_own, groups), out_sh...  7.64 us
    ppermute x9, waiting for transfers between devices, exchanged(): lax.ppermute(value, 'bond', [(source, int(partner(source, step, count)))...  6.85 us
    pallas_call x1, Pallas kernels, body(): pl.pallas_call(first_kernel, out_shape=on_chip((width, rows, height), bf1...  4.58 us
    ppermute x1, starting transfers between devices, body(): lax.ppermute(folded_part(k), 'seg', pairs)  3.39 us
    pallas_call x1, Pallas kernels, body(): pl.pallas_call(grow_second_kernel, out_shape=(on_chip(grown_shape, f32),)...  2.94 us
    pallas_call x1, Pallas kernels, body(): pl.pallas_call(functools.partial(prepare_kernel, (groups - 1) * part), ou...  2.23 us
    pallas_call x1, Pallas kernels, body(): pl.pallas_call(grow_first_kernel, out_shape=on_chip(grown_shape, f32), in...  1.58 us
  transfers between devices with their start and end apart: 11, of which 5 were waited for; matrix products, arithmetic and copies ran while one was open for 0% of the time, Pallas kernels for 27%

profile of v8, /device:TPU:0, one launch (start us, length us, event | category | flops | bytes accessed | tf_op | source)
XLA Modules:
  0.0 50.2 jit_solution(1569545294429797022)
XLA Ops:
  0.6 1.2 %fold.1 = bf16[65,16,128]{2,1,0:T(8,128)(2,1)S(1)} custom-call(bf16[128,32,128]{2,1,0:T(8,128)(2,1)} %bitcast.11), custom_call_target="tpu_custom_call" | custom-call | tf_op jit(solution)/shard_map/fold/pallas_call | solution.py:373
  1.9 3.4 %collective-permute-start.1 = (bf16[65,16,128]{2,1,0:T(8,128)(2,1)S(1)}, bf16[65,16,128]{2,1,0:T(8,128)(2,1)S(1)}, u32[]{:S(2)}, u32[]{:S(2)}) collective-permute-start(bf16[65,16,128]{2,1,0:T(8,128)(2,1)S(1)} %fold.1), channel_id=1, source_target_pairs={{0,28},{4,0},{8,4},{12,8},{16,12},{20,16},{24,20},{28,24},{1,29},{... | collective-permute-start | bytes 798728 | tf_op jit(solution)/shard_map/ppermute | solution.py:383
  5.3 2.2 %prepare.1 = (bf16[65,16,128]{2,1,0:T(8,128)(2,1)S(1)}, f32[1024,128]{1,0:T(8,128)S(1)}, bf16[128,1024]{1,0:T(8,128)(2,1)S(1)}, bf16[256,256]{1,0:T(8,128)(2,1)S(1)}, bf16[128,32,128]{2,1,0:T(8,128)(2,1)S(1)}) custom-call(bf16[128,32,128]{2,1,0:T(8,128)(2,1)} %bitcast.12, bf16[128,8,128]{2,1,0:T(8,128)(2,1)} %bitcast.15, bf16[32,8,8,32]{3,2,1,0:T(8,128)(2,1)} %bitcast.14, ...), custom_call_target="tpu_custom_call" | custom-call | tf_op jit(solution)/shard_map/prepare/pallas_call | solution.py:384
  7.5 0.7 %collective-permute-start = (bf16[65,16,128]{2,1,0:T(8,128)(2,1)S(1)}, bf16[65,16,128]{2,1,0:T(8,128)(2,1)S(1)}, u32[]{:S(2)}, u32[]{:S(2)}) collective-permute-start(bf16[65,16,128]{2,1,0:T(8,128)(2,1)S(1)} %get-tuple-element.29), channel_id=1, source_target_pairs={{0,28},{4,0},{8,4},{12,8},{16,12},{20,16},{24,20},{28,24},{1,29},{... | collective-permute-start | bytes 798728 | tf_op jit(solution)/shard_map/ppermute | solution.py:399
  8.2 4.6 %first_coupled.1.coupled_ref = bf16[32,1024,128]{2,1,0:T(8,128)(2,1)S(1)} custom-call(bf16[128,1024]{1,0:T(8,128)(2,1)S(1)} %get-tuple-element.26.vector_ref, bf16[256,256]{1,0:T(8,128)(2,1)S(1)} %get-tuple-element.27.mpo_ref.refs_8_, bf16[128,32,128]{2,1,0:T(8,128)(2,1)S(1)} %get-tuple-element.28.left_ref.refs_7_), custom_call_target="tpu_custom_call" | custom-call | flops 4294967296 | bytes 8388608 | tf_op jit(solution)/shard_map/first_coupled/pallas_call | solution.py:400
  12.8 0.0 collective-permute-done.1.folded_ref
  12.8 0.4 unfold.1.refs_0_.refs_4_
  13.2 0.0 collective-permute-done.folded_ref
  13.2 1.0 %image_first.1 = (bf16[2048,128]{1,0:T(8,128)(2,1)S(1)}, bf16[256,128]{1,0:T(8,128)(2,1)S(1)}) custom-call(bf16[32,1024,128]{2,1,0:T(8,128)(2,1)S(1)} %first_coupled.1.coupled_ref, bf16[65,16,128]{2,1,0:T(8,128)(2,1)S(1)} %collective-permute-done.folded_ref, bf16[2048,128]{1,0:T(8,128)(2,1)S(1)} %unfold.1.refs_0_.refs_4_), custom_call_target="tpu_custom_call" | custom-call | flops 268435456 | bytes 8388608 | tf_op jit(solution)/shard_map/image_first/pallas_call | solution.py:422
  14.2 3.7 %collective-permute-start.2 = (bf16[256,128]{1,0:T(8,128)(2,1)S(1)}, bf16[256,128]{1,0:T(8,128)(2,1)S(1)}, u32[]{:S(2)}, u32[]{:S(2)}) collective-permute-start(bf16[256,128]{1,0:T(8,128)(2,1)S(1)} %get-tuple-element.30), channel_id=1, source_target_pairs={{0,3},{1,2},{2,1},{3,0},{4,7},{5,6},{6,5},{7,4},{8,11},{9,10},{10,... | collective-permute-start | bytes 196616 | tf_op jit(solution)/shard_map/ppermute | solution.py:349
  17.9 1.2 %image_rest.1 = (bf16[256,128]{1,0:T(8,128)(2,1)S(1)}, bf16[256,128]{1,0:T(8,128)(2,1)S(1)}) custom-call(bf16[32,1024,128]{2,1,0:T(8,128)(2,1)S(1)} %first_coupled.1.coupled_ref, bf16[2048,128]{1,0:T(8,128)(2,1)S(1)} %unfold.1.refs_0_.refs_4_, bf16[2048,128]{1,0:T(8,128)(2,1)S(1)} %get-tuple-element.31.refs_1_.refs_5_), custom_call_target="tpu_custom_call" | custom-call | flops 536870912 | bytes 8388608 | tf_op jit(solution)/shard_map/image_rest/pallas_call | solution.py:432
  19.1 0.1 collective-permute-start.3
  19.2 0.8 %collective-permute-start.4 = (bf16[256,128]{1,0:T(8,128)(2,1)S(1)}, bf16[256,128]{1,0:T(8,128)(2,1)S(1)}, u32[]{:S(2)}, u32[]{:S(2)}) collective-permute-start(bf16[256,128]{1,0:T(8,128)(2,1)S(1)} %get-tuple-element.33), channel_id=1, source_target_pairs={{0,1},{1,0},{2,3},{3,2},{4,5},{5,4},{6,7},{7,6},{8,9},{9,8},{10,11... | collective-permute-start | bytes 196616 | tf_op jit(solution)/shard_map/ppermute | solution.py:349
  20.0 0.4 collective-permute-done.2.arrived_ref
  20.4 0.7 %image_own.1.own_ref = f32[256,128]{1,0:T(8,128)S(1)} custom-call(bf16[256,128]{1,0:T(8,128)(2,1)S(1)} %collective-permute-done.2.arrived_ref, bf16[32,1024,128]{2,1,0:T(8,128)(2,1)S(1)} %first_coupled.1.coupled_ref, bf16[2048,128]{1,0:T(8,128)(2,1)S(1)} %unfold.1.refs_0_.refs_4_, bf16[2048,128]{1,0:T(8,128)(2,1)S(1)} %get-tuple-element.31.refs_1_.refs_5_), custom_call_target="tpu_custom_call" | custom-call | flops 268435456 | bytes 8388608 | tf_op jit(solution)/shard_map/image_own/pallas_call | solution.py:454
  21.1 3.3 %collective-permute-done.3.refs_0_ = bf16[256,128]{1,0:T(8,128)(2,1)S(1)} collective-permute-done((bf16[256,128]{1,0:T(8,128)(2,1)S(1)}, bf16[256,128]{1,0:T(8,128)(2,1)S(1)}, u32[]{:S(2)}, u32[]{:S(2)}) %collective-permute-start.3) | collective-permute-done | bytes 65568 | tf_op jit(solution)/shard_map/ppermute | solution.py:349
  24.4 0.0 collective-permute-done.4.refs_1_
  24.5 0.6 %collective-permute-start.7 = (bf16[256,128]{1,0:T(8,128)(2,1)S(1)}, bf16[256,128]{1,0:T(8,128)(2,1)S(1)}, u32[]{:S(2)}, u32[]{:S(2)}) collective-permute-start(bf16[256,128]{1,0:T(8,128)(2,1)S(1)} %sum.1.refs_3_), channel_id=1, source_target_pairs={{0,1},{1,0},{2,3},{3,2},{4,5},{5,4},{6,7},{7,6},{8,9},{9,8},{10,11... | collective-permute-start | bytes 196616 | tf_op jit(solution)/shard_map/ppermute | solution.py:349
  25.0 2.2 %collective-permute-start.6 = (bf16[256,128]{1,0:T(8,128)(2,1)S(1)}, bf16[256,128]{1,0:T(8,128)(2,1)S(1)}, u32[]{:S(2)}, u32[]{:S(2)}) collective-permute-start(bf16[256,128]{1,0:T(8,128)(2,1)S(1)} %sum.1.refs_3_), channel_id=1, source_target_pairs={{0,2},{1,3},{2,0},{3,1},{4,6},{5,7},{6,4},{7,5},{8,10},{9,11},{10,... | collective-permute-start | bytes 196616 | tf_op jit(solution)/shard_map/ppermute | solution.py:349
  27.2 1.7 %collective-permute-start.5 = (bf16[256,128]{1,0:T(8,128)(2,1)S(1)}, bf16[256,128]{1,0:T(8,128)(2,1)S(1)}, u32[]{:S(2)}, u32[]{:S(2)}) collective-permute-start(bf16[256,128]{1,0:T(8,128)(2,1)S(1)} %sum.1.refs_3_), channel_id=1, source_target_pairs={{0,3},{1,2},{2,1},{3,0},{4,7},{5,6},{6,5},{7,4},{8,11},{9,10},{10,... | collective-permute-start | bytes 196616 | tf_op jit(solution)/shard_map/ppermute | solution.py:349
  28.9 1.6 %grow_first.1.refs_7_ = f32[128,32,128]{2,1,0:T(8,128)S(1)} custom-call(f32[1024,128]{1,0:T(8,128)S(1)} %get-tuple-element.34.refs_6_.basis_ref.refs_5_, bf16[32,1024,128]{2,1,0:T(8,128)(2,1)S(1)} %first_coupled.1.coupled_ref), custom_call_target="tpu_custom_call" | custom-call | flops 2147483648 | bytes 8388608 | tf_op jit(solution)/shard_map/grow_first/pallas_call | solution.py:444
  30.5 0.0 collective-permute-done.7.refs_2_
  30.5 1.4 %collective-permute-done.6.refs_1_ = bf16[256,128]{1,0:T(8,128)(2,1)S(1)} collective-permute-done((bf16[256,128]{1,0:T(8,128)(2,1)S(1)}, bf16[256,128]{1,0:T(8,128)(2,1)S(1)}, u32[]{:S(2)}, u32[]{:S(2)}) %collective-permute-start.6) | collective-permute-done | bytes 65568 | tf_op jit(solution)/shard_map/ppermute | solution.py:349
  31.9 1.4 %collective-permute-done.5.refs_0_ = bf16[256,128]{1,0:T(8,128)(2,1)S(1)} collective-permute-done((bf16[256,128]{1,0:T(8,128)(2,1)S(1)}, bf16[256,128]{1,0:T(8,128)(2,1)S(1)}, u32[]{:S(2)}, u32[]{:S(2)}) %collective-permute-start.5) | collective-permute-done | bytes 65568 | tf_op jit(solution)/shard_map/ppermute | solution.py:349
  33.3 7.6 %second_image.1 = (bf16[32,1024,128]{2,1,0:T(8,128)(2,1)S(1)}, f32[1024,128]{1,0:T(8,128)S(1)}, f32[8,128]{1,0:T(8,128)S(1)}, bf16[272,128]{1,0:T(8,128)(2,1)S(1...) custom-call(bf16[256,128]{1,0:T(8,128)(2,1)S(1)} %collective-permute-done.5.refs_0_, ...), custom_call_target="tpu_custom_call" | custom-call | tf_op jit(solution)/shard_map/second_image/pallas_call | solution.py:472
  41.0 1.7 %collective-permute-start.8 = (bf16[272,128]{1,0:T(8,128)(2,1)S(1)}, bf16[272,128]{1,0:T(8,128)(2,1)S(1)}, u32[]{:S(2)}, u32[]{:S(2)}) collective-permute-start(bf16[272,128]{1,0:T(8,128)(2,1)S(1)} %get-tuple-element.35), channel_id=1, source_target_pairs={{0,3},{1,2},{2,1},{3,0},{4,7},{5,6},{6,5},{7,4},{8,11},{9,10},{10,... | collective-permute-start | bytes 208904 | tf_op jit(solution)/shard_map/ppermute | solution.py:349
  42.7 2.6 %collective-permute-start.10 = (bf16[272,128]{1,0:T(8,128)(2,1)S(1)}, bf16[272,128]{1,0:T(8,128)(2,1)S(1)}, u32[]{:S(2)}, u32[]{:S(2)}) collective-permute-start(bf16[272,128]{1,0:T(8,128)(2,1)S(1)} %get-tuple-element.37), channel_id=1, source_target_pairs={{0,1},{1,0},{2,3},{3,2},{4,5},{5,4},{6,7},{7,6},{8,9},{9,8},{10,11... | collective-permute-start | bytes 208904 | tf_op jit(solution)/shard_map/ppermute | solution.py:349
  45.4 2.9 %grow_second.1 = (f32[128,32,128]{2,1,0:T(8,128)S(1)}, f32[128,32,128]{2,1,0:T(8,128)S(1)}) custom-call(f32[1024,128]{1,0:T(8,128)S(1)} %get-tuple-element.34.refs_6_.basis_ref.refs_5_, f32[1024,128]{1,0:T(8,128)S(1)} %get-tuple-element.40.second_ref.refs_6_, bf16[32,1024,128]{2,1,0:T(8,128)(2,1)S(1)} %get-tuple-element.41.coupled_ref), custom_call_target="tpu_custom_call" | custom-call | flops 4294967296 | bytes 16777216 | tf_op jit(solution)/shard_map/grow_second/pallas_call | solution.py:488
  48.3 0.0 collective-permute-done.8.refs_0_
  48.3 0.2 collective-permute-done.9.refs_1_
  48.6 0.0 collective-permute-done.10.refs_2_
  48.6 1.5 %last.1 = (bf16[128,8,128]{2,1,0:T(8,128)(2,1)}, bf16[128,32,128]{2,1,0:T(8,128)(2,1)}, f32[1,128]{1,0:T(1,128)}, f32[32,8,128]{2,1,0:T(8,128)}) custom-call(bf16[272,128]{1,0:T(8,128)(2,1)S(1)} %collective-permute-done.8.refs_0_, bf16[272,128]{1,0:T(8,128)(2,1)S(1)} %collective-permute-done.9.refs_1_, bf16[272,128]{1,0:T(8,128)(2,1)S(1)} %collective-permute-done.10.refs_2_, ...), custom_call_target="tpu_custom_call" | custom-call | tf_op jit(solution)/shard_map/last/pallas_call | solution.py:504
  (2 shorter events, 0.0 us)
Async XLA Ops:
  1.9 10.9 %collective-permute-start.1 = (bf16[65,16,128]{2,1,0:T(8,128)(2,1)S(1)}, bf16[65,16,128]{2,1,0:T(8,128)(2,1)S(1)}, u32[]{:S(2)}, u32[]{:S(2)}) collective-permute-start(bf16[65,16,128]{2,1,0:T(8,128)(2,1)S(1)} %fold.1), channel_id=1, source_target_pairs={{0,28},{4,0},{8,4},{12,8},{16,12},{20,16},{24,20},{28,24},{1,29},{... | collective-permute-start | bytes 798728 | tf_op jit(solution)/shard_map/ppermute | solution.py:383
  7.5 5.7 %collective-permute-start = (bf16[65,16,128]{2,1,0:T(8,128)(2,1)S(1)}, bf16[65,16,128]{2,1,0:T(8,128)(2,1)S(1)}, u32[]{:S(2)}, u32[]{:S(2)}) collective-permute-start(bf16[65,16,128]{2,1,0:T(8,128)(2,1)S(1)} %get-tuple-element.29), channel_id=1, source_target_pairs={{0,28},{4,0},{8,4},{12,8},{16,12},{20,16},{24,20},{28,24},{1,29},{... | collective-permute-start | bytes 798728 | tf_op jit(solution)/shard_map/ppermute | solution.py:399
  14.2 6.2 %collective-permute-start.2 = (bf16[256,128]{1,0:T(8,128)(2,1)S(1)}, bf16[256,128]{1,0:T(8,128)(2,1)S(1)}, u32[]{:S(2)}, u32[]{:S(2)}) collective-permute-start(bf16[256,128]{1,0:T(8,128)(2,1)S(1)} %get-tuple-element.30), channel_id=1, source_target_pairs={{0,3},{1,2},{2,1},{3,0},{4,7},{5,6},{6,5},{7,4},{8,11},{9,10},{10,... | collective-permute-start | bytes 196616 | tf_op jit(solution)/shard_map/ppermute | solution.py:349
  19.1 5.3 %collective-permute-start.3 = (bf16[256,128]{1,0:T(8,128)(2,1)S(1)}, bf16[256,128]{1,0:T(8,128)(2,1)S(1)}, u32[]{:S(2)}, u32[]{:S(2)}) collective-permute-start(bf16[256,128]{1,0:T(8,128)(2,1)S(1)} %get-tuple-element.32), channel_id=1, source_target_pairs={{0,2},{1,3},{2,0},{3,1},{4,6},{5,7},{6,4},{7,5},{8,10},{9,11},{10,... | collective-permute-start | bytes 196616 | tf_op jit(solution)/shard_map/ppermute | solution.py:349
  19.2 5.2 %collective-permute-start.4 = (bf16[256,128]{1,0:T(8,128)(2,1)S(1)}, bf16[256,128]{1,0:T(8,128)(2,1)S(1)}, u32[]{:S(2)}, u32[]{:S(2)}) collective-permute-start(bf16[256,128]{1,0:T(8,128)(2,1)S(1)} %get-tuple-element.33), channel_id=1, source_target_pairs={{0,1},{1,0},{2,3},{3,2},{4,5},{5,4},{6,7},{7,6},{8,9},{9,8},{10,11... | collective-permute-start | bytes 196616 | tf_op jit(solution)/shard_map/ppermute | solution.py:349
  24.5 6.0 %collective-permute-start.7 = (bf16[256,128]{1,0:T(8,128)(2,1)S(1)}, bf16[256,128]{1,0:T(8,128)(2,1)S(1)}, u32[]{:S(2)}, u32[]{:S(2)}) collective-permute-start(bf16[256,128]{1,0:T(8,128)(2,1)S(1)} %sum.1.refs_3_), channel_id=1, source_target_pairs={{0,1},{1,0},{2,3},{3,2},{4,5},{5,4},{6,7},{7,6},{8,9},{9,8},{10,11... | collective-permute-start | bytes 196616 | tf_op jit(solution)/shard_map/ppermute | solution.py:349
  25.0 6.9 %collective-permute-start.6 = (bf16[256,128]{1,0:T(8,128)(2,1)S(1)}, bf16[256,128]{1,0:T(8,128)(2,1)S(1)}, u32[]{:S(2)}, u32[]{:S(2)}) collective-permute-start(bf16[256,128]{1,0:T(8,128)(2,1)S(1)} %sum.1.refs_3_), channel_id=1, source_target_pairs={{0,2},{1,3},{2,0},{3,1},{4,6},{5,7},{6,4},{7,5},{8,10},{9,11},{10,... | collective-permute-start | bytes 196616 | tf_op jit(solution)/shard_map/ppermute | solution.py:349
  27.2 6.1 %collective-permute-start.5 = (bf16[256,128]{1,0:T(8,128)(2,1)S(1)}, bf16[256,128]{1,0:T(8,128)(2,1)S(1)}, u32[]{:S(2)}, u32[]{:S(2)}) collective-permute-start(bf16[256,128]{1,0:T(8,128)(2,1)S(1)} %sum.1.refs_3_), channel_id=1, source_target_pairs={{0,3},{1,2},{2,1},{3,0},{4,7},{5,6},{6,5},{7,4},{8,11},{9,10},{10,... | collective-permute-start | bytes 196616 | tf_op jit(solution)/shard_map/ppermute | solution.py:349
  41.0 7.3 %collective-permute-start.8 = (bf16[272,128]{1,0:T(8,128)(2,1)S(1)}, bf16[272,128]{1,0:T(8,128)(2,1)S(1)}, u32[]{:S(2)}, u32[]{:S(2)}) collective-permute-start(bf16[272,128]{1,0:T(8,128)(2,1)S(1)} %get-tuple-element.35), channel_id=1, source_target_pairs={{0,3},{1,2},{2,1},{3,0},{4,7},{5,6},{6,5},{7,4},{8,11},{9,10},{10,... | collective-permute-start | bytes 208904 | tf_op jit(solution)/shard_map/ppermute | solution.py:349
  42.7 5.9 %collective-permute-start.9 = (bf16[272,128]{1,0:T(8,128)(2,1)S(1)}, bf16[272,128]{1,0:T(8,128)(2,1)S(1)}, u32[]{:S(2)}, u32[]{:S(2)}) collective-permute-start(bf16[272,128]{1,0:T(8,128)(2,1)S(1)} %get-tuple-element.36), channel_id=1, source_target_pairs={{0,2},{1,3},{2,0},{3,1},{4,6},{5,7},{6,4},{7,5},{8,10},{9,11},{10,... | collective-permute-start | bytes 208904 | tf_op jit(solution)/shard_map/ppermute | solution.py:349
  42.7 5.9 %collective-permute-start.10 = (bf16[272,128]{1,0:T(8,128)(2,1)S(1)}, bf16[272,128]{1,0:T(8,128)(2,1)S(1)}, u32[]{:S(2)}, u32[]{:S(2)}) collective-permute-start(bf16[272,128]{1,0:T(8,128)(2,1)S(1)} %get-tuple-element.37), channel_id=1, source_target_pairs={{0,1},{1,0},{2,3},{3,2},{4,5},{5,4},{6,7},{7,6},{8,9},{9,8},{10,11... | collective-permute-start | bytes 208904 | tf_op jit(solution)/shard_map/ppermute | solution.py:349

commit v9 on v7

--- a/solution.py
+++ b/solution.py
@@ -64,23 +64,19 @@
             coupled_ref[:, place : place + 2 * levels, :] = jnp.concatenate(halves, axis=1).astype(bf16)
 
 
-def fold_kernel(offset, more, right_hbm, *refs):
-    sources, folded_ref, targets = refs[:more], refs[more], refs[more + 1 : 2 * more + 1]
-    right, sems, more_sems = refs[2 * more + 1 :]
+def fold_kernel(right_hbm, *refs):
+    folded_refs, (token_ref, right, sems) = refs[:-3], refs[-3:]
     height, width, _ = right.shape
+    part = width // len(folded_refs)
     half = height // 2
     pieces = sems.shape[0] // 2
     size = half // pieces
-    columns = pl.ds(offset, width)
     copies = []
     for k in range(pieces):
         for first in (k * size, half + k * size):
             rows = pl.ds(first, size)
-            copies.append(pltpu.make_async_copy(right_hbm.at[rows, columns], right.at[rows], sems.at[len(copies)]))
+            copies.append(pltpu.make_async_copy(right_hbm.at[rows], right.at[rows], sems.at[len(copies)]))
             copies[-1].start()
-    others = [pltpu.make_async_copy(*pair, more_sems.at[k]) for k, pair in enumerate(zip(sources, targets))]
-    for copy in others:
-        copy.start()
     diagonal = jnp.zeros((width, height), f32)
     for k in range(pieces):
         copies[2 * k].wait()
@@ -88,13 +84,14 @@
         lower = right[half + k * size : half + (k + 1) * size].astype(f32)
         row = lax.broadcasted_iota(jnp.int32, lower.shape, 0) + k * size
         lane = lax.broadcasted_iota(jnp.int32, lower.shape, 2)
-        turned = pltpu.roll(lower, half, 2)
         upper = right[k * size : (k + 1) * size].astype(f32)
-        folded_ref[k * size : (k + 1) * size] = jnp.where(lane >= row, upper, turned).astype(bf16)
+        folded = jnp.where(lane >= row, upper, pltpu.roll(lower, half, 2))
+        for g, folded_ref in enumerate(folded_refs):
+            folded_ref[k * size : (k + 1) * size] = folded[:, g * part : (g + 1) * part].astype(bf16)
         diagonal = diagonal + jnp.sum(jnp.where(lane == row + half, lower, 0.0), axis=0)
-    folded_ref[half] = diagonal.astype(bf16)
-    for copy in others:
-        copy.wait()
+    for g, folded_ref in enumerate(folded_refs):
+        folded_ref[half] = diagonal[g * part : (g + 1) * part].astype(bf16)
+    token_ref[...] = jnp.zeros_like(token_ref)
 
 
 def reorder(size, first, second):
@@ -103,16 +100,31 @@
     return jnp.where((row // second == lane % first) & (row % second == lane // first), 1.0, 0.0).astype(bf16)
 
 
-def first_kernel(start_ref, mpo_ref, left_ref, coupled_ref, mpo_rows_ref, basis_ref):
-    width, levels, _, right_width = mpo_ref.shape
-    terms = [mpo_ref[:, s].astype(f32).reshape(width * levels, right_width).T for s in range(levels)]
+def prepare_kernel(after_ref, start_hbm, mpo_hbm, left_hbm, *refs):
+    del after_ref
+    basis_ref, vector_ref, mpo_rows_ref, left_ref, start, mpo, sems = refs
+    start_copy = pltpu.make_async_copy(start_hbm, start, sems.at[0])
+    mpo_copy = pltpu.make_async_copy(mpo_hbm, mpo, sems.at[1])
+    left_copy = pltpu.make_async_copy(left_hbm, left_ref, sems.at[2])
+    for copy in (start_copy, mpo_copy, left_copy):
+        copy.start()
+    height, levels, _ = start.shape
+    start_copy.wait()
+    basis = normalised(start[...])
+    basis_ref[...] = basis
+    vector_ref[...] = by_level(basis, height, levels)
+    width, _, _, right_width = mpo.shape
+    mpo_copy.wait()
+    terms = [mpo[:, s].astype(f32).reshape(width * levels, right_width).T for s in range(levels)]
     terms = jnp.concatenate(terms, axis=0).astype(bf16)
     terms = jnp.dot(reorder(right_width * levels, right_width, levels), terms, preferred_element_type=f32)
     terms = jnp.dot(terms.astype(bf16), reorder(width * levels, width, levels), preferred_element_type=f32)
     mpo_rows_ref[...] = terms.astype(bf16)
-    basis_ref[...] = normalised(start_ref[...])
-    vector = by_level(basis_ref[...], left_ref.shape[0], levels)
-    couple(left_ref, vector, mpo_rows_ref[...], coupled_ref, 32)
+    left_copy.wait()
+
+
+def first_kernel(vector_ref, mpo_ref, left_ref, coupled_ref):
+    couple(left_ref, vector_ref[...], mpo_ref[...], coupled_ref, 32)
 
 
 def unfold_kernel(folded_ref, right_ref):
@@ -135,15 +147,18 @@
             right_ref[u * height + half : (u + 1) * height, :] = lower.astype(bf16)
 
 
+def part_image(where, coupled_ref, right_ref, first, block):
+    place = pl.ds(pl.multiple_of(where * block, block), block)
+    last = first + right_ref.shape[0] // coupled_ref.shape[2]
+    terms = jnp.concatenate([coupled_ref[u, place, :] for u in range(first, last)], axis=1)
+    return jnp.dot(terms, right_ref[...], preferred_element_type=f32)
+
+
 def block_image(where, coupled_ref, right_refs, block):
-    height = coupled_ref.shape[2]
-    place = pl.ds(pl.multiple_of(where * block, block), block)
     total, first = 0.0, 0
     for right_ref in right_refs:
-        last = first + right_ref.shape[0] // height
-        terms = jnp.concatenate([coupled_ref[u, place, :] for u in range(first, last)], axis=1)
-        total = total + jnp.dot(terms, right_ref[...], preferred_element_type=f32)
-        first = last
+        total = total + part_image(where, coupled_ref, right_ref, first, block)
+        first += right_ref.shape[0] // coupled_ref.shape[2]
     return total
 
 
@@ -155,9 +170,14 @@
     return partner(lax.axis_index("bond"), step, lax.axis_size("bond"))
 
 
-def images_kernel(steps, groups, coupled_ref, *refs):
-    for step, image_ref in zip(steps, refs[groups:]):
-        image_ref[...] = block_image(other(step), coupled_ref, refs[:groups], image_ref.shape[0]).astype(bf16)
+def unfold_image_kernel(steps, first, more, folded_ref, coupled_ref, *refs):
+    right_ref, image_refs = refs[more], refs[more + 1 :]
+    unfold_kernel(folded_ref, right_ref)
+    for k, (step, image_ref) in enumerate(zip(steps, image_refs)):
+        total = part_image(other(step), coupled_ref, right_ref, first, image_ref.shape[0])
+        if more:
+            total = total + refs[k][...]
+        image_ref[...] = total.astype(image_ref.dtype)
 
 
 def own_image_kernel(groups, arrived_ref, coupled_ref, *refs):
@@ -337,64 +357,55 @@
     mpo = jnp.transpose(mpo, (0, 2, 3, 1))
     groups = max(1, width // 16)
     part = width // groups
-    folded_shape = (height // 2 + 1, part, height)
     segments = lax.axis_size("seg")
     pairs = [(source, (source - 1) % segments) for source in range(segments)]
-
-    def folded_part(k, more, grant):
-        folded, *brought = pl.pallas_call(
-            functools.partial(fold_kernel, k * part, len(more)),
-            out_shape=(on_chip(folded_shape, bf16),) + tuple(on_chip(x.shape, bf16) for x in more),
-            in_specs=[HBM_BLOCK] * (1 + len(more)),
-            out_specs=(VMEM_BLOCK,) * (1 + len(more)),
-            scratch_shapes=[pltpu.VMEM((height, part, height), bf16), DMA((4,)), DMA((max(1, len(more)),))],
-            compiler_params=params(grant),
-            name="fold",
-        )(right, *more)
-        return lax.ppermute(folded, "seg", pairs), brought
-
-    arriving = [folded_part(k, (), 62)[0] for k in range(groups - 1)]
-    folded, (start_near, mpo_near, left_near) = folded_part(groups - 1, (start, mpo, left), 60)
-    arriving.append(folded)
-    first_coupled, mpo_rows, basis = pl.pallas_call(
+    *folded, token = pl.pallas_call(
+        fold_kernel,
+        out_shape=[on_chip((height // 2 + 1, part, height), bf16)] * groups + [on_chip((8, height), f32)],
+        in_specs=[HBM_BLOCK],
+        out_specs=[VMEM_BLOCK] * (groups + 1),
+        scratch_shapes=[pltpu.VMEM(right.shape, bf16), DMA((8,))],
+        compiler_params=params(61),
+        name="fold",
+    )(right)
+    arriving = [lax.ppermute(value, "seg", pairs) for value in folded]
+    basis, vector, mpo_rows, left_near = pl.pallas_call(
+        prepare_kernel,
+        out_shape=(
+            on_chip((rows, height), f32),
+            on_chip((height, rows), bf16),
+            on_chip((width * levels, levels * width), bf16),
+            on_chip(left.shape, bf16),
+        ),
+        in_specs=[VMEM_BLOCK] + [HBM_BLOCK] * 3,
+        out_specs=(VMEM_BLOCK,) * 4,
+        scratch_shapes=[pltpu.VMEM(start.shape, bf16), pltpu.VMEM(mpo.shape, bf16), DMA((3,))],
+        compiler_params=params(58),
+        name="prepare",
+    )(token, start, mpo, left)
+    first_coupled = pl.pallas_call(
         first_kernel,
-        out_shape=(
-            on_chip((width, rows, height), bf16),
-            on_chip((width * levels, levels * width), bf16),
-            on_chip((rows, height), f32),
-        ),
+        out_shape=on_chip((width, rows, height), bf16),
         in_specs=[VMEM_BLOCK] * 3,
-        out_specs=(VMEM_BLOCK,) * 3,
+        out_specs=VMEM_BLOCK,
         compiler_params=params(12),
         cost_estimate=cost(2 * apply_flops, 8 << 20),
         name="first_coupled",
-    )(start_near, mpo_near, left_near)
-    rights = [
-        pl.pallas_call(
-            unfold_kernel,
-            out_shape=on_chip((part * height, height), bf16),
-            in_specs=[VMEM_BLOCK],
-            out_specs=VMEM_BLOCK,
+    )(vector, mpo_rows, left_near)
+    rights, images = [], []
+    for k, value in enumerate(arriving):
+        kind = bf16 if k == groups - 1 else f32
+        unfolded, *images = pl.pallas_call(
+            functools.partial(unfold_image_kernel, steps, k * part, len(images)),
+            out_shape=[on_chip((part * height, height), bf16)] + [on_chip((block, height), kind)] * len(steps),
+            in_specs=[VMEM_BLOCK] * (2 + len(images)),
+            out_specs=[VMEM_BLOCK] * (1 + len(steps)),
             compiler_params=params(8),
-            cost_estimate=cost(1 << 20, 1 << 20),
-            name="unfold",
-        )(folded)
-        for folded in arriving
-    ]
-
-    def images(steps, name):
-        return pl.pallas_call(
-            functools.partial(images_kernel, steps, groups),
-            out_shape=(on_chip((block, height), bf16),) * len(steps),
-            in_specs=[VMEM_BLOCK] * (1 + groups),
-            out_specs=(VMEM_BLOCK,) * len(steps),
-            compiler_params=params(8),
-            cost_estimate=cost(apply_flops * len(steps) // (2 * count), 8 << 20),
-            name=name,
-        )(first_coupled, *rights)
-
-    sends = tuple(images(steps[:1], "image_first")) + tuple(images(steps[1:], "image_rest"))
-    arrived = [exchanged(value, step) for value, step in zip(sends, steps)]
+            cost_estimate=cost(apply_flops * len(steps) // (2 * count * groups), 4 << 20),
+            name="unfold_image",
+        )(value, first_coupled, *images)
+        rights.append(unfolded)
+    arrived = [exchanged(value, step) for value, step in zip(images, steps)]
     grown_shape = (height, width, height)
     one = pl.pallas_call(
         grow_first_kernel,

time: 50.4 us -> 51.8 us (1.028)
  waiting for transfers between devices: 6.86 us -> 7.73 us
  Pallas kernels: 25 us -> 25.6 us
    ppermute x9, waiting for transfers between devices: 6.86 us -> 7.72 us  [exchanged(): lax.ppermute(value, 'bond', [(source, int(partner(source, step, count)))...]
    pallas_call x7 -> x5, Pallas kernels: 10.6 us -> 11.2 us  [the longest x1 4.61 us: body(): pl.pallas_call(first_kernel, out_shape=on_chip((width, rows, height), bf1...]
where the time goes in v9:
time: 51.8 us; the launch traced here: 51.6 us
  Pallas kernels  25.6 us (49%)
  starting transfers between devices  17.4 us (34%)
  waiting for transfers between devices  7.73 us (15%)
  between operations  0.9 us (2%)
    ppermute x9, starting transfers between devices, exchanged(): lax.ppermute(value, 'bond', [(source, int(partner(source, step, count)))...  13.3 us
    ppermute x9, waiting for transfers between devices, exchanged(): lax.ppermute(value, 'bond', [(source, int(partner(source, step, count)))...  7.72 us
    pallas_call x1, Pallas kernels, body(): pl.pallas_call(functools.partial(second_kernel, with_own, groups), out_sh...  7.65 us
    pallas_call x1, Pallas kernels, body(): pl.pallas_call(first_kernel, out_shape=on_chip((width, rows, height), bf1...  4.61 us
    ppermute x2, starting transfers between devices, body(): arriving = [lax.ppermute(value, 'seg', pairs) for value in folded]  4.06 us
    pallas_call x1, Pallas kernels, body(): pl.pallas_call(grow_second_kernel, out_shape=(on_chip(grown_shape, f32),)...  2.96 us
    pallas_call x1, Pallas kernels, body(): pl.pallas_call(prepare_kernel, out_shape=(on_chip((rows, height), f32), o...  2.59 us
    pallas_call x2, Pallas kernels, body(): pl.pallas_call(functools.partial(unfold_image_kernel, steps, k * part, le...  2.55 us
  transfers between devices with their start and end apart: 11, of which 5 were waited for; matrix products, arithmetic and copies ran while one was open for 0% of the time, Pallas kernels for 27%

profile of v9, /device:TPU:0, one launch (start us, length us, event | category | flops | bytes accessed | tf_op | source)
XLA Modules:
  0.0 51.6 jit_solution(8697184580109047861)
XLA Ops:
  0.6 1.5 %fold.1 = (bf16[65,16,128]{2,1,0:T(8,128)(2,1)S(1)}, bf16[65,16,128]{2,1,0:T(8,128)(2,1)S(1)}, f32[8,128]{1,0:T(8,128)S(1)}) custom-call(bf16[128,32,128]{2,1,0:T(8,128)(2,1)} %bitcast.12), custom_call_target="tpu_custom_call" | custom-call | tf_op jit(solution)/shard_map/fold/pallas_call | solution.py:362
  2.1 0.0 copy-start
  2.1 3.4 %collective-permute-start = (bf16[65,16,128]{2,1,0:T(8,128)(2,1)S(1)}, bf16[65,16,128]{2,1,0:T(8,128)(2,1)S(1)}, u32[]{:S(2)}, u32[]{:S(2)}) collective-permute-start(bf16[65,16,128]{2,1,0:T(8,128)(2,1)S(1)} %get-tuple-element.32), channel_id=1, source_target_pairs={{0,28},{4,0},{8,4},{12,8},{16,12},{20,16},{24,20},{28,24},{1,29},{... | collective-permute-start | bytes 798728 | tf_op jit(solution)/shard_map/ppermute | solution.py:371
  5.5 0.7 %collective-permute-start.1 = (bf16[65,16,128]{2,1,0:T(8,128)(2,1)S(1)}, bf16[65,16,128]{2,1,0:T(8,128)(2,1)S(1)}, u32[]{:S(2)}, u32[]{:S(2)}) collective-permute-start(bf16[65,16,128]{2,1,0:T(8,128)(2,1)S(1)} %get-tuple-element.37), channel_id=1, source_target_pairs={{0,28},{4,0},{8,4},{12,8},{16,12},{20,16},{24,20},{28,24},{1,29},{... | collective-permute-start | bytes 798728 | tf_op jit(solution)/shard_map/ppermute | solution.py:371
  6.2 2.6 %prepare.1 = (f32[1024,128]{1,0:T(8,128)S(1)}, bf16[128,1024]{1,0:T(8,128)(2,1)S(1)}, bf16[256,256]{1,0:T(8,128)(2,1)S(1)}, bf16[128,32,128]{2,1,0:T(8,128)(2,1)S(1)}) custom-call(f32[8,128]{1,0:T(8,128)} %copy-done, bf16[128,8,128]{2,1,0:T(8,128)(2,1)} %bitcast.14, bf16[32,8,8,32]{3,2,1,0:T(8,128)(2,1)} %bitcast.13, bf16[128,32,128]{2,1,0:T(8,128)(2,1)} %bitcast.11), custom_call_target="tpu_custom_call" | custom-call | tf_op jit(solution)/shard_map/prepare/pallas_call | solution.py:372
  8.8 4.6 %first_coupled.1.coupled_ref = bf16[32,1024,128]{2,1,0:T(8,128)(2,1)S(1)} custom-call(bf16[128,1024]{1,0:T(8,128)(2,1)S(1)} %get-tuple-element.34.vector_ref, bf16[256,256]{1,0:T(8,128)(2,1)S(1)} %get-tuple-element.35.mpo_ref.refs_8_, bf16[128,32,128]{2,1,0:T(8,128)(2,1)S(1)} %get-tuple-element.36.left_ref.refs_7_), custom_call_target="tpu_custom_call" | custom-call | flops 4294967296 | bytes 8388608 | tf_op jit(solution)/shard_map/first_coupled/pallas_call | solution.py:386
  13.4 0.0 collective-permute-done.1.folded_ref
  13.4 1.3 %unfold_image.2 = (bf16[2048,128]{1,0:T(8,128)(2,1)S(1)}, f32[256,128]{1,0:T(8,128)S(1)}, f32[256,128]{1,0:T(8,128)S(1)}, f32[256,128]{1,0:T(8,128)S(1)}) custom-call(bf16[65,16,128]{2,1,0:T(8,128)(2,1)S(1)} %collective-permute-done.1.folded_ref, bf16[32,1024,128]{2,1,0:T(8,128)(2,1)S(1)} %first_coupled.1.coupled_ref), custom_call_target="tpu_custom_call" | custom-call | flops 402653184 | bytes 4194304 | tf_op jit(solution)/shard_map/unfold_image/pallas_call | solution.py:398
  14.7 0.0 collective-permute-done.folded_ref
  14.7 1.3 %unfold_image.3 = (bf16[2048,128]{1,0:T(8,128)(2,1)S(1)}, bf16[256,128]{1,0:T(8,128)(2,1)S(1)}, bf16[256,128]{1,0:T(8,128)(2,1)S(1)}, bf16[256,128]{1,0:T(8,128)(2,1)S(1)}) custom-call(bf16[65,16,128]{2,1,0:T(8,128)(2,1)S(1)} %collective-permute-done.folded_ref, bf16[32,1024,128]{2,1,0:T(8,128)(2,1)S(1)} %first_coupled.1.coupled_ref, ...), custom_call_target="tpu_custom_call" | custom-call | flops 402653184 | bytes 4194304 | tf_op jit(solution)/shard_map/unfold_image/pallas_call | solution.py:398
  16.0 3.7 %collective-permute-start.2 = (bf16[256,128]{1,0:T(8,128)(2,1)S(1)}, bf16[256,128]{1,0:T(8,128)(2,1)S(1)}, u32[]{:S(2)}, u32[]{:S(2)}) collective-permute-start(bf16[256,128]{1,0:T(8,128)(2,1)S(1)} %get-tuple-element.41), channel_id=1, source_target_pairs={{0,3},{1,2},{2,1},{3,0},{4,7},{5,6},{6,5},{7,4},{8,11},{9,10},{10,... | collective-permute-start | bytes 196616 | tf_op jit(solution)/shard_map/ppermute | solution.py:343
  19.7 0.0 collective-permute-start.3
  19.7 0.8 %collective-permute-start.4 = (bf16[256,128]{1,0:T(8,128)(2,1)S(1)}, bf16[256,128]{1,0:T(8,128)(2,1)S(1)}, u32[]{:S(2)}, u32[]{:S(2)}) collective-permute-start(bf16[256,128]{1,0:T(8,128)(2,1)S(1)} %get-tuple-element.45), channel_id=1, source_target_pairs={{0,1},{1,0},{2,3},{3,2},{4,5},{5,4},{6,7},{7,6},{8,9},{9,8},{10,11... | collective-permute-start | bytes 196616 | tf_op jit(solution)/shard_map/ppermute | solution.py:343
  20.5 2.2 %collective-permute-done.2.arrived_ref = bf16[256,128]{1,0:T(8,128)(2,1)S(1)} collective-permute-done((bf16[256,128]{1,0:T(8,128)(2,1)S(1)}, bf16[256,128]{1,0:T(8,128)(2,1)S(1)}, u32[]{:S(2)}, u32[]{:S(2)}) %collective-permute-start.2) | collective-permute-done | bytes 65568 | tf_op jit(solution)/shard_map/ppermute | solution.py:343
  22.6 0.7 %image_own.1.own_ref = f32[256,128]{1,0:T(8,128)S(1)} custom-call(bf16[256,128]{1,0:T(8,128)(2,1)S(1)} %collective-permute-done.2.arrived_ref, bf16[32,1024,128]{2,1,0:T(8,128)(2,1)S(1)} %first_coupled.1.coupled_ref, bf16[2048,128]{1,0:T(8,128)(2,1)S(1)} %get-tuple-element.42.refs_0_.refs_4_, bf16[2048,128]{1,0:T(8,128)(2,1)S(1)} %get-tuple-element.43.refs_1_.refs_5_), custom_call_target="tpu_custom_call" | custom-call | flops 268435456 | bytes 8388608 | tf_op jit(solution)/shard_map/image_own/pallas_call | solution.py:420
  23.3 1.9 %collective-permute-done.3.refs_0_ = bf16[256,128]{1,0:T(8,128)(2,1)S(1)} collective-permute-done((bf16[256,128]{1,0:T(8,128)(2,1)S(1)}, bf16[256,128]{1,0:T(8,128)(2,1)S(1)}, u32[]{:S(2)}, u32[]{:S(2)}) %collective-permute-start.3) | collective-permute-done | bytes 65568 | tf_op jit(solution)/shard_map/ppermute | solution.py:343
  25.3 1.1 %collective-permute-start.7 = (bf16[256,128]{1,0:T(8,128)(2,1)S(1)}, bf16[256,128]{1,0:T(8,128)(2,1)S(1)}, u32[]{:S(2)}, u32[]{:S(2)}) collective-permute-start(bf16[256,128]{1,0:T(8,128)(2,1)S(1)} %sum.1.refs_3_), channel_id=1, source_target_pairs={{0,1},{1,0},{2,3},{3,2},{4,5},{5,4},{6,7},{7,6},{8,9},{9,8},{10,11... | collective-permute-start | bytes 196616 | tf_op jit(solution)/shard_map/ppermute | solution.py:343
  26.4 2.2 %collective-permute-start.6 = (bf16[256,128]{1,0:T(8,128)(2,1)S(1)}, bf16[256,128]{1,0:T(8,128)(2,1)S(1)}, u32[]{:S(2)}, u32[]{:S(2)}) collective-permute-start(bf16[256,128]{1,0:T(8,128)(2,1)S(1)} %sum.1.refs_3_), channel_id=1, source_target_pairs={{0,2},{1,3},{2,0},{3,1},{4,6},{5,7},{6,4},{7,5},{8,10},{9,11},{10,... | collective-permute-start | bytes 196616 | tf_op jit(solution)/shard_map/ppermute | solution.py:343
  28.6 1.1 %collective-permute-start.5 = (bf16[256,128]{1,0:T(8,128)(2,1)S(1)}, bf16[256,128]{1,0:T(8,128)(2,1)S(1)}, u32[]{:S(2)}, u32[]{:S(2)}) collective-permute-start(bf16[256,128]{1,0:T(8,128)(2,1)S(1)} %sum.1.refs_3_), channel_id=1, source_target_pairs={{0,3},{1,2},{2,1},{3,0},{4,7},{5,6},{6,5},{7,4},{8,11},{9,10},{10,... | collective-permute-start | bytes 196616 | tf_op jit(solution)/shard_map/ppermute | solution.py:343
  29.7 1.6 %grow_first.1.refs_7_ = f32[128,32,128]{2,1,0:T(8,128)S(1)} custom-call(f32[1024,128]{1,0:T(8,128)S(1)} %get-tuple-element.46.refs_6_.basis_ref.refs_5_, bf16[32,1024,128]{2,1,0:T(8,128)(2,1)S(1)} %first_coupled.1.coupled_ref), custom_call_target="tpu_custom_call" | custom-call | flops 2147483648 | bytes 8388608 | tf_op jit(solution)/shard_map/grow_first/pallas_call | solution.py:410
  31.3 0.0 collective-permute-done.7.refs_2_
  31.3 1.8 %collective-permute-done.6.refs_1_ = bf16[256,128]{1,0:T(8,128)(2,1)S(1)} collective-permute-done((bf16[256,128]{1,0:T(8,128)(2,1)S(1)}, bf16[256,128]{1,0:T(8,128)(2,1)S(1)}, u32[]{:S(2)}, u32[]{:S(2)}) %collective-permute-start.6) | collective-permute-done | bytes 65568 | tf_op jit(solution)/shard_map/ppermute | solution.py:343
  33.2 1.5 %collective-permute-done.5.refs_0_ = bf16[256,128]{1,0:T(8,128)(2,1)S(1)} collective-permute-done((bf16[256,128]{1,0:T(8,128)(2,1)S(1)}, bf16[256,128]{1,0:T(8,128)(2,1)S(1)}, u32[]{:S(2)}, u32[]{:S(2)}) %collective-permute-start.5) | collective-permute-done | bytes 65568 | tf_op jit(solution)/shard_map/ppermute | solution.py:343
  34.7 7.7 %second_image.1 = (bf16[32,1024,128]{2,1,0:T(8,128)(2,1)S(1)}, f32[1024,128]{1,0:T(8,128)S(1)}, f32[8,128]{1,0:T(8,128)S(1)}, bf16[272,128]{1,0:T(8,128)(2,1)S(1...) custom-call(bf16[256,128]{1,0:T(8,128)(2,1)S(1)} %collective-permute-done.5.refs_0_, ...), custom_call_target="tpu_custom_call" | custom-call | tf_op jit(solution)/shard_map/second_image/pallas_call | solution.py:438
  42.4 1.2 %collective-permute-start.8 = (bf16[272,128]{1,0:T(8,128)(2,1)S(1)}, bf16[272,128]{1,0:T(8,128)(2,1)S(1)}, u32[]{:S(2)}, u32[]{:S(2)}) collective-permute-start(bf16[272,128]{1,0:T(8,128)(2,1)S(1)} %get-tuple-element.47), channel_id=1, source_target_pairs={{0,3},{1,2},{2,1},{3,0},{4,7},{5,6},{6,5},{7,4},{8,11},{9,10},{10,... | collective-permute-start | bytes 208904 | tf_op jit(solution)/shard_map/ppermute | solution.py:343
  43.5 0.0 collective-permute-start.9
  43.6 3.2 %collective-permute-start.10 = (bf16[272,128]{1,0:T(8,128)(2,1)S(1)}, bf16[272,128]{1,0:T(8,128)(2,1)S(1)}, u32[]{:S(2)}, u32[]{:S(2)}) collective-permute-start(bf16[272,128]{1,0:T(8,128)(2,1)S(1)} %get-tuple-element.49), channel_id=1, source_target_pairs={{0,1},{1,0},{2,3},{3,2},{4,5},{5,4},{6,7},{7,6},{8,9},{9,8},{10,11... | collective-permute-start | bytes 208904 | tf_op jit(solution)/shard_map/ppermute | solution.py:343
  46.7 3.0 %grow_second.1 = (f32[128,32,128]{2,1,0:T(8,128)S(1)}, f32[128,32,128]{2,1,0:T(8,128)S(1)}) custom-call(f32[1024,128]{1,0:T(8,128)S(1)} %get-tuple-element.46.refs_6_.basis_ref.refs_5_, f32[1024,128]{1,0:T(8,128)S(1)} %get-tuple-element.52.second_ref.refs_6_, bf16[32,1024,128]{2,1,0:T(8,128)(2,1)S(1)} %get-tuple-element.53.coupled_ref), custom_call_target="tpu_custom_call" | custom-call | flops 4294967296 | bytes 16777216 | tf_op jit(solution)/shard_map/grow_second/pallas_call | solution.py:454
  49.7 0.0 collective-permute-done.8.refs_0_
  49.7 0.2 collective-permute-done.9.refs_1_
  50.0 0.0 collective-permute-done.10.refs_2_
  50.0 1.5 %last.1 = (bf16[128,8,128]{2,1,0:T(8,128)(2,1)}, bf16[128,32,128]{2,1,0:T(8,128)(2,1)}, f32[1,128]{1,0:T(1,128)}, f32[32,8,128]{2,1,0:T(8,128)}) custom-call(bf16[272,128]{1,0:T(8,128)(2,1)S(1)} %collective-permute-done.8.refs_0_, bf16[272,128]{1,0:T(8,128)(2,1)S(1)} %collective-permute-done.9.refs_1_, bf16[272,128]{1,0:T(8,128)(2,1)S(1)} %collective-permute-done.10.refs_2_, ...), custom_call_target="tpu_custom_call" | custom-call | tf_op jit(solution)/shard_map/last/pallas_call | solution.py:470
  (3 shorter events, 0.0 us)
Async XLA Ops:
  2.1 4.1 %copy-start = (f32[8,128]{1,0:T(8,128)}, f32[8,128]{1,0:T(8,128)S(1)}, u32[]{:S(2)}) copy-start(f32[8,128]{1,0:T(8,128)S(1)} %get-tuple-element.33.after_ref) | copy-start | bytes 12292
  2.1 12.6 %collective-permute-start = (bf16[65,16,128]{2,1,0:T(8,128)(2,1)S(1)}, bf16[65,16,128]{2,1,0:T(8,128)(2,1)S(1)}, u32[]{:S(2)}, u32[]{:S(2)}) collective-permute-start(bf16[65,16,128]{2,1,0:T(8,128)(2,1)S(1)} %get-tuple-element.32), channel_id=1, source_target_pairs={{0,28},{4,0},{8,4},{12,8},{16,12},{20,16},{24,20},{28,24},{1,29},{... | collective-permute-start | bytes 798728 | tf_op jit(solution)/shard_map/ppermute | solution.py:371
  5.5 7.9 %collective-permute-start.1 = (bf16[65,16,128]{2,1,0:T(8,128)(2,1)S(1)}, bf16[65,16,128]{2,1,0:T(8,128)(2,1)S(1)}, u32[]{:S(2)}, u32[]{:S(2)}) collective-permute-start(bf16[65,16,128]{2,1,0:T(8,128)(2,1)S(1)} %get-tuple-element.37), channel_id=1, source_target_pairs={{0,28},{4,0},{8,4},{12,8},{16,12},{20,16},{24,20},{28,24},{1,29},{... | collective-permute-start | bytes 798728 | tf_op jit(solution)/shard_map/ppermute | solution.py:371
  16.0 6.6 %collective-permute-start.2 = (bf16[256,128]{1,0:T(8,128)(2,1)S(1)}, bf16[256,128]{1,0:T(8,128)(2,1)S(1)}, u32[]{:S(2)}, u32[]{:S(2)}) collective-permute-start(bf16[256,128]{1,0:T(8,128)(2,1)S(1)} %get-tuple-element.41), channel_id=1, source_target_pairs={{0,3},{1,2},{2,1},{3,0},{4,7},{5,6},{6,5},{7,4},{8,11},{9,10},{10,... | collective-permute-start | bytes 196616 | tf_op jit(solution)/shard_map/ppermute | solution.py:343
  19.7 5.6 %collective-permute-start.3 = (bf16[256,128]{1,0:T(8,128)(2,1)S(1)}, bf16[256,128]{1,0:T(8,128)(2,1)S(1)}, u32[]{:S(2)}, u32[]{:S(2)}) collective-permute-start(bf16[256,128]{1,0:T(8,128)(2,1)S(1)} %get-tuple-element.44), channel_id=1, source_target_pairs={{0,2},{1,3},{2,0},{3,1},{4,6},{5,7},{6,4},{7,5},{8,10},{9,11},{10,... | collective-permute-start | bytes 196616 | tf_op jit(solution)/shard_map/ppermute | solution.py:343
  19.7 5.6 %collective-permute-start.4 = (bf16[256,128]{1,0:T(8,128)(2,1)S(1)}, bf16[256,128]{1,0:T(8,128)(2,1)S(1)}, u32[]{:S(2)}, u32[]{:S(2)}) collective-permute-start(bf16[256,128]{1,0:T(8,128)(2,1)S(1)} %get-tuple-element.45), channel_id=1, source_target_pairs={{0,1},{1,0},{2,3},{3,2},{4,5},{5,4},{6,7},{7,6},{8,9},{9,8},{10,11... | collective-permute-start | bytes 196616 | tf_op jit(solution)/shard_map/ppermute | solution.py:343
  25.3 6.0 %collective-permute-start.7 = (bf16[256,128]{1,0:T(8,128)(2,1)S(1)}, bf16[256,128]{1,0:T(8,128)(2,1)S(1)}, u32[]{:S(2)}, u32[]{:S(2)}) collective-permute-start(bf16[256,128]{1,0:T(8,128)(2,1)S(1)} %sum.1.refs_3_), channel_id=1, source_target_pairs={{0,1},{1,0},{2,3},{3,2},{4,5},{5,4},{6,7},{7,6},{8,9},{9,8},{10,11... | collective-permute-start | bytes 196616 | tf_op jit(solution)/shard_map/ppermute | solution.py:343
  26.4 6.7 %collective-permute-start.6 = (bf16[256,128]{1,0:T(8,128)(2,1)S(1)}, bf16[256,128]{1,0:T(8,128)(2,1)S(1)}, u32[]{:S(2)}, u32[]{:S(2)}) collective-permute-start(bf16[256,128]{1,0:T(8,128)(2,1)S(1)} %sum.1.refs_3_), channel_id=1, source_target_pairs={{0,2},{1,3},{2,0},{3,1},{4,6},{5,7},{6,4},{7,5},{8,10},{9,11},{10,... | collective-permute-start | bytes 196616 | tf_op jit(solution)/shard_map/ppermute | solution.py:343
  28.6 6.1 %collective-permute-start.5 = (bf16[256,128]{1,0:T(8,128)(2,1)S(1)}, bf16[256,128]{1,0:T(8,128)(2,1)S(1)}, u32[]{:S(2)}, u32[]{:S(2)}) collective-permute-start(bf16[256,128]{1,0:T(8,128)(2,1)S(1)} %sum.1.refs_3_), channel_id=1, source_target_pairs={{0,3},{1,2},{2,1},{3,0},{4,7},{5,6},{6,5},{7,4},{8,11},{9,10},{10,... | collective-permute-start | bytes 196616 | tf_op jit(solution)/shard_map/ppermute | solution.py:343
  42.4 7.4 %collective-permute-start.8 = (bf16[272,128]{1,0:T(8,128)(2,1)S(1)}, bf16[272,128]{1,0:T(8,128)(2,1)S(1)}, u32[]{:S(2)}, u32[]{:S(2)}) collective-permute-start(bf16[272,128]{1,0:T(8,128)(2,1)S(1)} %get-tuple-element.47), channel_id=1, source_target_pairs={{0,3},{1,2},{2,1},{3,0},{4,7},{5,6},{6,5},{7,4},{8,11},{9,10},{10,... | collective-permute-start | bytes 208904 | tf_op jit(solution)/shard_map/ppermute | solution.py:343
  43.5 6.4 %collective-permute-start.9 = (bf16[272,128]{1,0:T(8,128)(2,1)S(1)}, bf16[272,128]{1,0:T(8,128)(2,1)S(1)}, u32[]{:S(2)}, u32[]{:S(2)}) collective-permute-start(bf16[272,128]{1,0:T(8,128)(2,1)S(1)} %get-tuple-element.48), channel_id=1, source_target_pairs={{0,2},{1,3},{2,0},{3,1},{4,6},{5,7},{6,4},{7,5},{8,10},{9,11},{10,... | collective-permute-start | bytes 208904 | tf_op jit(solution)/shard_map/ppermute | solution.py:343
  43.6 6.4 %collective-permute-start.10 = (bf16[272,128]{1,0:T(8,128)(2,1)S(1)}, bf16[272,128]{1,0:T(8,128)(2,1)S(1)}, u32[]{:S(2)}, u32[]{:S(2)}) collective-permute-start(bf16[272,128]{1,0:T(8,128)(2,1)S(1)} %get-tuple-element.49), channel_id=1, source_target_pairs={{0,1},{1,0},{2,3},{3,2},{4,5},{5,4},{6,7},{7,6},{8,9},{9,8},{10,11... | collective-permute-start | bytes 208904 | tf_op jit(solution)/shard_map/ppermute | solution.py:343

commit v10 on v8

--- a/solution.py
+++ b/solution.py
@@ -106,33 +106,26 @@
     return jnp.where((row // second == lane % first) & (row % second == lane // first), 1.0, 0.0).astype(bf16)
 
 
-def prepare_kernel(offset, right_hbm, start_hbm, mpo_hbm, left_hbm, *refs):
-    folded_ref, basis_ref, vector_ref, mpo_rows_ref, left_ref, right, sems, start, mpo, more_sems = refs
+def prepare_kernel(offset, right_hbm, start_hbm, *refs):
+    folded_ref, basis_ref, vector_ref, right, sems, start, more_sems = refs
     start_copy = pltpu.make_async_copy(start_hbm, start, more_sems.at[0])
-    mpo_copy = pltpu.make_async_copy(mpo_hbm, mpo, more_sems.at[1])
-    left_copy = pltpu.make_async_copy(left_hbm, left_ref, more_sems.at[2])
     start_copy.start()
-    mpo_copy.start()
     fold = Fold(right_hbm, offset, right, sems)
-    left_copy.start()
-    height, levels, _ = start.shape
     start_copy.wait()
     basis = normalised(start[...])
     basis_ref[...] = basis
-    vector_ref[...] = by_level(basis, height, levels)
-    width, _, _, right_width = mpo.shape
-    mpo_copy.wait()
+    vector_ref[...] = by_level(basis, start.shape[0], start.shape[1])
+    fold.finish(folded_ref)
+
+
+def first_kernel(vector_ref, mpo, left_ref, coupled_ref, mpo_rows_ref):
+    width, levels, _, right_width = mpo.shape
     terms = [mpo[:, s].astype(f32).reshape(width * levels, right_width).T for s in range(levels)]
     terms = jnp.concatenate(terms, axis=0).astype(bf16)
     terms = jnp.dot(reorder(right_width * levels, right_width, levels), terms, preferred_element_type=f32)
     terms = jnp.dot(terms.astype(bf16), reorder(width * levels, width, levels), preferred_element_type=f32)
     mpo_rows_ref[...] = terms.astype(bf16)
-    fold.finish(folded_ref)
-    left_copy.wait()
-
-
-def first_kernel(vector_ref, mpo_ref, left_ref, coupled_ref):
-    couple(left_ref, vector_ref[...], mpo_ref[...], coupled_ref, 32)
+    couple(left_ref, vector_ref[...], mpo_rows_ref[...], coupled_ref, 32)
 
 
 def unfold_kernel(folded_ref, right_ref):
@@ -376,36 +369,37 @@
             in_specs=[HBM_BLOCK],
             out_specs=VMEM_BLOCK,
             scratch_shapes=right_scratch,
-            compiler_params=params(62),
+            compiler_params=params(61),
             name="fold",
         )(right)
 
     arriving = [lax.ppermute(folded_part(k), "seg", pairs) for k in range(groups - 1)]
-    folded, basis, vector, mpo_rows, left_near = pl.pallas_call(
+    folded, basis, vector = pl.pallas_call(
         functools.partial(prepare_kernel, (groups - 1) * part),
         out_shape=(
             on_chip(folded_shape, bf16),
             on_chip((rows, height), f32),
             on_chip((height, rows), bf16),
+        ),
+        in_specs=[HBM_BLOCK] * 2,
+        out_specs=(VMEM_BLOCK,) * 3,
+        scratch_shapes=right_scratch + [pltpu.VMEM(start.shape, bf16), DMA((1,))],
+        compiler_params=params(58),
+        name="prepare",
+    )(right, start)
+    arriving.append(lax.ppermute(folded, "seg", pairs))
+    first_coupled, mpo_rows = pl.pallas_call(
+        first_kernel,
+        out_shape=(
+            on_chip((width, rows, height), bf16),
             on_chip((width * levels, levels * width), bf16),
-            on_chip(left.shape, bf16),
         ),
-        in_specs=[HBM_BLOCK] * 4,
-        out_specs=(VMEM_BLOCK,) * 5,
-        scratch_shapes=right_scratch + [pltpu.VMEM(start.shape, bf16), pltpu.VMEM(mpo.shape, bf16), DMA((3,))],
-        compiler_params=params(60),
-        name="prepare",
-    )(right, start, mpo, left)
-    arriving.append(lax.ppermute(folded, "seg", pairs))
-    first_coupled = pl.pallas_call(
-        first_kernel,
-        out_shape=on_chip((width, rows, height), bf16),
         in_specs=[VMEM_BLOCK] * 3,
-        out_specs=VMEM_BLOCK,
+        out_specs=(VMEM_BLOCK,) * 2,
         compiler_params=params(12),
         cost_estimate=cost(2 * apply_flops, 8 << 20),
         name="first_coupled",
-    )(vector, mpo_rows, left_near)
+    )(vector, mpo, left)
     right_shape = on_chip((part * height, height), bf16)
     rights = [
         pl.pallas_call(
@@ -481,7 +475,7 @@
         out_specs=(VMEM_BLOCK,) * (count + 3),
         compiler_params=params(12),
         name="second_image",
-    )(*blocks, *rights, basis, left_near, mpo_rows)
+    )(*blocks, *rights, basis, left, mpo_rows)
     second_coupled, second, scalars = outcome[:3]
     sends = outcome[3:]
     parts = [exchanged(value, step) for value, step in zip(sends, steps)] + [sends[-1]]

time: 50.4 us -> 50.4 us (level)
  no operation moved by 1% of the time
where the time goes in v10:
time: 50.4 us; the launch traced here: 50.2 us
  Pallas kernels  25 us (50%)
  starting transfers between devices  17.5 us (35%)
  waiting for transfers between devices  6.85 us (14%)
  between operations  0.92 us (2%)
    ppermute x9, starting transfers between devices, exchanged(): lax.ppermute(value, 'bond', [(source, int(partner(source, step, count)))...  13.4 us
    pallas_call x1, Pallas kernels, body(): pl.pallas_call(functools.partial(second_kernel, with_own, groups), out_sh...  7.61 us
    ppermute x9, waiting for transfers between devices, exchanged(): lax.ppermute(value, 'bond', [(source, int(partner(source, step, count)))...  6.84 us
    pallas_call x1, Pallas kernels, body(): pl.pallas_call(first_kernel, out_shape=(on_chip((width, rows, height), bf...  4.86 us
    ppermute x1, starting transfers between devices, body(): lax.ppermute(folded_part(k), 'seg', pairs)  3.39 us
    pallas_call x1, Pallas kernels, body(): pl.pallas_call(grow_second_kernel, out_shape=(on_chip(grown_shape, f32),)...  2.94 us
    pallas_call x1, Pallas kernels, body(): pl.pallas_call(functools.partial(prepare_kernel, (groups - 1) * part), ou...  1.85 us
    pallas_call x1, Pallas kernels, body(): pl.pallas_call(grow_first_kernel, out_shape=on_chip(grown_shape, f32), in...  1.59 us
  transfers between devices with their start and end apart: 11, of which 5 were waited for; matrix products, arithmetic and copies ran while one was open for 0% of the time, Pallas kernels for 27%

profile of v10, /device:TPU:0, one launch (start us, length us, event | category | flops | bytes accessed | tf_op | source)
XLA Modules:
  0.0 50.2 jit_solution(8490048289363881560)
XLA Ops:
  0.7 1.4 %fold.1 = bf16[65,16,128]{2,1,0:T(8,128)(2,1)S(1)} custom-call(bf16[128,32,128]{2,1,0:T(8,128)(2,1)} %bitcast.14), custom_call_target="tpu_custom_call" | custom-call | tf_op jit(solution)/shard_map/fold/pallas_call | solution.py:366
  2.0 3.4 %collective-permute-start.1 = (bf16[65,16,128]{2,1,0:T(8,128)(2,1)S(1)}, bf16[65,16,128]{2,1,0:T(8,128)(2,1)S(1)}, u32[]{:S(2)}, u32[]{:S(2)}) collective-permute-start(bf16[65,16,128]{2,1,0:T(8,128)(2,1)S(1)} %fold.1), channel_id=1, source_target_pairs={{0,28},{4,0},{8,4},{12,8},{16,12},{20,16},{24,20},{28,24},{1,29},{... | collective-permute-start | bytes 798728 | tf_op jit(solution)/shard_map/ppermute | solution.py:376
  5.4 1.8 %prepare.1 = (bf16[65,16,128]{2,1,0:T(8,128)(2,1)S(1)}, f32[1024,128]{1,0:T(8,128)S(1)}, bf16[128,1024]{1,0:T(8,128)(2,1)S(1)}) custom-call(bf16[128,32,128]{2,1,0:T(8,128)(2,1)} %bitcast.15, bf16[128,8,128]{2,1,0:T(8,128)(2,1)} %bitcast.16), custom_call_target="tpu_custom_call" | custom-call | tf_op jit(solution)/shard_map/prepare/pallas_call | solution.py:377
  7.2 0.7 %collective-permute-start = (bf16[65,16,128]{2,1,0:T(8,128)(2,1)S(1)}, bf16[65,16,128]{2,1,0:T(8,128)(2,1)S(1)}, u32[]{:S(2)}, u32[]{:S(2)}) collective-permute-start(bf16[65,16,128]{2,1,0:T(8,128)(2,1)S(1)} %get-tuple-element.28), channel_id=1, source_target_pairs={{0,28},{4,0},{8,4},{12,8},{16,12},{20,16},{24,20},{28,24},{1,29},{... | collective-permute-start | bytes 798728 | tf_op jit(solution)/shard_map/ppermute | solution.py:390
  8.0 4.9 %first_coupled.1 = (bf16[32,1024,128]{2,1,0:T(8,128)(2,1)S(1)}, bf16[256,256]{1,0:T(8,128)(2,1)S(1)}) custom-call(bf16[128,1024]{1,0:T(8,128)(2,1)S(1)} %get-tuple-element.26.vector_ref, bf16[32,8,8,32]{3,2,1,0:T(8,128)(2,1)S(1)} %bitcast.13, bf16[128,32,128]{2,1,0:T(8,128)(2,1)S(1)} %bitcast.11), custom_call_target="tpu_custom_call" | custom-call | flops 4294967296 | bytes 8388608 | tf_op jit(solution)/shard_map/first_coupled/pallas_call | solution.py:391
  12.8 0.0 collective-permute-done.1.folded_ref
  12.9 0.4 unfold.1.refs_0_.refs_4_
  13.2 0.0 collective-permute-done.folded_ref
  13.2 1.0 %image_first.1 = (bf16[2048,128]{1,0:T(8,128)(2,1)S(1)}, bf16[256,128]{1,0:T(8,128)(2,1)S(1)}) custom-call(bf16[32,1024,128]{2,1,0:T(8,128)(2,1)S(1)} %get-tuple-element.27.coupled_ref, bf16[65,16,128]{2,1,0:T(8,128)(2,1)S(1)} %collective-permute-done.folded_ref, bf16[2048,128]{1,0:T(8,128)(2,1)S(1)} %unfold.1.refs_0_.refs_4_), custom_call_target="tpu_custom_call" | custom-call | flops 268435456 | bytes 8388608 | tf_op jit(solution)/shard_map/image_first/pallas_call | solution.py:416
  14.2 3.7 %collective-permute-start.2 = (bf16[256,128]{1,0:T(8,128)(2,1)S(1)}, bf16[256,128]{1,0:T(8,128)(2,1)S(1)}, u32[]{:S(2)}, u32[]{:S(2)}) collective-permute-start(bf16[256,128]{1,0:T(8,128)(2,1)S(1)} %get-tuple-element.29), channel_id=1, source_target_pairs={{0,3},{1,2},{2,1},{3,0},{4,7},{5,6},{6,5},{7,4},{8,11},{9,10},{10,... | collective-permute-start | bytes 196616 | tf_op jit(solution)/shard_map/ppermute | solution.py:342
  17.9 1.2 %image_rest.1 = (bf16[256,128]{1,0:T(8,128)(2,1)S(1)}, bf16[256,128]{1,0:T(8,128)(2,1)S(1)}) custom-call(bf16[32,1024,128]{2,1,0:T(8,128)(2,1)S(1)} %get-tuple-element.27.coupled_ref, bf16[2048,128]{1,0:T(8,128)(2,1)S(1)} %unfold.1.refs_0_.refs_4_, bf16[2048,128]{1,0:T(8,128)(2,1)S(1)} %get-tuple-element.30.refs_1_.refs_5_), custom_call_target="tpu_custom_call" | custom-call | flops 536870912 | bytes 8388608 | tf_op jit(solution)/shard_map/image_rest/pallas_call | solution.py:426
  19.1 0.1 collective-permute-start.3
  19.2 0.8 %collective-permute-start.4 = (bf16[256,128]{1,0:T(8,128)(2,1)S(1)}, bf16[256,128]{1,0:T(8,128)(2,1)S(1)}, u32[]{:S(2)}, u32[]{:S(2)}) collective-permute-start(bf16[256,128]{1,0:T(8,128)(2,1)S(1)} %get-tuple-element.32), channel_id=1, source_target_pairs={{0,1},{1,0},{2,3},{3,2},{4,5},{5,4},{6,7},{7,6},{8,9},{9,8},{10,11... | collective-permute-start | bytes 196616 | tf_op jit(solution)/shard_map/ppermute | solution.py:342
  20.0 0.4 collective-permute-done.2.arrived_ref
  20.4 0.7 %image_own.1.own_ref = f32[256,128]{1,0:T(8,128)S(1)} custom-call(bf16[256,128]{1,0:T(8,128)(2,1)S(1)} %collective-permute-done.2.arrived_ref, bf16[32,1024,128]{2,1,0:T(8,128)(2,1)S(1)} %get-tuple-element.27.coupled_ref, bf16[2048,128]{1,0:T(8,128)(2,1)S(1)} %unfold.1.refs_0_.refs_4_, bf16[2048,128]{1,0:T(8,128)(2,1)S(1)} %get-tuple-element.30.refs_1_.refs_5_), custom_call_target="tpu_custom_call" | custom-call | flops 268435456 | bytes 8388608 | tf_op jit(solution)/shard_map/image_own/pallas_call | solution.py:448
  21.1 3.3 %collective-permute-done.3.refs_0_ = bf16[256,128]{1,0:T(8,128)(2,1)S(1)} collective-permute-done((bf16[256,128]{1,0:T(8,128)(2,1)S(1)}, bf16[256,128]{1,0:T(8,128)(2,1)S(1)}, u32[]{:S(2)}, u32[]{:S(2)}) %collective-permute-start.3) | collective-permute-done | bytes 65568 | tf_op jit(solution)/shard_map/ppermute | solution.py:342
  24.5 0.0 collective-permute-done.4.refs_1_
  24.5 0.6 %collective-permute-start.7 = (bf16[256,128]{1,0:T(8,128)(2,1)S(1)}, bf16[256,128]{1,0:T(8,128)(2,1)S(1)}, u32[]{:S(2)}, u32[]{:S(2)}) collective-permute-start(bf16[256,128]{1,0:T(8,128)(2,1)S(1)} %sum.1.refs_3_), channel_id=1, source_target_pairs={{0,1},{1,0},{2,3},{3,2},{4,5},{5,4},{6,7},{7,6},{8,9},{9,8},{10,11... | collective-permute-start | bytes 196616 | tf_op jit(solution)/shard_map/ppermute | solution.py:342
  25.1 2.2 %collective-permute-start.6 = (bf16[256,128]{1,0:T(8,128)(2,1)S(1)}, bf16[256,128]{1,0:T(8,128)(2,1)S(1)}, u32[]{:S(2)}, u32[]{:S(2)}) collective-permute-start(bf16[256,128]{1,0:T(8,128)(2,1)S(1)} %sum.1.refs_3_), channel_id=1, source_target_pairs={{0,2},{1,3},{2,0},{3,1},{4,6},{5,7},{6,4},{7,5},{8,10},{9,11},{10,... | collective-permute-start | bytes 196616 | tf_op jit(solution)/shard_map/ppermute | solution.py:342
  27.3 1.7 %collective-permute-start.5 = (bf16[256,128]{1,0:T(8,128)(2,1)S(1)}, bf16[256,128]{1,0:T(8,128)(2,1)S(1)}, u32[]{:S(2)}, u32[]{:S(2)}) collective-permute-start(bf16[256,128]{1,0:T(8,128)(2,1)S(1)} %sum.1.refs_3_), channel_id=1, source_target_pairs={{0,3},{1,2},{2,1},{3,0},{4,7},{5,6},{6,5},{7,4},{8,11},{9,10},{10,... | collective-permute-start | bytes 196616 | tf_op jit(solution)/shard_map/ppermute | solution.py:342
  28.9 1.6 %grow_first.1.refs_7_ = f32[128,32,128]{2,1,0:T(8,128)S(1)} custom-call(f32[1024,128]{1,0:T(8,128)S(1)} %get-tuple-element.33.refs_6_.basis_ref.refs_5_, bf16[32,1024,128]{2,1,0:T(8,128)(2,1)S(1)} %get-tuple-element.27.coupled_ref), custom_call_target="tpu_custom_call" | custom-call | flops 2147483648 | bytes 8388608 | tf_op jit(solution)/shard_map/grow_first/pallas_call | solution.py:438
  30.5 0.0 collective-permute-done.7.refs_2_
  30.6 1.4 %collective-permute-done.6.refs_1_ = bf16[256,128]{1,0:T(8,128)(2,1)S(1)} collective-permute-done((bf16[256,128]{1,0:T(8,128)(2,1)S(1)}, bf16[256,128]{1,0:T(8,128)(2,1)S(1)}, u32[]{:S(2)}, u32[]{:S(2)}) %collective-permute-start.6) | collective-permute-done | bytes 65568 | tf_op jit(solution)/shard_map/ppermute | solution.py:342
  32.0 1.4 %collective-permute-done.5.refs_0_ = bf16[256,128]{1,0:T(8,128)(2,1)S(1)} collective-permute-done((bf16[256,128]{1,0:T(8,128)(2,1)S(1)}, bf16[256,128]{1,0:T(8,128)(2,1)S(1)}, u32[]{:S(2)}, u32[]{:S(2)}) %collective-permute-start.5) | collective-permute-done | bytes 65568 | tf_op jit(solution)/shard_map/ppermute | solution.py:342
  33.4 7.6 %second_image.1 = (bf16[32,1024,128]{2,1,0:T(8,128)(2,1)S(1)}, f32[1024,128]{1,0:T(8,128)S(1)}, f32[8,128]{1,0:T(8,128)S(1)}, bf16[272,128]{1,0:T(8,128)(2,1)S(1...) custom-call(bf16[256,128]{1,0:T(8,128)(2,1)S(1)} %collective-permute-done.5.refs_0_, ...), custom_call_target="tpu_custom_call" | custom-call | tf_op jit(solution)/shard_map/second_image/pallas_call | solution.py:466
  41.0 1.7 %collective-permute-start.8 = (bf16[272,128]{1,0:T(8,128)(2,1)S(1)}, bf16[272,128]{1,0:T(8,128)(2,1)S(1)}, u32[]{:S(2)}, u32[]{:S(2)}) collective-permute-start(bf16[272,128]{1,0:T(8,128)(2,1)S(1)} %get-tuple-element.35), channel_id=1, source_target_pairs={{0,3},{1,2},{2,1},{3,0},{4,7},{5,6},{6,5},{7,4},{8,11},{9,10},{10,... | collective-permute-start | bytes 208904 | tf_op jit(solution)/shard_map/ppermute | solution.py:342
  42.7 2.6 %collective-permute-start.10 = (bf16[272,128]{1,0:T(8,128)(2,1)S(1)}, bf16[272,128]{1,0:T(8,128)(2,1)S(1)}, u32[]{:S(2)}, u32[]{:S(2)}) collective-permute-start(bf16[272,128]{1,0:T(8,128)(2,1)S(1)} %get-tuple-element.37), channel_id=1, source_target_pairs={{0,1},{1,0},{2,3},{3,2},{4,5},{5,4},{6,7},{7,6},{8,9},{9,8},{10,11... | collective-permute-start | bytes 208904 | tf_op jit(solution)/shard_map/ppermute | solution.py:342
  45.4 2.9 %grow_second.1 = (f32[128,32,128]{2,1,0:T(8,128)S(1)}, f32[128,32,128]{2,1,0:T(8,128)S(1)}) custom-call(f32[1024,128]{1,0:T(8,128)S(1)} %get-tuple-element.33.refs_6_.basis_ref.refs_5_, f32[1024,128]{1,0:T(8,128)S(1)} %get-tuple-element.40.second_ref.refs_6_, bf16[32,1024,128]{2,1,0:T(8,128)(2,1)S(1)} %get-tuple-element.41.coupled_ref), custom_call_target="tpu_custom_call" | custom-call | flops 4294967296 | bytes 16777216 | tf_op jit(solution)/shard_map/grow_second/pallas_call | solution.py:482
  48.3 0.0 collective-permute-done.8.refs_0_
  48.3 0.2 collective-permute-done.9.refs_1_
  48.6 0.0 collective-permute-done.10.refs_2_
  48.6 1.5 %last.1 = (bf16[128,8,128]{2,1,0:T(8,128)(2,1)}, bf16[128,32,128]{2,1,0:T(8,128)(2,1)}, f32[1,128]{1,0:T(1,128)}, f32[32,8,128]{2,1,0:T(8,128)}) custom-call(bf16[272,128]{1,0:T(8,128)(2,1)S(1)} %collective-permute-done.8.refs_0_, bf16[272,128]{1,0:T(8,128)(2,1)S(1)} %collective-permute-done.9.refs_1_, bf16[272,128]{1,0:T(8,128)(2,1)S(1)} %collective-permute-done.10.refs_2_, ...), custom_call_target="tpu_custom_call" | custom-call | tf_op jit(solution)/shard_map/last/pallas_call | solution.py:498
  (6 shorter events, 0.0 us)
Async XLA Ops:
  0.6 7.3 %copy-start.1 = (bf16[1,32,32,8,8]{2,4,3,1,0:T(8,128)(2,1)S(1)}, bf16[1,32,32,8,8]{2,4,3,1,0:T(8,128)(2,1)}, u32[]{:S(2)}) copy-start(bf16[1,32,32,8,8]{2,4,3,1,0:T(8,128)(2,1)} %param.6) | copy-start | bytes 393220
  0.6 7.3 %copy-start = (bf16[1,128,32,128]{3,2,1,0:T(8,128)(2,1)S(1)}, bf16[1,128,32,128]{3,2,1,0:T(8,128)(2,1)}, u32[]{:S(2)}) copy-start(bf16[1,128,32,128]{3,2,1,0:T(8,128)(2,1)} %param.4) | copy-start | bytes 3145732
  2.0 10.8 %collective-permute-start.1 = (bf16[65,16,128]{2,1,0:T(8,128)(2,1)S(1)}, bf16[65,16,128]{2,1,0:T(8,128)(2,1)S(1)}, u32[]{:S(2)}, u32[]{:S(2)}) collective-permute-start(bf16[65,16,128]{2,1,0:T(8,128)(2,1)S(1)} %fold.1), channel_id=1, source_target_pairs={{0,28},{4,0},{8,4},{12,8},{16,12},{20,16},{24,20},{28,24},{1,29},{... | collective-permute-start | bytes 798728 | tf_op jit(solution)/shard_map/ppermute | solution.py:376
  7.2 6.0 %collective-permute-start = (bf16[65,16,128]{2,1,0:T(8,128)(2,1)S(1)}, bf16[65,16,128]{2,1,0:T(8,128)(2,1)S(1)}, u32[]{:S(2)}, u32[]{:S(2)}) collective-permute-start(bf16[65,16,128]{2,1,0:T(8,128)(2,1)S(1)} %get-tuple-element.28), channel_id=1, source_target_pairs={{0,28},{4,0},{8,4},{12,8},{16,12},{20,16},{24,20},{28,24},{1,29},{... | collective-permute-start | bytes 798728 | tf_op jit(solution)/shard_map/ppermute | solution.py:390
  14.2 6.2 %collective-permute-start.2 = (bf16[256,128]{1,0:T(8,128)(2,1)S(1)}, bf16[256,128]{1,0:T(8,128)(2,1)S(1)}, u32[]{:S(2)}, u32[]{:S(2)}) collective-permute-start(bf16[256,128]{1,0:T(8,128)(2,1)S(1)} %get-tuple-element.29), channel_id=1, source_target_pairs={{0,3},{1,2},{2,1},{3,0},{4,7},{5,6},{6,5},{7,4},{8,11},{9,10},{10,... | collective-permute-start | bytes 196616 | tf_op jit(solution)/shard_map/ppermute | solution.py:342
  19.1 5.3 %collective-permute-start.3 = (bf16[256,128]{1,0:T(8,128)(2,1)S(1)}, bf16[256,128]{1,0:T(8,128)(2,1)S(1)}, u32[]{:S(2)}, u32[]{:S(2)}) collective-permute-start(bf16[256,128]{1,0:T(8,128)(2,1)S(1)} %get-tuple-element.31), channel_id=1, source_target_pairs={{0,2},{1,3},{2,0},{3,1},{4,6},{5,7},{6,4},{7,5},{8,10},{9,11},{10,... | collective-permute-start | bytes 196616 | tf_op jit(solution)/shard_map/ppermute | solution.py:342
  19.2 5.2 %collective-permute-start.4 = (bf16[256,128]{1,0:T(8,128)(2,1)S(1)}, bf16[256,128]{1,0:T(8,128)(2,1)S(1)}, u32[]{:S(2)}, u32[]{:S(2)}) collective-permute-start(bf16[256,128]{1,0:T(8,128)(2,1)S(1)} %get-tuple-element.32), channel_id=1, source_target_pairs={{0,1},{1,0},{2,3},{3,2},{4,5},{5,4},{6,7},{7,6},{8,9},{9,8},{10,11... | collective-permute-start | bytes 196616 | tf_op jit(solution)/shard_map/ppermute | solution.py:342
  24.5 6.1 %collective-permute-start.7 = (bf16[256,128]{1,0:T(8,128)(2,1)S(1)}, bf16[256,128]{1,0:T(8,128)(2,1)S(1)}, u32[]{:S(2)}, u32[]{:S(2)}) collective-permute-start(bf16[256,128]{1,0:T(8,128)(2,1)S(1)} %sum.1.refs_3_), channel_id=1, source_target_pairs={{0,1},{1,0},{2,3},{3,2},{4,5},{5,4},{6,7},{7,6},{8,9},{9,8},{10,11... | collective-permute-start | bytes 196616 | tf_op jit(solution)/shard_map/ppermute | solution.py:342
  25.1 6.9 %collective-permute-start.6 = (bf16[256,128]{1,0:T(8,128)(2,1)S(1)}, bf16[256,128]{1,0:T(8,128)(2,1)S(1)}, u32[]{:S(2)}, u32[]{:S(2)}) collective-permute-start(bf16[256,128]{1,0:T(8,128)(2,1)S(1)} %sum.1.refs_3_), channel_id=1, source_target_pairs={{0,2},{1,3},{2,0},{3,1},{4,6},{5,7},{6,4},{7,5},{8,10},{9,11},{10,... | collective-permute-start | bytes 196616 | tf_op jit(solution)/shard_map/ppermute | solution.py:342
  27.3 6.1 %collective-permute-start.5 = (bf16[256,128]{1,0:T(8,128)(2,1)S(1)}, bf16[256,128]{1,0:T(8,128)(2,1)S(1)}, u32[]{:S(2)}, u32[]{:S(2)}) collective-permute-start(bf16[256,128]{1,0:T(8,128)(2,1)S(1)} %sum.1.refs_3_), channel_id=1, source_target_pairs={{0,3},{1,2},{2,1},{3,0},{4,7},{5,6},{6,5},{7,4},{8,11},{9,10},{10,... | collective-permute-start | bytes 196616 | tf_op jit(solution)/shard_map/ppermute | solution.py:342
  41.0 7.3 %collective-permute-start.8 = (bf16[272,128]{1,0:T(8,128)(2,1)S(1)}, bf16[272,128]{1,0:T(8,128)(2,1)S(1)}, u32[]{:S(2)}, u32[]{:S(2)}) collective-permute-start(bf16[272,128]{1,0:T(8,128)(2,1)S(1)} %get-tuple-element.35), channel_id=1, source_target_pairs={{0,3},{1,2},{2,1},{3,0},{4,7},{5,6},{6,5},{7,4},{8,11},{9,10},{10,... | collective-permute-start | bytes 208904 | tf_op jit(solution)/shard_map/ppermute | solution.py:342
  42.7 5.9 %collective-permute-start.9 = (bf16[272,128]{1,0:T(8,128)(2,1)S(1)}, bf16[272,128]{1,0:T(8,128)(2,1)S(1)}, u32[]{:S(2)}, u32[]{:S(2)}) collective-permute-start(bf16[272,128]{1,0:T(8,128)(2,1)S(1)} %get-tuple-element.36), channel_id=1, source_target_pairs={{0,2},{1,3},{2,0},{3,1},{4,6},{5,7},{6,4},{7,5},{8,10},{9,11},{10,... | collective-permute-start | bytes 208904 | tf_op jit(solution)/shard_map/ppermute | solution.py:342
  42.7 5.9 %collective-permute-start.10 = (bf16[272,128]{1,0:T(8,128)(2,1)S(1)}, bf16[272,128]{1,0:T(8,128)(2,1)S(1)}, u32[]{:S(2)}, u32[]{:S(2)}) collective-permute-start(bf16[272,128]{1,0:T(8,128)(2,1)S(1)} %get-tuple-element.37), channel_id=1, source_target_pairs={{0,1},{1,0},{2,3},{3,2},{4,5},{5,4},{6,7},{7,6},{8,9},{9,8},{10,11... | collective-permute-start | bytes 208904 | tf_op jit(solution)/shard_map/ppermute | solution.py:342

commit v11 on v10

--- a/solution.py
+++ b/solution.py
@@ -106,26 +106,17 @@
     return jnp.where((row // second == lane % first) & (row % second == lane // first), 1.0, 0.0).astype(bf16)
 
 
-def prepare_kernel(offset, right_hbm, start_hbm, *refs):
-    folded_ref, basis_ref, vector_ref, right, sems, start, more_sems = refs
-    start_copy = pltpu.make_async_copy(start_hbm, start, more_sems.at[0])
-    start_copy.start()
-    fold = Fold(right_hbm, offset, right, sems)
-    start_copy.wait()
-    basis = normalised(start[...])
+def first_kernel(start_ref, mpo, left_ref, coupled_ref, mpo_rows_ref, basis_ref):
+    basis = normalised(start_ref[...])
     basis_ref[...] = basis
-    vector_ref[...] = by_level(basis, start.shape[0], start.shape[1])
-    fold.finish(folded_ref)
-
-
-def first_kernel(vector_ref, mpo, left_ref, coupled_ref, mpo_rows_ref):
+    vector = by_level(basis, start_ref.shape[0], start_ref.shape[1])
     width, levels, _, right_width = mpo.shape
     terms = [mpo[:, s].astype(f32).reshape(width * levels, right_width).T for s in range(levels)]
     terms = jnp.concatenate(terms, axis=0).astype(bf16)
     terms = jnp.dot(reorder(right_width * levels, right_width, levels), terms, preferred_element_type=f32)
     terms = jnp.dot(terms.astype(bf16), reorder(width * levels, width, levels), preferred_element_type=f32)
     mpo_rows_ref[...] = terms.astype(bf16)
-    couple(left_ref, vector_ref[...], mpo_rows_ref[...], coupled_ref, 32)
+    couple(left_ref, vector, mpo_rows_ref[...], coupled_ref, 32)
 
 
 def unfold_kernel(folded_ref, right_ref):
@@ -252,9 +243,9 @@
         store_group(one_ref, first, ones)
 
 
-def grow_second_kernel(basis_ref, second_ref, coupled_ref, cross_ref, two_ref, turned):
+def grow_second_kernel(basis_turned_ref, second_ref, coupled_ref, cross_ref, two_ref, turned):
     width, _, height = coupled_ref.shape
-    turned[:height, :] = basis_ref[...].T.astype(bf16)
+    turned[:height, :] = basis_turned_ref[...]
     turned[height:, :] = second_ref[...].T.astype(bf16)
     for first in range(0, width, 8):
         crosses, twos = [], []
@@ -373,33 +364,20 @@
             name="fold",
         )(right)
 
-    arriving = [lax.ppermute(folded_part(k), "seg", pairs) for k in range(groups - 1)]
-    folded, basis, vector = pl.pallas_call(
-        functools.partial(prepare_kernel, (groups - 1) * part),
-        out_shape=(
-            on_chip(folded_shape, bf16),
-            on_chip((rows, height), f32),
-            on_chip((height, rows), bf16),
-        ),
-        in_specs=[HBM_BLOCK] * 2,
-        out_specs=(VMEM_BLOCK,) * 3,
-        scratch_shapes=right_scratch + [pltpu.VMEM(start.shape, bf16), DMA((1,))],
-        compiler_params=params(58),
-        name="prepare",
-    )(right, start)
-    arriving.append(lax.ppermute(folded, "seg", pairs))
-    first_coupled, mpo_rows = pl.pallas_call(
+    arriving = [lax.ppermute(folded_part(k), "seg", pairs) for k in range(groups)]
+    first_coupled, mpo_rows, basis = pl.pallas_call(
         first_kernel,
         out_shape=(
             on_chip((width, rows, height), bf16),
             on_chip((width * levels, levels * width), bf16),
+            on_chip((rows, height), f32),
         ),
         in_specs=[VMEM_BLOCK] * 3,
-        out_specs=(VMEM_BLOCK,) * 2,
+        out_specs=(VMEM_BLOCK,) * 3,
         compiler_params=params(12),
         cost_estimate=cost(2 * apply_flops, 8 << 20),
         name="first_coupled",
-    )(vector, mpo, left)
+    )(start, mpo, left)
     right_shape = on_chip((part * height, height), bf16)
     rights = [
         pl.pallas_call(
@@ -435,12 +413,11 @@
     sends = [sending, *others]
     arrived = [exchanged(value, step) for value, step in zip(sends, steps)]
     grown_shape = (height, width, height)
-    one = pl.pallas_call(
+    one, basis_turned = pl.pallas_call(
         grow_first_kernel,
-        out_shape=on_chip(grown_shape, f32),
+        out_shape=(on_chip(grown_shape, f32), on_chip((height, rows), bf16)),
         in_specs=[VMEM_BLOCK] * 2,
-        out_specs=VMEM_BLOCK,
-        scratch_shapes=[pltpu.VMEM((height, rows), bf16)],
+        out_specs=(VMEM_BLOCK,) * 2,
         compiler_params=params(8),
         cost_estimate=cost(apply_flops, 8 << 20),
         name="grow_first",
@@ -488,7 +465,7 @@
         compiler_params=params(8),
         cost_estimate=cost(2 * apply_flops, 16 << 20),
         name="grow_second",
-    )(basis, second, second_coupled)
+    )(basis_turned, second, second_coupled)
     outputs = (
         jax.ShapeDtypeStruct((height, levels, height), bf16),
         jax.ShapeDtypeStruct((height, width, height), bf16),

time: 50.4 us -> 49.9 us (0.990)
  Pallas kernels: 25 us -> 24.4 us
    pallas_call x2 -> x1, Pallas kernels: 3.44 us -> 1.58 us  [body(): pl.pallas_call(grow_first_kernel, out_shape=(on_chip(grown_shape, f32), o...]
    pallas_call x1 -> x2, Pallas kernels: 1.35 us -> 2.6 us  [folded_part(): pl.pallas_call(functools.partial(fold_kernel, k * part), out_shape=on_chi...]
    ppermute x1 -> x2, starting transfers between devices: 3.39 us -> 4.11 us  [body(): lax.ppermute(folded_part(k), 'seg', pairs)]
    ppermute x1 -> x0, starting transfers between devices: 0.73 us -> none  [body(): arriving.append(lax.ppermute(folded, 'seg', pairs))]
  transfers between devices with their start and end apart: 11 -> 11, of which waited for: 5 -> 5; matrix products, arithmetic and copies ran while one was open for 0% -> 0% of each run, Pallas kernels for 27% -> 26%
where the time goes in v11:
time: 49.9 us; the launch traced here: 49.8 us
  Pallas kernels  24.4 us (49%)
  starting transfers between devices  17.5 us (35%)
  waiting for transfers between devices  6.91 us (14%)
  between operations  0.93 us (2%)
    ppermute x9, starting transfers between devices, exchanged(): lax.ppermute(value, 'bond', [(source, int(partner(source, step, count)))...  13.4 us
    pallas_call x1, Pallas kernels, body(): pl.pallas_call(functools.partial(second_kernel, with_own, groups), out_sh...  7.59 us
    ppermute x9, waiting for transfers between devices, exchanged(): lax.ppermute(value, 'bond', [(source, int(partner(source, step, count)))...  6.9 us
    pallas_call x1, Pallas kernels, body(): pl.pallas_call(first_kernel, out_shape=(on_chip((width, rows, height), bf...  5.02 us
    ppermute x2, starting transfers between devices, body(): lax.ppermute(folded_part(k), 'seg', pairs)  4.11 us
    pallas_call x1, Pallas kernels, body(): pl.pallas_call(grow_second_kernel, out_shape=(on_chip(grown_shape, f32),)...  2.89 us
    pallas_call x2, Pallas kernels, folded_part(): pl.pallas_call(functools.partial(fold_kernel, k * part), out_shape=on_chi...  2.6 us
    pallas_call x1, Pallas kernels, body(): pl.pallas_call(grow_first_kernel, out_shape=(on_chip(grown_shape, f32), o...  1.58 us
  transfers between devices with their start and end apart: 11, of which 5 were waited for; matrix products, arithmetic and copies ran while one was open for 0% of the time, Pallas kernels for 26%

profile of v11, /device:TPU:0, one launch (start us, length us, event | category | flops | bytes accessed | tf_op | source)
XLA Modules:
  0.0 49.8 jit_solution(9523804339556910452)
XLA Ops:
  0.7 1.4 %fold.2 = bf16[65,16,128]{2,1,0:T(8,128)(2,1)S(1)} custom-call(bf16[128,32,128]{2,1,0:T(8,128)(2,1)} %bitcast.15), custom_call_target="tpu_custom_call" | custom-call | tf_op jit(solution)/shard_map/fold/pallas_call | solution.py:357
  2.0 3.4 %collective-permute-start = (bf16[65,16,128]{2,1,0:T(8,128)(2,1)S(1)}, bf16[65,16,128]{2,1,0:T(8,128)(2,1)S(1)}, u32[]{:S(2)}, u32[]{:S(2)}) collective-permute-start(bf16[65,16,128]{2,1,0:T(8,128)(2,1)S(1)} %fold.2), channel_id=1, source_target_pairs={{0,28},{4,0},{8,4},{12,8},{16,12},{20,16},{24,20},{28,24},{1,29},{... | collective-permute-start | bytes 798728 | tf_op jit(solution)/shard_map/ppermute | solution.py:367
  5.4 1.2 %fold.3 = bf16[65,16,128]{2,1,0:T(8,128)(2,1)S(1)} custom-call(bf16[128,32,128]{2,1,0:T(8,128)(2,1)} %bitcast.16), custom_call_target="tpu_custom_call" | custom-call | tf_op jit(solution)/shard_map/fold/pallas_call | solution.py:357
  6.7 0.7 %collective-permute-start.1 = (bf16[65,16,128]{2,1,0:T(8,128)(2,1)S(1)}, bf16[65,16,128]{2,1,0:T(8,128)(2,1)S(1)}, u32[]{:S(2)}, u32[]{:S(2)}) collective-permute-start(bf16[65,16,128]{2,1,0:T(8,128)(2,1)S(1)} %fold.3), channel_id=1, source_target_pairs={{0,28},{4,0},{8,4},{12,8},{16,12},{20,16},{24,20},{28,24},{1,29},{... | collective-permute-start | bytes 798728 | tf_op jit(solution)/shard_map/ppermute | solution.py:367
  7.4 5.0 %first_coupled.1 = (bf16[32,1024,128]{2,1,0:T(8,128)(2,1)S(1)}, bf16[256,256]{1,0:T(8,128)(2,1)S(1)}, f32[1024,128]{1,0:T(8,128)S(1)}) custom-call(bf16[128,8,128]{2,1,0:T(8,128)(2,1)S(1)} %bitcast.14, bf16[32,8,8,32]{3,2,1,0:T(8,128)(2,1)S(1)} %bitcast.13, bf16[128,32,128]{2,1,0:T(8,128)(2,1)S(1)} %bitcast.11), custom_call_target="tpu_custom_call" | custom-call | flops 4294967296 | bytes 8388608 | tf_op jit(solution)/shard_map/first_coupled/pallas_call | solution.py:368
  12.4 0.0 collective-permute-done.1.folded_ref
  12.4 0.4 unfold.1.refs_0_.refs_4_
  12.8 0.0 collective-permute-done.folded_ref
  12.8 1.0 %image_first.1 = (bf16[2048,128]{1,0:T(8,128)(2,1)S(1)}, bf16[256,128]{1,0:T(8,128)(2,1)S(1)}) custom-call(bf16[32,1024,128]{2,1,0:T(8,128)(2,1)S(1)} %get-tuple-element.26.coupled_ref, bf16[65,16,128]{2,1,0:T(8,128)(2,1)S(1)} %collective-permute-done.folded_ref, bf16[2048,128]{1,0:T(8,128)(2,1)S(1)} %unfold.1.refs_0_.refs_4_), custom_call_target="tpu_custom_call" | custom-call | flops 268435456 | bytes 8388608 | tf_op jit(solution)/shard_map/image_first/pallas_call | solution.py:394
  13.8 3.7 %collective-permute-start.2 = (bf16[256,128]{1,0:T(8,128)(2,1)S(1)}, bf16[256,128]{1,0:T(8,128)(2,1)S(1)}, u32[]{:S(2)}, u32[]{:S(2)}) collective-permute-start(bf16[256,128]{1,0:T(8,128)(2,1)S(1)} %get-tuple-element.27), channel_id=1, source_target_pairs={{0,3},{1,2},{2,1},{3,0},{4,7},{5,6},{6,5},{7,4},{8,11},{9,10},{10,... | collective-permute-start | bytes 196616 | tf_op jit(solution)/shard_map/ppermute | solution.py:333
  17.5 1.2 %image_rest.1 = (bf16[256,128]{1,0:T(8,128)(2,1)S(1)}, bf16[256,128]{1,0:T(8,128)(2,1)S(1)}) custom-call(bf16[32,1024,128]{2,1,0:T(8,128)(2,1)S(1)} %get-tuple-element.26.coupled_ref, bf16[2048,128]{1,0:T(8,128)(2,1)S(1)} %unfold.1.refs_0_.refs_4_, bf16[2048,128]{1,0:T(8,128)(2,1)S(1)} %get-tuple-element.28.refs_1_.refs_5_), custom_call_target="tpu_custom_call" | custom-call | flops 536870912 | bytes 8388608 | tf_op jit(solution)/shard_map/image_rest/pallas_call | solution.py:404
  18.7 0.1 collective-permute-start.3
  18.8 0.8 %collective-permute-start.4 = (bf16[256,128]{1,0:T(8,128)(2,1)S(1)}, bf16[256,128]{1,0:T(8,128)(2,1)S(1)}, u32[]{:S(2)}, u32[]{:S(2)}) collective-permute-start(bf16[256,128]{1,0:T(8,128)(2,1)S(1)} %get-tuple-element.30), channel_id=1, source_target_pairs={{0,1},{1,0},{2,3},{3,2},{4,5},{5,4},{6,7},{7,6},{8,9},{9,8},{10,11... | collective-permute-start | bytes 196616 | tf_op jit(solution)/shard_map/ppermute | solution.py:333
  19.6 0.4 collective-permute-done.2.arrived_ref
  20.0 0.7 %image_own.1.own_ref = f32[256,128]{1,0:T(8,128)S(1)} custom-call(bf16[256,128]{1,0:T(8,128)(2,1)S(1)} %collective-permute-done.2.arrived_ref, bf16[32,1024,128]{2,1,0:T(8,128)(2,1)S(1)} %get-tuple-element.26.coupled_ref, bf16[2048,128]{1,0:T(8,128)(2,1)S(1)} %unfold.1.refs_0_.refs_4_, bf16[2048,128]{1,0:T(8,128)(2,1)S(1)} %get-tuple-element.28.refs_1_.refs_5_), custom_call_target="tpu_custom_call" | custom-call | flops 268435456 | bytes 8388608 | tf_op jit(solution)/shard_map/image_own/pallas_call | solution.py:425
  20.7 3.3 %collective-permute-done.3.refs_0_ = bf16[256,128]{1,0:T(8,128)(2,1)S(1)} collective-permute-done((bf16[256,128]{1,0:T(8,128)(2,1)S(1)}, bf16[256,128]{1,0:T(8,128)(2,1)S(1)}, u32[]{:S(2)}, u32[]{:S(2)}) %collective-permute-start.3) | collective-permute-done | bytes 65568 | tf_op jit(solution)/shard_map/ppermute | solution.py:333
  24.0 0.0 collective-permute-done.4.refs_1_
  24.1 0.6 %collective-permute-start.7 = (bf16[256,128]{1,0:T(8,128)(2,1)S(1)}, bf16[256,128]{1,0:T(8,128)(2,1)S(1)}, u32[]{:S(2)}, u32[]{:S(2)}) collective-permute-start(bf16[256,128]{1,0:T(8,128)(2,1)S(1)} %sum.1.refs_3_), channel_id=1, source_target_pairs={{0,1},{1,0},{2,3},{3,2},{4,5},{5,4},{6,7},{7,6},{8,9},{9,8},{10,11... | collective-permute-start | bytes 196616 | tf_op jit(solution)/shard_map/ppermute | solution.py:333
  24.6 2.2 %collective-permute-start.6 = (bf16[256,128]{1,0:T(8,128)(2,1)S(1)}, bf16[256,128]{1,0:T(8,128)(2,1)S(1)}, u32[]{:S(2)}, u32[]{:S(2)}) collective-permute-start(bf16[256,128]{1,0:T(8,128)(2,1)S(1)} %sum.1.refs_3_), channel_id=1, source_target_pairs={{0,2},{1,3},{2,0},{3,1},{4,6},{5,7},{6,4},{7,5},{8,10},{9,11},{10,... | collective-permute-start | bytes 196616 | tf_op jit(solution)/shard_map/ppermute | solution.py:333
  26.8 1.7 %collective-permute-start.5 = (bf16[256,128]{1,0:T(8,128)(2,1)S(1)}, bf16[256,128]{1,0:T(8,128)(2,1)S(1)}, u32[]{:S(2)}, u32[]{:S(2)}) collective-permute-start(bf16[256,128]{1,0:T(8,128)(2,1)S(1)} %sum.1.refs_3_), channel_id=1, source_target_pairs={{0,3},{1,2},{2,1},{3,0},{4,7},{5,6},{6,5},{7,4},{8,11},{9,10},{10,... | collective-permute-start | bytes 196616 | tf_op jit(solution)/shard_map/ppermute | solution.py:333
  28.5 1.6 %grow_first.1 = (f32[128,32,128]{2,1,0:T(8,128)S(1)}, bf16[128,1024]{1,0:T(8,128)(2,1)S(1)}) custom-call(f32[1024,128]{1,0:T(8,128)S(1)} %get-tuple-element.31.refs_6_.basis_ref.refs_5_, bf16[32,1024,128]{2,1,0:T(8,128)(2,1)S(1)} %get-tuple-element.26.coupled_ref), custom_call_target="tpu_custom_call" | custom-call | flops 2147483648 | bytes 8388608 | tf_op jit(solution)/shard_map/grow_first/pallas_call | solution.py:416
  30.1 0.0 collective-permute-done.7.refs_2_
  30.1 1.4 %collective-permute-done.6.refs_1_ = bf16[256,128]{1,0:T(8,128)(2,1)S(1)} collective-permute-done((bf16[256,128]{1,0:T(8,128)(2,1)S(1)}, bf16[256,128]{1,0:T(8,128)(2,1)S(1)}, u32[]{:S(2)}, u32[]{:S(2)}) %collective-permute-start.6) | collective-permute-done | bytes 65568 | tf_op jit(solution)/shard_map/ppermute | solution.py:333
  31.5 1.4 %collective-permute-done.5.refs_0_ = bf16[256,128]{1,0:T(8,128)(2,1)S(1)} collective-permute-done((bf16[256,128]{1,0:T(8,128)(2,1)S(1)}, bf16[256,128]{1,0:T(8,128)(2,1)S(1)}, u32[]{:S(2)}, u32[]{:S(2)}) %collective-permute-start.5) | collective-permute-done | bytes 65568 | tf_op jit(solution)/shard_map/ppermute | solution.py:333
  32.9 7.6 %second_image.1 = (bf16[32,1024,128]{2,1,0:T(8,128)(2,1)S(1)}, f32[1024,128]{1,0:T(8,128)S(1)}, f32[8,128]{1,0:T(8,128)S(1)}, bf16[272,128]{1,0:T(8,128)(2,1)S(1...) custom-call(bf16[256,128]{1,0:T(8,128)(2,1)S(1)} %collective-permute-done.5.refs_0_, ...), custom_call_target="tpu_custom_call" | custom-call | tf_op jit(solution)/shard_map/second_image/pallas_call | solution.py:443
  40.5 1.7 %collective-permute-start.8 = (bf16[272,128]{1,0:T(8,128)(2,1)S(1)}, bf16[272,128]{1,0:T(8,128)(2,1)S(1)}, u32[]{:S(2)}, u32[]{:S(2)}) collective-permute-start(bf16[272,128]{1,0:T(8,128)(2,1)S(1)} %get-tuple-element.33), channel_id=1, source_target_pairs={{0,3},{1,2},{2,1},{3,0},{4,7},{5,6},{6,5},{7,4},{8,11},{9,10},{10,... | collective-permute-start | bytes 208904 | tf_op jit(solution)/shard_map/ppermute | solution.py:333
  42.3 2.6 %collective-permute-start.10 = (bf16[272,128]{1,0:T(8,128)(2,1)S(1)}, bf16[272,128]{1,0:T(8,128)(2,1)S(1)}, u32[]{:S(2)}, u32[]{:S(2)}) collective-permute-start(bf16[272,128]{1,0:T(8,128)(2,1)S(1)} %get-tuple-element.35), channel_id=1, source_target_pairs={{0,1},{1,0},{2,3},{3,2},{4,5},{5,4},{6,7},{7,6},{8,9},{9,8},{10,11... | collective-permute-start | bytes 208904 | tf_op jit(solution)/shard_map/ppermute | solution.py:333
  44.9 2.9 %grow_second.1 = (f32[128,32,128]{2,1,0:T(8,128)S(1)}, f32[128,32,128]{2,1,0:T(8,128)S(1)}) custom-call(bf16[128,1024]{1,0:T(8,128)(2,1)S(1)} %get-tuple-element.40.basis_turned_ref, f32[1024,128]{1,0:T(8,128)S(1)} %get-tuple-element.38.second_ref.refs_6_, bf16[32,1024,128]{2,1,0:T(8,128)(2,1)S(1)} %get-tuple-element.41.coupled_ref), custom_call_target="tpu_custom_call" | custom-call | flops 4294967296 | bytes 16777216 | tf_op jit(solution)/shard_map/grow_second/pallas_call | solution.py:459
  47.8 0.0 collective-permute-done.8.refs_0_
  47.8 0.3 collective-permute-done.9.refs_1_
  48.1 0.0 collective-permute-done.10.refs_2_
  48.1 1.5 %last.1 = (bf16[128,8,128]{2,1,0:T(8,128)(2,1)}, bf16[128,32,128]{2,1,0:T(8,128)(2,1)}, f32[1,128]{1,0:T(1,128)}, f32[32,8,128]{2,1,0:T(8,128)}) custom-call(bf16[272,128]{1,0:T(8,128)(2,1)S(1)} %collective-permute-done.8.refs_0_, bf16[272,128]{1,0:T(8,128)(2,1)S(1)} %collective-permute-done.9.refs_1_, bf16[272,128]{1,0:T(8,128)(2,1)S(1)} %collective-permute-done.10.refs_2_, ...), custom_call_target="tpu_custom_call" | custom-call | tf_op jit(solution)/shard_map/last/pallas_call | solution.py:475
  (8 shorter events, 0.0 us)
Async XLA Ops:
  0.6 6.8 %copy-start.2 = (bf16[1,128,8,128]{3,2,1,0:T(8,128)(2,1)S(1)}, bf16[1,128,8,128]{3,2,1,0:T(8,128)(2,1)}, u32[]{:S(2)}) copy-start(bf16[1,128,8,128]{3,2,1,0:T(8,128)(2,1)} %param.7) | copy-start | bytes 786436
  0.6 6.8 %copy-start.1 = (bf16[1,32,32,8,8]{2,4,3,1,0:T(8,128)(2,1)S(1)}, bf16[1,32,32,8,8]{2,4,3,1,0:T(8,128)(2,1)}, u32[]{:S(2)}) copy-start(bf16[1,32,32,8,8]{2,4,3,1,0:T(8,128)(2,1)} %param.6) | copy-start | bytes 393220
  0.7 6.7 %copy-start = (bf16[1,128,32,128]{3,2,1,0:T(8,128)(2,1)S(1)}, bf16[1,128,32,128]{3,2,1,0:T(8,128)(2,1)}, u32[]{:S(2)}) copy-start(bf16[1,128,32,128]{3,2,1,0:T(8,128)(2,1)} %param.4) | copy-start | bytes 3145732
  2.0 10.8 %collective-permute-start = (bf16[65,16,128]{2,1,0:T(8,128)(2,1)S(1)}, bf16[65,16,128]{2,1,0:T(8,128)(2,1)S(1)}, u32[]{:S(2)}, u32[]{:S(2)}) collective-permute-start(bf16[65,16,128]{2,1,0:T(8,128)(2,1)S(1)} %fold.2), channel_id=1, source_target_pairs={{0,28},{4,0},{8,4},{12,8},{16,12},{20,16},{24,20},{28,24},{1,29},{... | collective-permute-start | bytes 798728 | tf_op jit(solution)/shard_map/ppermute | solution.py:367
  6.7 5.8 %collective-permute-start.1 = (bf16[65,16,128]{2,1,0:T(8,128)(2,1)S(1)}, bf16[65,16,128]{2,1,0:T(8,128)(2,1)S(1)}, u32[]{:S(2)}, u32[]{:S(2)}) collective-permute-start(bf16[65,16,128]{2,1,0:T(8,128)(2,1)S(1)} %fold.3), channel_id=1, source_target_pairs={{0,28},{4,0},{8,4},{12,8},{16,12},{20,16},{24,20},{28,24},{1,29},{... | collective-permute-start | bytes 798728 | tf_op jit(solution)/shard_map/ppermute | solution.py:367
  13.8 6.2 %collective-permute-start.2 = (bf16[256,128]{1,0:T(8,128)(2,1)S(1)}, bf16[256,128]{1,0:T(8,128)(2,1)S(1)}, u32[]{:S(2)}, u32[]{:S(2)}) collective-permute-start(bf16[256,128]{1,0:T(8,128)(2,1)S(1)} %get-tuple-element.27), channel_id=1, source_target_pairs={{0,3},{1,2},{2,1},{3,0},{4,7},{5,6},{6,5},{7,4},{8,11},{9,10},{10,... | collective-permute-start | bytes 196616 | tf_op jit(solution)/shard_map/ppermute | solution.py:333
  18.7 5.3 %collective-permute-start.3 = (bf16[256,128]{1,0:T(8,128)(2,1)S(1)}, bf16[256,128]{1,0:T(8,128)(2,1)S(1)}, u32[]{:S(2)}, u32[]{:S(2)}) collective-permute-start(bf16[256,128]{1,0:T(8,128)(2,1)S(1)} %get-tuple-element.29), channel_id=1, source_target_pairs={{0,2},{1,3},{2,0},{3,1},{4,6},{5,7},{6,4},{7,5},{8,10},{9,11},{10,... | collective-permute-start | bytes 196616 | tf_op jit(solution)/shard_map/ppermute | solution.py:333
  18.8 5.2 %collective-permute-start.4 = (bf16[256,128]{1,0:T(8,128)(2,1)S(1)}, bf16[256,128]{1,0:T(8,128)(2,1)S(1)}, u32[]{:S(2)}, u32[]{:S(2)}) collective-permute-start(bf16[256,128]{1,0:T(8,128)(2,1)S(1)} %get-tuple-element.30), channel_id=1, source_target_pairs={{0,1},{1,0},{2,3},{3,2},{4,5},{5,4},{6,7},{7,6},{8,9},{9,8},{10,11... | collective-permute-start | bytes 196616 | tf_op jit(solution)/shard_map/ppermute | solution.py:333
  24.1 6.0 %collective-permute-start.7 = (bf16[256,128]{1,0:T(8,128)(2,1)S(1)}, bf16[256,128]{1,0:T(8,128)(2,1)S(1)}, u32[]{:S(2)}, u32[]{:S(2)}) collective-permute-start(bf16[256,128]{1,0:T(8,128)(2,1)S(1)} %sum.1.refs_3_), channel_id=1, source_target_pairs={{0,1},{1,0},{2,3},{3,2},{4,5},{5,4},{6,7},{7,6},{8,9},{9,8},{10,11... | collective-permute-start | bytes 196616 | tf_op jit(solution)/shard_map/ppermute | solution.py:333
  24.6 6.9 %collective-permute-start.6 = (bf16[256,128]{1,0:T(8,128)(2,1)S(1)}, bf16[256,128]{1,0:T(8,128)(2,1)S(1)}, u32[]{:S(2)}, u32[]{:S(2)}) collective-permute-start(bf16[256,128]{1,0:T(8,128)(2,1)S(1)} %sum.1.refs_3_), channel_id=1, source_target_pairs={{0,2},{1,3},{2,0},{3,1},{4,6},{5,7},{6,4},{7,5},{8,10},{9,11},{10,... | collective-permute-start | bytes 196616 | tf_op jit(solution)/shard_map/ppermute | solution.py:333
  26.8 6.1 %collective-permute-start.5 = (bf16[256,128]{1,0:T(8,128)(2,1)S(1)}, bf16[256,128]{1,0:T(8,128)(2,1)S(1)}, u32[]{:S(2)}, u32[]{:S(2)}) collective-permute-start(bf16[256,128]{1,0:T(8,128)(2,1)S(1)} %sum.1.refs_3_), channel_id=1, source_target_pairs={{0,3},{1,2},{2,1},{3,0},{4,7},{5,6},{6,5},{7,4},{8,11},{9,10},{10,... | collective-permute-start | bytes 196616 | tf_op jit(solution)/shard_map/ppermute | solution.py:333
  40.5 7.3 %collective-permute-start.8 = (bf16[272,128]{1,0:T(8,128)(2,1)S(1)}, bf16[272,128]{1,0:T(8,128)(2,1)S(1)}, u32[]{:S(2)}, u32[]{:S(2)}) collective-permute-start(bf16[272,128]{1,0:T(8,128)(2,1)S(1)} %get-tuple-element.33), channel_id=1, source_target_pairs={{0,3},{1,2},{2,1},{3,0},{4,7},{5,6},{6,5},{7,4},{8,11},{9,10},{10,... | collective-permute-start | bytes 208904 | tf_op jit(solution)/shard_map/ppermute | solution.py:333
  42.3 5.9 %collective-permute-start.9 = (bf16[272,128]{1,0:T(8,128)(2,1)S(1)}, bf16[272,128]{1,0:T(8,128)(2,1)S(1)}, u32[]{:S(2)}, u32[]{:S(2)}) collective-permute-start(bf16[272,128]{1,0:T(8,128)(2,1)S(1)} %get-tuple-element.34), channel_id=1, source_target_pairs={{0,2},{1,3},{2,0},{3,1},{4,6},{5,7},{6,4},{7,5},{8,10},{9,11},{10,... | collective-permute-start | bytes 208904 | tf_op jit(solution)/shard_map/ppermute | solution.py:333
  42.3 5.9 %collective-permute-start.10 = (bf16[272,128]{1,0:T(8,128)(2,1)S(1)}, bf16[272,128]{1,0:T(8,128)(2,1)S(1)}, u32[]{:S(2)}, u32[]{:S(2)}) collective-permute-start(bf16[272,128]{1,0:T(8,128)(2,1)S(1)} %get-tuple-element.35), channel_id=1, source_target_pairs={{0,1},{1,0},{2,3},{3,2},{4,5},{5,4},{6,7},{7,6},{8,9},{9,8},{10,11... | collective-permute-start | bytes 208904 | tf_op jit(solution)/shard_map/ppermute | solution.py:333

commit v12 on v11

--- a/solution.py
+++ b/solution.py
@@ -157,12 +157,6 @@
 
 def other(step):
     return partner(lax.axis_index("bond"), step, lax.axis_size("bond"))
-
-
-def first_image_kernel(step, groups, coupled_ref, folded_ref, *refs):
-    right_refs, image_ref = refs[:groups], refs[groups]
-    unfold_kernel(folded_ref, right_refs[-1])
-    image_ref[...] = block_image(other(step), coupled_ref, right_refs, image_ref.shape[0]).astype(bf16)
 
 
 def images_kernel(steps, groups, coupled_ref, *refs):
@@ -389,28 +383,21 @@
             cost_estimate=cost(1 << 20, 1 << 20),
             name="unfold",
         )(folded)
-        for folded in arriving[:-1]
+        for folded in arriving
     ]
-    last_right, sending = pl.pallas_call(
-        functools.partial(first_image_kernel, steps[0], groups),
-        out_shape=(right_shape, on_chip((block, height), bf16)),
-        in_specs=[VMEM_BLOCK] * (1 + groups),
-        out_specs=(VMEM_BLOCK,) * 2,
-        compiler_params=params(8),
-        cost_estimate=cost(apply_flops // (2 * count), 8 << 20),
-        name="image_first",
-    )(first_coupled, arriving[-1], *rights)
-    rights.append(last_right)
-    others = pl.pallas_call(
-        functools.partial(images_kernel, steps[1:], groups),
-        out_shape=[on_chip((block, height), bf16)] * (count - 2),
-        in_specs=[VMEM_BLOCK] * (1 + groups),
-        out_specs=[VMEM_BLOCK] * (count - 2),
-        compiler_params=params(8),
-        cost_estimate=cost(apply_flops * (count - 2) // (2 * count), 8 << 20),
-        name="image_rest",
-    )(first_coupled, *rights)
-    sends = [sending, *others]
+
+    def images(steps, name):
+        return pl.pallas_call(
+            functools.partial(images_kernel, steps, groups),
+            out_shape=[on_chip((block, height), bf16)] * len(steps),
+            in_specs=[VMEM_BLOCK] * (1 + groups),
+            out_specs=[VMEM_BLOCK] * len(steps),
+            compiler_params=params(8),
+            cost_estimate=cost(apply_flops * len(steps) // (2 * count), 8 << 20),
+            name=name,
+        )(first_coupled, *rights)
+
+    sends = [*images(steps[:1], "image_first"), *images(steps[1:], "image_rest")]
     arrived = [exchanged(value, step) for value, step in zip(sends, steps)]
     grown_shape = (height, width, height)
     one, basis_turned = pl.pallas_call(

time: 49.9 us -> 50 us (level)
  no operation moved by 1% of the time
where the time goes in v12:
time: 50 us; the launch traced here: 49.8 us
  Pallas kernels  24.5 us (49%)
  starting transfers between devices  17.5 us (35%)
  waiting for transfers between devices  6.91 us (14%)
  between operations  0.93 us (2%)
    ppermute x9, starting transfers between devices, exchanged(): lax.ppermute(value, 'bond', [(source, int(partner(source, step, count)))...  13.4 us
    pallas_call x1, Pallas kernels, body(): pl.pallas_call(functools.partial(second_kernel, with_own, groups), out_sh...  7.59 us
    ppermute x9, waiting for transfers between devices, exchanged(): lax.ppermute(value, 'bond', [(source, int(partner(source, step, count)))...  6.9 us
    pallas_call x1, Pallas kernels, body(): pl.pallas_call(first_kernel, out_shape=(on_chip((width, rows, height), bf...  5.02 us
    ppermute x2, starting transfers between devices, body(): lax.ppermute(folded_part(k), 'seg', pairs)  4.11 us
    pallas_call x1, Pallas kernels, body(): pl.pallas_call(grow_second_kernel, out_shape=(on_chip(grown_shape, f32),)...  2.89 us
    pallas_call x2, Pallas kernels, folded_part(): pl.pallas_call(functools.partial(fold_kernel, k * part), out_shape=on_chi...  2.6 us
    pallas_call x2, Pallas kernels, images(): pl.pallas_call(functools.partial(images_kernel, steps, groups), out_shape...  1.93 us
  transfers between devices with their start and end apart: 11, of which 5 were waited for; matrix products, arithmetic and copies ran while one was open for 0% of the time, Pallas kernels for 26%

profile of v12, /device:TPU:0, one launch (start us, length us, event | category | flops | bytes accessed | tf_op | source)
XLA Modules:
  0.0 49.8 jit_solution(16272776812136872256)
XLA Ops:
  0.7 1.4 %fold.2 = bf16[65,16,128]{2,1,0:T(8,128)(2,1)S(1)} custom-call(bf16[128,32,128]{2,1,0:T(8,128)(2,1)} %bitcast.15), custom_call_target="tpu_custom_call" | custom-call | tf_op jit(solution)/shard_map/fold/pallas_call | solution.py:351
  2.0 3.4 %collective-permute-start = (bf16[65,16,128]{2,1,0:T(8,128)(2,1)S(1)}, bf16[65,16,128]{2,1,0:T(8,128)(2,1)S(1)}, u32[]{:S(2)}, u32[]{:S(2)}) collective-permute-start(bf16[65,16,128]{2,1,0:T(8,128)(2,1)S(1)} %fold.2), channel_id=1, source_target_pairs={{0,28},{4,0},{8,4},{12,8},{16,12},{20,16},{24,20},{28,24},{1,29},{... | collective-permute-start | bytes 798728 | tf_op jit(solution)/shard_map/ppermute | solution.py:361
  5.4 1.2 %fold.3 = bf16[65,16,128]{2,1,0:T(8,128)(2,1)S(1)} custom-call(bf16[128,32,128]{2,1,0:T(8,128)(2,1)} %bitcast.16), custom_call_target="tpu_custom_call" | custom-call | tf_op jit(solution)/shard_map/fold/pallas_call | solution.py:351
  6.7 0.7 %collective-permute-start.1 = (bf16[65,16,128]{2,1,0:T(8,128)(2,1)S(1)}, bf16[65,16,128]{2,1,0:T(8,128)(2,1)S(1)}, u32[]{:S(2)}, u32[]{:S(2)}) collective-permute-start(bf16[65,16,128]{2,1,0:T(8,128)(2,1)S(1)} %fold.3), channel_id=1, source_target_pairs={{0,28},{4,0},{8,4},{12,8},{16,12},{20,16},{24,20},{28,24},{1,29},{... | collective-permute-start | bytes 798728 | tf_op jit(solution)/shard_map/ppermute | solution.py:361
  7.4 5.0 %first_coupled.1 = (bf16[32,1024,128]{2,1,0:T(8,128)(2,1)S(1)}, bf16[256,256]{1,0:T(8,128)(2,1)S(1)}, f32[1024,128]{1,0:T(8,128)S(1)}) custom-call(bf16[128,8,128]{2,1,0:T(8,128)(2,1)S(1)} %bitcast.14, bf16[32,8,8,32]{3,2,1,0:T(8,128)(2,1)S(1)} %bitcast.13, bf16[128,32,128]{2,1,0:T(8,128)(2,1)S(1)} %bitcast.11), custom_call_target="tpu_custom_call" | custom-call | flops 4294967296 | bytes 8388608 | tf_op jit(solution)/shard_map/first_coupled/pallas_call | solution.py:362
  12.4 0.0 collective-permute-done.folded_ref
  12.4 0.4 unfold.2.refs_0_.refs_4_
  12.8 0.0 collective-permute-done.1.folded_ref
  12.8 0.4 unfold.3.refs_1_.refs_5_
  13.2 0.7 %image_first.1 = bf16[256,128]{1,0:T(8,128)(2,1)S(1)} custom-call(bf16[32,1024,128]{2,1,0:T(8,128)(2,1)S(1)} %get-tuple-element.24.coupled_ref, bf16[2048,128]{1,0:T(8,128)(2,1)S(1)} %unfold.2.refs_0_.refs_4_, bf16[2048,128]{1,0:T(8,128)(2,1)S(1)} %unfold.3.refs_1_.refs_5_), custom_call_target="tpu_custom_call" | custom-call | flops 268435456 | bytes 8388608 | tf_op jit(solution)/shard_map/image_first/pallas_call | solution.py:390
  13.9 3.7 %collective-permute-start.2 = (bf16[256,128]{1,0:T(8,128)(2,1)S(1)}, bf16[256,128]{1,0:T(8,128)(2,1)S(1)}, u32[]{:S(2)}, u32[]{:S(2)}) collective-permute-start(bf16[256,128]{1,0:T(8,128)(2,1)S(1)} %image_first.1), channel_id=1, source_target_pairs={{0,3},{1,2},{2,1},{3,0},{4,7},{5,6},{6,5},{7,4},{8,11},{9,10},{10,... | collective-permute-start | bytes 196616 | tf_op jit(solution)/shard_map/ppermute | solution.py:327
  17.5 1.2 %image_rest.1 = (bf16[256,128]{1,0:T(8,128)(2,1)S(1)}, bf16[256,128]{1,0:T(8,128)(2,1)S(1)}) custom-call(bf16[32,1024,128]{2,1,0:T(8,128)(2,1)S(1)} %get-tuple-element.24.coupled_ref, bf16[2048,128]{1,0:T(8,128)(2,1)S(1)} %unfold.2.refs_0_.refs_4_, bf16[2048,128]{1,0:T(8,128)(2,1)S(1)} %unfold.3.refs_1_.refs_5_), custom_call_target="tpu_custom_call" | custom-call | flops 536870912 | bytes 8388608 | tf_op jit(solution)/shard_map/image_rest/pallas_call | solution.py:390
  18.8 0.1 collective-permute-start.3
  18.8 0.8 %collective-permute-start.4 = (bf16[256,128]{1,0:T(8,128)(2,1)S(1)}, bf16[256,128]{1,0:T(8,128)(2,1)S(1)}, u32[]{:S(2)}, u32[]{:S(2)}) collective-permute-start(bf16[256,128]{1,0:T(8,128)(2,1)S(1)} %get-tuple-element.26), channel_id=1, source_target_pairs={{0,1},{1,0},{2,3},{3,2},{4,5},{5,4},{6,7},{7,6},{8,9},{9,8},{10,11... | collective-permute-start | bytes 196616 | tf_op jit(solution)/shard_map/ppermute | solution.py:327
  19.6 0.4 collective-permute-done.2.arrived_ref
  20.0 0.7 %image_own.1.own_ref = f32[256,128]{1,0:T(8,128)S(1)} custom-call(bf16[256,128]{1,0:T(8,128)(2,1)S(1)} %collective-permute-done.2.arrived_ref, bf16[32,1024,128]{2,1,0:T(8,128)(2,1)S(1)} %get-tuple-element.24.coupled_ref, bf16[2048,128]{1,0:T(8,128)(2,1)S(1)} %unfold.2.refs_0_.refs_4_, bf16[2048,128]{1,0:T(8,128)(2,1)S(1)} %unfold.3.refs_1_.refs_5_), custom_call_target="tpu_custom_call" | custom-call | flops 268435456 | bytes 8388608 | tf_op jit(solution)/shard_map/image_own/pallas_call | solution.py:412
  20.7 3.3 %collective-permute-done.3.refs_0_ = bf16[256,128]{1,0:T(8,128)(2,1)S(1)} collective-permute-done((bf16[256,128]{1,0:T(8,128)(2,1)S(1)}, bf16[256,128]{1,0:T(8,128)(2,1)S(1)}, u32[]{:S(2)}, u32[]{:S(2)}) %collective-permute-start.3) | collective-permute-done | bytes 65568 | tf_op jit(solution)/shard_map/ppermute | solution.py:327
  24.1 0.0 collective-permute-done.4.refs_1_
  24.1 0.6 %collective-permute-start.7 = (bf16[256,128]{1,0:T(8,128)(2,1)S(1)}, bf16[256,128]{1,0:T(8,128)(2,1)S(1)}, u32[]{:S(2)}, u32[]{:S(2)}) collective-permute-start(bf16[256,128]{1,0:T(8,128)(2,1)S(1)} %sum.1.refs_3_), channel_id=1, source_target_pairs={{0,1},{1,0},{2,3},{3,2},{4,5},{5,4},{6,7},{7,6},{8,9},{9,8},{10,11... | collective-permute-start | bytes 196616 | tf_op jit(solution)/shard_map/ppermute | solution.py:327
  24.7 2.2 %collective-permute-start.6 = (bf16[256,128]{1,0:T(8,128)(2,1)S(1)}, bf16[256,128]{1,0:T(8,128)(2,1)S(1)}, u32[]{:S(2)}, u32[]{:S(2)}) collective-permute-start(bf16[256,128]{1,0:T(8,128)(2,1)S(1)} %sum.1.refs_3_), channel_id=1, source_target_pairs={{0,2},{1,3},{2,0},{3,1},{4,6},{5,7},{6,4},{7,5},{8,10},{9,11},{10,... | collective-permute-start | bytes 196616 | tf_op jit(solution)/shard_map/ppermute | solution.py:327
  26.9 1.7 %collective-permute-start.5 = (bf16[256,128]{1,0:T(8,128)(2,1)S(1)}, bf16[256,128]{1,0:T(8,128)(2,1)S(1)}, u32[]{:S(2)}, u32[]{:S(2)}) collective-permute-start(bf16[256,128]{1,0:T(8,128)(2,1)S(1)} %sum.1.refs_3_), channel_id=1, source_target_pairs={{0,3},{1,2},{2,1},{3,0},{4,7},{5,6},{6,5},{7,4},{8,11},{9,10},{10,... | collective-permute-start | bytes 196616 | tf_op jit(solution)/shard_map/ppermute | solution.py:327
  28.6 1.6 %grow_first.1 = (f32[128,32,128]{2,1,0:T(8,128)S(1)}, bf16[128,1024]{1,0:T(8,128)(2,1)S(1)}) custom-call(f32[1024,128]{1,0:T(8,128)S(1)} %get-tuple-element.27.refs_6_.basis_ref.refs_5_, bf16[32,1024,128]{2,1,0:T(8,128)(2,1)S(1)} %get-tuple-element.24.coupled_ref), custom_call_target="tpu_custom_call" | custom-call | flops 2147483648 | bytes 8388608 | tf_op jit(solution)/shard_map/grow_first/pallas_call | solution.py:403
  30.2 1.4 %collective-permute-done.6.refs_1_ = bf16[256,128]{1,0:T(8,128)(2,1)S(1)} collective-permute-done((bf16[256,128]{1,0:T(8,128)(2,1)S(1)}, bf16[256,128]{1,0:T(8,128)(2,1)S(1)}, u32[]{:S(2)}, u32[]{:S(2)}) %collective-permute-start.6) | collective-permute-done | bytes 65568 | tf_op jit(solution)/shard_map/ppermute | solution.py:327
  31.6 1.4 %collective-permute-done.5.refs_0_ = bf16[256,128]{1,0:T(8,128)(2,1)S(1)} collective-permute-done((bf16[256,128]{1,0:T(8,128)(2,1)S(1)}, bf16[256,128]{1,0:T(8,128)(2,1)S(1)}, u32[]{:S(2)}, u32[]{:S(2)}) %collective-permute-start.5) | collective-permute-done | bytes 65568 | tf_op jit(solution)/shard_map/ppermute | solution.py:327
  33.0 7.6 %second_image.1 = (bf16[32,1024,128]{2,1,0:T(8,128)(2,1)S(1)}, f32[1024,128]{1,0:T(8,128)S(1)}, f32[8,128]{1,0:T(8,128)S(1)}, bf16[272,128]{1,0:T(8,128)(2,1)S(1...) custom-call(bf16[256,128]{1,0:T(8,128)(2,1)S(1)} %collective-permute-done.5.refs_0_, ...), custom_call_target="tpu_custom_call" | custom-call | tf_op jit(solution)/shard_map/second_image/pallas_call | solution.py:430
  40.6 1.7 %collective-permute-start.8 = (bf16[272,128]{1,0:T(8,128)(2,1)S(1)}, bf16[272,128]{1,0:T(8,128)(2,1)S(1)}, u32[]{:S(2)}, u32[]{:S(2)}) collective-permute-start(bf16[272,128]{1,0:T(8,128)(2,1)S(1)} %get-tuple-element.29), channel_id=1, source_target_pairs={{0,3},{1,2},{2,1},{3,0},{4,7},{5,6},{6,5},{7,4},{8,11},{9,10},{10,... | collective-permute-start | bytes 208904 | tf_op jit(solution)/shard_map/ppermute | solution.py:327
  42.3 0.0 collective-permute-start.9
  42.3 2.6 %collective-permute-start.10 = (bf16[272,128]{1,0:T(8,128)(2,1)S(1)}, bf16[272,128]{1,0:T(8,128)(2,1)S(1)}, u32[]{:S(2)}, u32[]{:S(2)}) collective-permute-start(bf16[272,128]{1,0:T(8,128)(2,1)S(1)} %get-tuple-element.31), channel_id=1, source_target_pairs={{0,1},{1,0},{2,3},{3,2},{4,5},{5,4},{6,7},{7,6},{8,9},{9,8},{10,11... | collective-permute-start | bytes 208904 | tf_op jit(solution)/shard_map/ppermute | solution.py:327
  45.0 2.9 %grow_second.1 = (f32[128,32,128]{2,1,0:T(8,128)S(1)}, f32[128,32,128]{2,1,0:T(8,128)S(1)}) custom-call(bf16[128,1024]{1,0:T(8,128)(2,1)S(1)} %get-tuple-element.36.basis_turned_ref, f32[1024,128]{1,0:T(8,128)S(1)} %get-tuple-element.34.second_ref.refs_6_, bf16[32,1024,128]{2,1,0:T(8,128)(2,1)S(1)} %get-tuple-element.37.coupled_ref), custom_call_target="tpu_custom_call" | custom-call | flops 4294967296 | bytes 16777216 | tf_op jit(solution)/shard_map/grow_second/pallas_call | solution.py:446
  47.9 0.3 collective-permute-done.9.refs_1_
  48.2 0.0 collective-permute-done.10.refs_2_
  48.2 1.5 %last.1 = (bf16[128,8,128]{2,1,0:T(8,128)(2,1)}, bf16[128,32,128]{2,1,0:T(8,128)(2,1)}, f32[1,128]{1,0:T(1,128)}, f32[32,8,128]{2,1,0:T(8,128)}) custom-call(bf16[272,128]{1,0:T(8,128)(2,1)S(1)} %collective-permute-done.8.refs_0_, bf16[272,128]{1,0:T(8,128)(2,1)S(1)} %collective-permute-done.9.refs_1_, bf16[272,128]{1,0:T(8,128)(2,1)S(1)} %collective-permute-done.10.refs_2_, ...), custom_call_target="tpu_custom_call" | custom-call | tf_op jit(solution)/shard_map/last/pallas_call | solution.py:462
  (9 shorter events, 0.0 us)
Async XLA Ops:
  0.6 6.8 %copy-start.2 = (bf16[1,128,8,128]{3,2,1,0:T(8,128)(2,1)S(1)}, bf16[1,128,8,128]{3,2,1,0:T(8,128)(2,1)}, u32[]{:S(2)}) copy-start(bf16[1,128,8,128]{3,2,1,0:T(8,128)(2,1)} %param.7) | copy-start | bytes 786436
  0.6 6.8 %copy-start.1 = (bf16[1,32,32,8,8]{2,4,3,1,0:T(8,128)(2,1)S(1)}, bf16[1,32,32,8,8]{2,4,3,1,0:T(8,128)(2,1)}, u32[]{:S(2)}) copy-start(bf16[1,32,32,8,8]{2,4,3,1,0:T(8,128)(2,1)} %param.6) | copy-start | bytes 393220
  0.7 6.7 %copy-start = (bf16[1,128,32,128]{3,2,1,0:T(8,128)(2,1)S(1)}, bf16[1,128,32,128]{3,2,1,0:T(8,128)(2,1)}, u32[]{:S(2)}) copy-start(bf16[1,128,32,128]{3,2,1,0:T(8,128)(2,1)} %param.4) | copy-start | bytes 3145732
  2.0 10.4 %collective-permute-start = (bf16[65,16,128]{2,1,0:T(8,128)(2,1)S(1)}, bf16[65,16,128]{2,1,0:T(8,128)(2,1)S(1)}, u32[]{:S(2)}, u32[]{:S(2)}) collective-permute-start(bf16[65,16,128]{2,1,0:T(8,128)(2,1)S(1)} %fold.2), channel_id=1, source_target_pairs={{0,28},{4,0},{8,4},{12,8},{16,12},{20,16},{24,20},{28,24},{1,29},{... | collective-permute-start | bytes 798728 | tf_op jit(solution)/shard_map/ppermute | solution.py:361
  6.7 6.1 %collective-permute-start.1 = (bf16[65,16,128]{2,1,0:T(8,128)(2,1)S(1)}, bf16[65,16,128]{2,1,0:T(8,128)(2,1)S(1)}, u32[]{:S(2)}, u32[]{:S(2)}) collective-permute-start(bf16[65,16,128]{2,1,0:T(8,128)(2,1)S(1)} %fold.3), channel_id=1, source_target_pairs={{0,28},{4,0},{8,4},{12,8},{16,12},{20,16},{24,20},{28,24},{1,29},{... | collective-permute-start | bytes 798728 | tf_op jit(solution)/shard_map/ppermute | solution.py:361
  13.9 6.2 %collective-permute-start.2 = (bf16[256,128]{1,0:T(8,128)(2,1)S(1)}, bf16[256,128]{1,0:T(8,128)(2,1)S(1)}, u32[]{:S(2)}, u32[]{:S(2)}) collective-permute-start(bf16[256,128]{1,0:T(8,128)(2,1)S(1)} %image_first.1), channel_id=1, source_target_pairs={{0,3},{1,2},{2,1},{3,0},{4,7},{5,6},{6,5},{7,4},{8,11},{9,10},{10,... | collective-permute-start | bytes 196616 | tf_op jit(solution)/shard_map/ppermute | solution.py:327
  18.8 5.3 %collective-permute-start.3 = (bf16[256,128]{1,0:T(8,128)(2,1)S(1)}, bf16[256,128]{1,0:T(8,128)(2,1)S(1)}, u32[]{:S(2)}, u32[]{:S(2)}) collective-permute-start(bf16[256,128]{1,0:T(8,128)(2,1)S(1)} %get-tuple-element.25), channel_id=1, source_target_pairs={{0,2},{1,3},{2,0},{3,1},{4,6},{5,7},{6,4},{7,5},{8,10},{9,11},{10,... | collective-permute-start | bytes 196616 | tf_op jit(solution)/shard_map/ppermute | solution.py:327
  18.8 5.2 %collective-permute-start.4 = (bf16[256,128]{1,0:T(8,128)(2,1)S(1)}, bf16[256,128]{1,0:T(8,128)(2,1)S(1)}, u32[]{:S(2)}, u32[]{:S(2)}) collective-permute-start(bf16[256,128]{1,0:T(8,128)(2,1)S(1)} %get-tuple-element.26), channel_id=1, source_target_pairs={{0,1},{1,0},{2,3},{3,2},{4,5},{5,4},{6,7},{7,6},{8,9},{9,8},{10,11... | collective-permute-start | bytes 196616 | tf_op jit(solution)/shard_map/ppermute | solution.py:327
  24.1 6.0 %collective-permute-start.7 = (bf16[256,128]{1,0:T(8,128)(2,1)S(1)}, bf16[256,128]{1,0:T(8,128)(2,1)S(1)}, u32[]{:S(2)}, u32[]{:S(2)}) collective-permute-start(bf16[256,128]{1,0:T(8,128)(2,1)S(1)} %sum.1.refs_3_), channel_id=1, source_target_pairs={{0,1},{1,0},{2,3},{3,2},{4,5},{5,4},{6,7},{7,6},{8,9},{9,8},{10,11... | collective-permute-start | bytes 196616 | tf_op jit(solution)/shard_map/ppermute | solution.py:327
  24.7 6.9 %collective-permute-start.6 = (bf16[256,128]{1,0:T(8,128)(2,1)S(1)}, bf16[256,128]{1,0:T(8,128)(2,1)S(1)}, u32[]{:S(2)}, u32[]{:S(2)}) collective-permute-start(bf16[256,128]{1,0:T(8,128)(2,1)S(1)} %sum.1.refs_3_), channel_id=1, source_target_pairs={{0,2},{1,3},{2,0},{3,1},{4,6},{5,7},{6,4},{7,5},{8,10},{9,11},{10,... | collective-permute-start | bytes 196616 | tf_op jit(solution)/shard_map/ppermute | solution.py:327
  26.9 6.1 %collective-permute-start.5 = (bf16[256,128]{1,0:T(8,128)(2,1)S(1)}, bf16[256,128]{1,0:T(8,128)(2,1)S(1)}, u32[]{:S(2)}, u32[]{:S(2)}) collective-permute-start(bf16[256,128]{1,0:T(8,128)(2,1)S(1)} %sum.1.refs_3_), channel_id=1, source_target_pairs={{0,3},{1,2},{2,1},{3,0},{4,7},{5,6},{6,5},{7,4},{8,11},{9,10},{10,... | collective-permute-start | bytes 196616 | tf_op jit(solution)/shard_map/ppermute | solution.py:327
  40.6 7.3 %collective-permute-start.8 = (bf16[272,128]{1,0:T(8,128)(2,1)S(1)}, bf16[272,128]{1,0:T(8,128)(2,1)S(1)}, u32[]{:S(2)}, u32[]{:S(2)}) collective-permute-start(bf16[272,128]{1,0:T(8,128)(2,1)S(1)} %get-tuple-element.29), channel_id=1, source_target_pairs={{0,3},{1,2},{2,1},{3,0},{4,7},{5,6},{6,5},{7,4},{8,11},{9,10},{10,... | collective-permute-start | bytes 208904 | tf_op jit(solution)/shard_map/ppermute | solution.py:327
  42.3 5.9 %collective-permute-start.9 = (bf16[272,128]{1,0:T(8,128)(2,1)S(1)}, bf16[272,128]{1,0:T(8,128)(2,1)S(1)}, u32[]{:S(2)}, u32[]{:S(2)}) collective-permute-start(bf16[272,128]{1,0:T(8,128)(2,1)S(1)} %get-tuple-element.30), channel_id=1, source_target_pairs={{0,2},{1,3},{2,0},{3,1},{4,6},{5,7},{6,4},{7,5},{8,10},{9,11},{10,... | collective-permute-start | bytes 208904 | tf_op jit(solution)/shard_map/ppermute | solution.py:327
  42.3 5.9 %collective-permute-start.10 = (bf16[272,128]{1,0:T(8,128)(2,1)S(1)}, bf16[272,128]{1,0:T(8,128)(2,1)S(1)}, u32[]{:S(2)}, u32[]{:S(2)}) collective-permute-start(bf16[272,128]{1,0:T(8,128)(2,1)S(1)} %get-tuple-element.31), channel_id=1, source_target_pairs={{0,1},{1,0},{2,3},{3,2},{4,5},{5,4},{6,7},{7,6},{8,9},{9,8},{10,11... | collective-permute-start | bytes 208904 | tf_op jit(solution)/shard_map/ppermute | solution.py:327
